TPU v7x, 512 devices: a whole 4x4x16 slice. The times are simulated.
512 devices in a mesh: expert: 32 (over y, z_hi, x), tensor: 16 (over z_lo, core).
Axes of the slice: x: 4, y: 4, z: 16 (z_hi: 2, z_lo: 8; z = z_hi * 8 + z_lo), core: 2. Of those that a mesh axis runs over, the one named last changes fastest.
Arguments:
- tokens: bfloat16 [2048, 3616], P('expert', 'tensor'), may hold values from -6 to 6
- gate_codes: int32 [2048, 8], P('expert'), may hold values from 1 to 1023
- routes: int32 [2048, 8], P('expert'), may hold values from 0 to 31, all different within a row; in each aligned block of 64 rows (0 to 63, 64 to 127, ...) at most 32 rows name the same one
- routed_gate: bfloat16 [32, 3616, 2048], P('expert', None, 'tensor'), may hold values from -0.09375 to 0.09375
- routed_up: bfloat16 [32, 3616, 2048], P('expert', None, 'tensor'), may hold values from -0.09375 to 0.09375
- routed_down: bfloat16 [32, 2048, 3616], P('expert', 'tensor'), may hold values from -0.125 to 0.125
- shared_gate: bfloat16 [3616, 2048], P('expert', 'tensor'), may hold values from -0.09375 to 0.09375
- shared_up: bfloat16 [3616, 2048], P('expert', 'tensor'), may hold values from -0.09375 to 0.09375
- shared_down: bfloat16 [2048, 3616], P('tensor', 'expert'), may hold values from -0.125 to 0.125
Outputs:
- mixed: bfloat16 [2048, 3616], P('expert', 'tensor')
Inputs may be any that keep to these rules, and one draw needn't show every extreme that they name: `routes`: within the 64 rows of one device no expert is named by more than 32 rows, a bound that some block reaches; the 8 experts of a row differ.
All inputs are finite; a program needn't handle non-finite values.
Results may differ from a plain program's by a relative error of at most 0.023.
Values may be sent and summed in bfloat16 or wider, within the bound.
No kernel may reach another device: no remote copies, remote signals or barrier semaphores. Data moves between devices by JAX's collectives and lax.ppermute only.
A program may use at most 64 MiB of HBM per device.

v0:
```python
import jax
import jax.numpy as jnp
from jax import lax
from jax.sharding import PartitionSpec as P


def local(
    tokens,
    gate_codes,
    routes,
    routed_gate,
    routed_up,
    routed_down,
    shared_gate,
    shared_up,
    shared_down,
):
    expert_count = lax.axis_size("expert")
    tok_count = tokens.shape[0]
    top_count = routes.shape[1]
    capacity = min(tok_count, tok_count * top_count * 2 // expert_count)
    feature_width = tokens.shape[1]
    buffer_rows = expert_count * capacity
    full_gate, full_up, full_down = (
        lax.all_gather(shared_gate, "expert", axis=0, tiled=True),
        lax.all_gather(shared_up, "expert", axis=0, tiled=True),
        lax.all_gather(shared_down, "expert", axis=1, tiled=True),
    )
    onehot = (
        routes[:, :, None] == jnp.arange(expert_count, dtype=jnp.int32)[None, None, :]
    ).astype(jnp.int32)
    counts = jnp.sum(onehot, axis=1)
    before = jnp.cumsum(counts, axis=0) - counts
    slot_index = jnp.sum(onehot * before[:, None, :], axis=2)
    target_rows = routes * capacity + slot_index
    matches = target_rows[None, :, :] == jnp.arange(buffer_rows, dtype=jnp.int32)[:, None, None]
    placer = jnp.any(matches, axis=2).astype(jnp.bfloat16)
    gate_values = gate_codes.astype(jnp.float32)
    weights = 2.5 * gate_values / jnp.sum(gate_values, axis=1, keepdims=True)
    w_gate = routed_gate[0]
    w_up = routed_up[0]
    w_down = routed_down[0]
    shard_piece = lax.all_gather(tokens, "tensor", axis=1, tiled=True)
    gate_rows = full_gate
    up_rows = full_up
    shared_gate_acts = jnp.dot(shard_piece, gate_rows, preferred_element_type=jnp.float32)
    shared_up_acts = jnp.dot(shard_piece, up_rows, preferred_element_type=jnp.float32)
    outgoing = jnp.dot(placer, tokens, preferred_element_type=jnp.float32).astype(jnp.bfloat16)
    outgoing = outgoing.reshape(expert_count, capacity, feature_width)
    arrived = lax.all_to_all(outgoing, "expert", split_axis=0, concat_axis=0, tiled=True)
    row_block = arrived.reshape(buffer_rows, feature_width)
    shard_piece = lax.all_gather(row_block, "tensor", axis=1, tiled=True)
    gate_rows = w_gate
    up_rows = w_up
    expert_gate = jnp.dot(shard_piece, gate_rows, preferred_element_type=jnp.float32)
    expert_up = jnp.dot(shard_piece, up_rows, preferred_element_type=jnp.float32)
    expert_hidden = (jax.nn.silu(expert_gate) * expert_up).astype(jnp.bfloat16)
    summed = lax.psum_scatter(
        lax.dot_general(
            w_down, expert_hidden, (((0,), (1,)), ((), ())), preferred_element_type=jnp.float32
        ).astype(jnp.bfloat16),
        "tensor",
        scatter_dimension=0,
        tiled=True,
    ).astype(jnp.float32)
    expert_rows = (
        jnp.transpose(summed).astype(jnp.bfloat16).reshape(expert_count, capacity, feature_width)
    )
    returned = lax.all_to_all(
        expert_rows, "expert", split_axis=0, concat_axis=0, tiled=True
    ).reshape(buffer_rows, feature_width)
    picked = returned[target_rows.reshape(-1)].reshape(tok_count, top_count, feature_width)
    combined = jnp.sum(weights[:, :, None] * picked.astype(jnp.float32), axis=1)
    shared_hidden = (jax.nn.silu(shared_gate_acts) * shared_up_acts).astype(jnp.bfloat16)
    shared_partial = jnp.dot(shared_hidden, full_down, preferred_element_type=jnp.float32)
    shared_out = lax.psum_scatter(
        shared_partial.astype(jnp.bfloat16), "tensor", scatter_dimension=1, tiled=True
    ).astype(jnp.float32)
    return (shared_out + combined).astype(jnp.bfloat16)


def solution(mesh):
    in_specs = (
        P("expert", "tensor"),
        P("expert", None),
        P("expert", None),
        P("expert", None, "tensor"),
        P("expert", None, "tensor"),
        P("expert", "tensor", None),
        P("expert", "tensor"),
        P("expert", "tensor"),
        P("tensor", "expert"),
    )
    out_specs = P("expert", "tensor")
    return jax.shard_map(local, mesh=mesh, in_specs=in_specs, out_specs=out_specs, check_vma=False)
```

profile of v0, /device:TPU:1, one launch (start us, length us, event | category | flops | bytes accessed | tf_op | source)
XLA Modules:
  0.0 910.0 jit_solution(12521421800269920313)
XLA Ops:
  6.5 0.8 convert_reduce_fusion
  7.3 0.1 copy.32
  7.4 0.1 reduce_window_sum.11
  7.5 0.1 copy.34
  7.6 0.7 select_reduce_fusion
  8.3 0.7 multiply_add_fusion
  9.0 0.1 copy.35
  9.1 0.7 fusion.2
  9.8 1.1 convolution_convert_fusion.2
  10.9 0.2 copy.36
  11.1 40.0 %all_to_all.10 = bf16[32,32,226]{2,1,0:T(8,128)(2,1)S(1)} all-to-all(bf16[32,32,226]{2,1,0:T(8,128)(2,1)S(1)} %bitcast.51), channel_id=1, replica_groups=mesh['expert'=32,'tensor'=16] {'expert'}, dimensions={0} | all-to-all | bytes 925696 | tf_op jit(solution)/shard_map/all_to_all | solution.py:50
  51.1 1.0 copy.37
  52.1 0.0 all-gather.7.cloned.1.call-update
  52.1 153.5 %all-gather.1 = bf16[32,113,128]{2,1,0:T(8,128)(2,1)S(1)} all-gather(bf16[1,113,128]{2,1,0:T(8,128)(2,1)} %bitcast.54), channel_id=1, replica_groups=mesh['expert'=32,'tensor'=16] {'expert'}, dimensions={0}, use_global_device_ids=true | all-gather | bytes 954624 | tf_op jit(solution)/shard_map/all_gather | solution.py:25
  205.5 7.3 reshape.82
  212.9 5.5 fusion.8
  218.4 0.0 copy-done
  218.4 0.0 copy-done.1
  218.4 12.3 %fusion.1 = bf16[3616,1024]{1,0:T(8,128)(2,1)} fusion(bf16[3616,1024]{1,0:T(8,128)(2,1)} %reshape.82, bf16[1,128,3616]{1,2,0:T(8,128)(2,1)S(1)} %copy-done, bf16[1,3616,128]{2,1,0:T(8,128)(2,1)S(1)} %copy-done.1, f32[1024,128]{1,0:T(8,128)S(1)} %fusion.8), kind=kOutput, calls=%fused_computation.2 | convolution fusion | flops 1900314624 | bytes 17186816 | tf_op jit(solution)/shard_map/dot_general | solution.py:59
  230.7 107.5 %fusion = bf16[232,1024]{1,0:T(8,128)(2,1)S(1)} fusion(bf16[3616,1024]{1,0:T(8,128)(2,1)} %fusion.1), kind=kCustom, calls=%all-reduce-scatter | all-reduce-scatter fusion | flops 3801089 | bytes 7882752
  338.3 0.0 copy-start.4
  338.3 4.4 collective-permute-start
  342.8 149.8 %all-gather.2 = bf16[32,113,128]{2,1,0:T(8,128)(2,1)} all-gather(bf16[1,113,128]{2,1,0:T(8,128)(2,1)S(1)} %bitcast.55), channel_id=1, replica_groups=mesh['expert'=32,'tensor'=16] {'expert'}, dimensions={0}, use_global_device_ids=true | all-gather | bytes 954624 | tf_op jit(solution)/shard_map/all_gather | solution.py:26
  492.6 0.7 fusion.25
  493.9 0.0 collective-permute-done
  493.9 0.8 concatenate
  494.7 0.1 constant_dynamic-slice_fusion
  494.9 1.0 copy.38
  495.9 4.0 all-to-all-start.1
  499.9 0.0 all-reduce.5.cloned.1.call-start
  499.9 0.0 copy-done.2
  500.0 45.6 %all-gather = bf16[16,226,64]{1,2,0:T(8,128)(2,1)S(1)} all-gather(bf16[1,226,64]{1,2,0:T(8,128)(2,1)S(1)} %bitcast.53), channel_id=1, replica_groups=mesh['expert'=32,'tensor'=16] {'tensor'}, dimensions={0}, use_global_device_ids=true | all-gather | bytes 491776 | tf_op jit(solution)/shard_map/all_gather | solution.py:43
  545.6 0.3 copy.30
  545.9 0.7 reshape.74
  546.6 1.2 reshape.76
  547.8 2.3 reshape.78
  550.1 153.0 %all-gather.3 = bf16[32,113,128]{2,1,0:T(8,128)(2,1)S(1)} all-gather(bf16[1,113,128]{2,1,0:T(8,128)(2,1)S(1)} %bitcast.56), channel_id=1, replica_groups=mesh['expert'=32,'tensor'=16] {'expert'}, dimensions={0}, use_global_device_ids=true | all-gather | bytes 954624 | tf_op jit(solution)/shard_map/all_gather | solution.py:27
  703.2 1.2 reshape.80
  704.4 1.5 fusion.26
  705.9 3.0 convolution_convert_fusion.1
  708.9 0.0 all-reduce.5.cloned.1.call-update
  708.9 0.1 reshape.63
  709.1 0.1 copy.31
  709.8 0.0 all-to-all-done.1
  709.8 2.0 gather_fusion
  711.8 0.2 fusion.10
  712.0 189.6 %all-reduce.5.cloned.1.call-done = bf16[64,3616]{1,0:T(8,128)(2,1)} async-done(((bf16[64,3616]{1,0:T(8,128)(2,1)}), bf16[64,3616]{1,0:T(8,128)(2,1)}) %all-reduce.5.cloned.1.call-update) | async-done | bytes 462864
  901.7 1.5 add_convert_fusion
  (18 shorter events, 0.1 us)
Async XLA Ops:
  6.5 211.9 %copy-start = (bf16[1,128,3616]{1,2,0:T(8,128)(2,1)S(1)}, bf16[1,128,3616]{1,2,0:T(8,128)(2,1)}, u32[]{:S(2)}) copy-start(bf16[1,128,3616]{1,2,0:T(8,128)(2,1)} %param.14) | copy-start | bytes 2777092
  6.5 199.0 %all-gather.7.cloned.1.call-start = ((), (), s32[]{:S(2)}) async-start(), calls=%async_computation.2 | async-start | bytes 8077312 | tf_op jit(solution)/shard_map/all_gather | solution.py:52
  212.9 5.6 copy-start.1
  230.7 112.0 %copy-start.3 = (bf16[113,128]{1,0:T(8,128)(2,1)S(1)}, bf16[113,128]{1,0:T(8,128)(2,1)}, u32[]{:S(2)}) copy-start(bf16[113,128]{1,0:T(8,128)(2,1)} %param.16) | copy-start | bytes 86788
  230.7 261.8 %copy-start.6 = (u32[512]{0:T(512)S(1)}, u32[512]{0:T(512)}, u32[]{:S(2)}) copy-start(u32[512]{0:T(512)} %constant.31) | copy-start | bytes 6148
  230.7 269.2 %copy-start.2 = (bf16[64,226]{1,0:T(8,128)(2,1)S(1)}, bf16[64,226]{1,0:T(8,128)(2,1)}, u32[]{:S(2)}) copy-start(bf16[64,226]{1,0:T(8,128)(2,1)} %param.9) | copy-start | bytes 86788
  338.3 211.9 %copy-start.4 = (bf16[128,113]{0,1:T(8,128)(2,1)S(1)}, bf16[128,113]{0,1:T(8,128)(2,1)}, u32[]{:S(2)}) copy-start(bf16[128,113]{0,1:T(8,128)(2,1)} %param.17) | copy-start | bytes 86788
  338.3 155.6 %collective-permute-start = (bf16[90,1024]{1,0:T(8,128)(2,1)S(1)}, bf16[90,1024]{1,0:T(8,128)(2,1)S(1)}, u32[]{:S(2)}, u32[]{:S(2)}) collective-permute-start(bf16[90,1024]{1,0:T(8,128)(2,1)S(1)} %slice.2), channel_id=1, source_target_pairs={{0,1},{1,2},{2,3},{3,4},{4,5},{5,6},{6,7},{7,8},{8,9},{9,10},{10,1... | collective-permute-start | bytes 552968
  495.9 213.2 %copy-start.5 = (s32[64,8]{0,1:T(8,128)S(1)}, s32[64,8]{0,1:T(8,128)}, u32[]{:S(2)}) copy-start(s32[64,8]{0,1:T(8,128)} %param.10) | copy-start | bytes 6148
  495.9 214.0 %all-to-all-start.1 = ((bf16[32,32,226]{2,1,0:T(8,128)(2,1)}), bf16[32,32,226]{2,1,0:T(8,128)(2,1)S(1)}, u32[]{:S(2)}, u32[]{:S(2)}) async-start(bf16[32,32,226]{2,1,0:T(8,128)(2,1)} %bitcast.15), calls=%async_computation.1 | async-start | bytes 1048576 | tf_op jit(solution)/shard_map/all_to_all | solution.py:69
  499.9 401.8 %all-reduce.5.cloned.1.call-start = ((), (), s32[]{:S(2)}) async-start(), calls=%async_computation.3 | async-start | bytes 950272
Sparse Core Ops, SparseCore 0:
  52.2 137.8 all-gather.6
  709.1 192.5 all-reduce.4
where the time goes:
time: 913 us; the launch traced here: 910 us
  blocking collectives  649 us (71%)
  waiting for transfers between devices  190 us (21%)
  matrix products  23.4 us (3%)
  local copies, waits for them, and re-layouts  19.3 us (2%)
  between operations  14.9 us (2%)
    unnamed x4, waiting for transfers between devices  190 us
    all_gather x1, blocking collectives, local(): lax.all_gather(shared_gate, 'expert', axis=0, tiled=True)  153 us
    all_gather x1, blocking collectives, local(): lax.all_gather(shared_down, 'expert', axis=1, tiled=True)  153 us
    all_gather x1, blocking collectives, local(): lax.all_gather(shared_up, 'expert', axis=0, tiled=True)  150 us
    unnamed x1, blocking collectives  108 us
    all_gather x1, blocking collectives, local(): shard_piece = lax.all_gather(tokens, 'tensor', axis=1, tiled=True)  45.6 us
    all_to_all x1, blocking collectives, local(): lax.all_to_all(outgoing, 'expert', split_axis=0, concat_axis=0, tiled=True)  40 us
  transfers between devices with their start and end apart: 4, of which 1 were waited for; matrix products, arithmetic and copies ran while one was open for 1% of the time, Pallas kernels for 0%

commit v1 on v0

v1 whole, which is shorter than its diff:
```python
import jax
import jax.numpy as jnp
from jax import lax
from jax.sharding import Mesh, PartitionSpec as P

Y, H, X, L, C = 4, 2, 4, 8, 2
AXES = ("y", "h", "x", "l", "c")
EXPERT = ("y", "h", "x")
TENSOR = ("l", "c")
Z = ("h", "l")
f32 = jnp.float32
bf16 = jnp.bfloat16


def shift(a, axis, k):
    return lax.ppermute(a, axis, [(j, (j + k) % 4) for j in range(4)])


def swap(a):
    return lax.ppermute(a, "c", [(0, 1), (1, 0)])


def gather4(a, axis):
    m = a.shape[0] // 2
    p, n = shift(a, axis, 1), shift(a, axis, -1)
    p2, n2 = shift(p[:m], axis, 1), shift(n[m:], axis, -1)
    return a, p, n, jnp.concatenate([p2, n2], 0)


def add(*terms):
    total = terms[0].astype(f32)
    for t in terms[1:]:
        total = total + t.astype(f32)
    return total.astype(bf16)


def scatter4(own, p, n, d, axis):
    m = d.shape[0] // 2
    rp, rn = shift(d[:m], axis, 1), shift(d[m:], axis, -1)
    to_n = jnp.concatenate([add(n[:m], rp), n[m:]], 0)
    to_p = jnp.concatenate([p[:m], add(p[m:], rn)], 0)
    return add(own, shift(to_n, axis, 1), shift(to_p, axis, -1))


def local(
    tokens,
    gate_codes,
    routes,
    routed_gate,
    routed_up,
    routed_down,
    shared_gate,
    shared_up,
    shared_down,
):
    core = lax.axis_index("c")
    expert = lax.axis_index(EXPERT)
    toks, width = tokens.shape
    half = toks // C
    feats = width * L * C
    pair = width * C
    top = routes.shape[1]

    mine = lax.dynamic_slice_in_dim(tokens, core * half, half, 0)
    theirs = lax.dynamic_slice_in_dim(tokens, (1 - core) * half, half, 0)
    other = swap(theirs)
    two = jnp.where(
        core == 0, jnp.concatenate([mine, other], 1), jnp.concatenate([other, mine], 1)
    )
    meta = jnp.concatenate([routes, gate_codes // 32, gate_codes % 32], 1).astype(bf16)
    meta = lax.dynamic_slice_in_dim(meta, core * half, half, 0)
    sent = jnp.concatenate([two, meta, jnp.zeros((half, 512 - pair - 3 * top), bf16)], 1)
    got = lax.all_gather(sent, Z, axis=0, tiled=False)
    got = got.reshape(H, L, half, 512)
    rows = got[:, :, :, :pair].transpose(0, 2, 1, 3).reshape(H * half, feats)
    metas = got[:, 0, :, pair : pair + 3 * top].reshape(H * half, 3 * top)
    full = -(-feats // 128) * 128
    rows = jnp.concatenate(
        [rows, metas, jnp.zeros((H * half, full - feats - 3 * top), bf16)], 1
    )

    w_in = [routed_gate[0], routed_up[0]]
    w_in = jnp.concatenate([w_in[0], swap(w_in[0]), w_in[1], swap(w_in[1])], 1)
    hid = routed_gate.shape[2] * C
    n_exp = Y * H * X
    units = shared_gate.shape[1] // n_exp
    depth = shared_gate.shape[0]
    s = jnp.stack([shared_gate.T, shared_up.T, shared_down]).reshape(3, n_exp, units, depth)
    s = s.transpose(1, 0, 2, 3).reshape(n_exp, 3 * units, depth)
    s = lax.all_to_all(s, EXPERT, split_axis=0, concat_axis=0, tiled=True)
    s = s.transpose(1, 0, 2).reshape(3, units, feats)
    s = jnp.concatenate([s, swap(s)], 1)
    s_hid = units * C
    s_in = s[:2].reshape(2 * s_hid, feats)
    w_out = jnp.concatenate([routed_down[0], swap(routed_down[0]), s[2]], 0)

    def apply(block):
        x = block[:, :feats]
        codes = block[:, feats : feats + 3 * top].astype(f32)
        gates = codes[:, top : 2 * top] * 32.0 + codes[:, 2 * top :]
        chosen = jnp.sum(
            jnp.where(codes[:, :top] == expert.astype(f32), gates, 0.0), axis=1, keepdims=True
        )
        weight = 2.5 * chosen / jnp.sum(gates, axis=1, keepdims=True)
        acts = jnp.dot(x, w_in, preferred_element_type=f32)
        s_acts = lax.dot_general(x, s_in, (((1,), (1,)), ((), ())), preferred_element_type=f32)
        hidden = jax.nn.silu(acts[:, :hid]) * acts[:, hid:] * weight
        s_hidden = jax.nn.silu(s_acts[:, :s_hid]) * s_acts[:, s_hid:]
        both = jnp.concatenate([hidden, s_hidden], 1).astype(bf16)
        return jnp.dot(both, w_out, preferred_element_type=f32).astype(bf16)

    def chunk(part, first, second):
        r = part.shape[0]
        near = jnp.concatenate(gather4(part, first), 0)
        outs = [apply(b) for b in gather4(near, second)]
        near = scatter4(*outs, second)
        return scatter4(*[near[i * r : (i + 1) * r] for i in range(4)], first)

    summed = [chunk(rows[:half], "y", "x"), chunk(rows[half:], "x", "y")]
    back = jnp.concatenate(summed, 0).reshape(H, half, L, pair).transpose(0, 2, 1, 3)
    back = lax.all_to_all(
        back.reshape(H * L, half, pair), Z, split_axis=0, concat_axis=0, tiled=True
    )
    done = jnp.sum(back.astype(f32), axis=0).astype(bf16)
    lo, hi = done[:, :width], done[:, width:]
    keep, give = jnp.where(core == 0, lo, hi), jnp.where(core == 0, hi, lo)
    take = swap(give)
    return jnp.where(
        core == 0, jnp.concatenate([keep, take], 0), jnp.concatenate([take, keep], 0)
    )


def solution(mesh):
    fine = Mesh(mesh.devices.reshape(Y, H, X, L, C), AXES)
    in_specs = (
        P(EXPERT, TENSOR),
        P(EXPERT, None),
        P(EXPERT, None),
        P(EXPERT, None, TENSOR),
        P(EXPERT, None, TENSOR),
        P(EXPERT, TENSOR, None),
        P(EXPERT, TENSOR),
        P(EXPERT, TENSOR),
        P(TENSOR, EXPERT),
    )
    return jax.shard_map(
        local, mesh=fine, in_specs=in_specs, out_specs=P(EXPERT, TENSOR), check_vma=False
    )
```

time: 913 us -> 346 us (0.38)
  blocking collectives: 649 us -> 53.8 us
  waiting for transfers between devices: 190 us -> 38.9 us
  starting transfers between devices: 8.45 us -> 154 us
  local copies, waits for them, and re-layouts: 19.3 us -> 38.3 us
  matrix products: 23.4 us -> 40.4 us
  between operations: 14.9 us -> 1.55 us
  other arithmetic: 4.77 us -> 16.7 us
    all_gather x4 -> x1, blocking collectives: 502 us -> 25.9 us  [local(): got = lax.all_gather(sent, Z, axis=0, tiled=False)]
    unnamed x4 -> x0, waiting for transfers between devices: 190 us -> none
    ppermute x0 -> x38, starting transfers between devices: none -> 142 us  [the longest x32 98 us: shift(): return lax.ppermute(a, axis, [(j, (j + k) % 4) for j in range(4)])]
    unnamed x1 -> x0, blocking collectives: 108 us -> none
    ppermute x0 -> x38, waiting for transfers between devices: none -> 38.9 us  [the longest x32 38 us: shift(): return lax.ppermute(a, axis, [(j, (j + k) % 4) for j in range(4)])]
    dot_general x5 -> x24, matrix products: 23.4 us -> 40.4 us  [the longest x8 19.5 us: apply(): return jnp.dot(both, w_out, preferred_element_type=f32).astype(bf16)]
    all_to_all x1, blocking collectives: 40 us -> 27.9 us  [local(): lax.all_to_all(back.reshape(H * L, half, pair), Z, split_axis=0, concat_a...]
    slice x0 -> x26, local copies, waits for them, and re-layouts: none -> 10.4 us  [the longest x8 5.89 us: scatter4(): rp, rn = (shift(d[:m], axis, 1), shift(d[m:], axis, -1))]
  transfers between devices with their start and end apart: 4 -> 39, of which waited for: 1 -> 10; matrix products, arithmetic and copies ran while one was open for 1% -> 24% of each run, Pallas kernels for 0% -> 0%
where the time goes in v1:
time: 346 us; the launch traced here: 343 us
  starting transfers between devices  154 us (45%)
  blocking collectives  53.8 us (16%)
  matrix products  40.4 us (12%)
  waiting for transfers between devices  38.9 us (11%)
  local copies, waits for them, and re-layouts  38.3 us (11%)
  other arithmetic  16.7 us (5%)
    ppermute x32, starting transfers between devices, shift(): return lax.ppermute(a, axis, [(j, (j + k) % 4) for j in range(4)])  98 us
    ppermute x6, starting transfers between devices, swap(): return lax.ppermute(a, 'c', [(0, 1), (1, 0)])  43.9 us
    ppermute x32, waiting for transfers between devices, shift(): return lax.ppermute(a, axis, [(j, (j + k) % 4) for j in range(4)])  38 us
    all_to_all x1, blocking collectives, local(): lax.all_to_all(back.reshape(H * L, half, pair), Z, split_axis=0, concat_a...  27.9 us
    all_gather x1, blocking collectives, local(): got = lax.all_gather(sent, Z, axis=0, tiled=False)  25.9 us
    dot_general x8, matrix products, apply(): return jnp.dot(both, w_out, preferred_element_type=f32).astype(bf16)  19.5 us
    dot_general x8, matrix products, apply(): acts = jnp.dot(x, w_in, preferred_element_type=f32)  15.9 us
    all_to_all x1, starting transfers between devices, local(): s = lax.all_to_all(s, EXPERT, split_axis=0, concat_axis=0, tiled=True)  11.7 us
  transfers between devices with their start and end apart: 39, of which 10 were waited for; matrix products, arithmetic and copies ran while one was open for 24% of the time, Pallas kernels for 0%

profile of v1, /device:TPU:1, one launch (start us, length us, event | category | flops | bytes accessed | tf_op | source)
XLA Modules:
  0.0 343.2 jit_solution(3862843703136357969)
XLA Ops:
  0.8 8.7 %collective-permute-start = (bf16[32,226]{1,0:T(8,128)(2,1)S(1)}, bf16[32,226]{1,0:T(8,128)(2,1)S(1)}, u32[]{:S(2)}, u32[]{:S(2)}) collective-permute-start(bf16[32,226]{1,0:T(8,128)(2,1)S(1)} %get-tuple-element.44), channel_id=1, source_target_pairs={{0,1},{1,0},{2,3},{3,2},{4,5},{5,4},{6,7},{7,6},{8,9},{9,8},{10,11... | collective-permute-start | bytes 43400 | tf_op jit(solution)/shard_map/ppermute | solution.py:20
  11.4 25.9 %all-gather = bf16[512,512]{1,0:T(8,128)(2,1)S(1)} all-gather(bf16[32,512]{1,0:T(8,128)(2,1)S(1)} %maximum_maximum_fusion), channel_id=2, replica_groups=mesh['y'=4,'h'=2,'x'=4,'l'=8,'c'=2] {'h','l'}, dimensions={0}, use_global_device_ids=true | all-gather | bytes 557056 | tf_op jit(solution)/shard_map/all_gather | solution.py:73
  39.3 4.6 %collective-permute-start.2 = (bf16[32,3712]{1,0:T(8,128)(2,1)S(1)}, bf16[32,3712]{1,0:T(8,128)(2,1)S(1)}, u32[]{:S(2)}, u32[]{:S(2)}) collective-permute-start(bf16[32,3712]{1,0:T(8,128)(2,1)S(1)} %get-tuple-element.37), channel_id=1, source_target_pairs={{0,384},{128,0},{256,128},{384,256},{1,385},{129,1},{257,129},{385... | collective-permute-start | bytes 712712 | tf_op jit(solution)/shard_map/ppermute | solution.py:16
  47.1 11.7 %all-to-all-start = ((bf16[32,12,113]{2,1,0:T(8,128)(2,1)}), bf16[32,12,113]{2,1,0:T(8,128)(2,1)S(1)}, u32[]{:S(2)}, u32[]{:S(2)}) async-start(bf16[32,12,113]{2,1,0:T(8,128)(2,1)} %copy.145), calls=%async_computation | async-start | bytes 262144 | tf_op jit(solution)/shard_map/all_to_all | solution.py:90
  58.8 9.7 %collective-permute-start.5 = (bf16[3616,128]{1,0:T(8,128)(2,1)}, bf16[3616,128]{1,0:T(8,128)(2,1)S(1)}, u32[]{:S(2)}, u32[]{:S(2)}) collective-permute-start(bf16[3616,128]{1,0:T(8,128)(2,1)} %bitcast.53), channel_id=1, source_target_pairs={{0,1},{1,0},{2,3},{3,2},{4,5},{5,4},{6,7},{7,6},{8,9},{9,8},{10,11... | collective-permute-start | bytes 2777096 | tf_op jit(solution)/shard_map/ppermute | solution.py:20
  70.5 2.4 collective-permute-start.8
  72.9 4.6 %collective-permute-start.22 = (bf16[32,3712]{1,0:T(8,128)(2,1)S(1)}, bf16[32,3712]{1,0:T(8,128)(2,1)S(1)}, u32[]{:S(2)}, u32[]{:S(2)}) collective-permute-start(bf16[32,3712]{1,0:T(8,128)(2,1)S(1)} %get-tuple-element.40), channel_id=1, source_target_pairs={{0,48},{16,0},{32,16},{48,32},{1,49},{17,1},{33,17},{49,33},{2,50}... | collective-permute-start | bytes 712712 | tf_op jit(solution)/shard_map/ppermute | solution.py:16
  79.6 8.2 %collective-permute-done.21 = bf16[32,3712]{1,0:T(8,128)(2,1)S(1)} collective-permute-done((bf16[32,3712]{1,0:T(8,128)(2,1)S(1)}, bf16[32,3712]{1,0:T(8,128)(2,1)S(1)}, u32[]{:S(2)}, u32[]{:S(2)}) %collective-permute-start.21) | collective-permute-done | bytes 237600 | tf_op jit(solution)/shard_map/ppermute | solution.py:16
  87.8 4.4 %collective-permute-start.4 = (bf16[16,3712]{1,0:T(8,128)(2,1)S(1)}, bf16[16,3712]{1,0:T(8,128)(2,1)S(1)}, u32[]{:S(2)}, u32[]{:S(2)}) collective-permute-start(bf16[16,3712]{1,0:T(8,128)(2,1)S(1)} %slice.478), channel_id=1, source_target_pairs={{0,384},{128,0},{256,128},{384,256},{1,385},{129,1},{257,129},{385... | collective-permute-start | bytes 356360 | tf_op jit(solution)/shard_map/ppermute | solution.py:16
  95.8 3.8 %collective-permute-done.3 = bf16[16,3712]{1,0:T(8,128)(2,1)S(1)} collective-permute-done((bf16[16,3712]{1,0:T(8,128)(2,1)S(1)}, bf16[16,3712]{1,0:T(8,128)(2,1)S(1)}, u32[]{:S(2)}, u32[]{:S(2)}) %collective-permute-start.3) | collective-permute-done | bytes 118816 | tf_op jit(solution)/shard_map/ppermute | solution.py:16
  101.6 4.8 %collective-permute-done.23 = bf16[16,3712]{1,0:T(8,128)(2,1)S(1)} collective-permute-done((bf16[16,3712]{1,0:T(8,128)(2,1)S(1)}, bf16[16,3712]{1,0:T(8,128)(2,1)S(1)}, u32[]{:S(2)}, u32[]{:S(2)}) %collective-permute-start.23) | collective-permute-done | bytes 118816 | tf_op jit(solution)/shard_map/ppermute | solution.py:16
  109.0 3.0 collective-permute-done.24
  112.0 6.7 %collective-permute-start.7 = (bf16[3,4,3616]{2,1,0:T(4,128)(2,1)S(1)}, bf16[3,4,3616]{2,1,0:T(4,128)(2,1)S(1)}, u32[]{:S(2)}, u32[]{:S(2)}) collective-permute-start(bf16[3,4,3616]{2,1,0:T(4,128)(2,1)S(1)} %reshape.95), channel_id=1, source_target_pairs={{0,1},{1,0},{2,3},{3,2},{4,5},{5,4},{6,7},{7,6},{8,9},{9,8},{10,11... | collective-permute-start | bytes 260360 | tf_op jit(solution)/shard_map/ppermute | solution.py:20
  122.7 4.6 %collective-permute-start.25 = (bf16[128,3712]{1,0:T(8,128)(2,1)}, bf16[128,3712]{1,0:T(8,128)(2,1)S(1)}, u32[]{:S(2)}, u32[]{:S(2)}) collective-permute-start(bf16[128,3712]{1,0:T(8,128)(2,1)} %constant_dynamic-update-slice_fusion.7), channel_id=1, source_target_pairs={{0,384},{128,0},{256,128},{384,256},{1,385},{129,1},{257,129},{385... | collective-permute-start | bytes 2850824 | tf_op jit(solution)/shard_map/ppermute | solution.py:16
  133.5 4.6 %collective-permute-start.9 = (bf16[128,3712]{1,0:T(8,128)(2,1)}, bf16[128,3712]{1,0:T(8,128)(2,1)S(1)}, u32[]{:S(2)}, u32[]{:S(2)}) collective-permute-start(bf16[128,3712]{1,0:T(8,128)(2,1)} %copy-done.7), channel_id=1, source_target_pairs={{0,48},{16,0},{32,16},{48,32},{1,49},{17,1},{33,17},{49,33},{2,50}... | collective-permute-start | bytes 2850824 | tf_op jit(solution)/shard_map/ppermute | solution.py:16
  138.0 2.2 pad_maximum_fusion
  140.3 2.7 fusion.22
  153.6 3.0 fusion.10
  156.7 2.3 convolution_convert_fusion
  162.2 4.6 %collective-permute-start.28 = (bf16[64,3712]{1,0:T(8,128)(2,1)}, bf16[64,3712]{1,0:T(8,128)(2,1)}, u32[]{:S(2)}, u32[]{:S(2)}) collective-permute-start(bf16[64,3712]{1,0:T(8,128)(2,1)} %slice.555), channel_id=1, source_target_pairs={{0,384},{128,0},{256,128},{384,256},{1,385},{129,1},{257,129},{385... | collective-permute-start | bytes 1425416 | tf_op jit(solution)/shard_map/ppermute | solution.py:16
  166.8 2.7 fusion.18
  169.6 2.2 convolution_convert_fusion.2
  175.5 2.7 fusion.26
  178.3 2.3 convolution_convert_fusion.4
  182.4 4.8 %collective-permute-start.12 = (bf16[64,3712]{1,0:T(8,128)(2,1)S(1)}, bf16[64,3712]{1,0:T(8,128)(2,1)S(1)}, u32[]{:S(2)}, u32[]{:S(2)}) collective-permute-start(bf16[64,3712]{1,0:T(8,128)(2,1)S(1)} %slice.501), channel_id=1, source_target_pairs={{0,48},{16,0},{32,16},{48,32},{1,49},{17,1},{33,17},{49,33},{2,50}... | collective-permute-start | bytes 1425416 | tf_op jit(solution)/shard_map/ppermute | solution.py:16
  187.1 2.7 fusion.34
  190.0 2.7 convolution_convert_fusion.6
  198.2 2.1 convolution_convert_fusion.5
  201.8 4.6 %collective-permute-start.15 = (bf16[64,3616]{1,0:T(8,128)(2,1)}, bf16[64,3616]{1,0:T(8,128)(2,1)}, u32[]{:S(2)}, u32[]{:S(2)}) collective-permute-start(bf16[64,3616]{1,0:T(8,128)(2,1)} %copy.158), channel_id=1, source_target_pairs={{0,48},{16,0},{32,16},{48,32},{1,49},{17,1},{33,17},{49,33},{2,50}... | collective-permute-start | bytes 1388552 | tf_op jit(solution)/shard_map/ppermute | solution.py:16
  206.5 2.3 convolution_convert_fusion.1
  211.5 2.2 collective-permute-start.31
  213.7 3.1 collective-permute-start.29
  222.5 7.8 %collective-permute-done.13 = bf16[64,3616]{1,0:T(8,128)(2,1)} collective-permute-done((bf16[64,3616]{1,0:T(8,128)(2,1)}, bf16[64,3616]{1,0:T(8,128)(2,1)}, u32[]{:S(2)}, u32[]{:S(2)}) %collective-permute-start.13) | collective-permute-done | bytes 462880 | tf_op jit(solution)/shard_map/ppermute | solution.py:16
  235.1 4.6 %collective-permute-start.16 = (bf16[128,3616]{0,1:T(8,128)(2,1)}, bf16[128,3616]{0,1:T(8,128)(2,1)}, u32[]{:S(2)}, u32[]{:S(2)}) collective-permute-start(bf16[128,3616]{0,1:T(8,128)(2,1)} %copy.159), channel_id=1, source_target_pairs={{0,48},{16,0},{32,16},{48,32},{1,49},{17,1},{33,17},{49,33},{2,50}... | collective-permute-start | bytes 2777096 | tf_op jit(solution)/shard_map/ppermute | solution.py:16
  244.9 2.2 collective-permute-start.30
  247.1 4.3 %collective-permute-start.32 = (bf16[128,3616]{0,1:T(8,128)(2,1)}, bf16[128,3616]{0,1:T(8,128)(2,1)}, u32[]{:S(2)}, u32[]{:S(2)}) collective-permute-start(bf16[128,3616]{0,1:T(8,128)(2,1)} %copy.172), channel_id=1, source_target_pairs={{0,384},{128,0},{256,128},{384,256},{1,385},{129,1},{257,129},{385... | collective-permute-start | bytes 2777096 | tf_op jit(solution)/shard_map/ppermute | solution.py:16
  251.4 2.8 collective-permute-done.14
  257.5 2.8 fusion.7
  261.0 2.5 collective-permute-start.17
  263.5 4.2 %collective-permute-start.19 = (bf16[16,3616]{1,0:T(8,128)(2,1)S(1)}, bf16[16,3616]{1,0:T(8,128)(2,1)S(1)}, u32[]{:S(2)}, u32[]{:S(2)}) collective-permute-start(bf16[16,3616]{1,0:T(8,128)(2,1)S(1)} %get-tuple-element.24), channel_id=1, source_target_pairs={{0,384},{128,0},{256,128},{384,256},{1,385},{129,1},{257,129},{385... | collective-permute-start | bytes 347144 | tf_op jit(solution)/shard_map/ppermute | solution.py:16
  271.0 2.9 fusion.3
  275.8 4.6 %collective-permute-start.35 = (bf16[16,3616]{1,0:T(8,128)(2,1)S(1)}, bf16[16,3616]{1,0:T(8,128)(2,1)S(1)}, u32[]{:S(2)}, u32[]{:S(2)}) collective-permute-start(bf16[16,3616]{1,0:T(8,128)(2,1)S(1)} %get-tuple-element.30), channel_id=1, source_target_pairs={{0,48},{16,0},{32,16},{48,32},{1,49},{17,1},{33,17},{49,33},{2,50}... | collective-permute-start | bytes 347144 | tf_op jit(solution)/shard_map/ppermute | solution.py:16
  280.6 2.7 collective-permute-start.20
  283.4 2.5 collective-permute-start.18
  286.0 3.4 collective-permute-start.36
  293.2 4.6 %collective-permute-done.34 = bf16[32,3616]{1,0:T(8,128)(2,1)S(1)} collective-permute-done((bf16[32,3616]{1,0:T(8,128)(2,1)S(1)}, bf16[32,3616]{1,0:T(8,128)(2,1)S(1)}, u32[]{:S(2)}, u32[]{:S(2)}) %collective-permute-start.34) | collective-permute-done | bytes 231456 | tf_op jit(solution)/shard_map/ppermute | solution.py:16
  299.3 27.9 %all_to_all.10 = bf16[16,32,452]{2,1,0:T(8,128)(2,1)S(1)} all-to-all(bf16[16,32,452]{2,1,0:T(8,128)(2,1)S(1)} %bitcast.50), channel_id=1, replica_groups=mesh['y'=4,'h'=2,'x'=4,'l'=8,'c'=2] {'h','l'}, dimensions={0} | all-to-all | bytes 925696 | tf_op jit(solution)/shard_map/all_to_all | solution.py:121
  327.3 14.4 %collective-permute-start.37 = (bf16[32,226]{1,0:T(8,128)(2,1)S(1)}, bf16[32,226]{1,0:T(8,128)(2,1)S(1)}, u32[]{:S(2)}, u32[]{:S(2)}) collective-permute-start(bf16[32,226]{1,0:T(8,128)(2,1)S(1)} %get-tuple-element.42), channel_id=1, source_target_pairs={{0,1},{1,0},{2,3},{3,2},{4,5},{5,4},{6,7},{7,6},{8,9},{9,8},{10,11... | collective-permute-start | bytes 43400 | tf_op jit(solution)/shard_map/ppermute | solution.py:20
  (254 shorter events, 90.5 us)
Async XLA Ops:
  0.0 45.9 %copy-start.22 = (bf16[113,128]{1,0:T(8,128)(2,1)S(1)}, bf16[113,128]{1,0:T(8,128)(2,1)}, u32[]{:S(2)}) copy-start(bf16[113,128]{1,0:T(8,128)(2,1)} %param.15) | copy-start | bytes 86788
  0.0 46.0 %copy-start.23 = (bf16[113,128]{1,0:T(8,128)(2,1)S(1)}, bf16[113,128]{1,0:T(8,128)(2,1)}, u32[]{:S(2)}) copy-start(bf16[113,128]{1,0:T(8,128)(2,1)} %param.16) | copy-start | bytes 86788
  0.0 46.1 %copy-start.24 = (bf16[128,113]{0,1:T(8,128)(2,1)S(1)}, bf16[128,113]{0,1:T(8,128)(2,1)}, u32[]{:S(2)}) copy-start(bf16[128,113]{0,1:T(8,128)(2,1)} %param.17) | copy-start | bytes 86788
  0.8 10.4 %collective-permute-start = (bf16[32,226]{1,0:T(8,128)(2,1)S(1)}, bf16[32,226]{1,0:T(8,128)(2,1)S(1)}, u32[]{:S(2)}, u32[]{:S(2)}) collective-permute-start(bf16[32,226]{1,0:T(8,128)(2,1)S(1)} %get-tuple-element.44), channel_id=1, source_target_pairs={{0,1},{1,0},{2,3},{3,2},{4,5},{5,4},{6,7},{7,6},{8,9},{9,8},{10,11... | collective-permute-start | bytes 43400 | tf_op jit(solution)/shard_map/ppermute | solution.py:20
  39.3 33.6 %collective-permute-start.2 = (bf16[32,3712]{1,0:T(8,128)(2,1)S(1)}, bf16[32,3712]{1,0:T(8,128)(2,1)S(1)}, u32[]{:S(2)}, u32[]{:S(2)}) collective-permute-start(bf16[32,3712]{1,0:T(8,128)(2,1)S(1)} %get-tuple-element.37), channel_id=1, source_target_pairs={{0,384},{128,0},{256,128},{384,256},{1,385},{129,1},{257,129},{385... | collective-permute-start | bytes 712712 | tf_op jit(solution)/shard_map/ppermute | solution.py:16
  43.9 33.6 %collective-permute-start.1 = (bf16[32,3712]{1,0:T(8,128)(2,1)S(1)}, bf16[32,3712]{1,0:T(8,128)(2,1)S(1)}, u32[]{:S(2)}, u32[]{:S(2)}) collective-permute-start(bf16[32,3712]{1,0:T(8,128)(2,1)S(1)} %get-tuple-element.37), channel_id=1, source_target_pairs={{0,128},{128,256},{256,384},{384,0},{1,129},{129,257},{257,385},{3... | collective-permute-start | bytes 712712 | tf_op jit(solution)/shard_map/ppermute | solution.py:16
  47.1 48.4 %all-to-all-start = ((bf16[32,12,113]{2,1,0:T(8,128)(2,1)}), bf16[32,12,113]{2,1,0:T(8,128)(2,1)S(1)}, u32[]{:S(2)}, u32[]{:S(2)}) async-start(bf16[32,12,113]{2,1,0:T(8,128)(2,1)} %copy.145), calls=%async_computation | async-start | bytes 262144 | tf_op jit(solution)/shard_map/all_to_all | solution.py:90
  58.8 72.7 %collective-permute-start.5 = (bf16[3616,128]{1,0:T(8,128)(2,1)}, bf16[3616,128]{1,0:T(8,128)(2,1)S(1)}, u32[]{:S(2)}, u32[]{:S(2)}) collective-permute-start(bf16[3616,128]{1,0:T(8,128)(2,1)} %bitcast.53), channel_id=1, source_target_pairs={{0,1},{1,0},{2,3},{3,2},{4,5},{5,4},{6,7},{7,6},{8,9},{9,8},{10,11... | collective-permute-start | bytes 2777096 | tf_op jit(solution)/shard_map/ppermute | solution.py:20
  68.6 64.9 %collective-permute-start.6 = (bf16[3616,128]{1,0:T(8,128)(2,1)}, bf16[3616,128]{1,0:T(8,128)(2,1)}, u32[]{:S(2)}, u32[]{:S(2)}) collective-permute-start(bf16[3616,128]{1,0:T(8,128)(2,1)} %bitcast.51), channel_id=1, source_target_pairs={{0,1},{1,0},{2,3},{3,2},{4,5},{5,4},{6,7},{7,6},{8,9},{9,8},{10,11... | collective-permute-start | bytes 2777096 | tf_op jit(solution)/shard_map/ppermute | solution.py:20
  70.5 86.2 %collective-permute-start.8 = (bf16[128,3616]{0,1:T(8,128)(2,1)}, bf16[128,3616]{0,1:T(8,128)(2,1)}, u32[]{:S(2)}, u32[]{:S(2)}) collective-permute-start(bf16[128,3616]{0,1:T(8,128)(2,1)} %bitcast.61), channel_id=1, source_target_pairs={{0,1},{1,0},{2,3},{3,2},{4,5},{5,4},{6,7},{7,6},{8,9},{9,8},{10,11... | collective-permute-start | bytes 2777096 | tf_op jit(solution)/shard_map/ppermute | solution.py:20
  72.9 19.9 %collective-permute-start.22 = (bf16[32,3712]{1,0:T(8,128)(2,1)S(1)}, bf16[32,3712]{1,0:T(8,128)(2,1)S(1)}, u32[]{:S(2)}, u32[]{:S(2)}) collective-permute-start(bf16[32,3712]{1,0:T(8,128)(2,1)S(1)} %get-tuple-element.40), channel_id=1, source_target_pairs={{0,48},{16,0},{32,16},{48,32},{1,49},{17,1},{33,17},{49,33},{2,50}... | collective-permute-start | bytes 712712 | tf_op jit(solution)/shard_map/ppermute | solution.py:16
  77.6 10.2 %collective-permute-start.21 = (bf16[32,3712]{1,0:T(8,128)(2,1)S(1)}, bf16[32,3712]{1,0:T(8,128)(2,1)S(1)}, u32[]{:S(2)}, u32[]{:S(2)}) collective-permute-start(bf16[32,3712]{1,0:T(8,128)(2,1)S(1)} %get-tuple-element.40), channel_id=1, source_target_pairs={{0,16},{16,32},{32,48},{48,0},{1,17},{17,33},{33,49},{49,1},{2,18}... | collective-permute-start | bytes 712712 | tf_op jit(solution)/shard_map/ppermute | solution.py:16
  87.8 32.4 %collective-permute-start.4 = (bf16[16,3712]{1,0:T(8,128)(2,1)S(1)}, bf16[16,3712]{1,0:T(8,128)(2,1)S(1)}, u32[]{:S(2)}, u32[]{:S(2)}) collective-permute-start(bf16[16,3712]{1,0:T(8,128)(2,1)S(1)} %slice.478), channel_id=1, source_target_pairs={{0,384},{128,0},{256,128},{384,256},{1,385},{129,1},{257,129},{385... | collective-permute-start | bytes 356360 | tf_op jit(solution)/shard_map/ppermute | solution.py:16
  92.9 6.8 %collective-permute-start.3 = (bf16[16,3712]{1,0:T(8,128)(2,1)S(1)}, bf16[16,3712]{1,0:T(8,128)(2,1)S(1)}, u32[]{:S(2)}, u32[]{:S(2)}) collective-permute-start(bf16[16,3712]{1,0:T(8,128)(2,1)S(1)} %slice.477), channel_id=1, source_target_pairs={{0,128},{128,256},{256,384},{384,0},{1,129},{129,257},{257,385},{3... | collective-permute-start | bytes 356360 | tf_op jit(solution)/shard_map/ppermute | solution.py:16
  99.6 6.8 %collective-permute-start.23 = (bf16[16,3712]{1,0:T(8,128)(2,1)S(1)}, bf16[16,3712]{1,0:T(8,128)(2,1)S(1)}, u32[]{:S(2)}, u32[]{:S(2)}) collective-permute-start(bf16[16,3712]{1,0:T(8,128)(2,1)S(1)} %slice.533), channel_id=1, source_target_pairs={{0,16},{16,32},{32,48},{48,0},{1,17},{17,33},{33,49},{49,1},{2,18}... | collective-permute-start | bytes 356360 | tf_op jit(solution)/shard_map/ppermute | solution.py:16
  106.4 5.6 %collective-permute-start.24 = (bf16[16,3712]{1,0:T(8,128)(2,1)S(1)}, bf16[16,3712]{1,0:T(8,128)(2,1)S(1)}, u32[]{:S(2)}, u32[]{:S(2)}) collective-permute-start(bf16[16,3712]{1,0:T(8,128)(2,1)S(1)} %slice.534), channel_id=1, source_target_pairs={{0,48},{16,0},{32,16},{48,32},{1,49},{17,1},{33,17},{49,33},{2,50}... | collective-permute-start | bytes 356360 | tf_op jit(solution)/shard_map/ppermute | solution.py:16
  112.0 10.7 %collective-permute-start.7 = (bf16[3,4,3616]{2,1,0:T(4,128)(2,1)S(1)}, bf16[3,4,3616]{2,1,0:T(4,128)(2,1)S(1)}, u32[]{:S(2)}, u32[]{:S(2)}) collective-permute-start(bf16[3,4,3616]{2,1,0:T(4,128)(2,1)S(1)} %reshape.95), channel_id=1, source_target_pairs={{0,1},{1,0},{2,3},{3,2},{4,5},{5,4},{6,7},{7,6},{8,9},{9,8},{10,11... | collective-permute-start | bytes 260360 | tf_op jit(solution)/shard_map/ppermute | solution.py:20
  120.2 26.1 %collective-permute-start.26 = (bf16[128,3712]{1,0:T(8,128)(2,1)}, bf16[128,3712]{1,0:T(8,128)(2,1)}, u32[]{:S(2)}, u32[]{:S(2)}) collective-permute-start(bf16[128,3712]{1,0:T(8,128)(2,1)} %constant_dynamic-update-slice_fusion.7), channel_id=1, source_target_pairs={{0,128},{128,256},{256,384},{384,0},{1,129},{129,257},{257,385},{3... | collective-permute-start | bytes 2850824 | tf_op jit(solution)/shard_map/ppermute | solution.py:16
  122.7 36.3 %collective-permute-start.25 = (bf16[128,3712]{1,0:T(8,128)(2,1)}, bf16[128,3712]{1,0:T(8,128)(2,1)S(1)}, u32[]{:S(2)}, u32[]{:S(2)}) collective-permute-start(bf16[128,3712]{1,0:T(8,128)(2,1)} %constant_dynamic-update-slice_fusion.7), channel_id=1, source_target_pairs={{0,384},{128,0},{256,128},{384,256},{1,385},{129,1},{257,129},{385... | collective-permute-start | bytes 2850824 | tf_op jit(solution)/shard_map/ppermute | solution.py:16
  128.6 17.7 %copy-start.14 = (bf16[16,3616]{1,0:T(8,128)(2,1)}, bf16[16,3616]{1,0:T(8,128)(2,1)S(1)}, u32[]{:S(2)}) copy-start(bf16[16,3616]{1,0:T(8,128)(2,1)S(1)} %fusion.57) | copy-start | bytes 347140
  131.5 40.4 %collective-permute-start.10 = (bf16[128,3712]{1,0:T(8,128)(2,1)}, bf16[128,3712]{1,0:T(8,128)(2,1)S(1)}, u32[]{:S(2)}, u32[]{:S(2)}) collective-permute-start(bf16[128,3712]{1,0:T(8,128)(2,1)} %copy-done.7), channel_id=1, source_target_pairs={{0,16},{16,32},{32,48},{48,0},{1,17},{17,33},{33,49},{49,1},{2,18}... | collective-permute-start | bytes 2850824 | tf_op jit(solution)/shard_map/ppermute | solution.py:16
  133.5 47.1 %collective-permute-start.9 = (bf16[128,3712]{1,0:T(8,128)(2,1)}, bf16[128,3712]{1,0:T(8,128)(2,1)S(1)}, u32[]{:S(2)}, u32[]{:S(2)}) collective-permute-start(bf16[128,3712]{1,0:T(8,128)(2,1)} %copy-done.7), channel_id=1, source_target_pairs={{0,48},{16,0},{32,16},{48,32},{1,49},{17,1},{33,17},{49,33},{2,50}... | collective-permute-start | bytes 2850824 | tf_op jit(solution)/shard_map/ppermute | solution.py:16
  150.6 42.1 %collective-permute-start.27 = (bf16[64,3712]{1,0:T(8,128)(2,1)}, bf16[64,3712]{1,0:T(8,128)(2,1)S(1)}, u32[]{:S(2)}, u32[]{:S(2)}) collective-permute-start(bf16[64,3712]{1,0:T(8,128)(2,1)} %slice.554), channel_id=1, source_target_pairs={{0,128},{128,256},{256,384},{384,0},{1,129},{129,257},{257,385},{3... | collective-permute-start | bytes 1425416 | tf_op jit(solution)/shard_map/ppermute | solution.py:16
  162.2 30.6 %collective-permute-start.28 = (bf16[64,3712]{1,0:T(8,128)(2,1)}, bf16[64,3712]{1,0:T(8,128)(2,1)}, u32[]{:S(2)}, u32[]{:S(2)}) collective-permute-start(bf16[64,3712]{1,0:T(8,128)(2,1)} %slice.555), channel_id=1, source_target_pairs={{0,384},{128,0},{256,128},{384,256},{1,385},{129,1},{257,129},{385... | collective-permute-start | bytes 1425416 | tf_op jit(solution)/shard_map/ppermute | solution.py:16
  173.5 21.7 %collective-permute-start.11 = (bf16[64,3712]{1,0:T(8,128)(2,1)}, bf16[64,3712]{1,0:T(8,128)(2,1)}, u32[]{:S(2)}, u32[]{:S(2)}) collective-permute-start(bf16[64,3712]{1,0:T(8,128)(2,1)} %slice.500), channel_id=1, source_target_pairs={{0,16},{16,32},{32,48},{48,0},{1,17},{17,33},{33,49},{49,1},{2,18}... | collective-permute-start | bytes 1425416 | tf_op jit(solution)/shard_map/ppermute | solution.py:16
  182.4 14.0 %collective-permute-start.12 = (bf16[64,3712]{1,0:T(8,128)(2,1)S(1)}, bf16[64,3712]{1,0:T(8,128)(2,1)S(1)}, u32[]{:S(2)}, u32[]{:S(2)}) collective-permute-start(bf16[64,3712]{1,0:T(8,128)(2,1)S(1)} %slice.501), channel_id=1, source_target_pairs={{0,48},{16,0},{32,16},{48,32},{1,49},{17,1},{33,17},{49,33},{2,50}... | collective-permute-start | bytes 1425416 | tf_op jit(solution)/shard_map/ppermute | solution.py:16
  201.8 18.0 %collective-permute-start.15 = (bf16[64,3616]{1,0:T(8,128)(2,1)}, bf16[64,3616]{1,0:T(8,128)(2,1)}, u32[]{:S(2)}, u32[]{:S(2)}) collective-permute-start(bf16[64,3616]{1,0:T(8,128)(2,1)} %copy.158), channel_id=1, source_target_pairs={{0,48},{16,0},{32,16},{48,32},{1,49},{17,1},{33,17},{49,33},{2,50}... | collective-permute-start | bytes 1388552 | tf_op jit(solution)/shard_map/ppermute | solution.py:16
  211.5 28.1 %collective-permute-start.31 = (bf16[64,3616]{1,0:T(8,128)(2,1)}, bf16[64,3616]{1,0:T(8,128)(2,1)}, u32[]{:S(2)}, u32[]{:S(2)}) collective-permute-start(bf16[64,3616]{1,0:T(8,128)(2,1)} %copy.171), channel_id=1, source_target_pairs={{0,384},{128,0},{256,128},{384,256},{1,385},{129,1},{257,129},{385... | collective-permute-start | bytes 1388552 | tf_op jit(solution)/shard_map/ppermute | solution.py:16
  213.7 27.1 %collective-permute-start.29 = (bf16[64,3616]{1,0:T(8,128)(2,1)}, bf16[64,3616]{1,0:T(8,128)(2,1)}, u32[]{:S(2)}, u32[]{:S(2)}) collective-permute-start(bf16[64,3616]{1,0:T(8,128)(2,1)} %copy.166), channel_id=1, source_target_pairs={{0,128},{128,256},{256,384},{384,0},{1,129},{129,257},{257,385},{3... | collective-permute-start | bytes 1388552 | tf_op jit(solution)/shard_map/ppermute | solution.py:16
  216.8 14.8 %slice-start.3 = ((bf16[128,3616]{1,0:T(8,128)(2,1)}), bf16[64,3616]{1,0:T(8,128)(2,1)S(1)}, s32[]{:S(2)}) async-start(bf16[128,3616]{1,0:T(8,128)(2,1)} %copy-done.6), calls=%async_computation.5 | async-start | bytes 950272 | tf_op jit(solution)/shard_map/slice | solution.py:40
  217.9 12.4 %collective-permute-start.13 = (bf16[64,3616]{1,0:T(8,128)(2,1)}, bf16[64,3616]{1,0:T(8,128)(2,1)}, u32[]{:S(2)}, u32[]{:S(2)}) collective-permute-start(bf16[64,3616]{1,0:T(8,128)(2,1)} %copy.153), channel_id=1, source_target_pairs={{0,16},{16,32},{32,48},{48,0},{1,17},{17,33},{33,49},{49,1},{2,18}... | collective-permute-start | bytes 1388552 | tf_op jit(solution)/shard_map/ppermute | solution.py:16
  221.2 18.5 %copy-start.3 = (bf16[128,3616]{1,0:T(8,128)(2,1)S(1)}, bf16[128,3616]{1,0:T(8,128)(2,1)}, u32[]{:S(2)}) copy-start(bf16[128,3616]{1,0:T(8,128)(2,1)} %copy-done.2) | copy-start | bytes 2777092
  222.5 19.6 %slice-start = ((bf16[128,3616]{1,0:T(8,128)(2,1)}), bf16[64,3616]{1,0:T(8,128)(2,1)S(1)}, s32[]{:S(2)}) async-start(bf16[128,3616]{1,0:T(8,128)(2,1)} %copy-done.2), calls=%async_computation.2 | async-start | bytes 950272 | tf_op jit(solution)/shard_map/slice | solution.py:41
  233.0 21.3 %collective-permute-start.14 = (bf16[128,3616]{0,1:T(8,128)(2,1)}, bf16[128,3616]{0,1:T(8,128)(2,1)}, u32[]{:S(2)}, u32[]{:S(2)}) collective-permute-start(bf16[128,3616]{0,1:T(8,128)(2,1)} %copy.154), channel_id=1, source_target_pairs={{0,16},{16,32},{32,48},{48,0},{1,17},{17,33},{33,49},{49,1},{2,18}... | collective-permute-start | bytes 2777096 | tf_op jit(solution)/shard_map/ppermute | solution.py:16
  235.1 20.8 %collective-permute-start.16 = (bf16[128,3616]{0,1:T(8,128)(2,1)}, bf16[128,3616]{0,1:T(8,128)(2,1)}, u32[]{:S(2)}, u32[]{:S(2)}) collective-permute-start(bf16[128,3616]{0,1:T(8,128)(2,1)} %copy.159), channel_id=1, source_target_pairs={{0,48},{16,0},{32,16},{48,32},{1,49},{17,1},{33,17},{49,33},{2,50}... | collective-permute-start | bytes 2777096 | tf_op jit(solution)/shard_map/ppermute | solution.py:16
  243.5 14.0 %copy-start.18 = (bf16[128,256]{1,0:T(8,128)(2,1)S(1)}, bf16[128,256]{1,0:T(8,128)(2,1)}, u32[]{:S(2)}) copy-start(bf16[128,256]{1,0:T(8,128)(2,1)} %fusion.55) | copy-start | bytes 196612
  243.5 14.0 %copy-start.19 = (bf16[128,8]{1,0:T(8,128)(2,1)S(1)}, bf16[128,8]{1,0:T(8,128)(2,1)}, u32[]{:S(2)}) copy-start(bf16[128,8]{1,0:T(8,128)(2,1)} %copy.147) | copy-start | bytes 6148
  244.9 22.8 %collective-permute-start.30 = (bf16[128,3616]{0,1:T(8,128)(2,1)}, bf16[128,3616]{0,1:T(8,128)(2,1)}, u32[]{:S(2)}, u32[]{:S(2)}) collective-permute-start(bf16[128,3616]{0,1:T(8,128)(2,1)} %copy.167), channel_id=1, source_target_pairs={{0,128},{128,256},{256,384},{384,0},{1,129},{129,257},{257,385},{3... | collective-permute-start | bytes 2777096 | tf_op jit(solution)/shard_map/ppermute | solution.py:16
  247.1 22.3 %collective-permute-start.32 = (bf16[128,3616]{0,1:T(8,128)(2,1)}, bf16[128,3616]{0,1:T(8,128)(2,1)}, u32[]{:S(2)}, u32[]{:S(2)}) collective-permute-start(bf16[128,3616]{0,1:T(8,128)(2,1)} %copy.172), channel_id=1, source_target_pairs={{0,384},{128,0},{256,128},{384,256},{1,385},{129,1},{257,129},{385... | collective-permute-start | bytes 2777096 | tf_op jit(solution)/shard_map/ppermute | solution.py:16
  261.0 19.4 %collective-permute-start.17 = (bf16[16,3616]{1,0:T(8,128)(2,1)}, bf16[16,3616]{1,0:T(8,128)(2,1)S(1)}, u32[]{:S(2)}, u32[]{:S(2)}) collective-permute-start(bf16[16,3616]{1,0:T(8,128)(2,1)} %get-tuple-element.23), channel_id=1, source_target_pairs={{0,128},{128,256},{256,384},{384,0},{1,129},{129,257},{257,385},{3... | collective-permute-start | bytes 347144 | tf_op jit(solution)/shard_map/ppermute | solution.py:16
  263.5 16.9 %collective-permute-start.19 = (bf16[16,3616]{1,0:T(8,128)(2,1)S(1)}, bf16[16,3616]{1,0:T(8,128)(2,1)S(1)}, u32[]{:S(2)}, u32[]{:S(2)}) collective-permute-start(bf16[16,3616]{1,0:T(8,128)(2,1)S(1)} %get-tuple-element.24), channel_id=1, source_target_pairs={{0,384},{128,0},{256,128},{384,256},{1,385},{129,1},{257,129},{385... | collective-permute-start | bytes 347144 | tf_op jit(solution)/shard_map/ppermute | solution.py:16
  273.9 12.0 %collective-permute-start.33 = (bf16[16,3616]{1,0:T(8,128)(2,1)S(1)}, bf16[16,3616]{1,0:T(8,128)(2,1)S(1)}, u32[]{:S(2)}, u32[]{:S(2)}) collective-permute-start(bf16[16,3616]{1,0:T(8,128)(2,1)S(1)} %get-tuple-element.29), channel_id=1, source_target_pairs={{0,16},{16,32},{32,48},{48,0},{1,17},{17,33},{33,49},{49,1},{2,18}... | collective-permute-start | bytes 347144 | tf_op jit(solution)/shard_map/ppermute | solution.py:16
  275.8 10.1 %collective-permute-start.35 = (bf16[16,3616]{1,0:T(8,128)(2,1)S(1)}, bf16[16,3616]{1,0:T(8,128)(2,1)S(1)}, u32[]{:S(2)}, u32[]{:S(2)}) collective-permute-start(bf16[16,3616]{1,0:T(8,128)(2,1)S(1)} %get-tuple-element.30), channel_id=1, source_target_pairs={{0,48},{16,0},{32,16},{48,32},{1,49},{17,1},{33,17},{49,33},{2,50}... | collective-permute-start | bytes 347144 | tf_op jit(solution)/shard_map/ppermute | solution.py:16
  280.6 10.8 %collective-permute-start.20 = (bf16[32,3616]{1,0:T(8,128)(2,1)S(1)}, bf16[32,3616]{1,0:T(8,128)(2,1)S(1)}, u32[]{:S(2)}, u32[]{:S(2)}) collective-permute-start(bf16[32,3616]{1,0:T(8,128)(2,1)S(1)} %pad_maximum_fusion.8), channel_id=1, source_target_pairs={{0,384},{128,0},{256,128},{384,256},{1,385},{129,1},{257,129},{385... | collective-permute-start | bytes 694280 | tf_op jit(solution)/shard_map/ppermute | solution.py:16
  283.4 8.1 %collective-permute-start.18 = (bf16[32,3616]{1,0:T(8,128)(2,1)S(1)}, bf16[32,3616]{1,0:T(8,128)(2,1)S(1)}, u32[]{:S(2)}, u32[]{:S(2)}) collective-permute-start(bf16[32,3616]{1,0:T(8,128)(2,1)S(1)} %pad_maximum_fusion.7), channel_id=1, source_target_pairs={{0,128},{128,256},{256,384},{384,0},{1,129},{129,257},{257,385},{3... | collective-permute-start | bytes 694280 | tf_op jit(solution)/shard_map/ppermute | solution.py:16
  286.0 7.1 %collective-permute-start.36 = (bf16[32,3616]{1,0:T(8,128)(2,1)S(1)}, bf16[32,3616]{1,0:T(8,128)(2,1)S(1)}, u32[]{:S(2)}, u32[]{:S(2)}) collective-permute-start(bf16[32,3616]{1,0:T(8,128)(2,1)S(1)} %pad_maximum_fusion.10), channel_id=1, source_target_pairs={{0,48},{16,0},{32,16},{48,32},{1,49},{17,1},{33,17},{49,33},{2,50}... | collective-permute-start | bytes 694280 | tf_op jit(solution)/shard_map/ppermute | solution.py:16
  289.4 8.4 %collective-permute-start.34 = (bf16[32,3616]{1,0:T(8,128)(2,1)S(1)}, bf16[32,3616]{1,0:T(8,128)(2,1)S(1)}, u32[]{:S(2)}, u32[]{:S(2)}) collective-permute-start(bf16[32,3616]{1,0:T(8,128)(2,1)S(1)} %pad_maximum_fusion.9), channel_id=1, source_target_pairs={{0,16},{16,32},{32,48},{48,0},{1,17},{17,33},{33,49},{49,1},{2,18}... | collective-permute-start | bytes 694280 | tf_op jit(solution)/shard_map/ppermute | solution.py:16
  327.3 15.2 %collective-permute-start.37 = (bf16[32,226]{1,0:T(8,128)(2,1)S(1)}, bf16[32,226]{1,0:T(8,128)(2,1)S(1)}, u32[]{:S(2)}, u32[]{:S(2)}) collective-permute-start(bf16[32,226]{1,0:T(8,128)(2,1)S(1)} %get-tuple-element.42), channel_id=1, source_target_pairs={{0,1},{1,0},{2,3},{3,2},{4,5},{5,4},{6,7},{7,6},{8,9},{9,8},{10,11... | collective-permute-start | bytes 43400 | tf_op jit(solution)/shard_map/ppermute | solution.py:20
  (24 other events, 145.5 us)

commit v2 on v1

v2 whole, which is shorter than its diff:
```python
import functools

import jax
import jax.numpy as jnp
from jax import lax
from jax.experimental import pallas as pl
from jax.experimental.pallas import tpu as pltpu
from jax.sharding import Mesh, PartitionSpec as P

Y, H, X, L, C = 4, 2, 4, 8, 2
AXES = ("y", "h", "x", "l", "c")
EXPERT = ("y", "h", "x")
TENSOR = ("l", "c")
Z = ("h", "l")
f32 = jnp.float32
bf16 = jnp.bfloat16


def move(a, stage, k):
    pairs = []
    for y in range(Y):
        for x in range(X):
            for c in range(C):
                to = ((y + k) % Y, x) if (stage + c) % 2 == 0 else (y, (x + k) % X)
                pairs.append(((y * X + x) * C + c, (to[0] * X + to[1]) * C + c))
    return lax.ppermute(a, ("y", "x", "c"), pairs)


def swap(a):
    return lax.ppermute(a, "c", [(0, 1), (1, 0)])


def turn(a):
    return lax.ppermute(a, ("h", "c"), [(h * 2 + c, c * 2 + h) for h in range(2) for c in range(2)])


def add(*terms):
    total = terms[0].astype(f32)
    for t in terms[1:]:
        total = total + t.astype(f32)
    return total.astype(bf16)


def ffn_kernel(at_ref, x_ref, w_ref, s_ref, d_ref, sd_ref, o_ref, *, hid, units):
    width = x_ref.shape[1]
    tail = x_ref[:, width - 128 :].astype(f32)
    lane = lax.broadcasted_iota(jnp.int32, tail.shape, 1)
    at = at_ref[0]
    weight = jnp.sum(
        jnp.where((lane == at) | (lane == at + 2), tail, 0.0), axis=1, keepdims=True
    )
    x = x_ref[...]
    acts = jnp.dot(x, w_ref[...], preferred_element_type=f32)
    gate, up = acts[:, :hid], acts[:, hid:]
    hidden = (gate / (1.0 + jnp.exp(-gate)) * up * weight).astype(bf16)
    nt = (((1,), (1,)), ((), ()))
    s_gate = lax.dot_general(x, s_ref[:units], nt, preferred_element_type=f32)
    s_up = lax.dot_general(x, s_ref[units:], nt, preferred_element_type=f32)
    s_hidden = (s_gate / (1.0 + jnp.exp(-s_gate)) * s_up).astype(bf16)
    cols = o_ref.shape[1]
    for lo in range(0, cols, 512):
        hi = min(lo + 512, cols)
        o_ref[:, lo:hi] = (
            jnp.dot(hidden, d_ref[:, lo:hi], preferred_element_type=f32)
            + jnp.dot(s_hidden, sd_ref[:, lo:hi], preferred_element_type=f32)
        ).astype(bf16)


def ffn(at, x, w_in, s_in, w_out, s_out):
    rows, width = x.shape
    hid, units, cols = w_in.shape[1] // 2, s_in.shape[0] // 2, w_out.shape[1]
    whole = pl.BlockSpec(memory_space=pltpu.VMEM)
    return pl.pallas_call(
        functools.partial(ffn_kernel, hid=hid, units=units),
        out_shape=jax.ShapeDtypeStruct((rows, cols), bf16),
        in_specs=[pl.BlockSpec(memory_space=pltpu.SMEM)] + [whole] * 5,
        out_specs=whole,
        compiler_params=pltpu.CompilerParams(vmem_limit_bytes=40 * 1024 * 1024),
        cost_estimate=pl.CostEstimate(
            flops=2 * rows * (width * 3 * hid + 2 * hid * cols),
            bytes_accessed=2 * (rows * (width + cols) + width * 2 * hid + hid * cols),
            transcendentals=rows * hid,
        ),
    )(at, x, w_in, s_in, w_out, s_out)


def local(
    tokens,
    gate_codes,
    routes,
    routed_gate,
    routed_up,
    routed_down,
    shared_gate,
    shared_up,
    shared_down,
):
    expert = lax.axis_index(EXPERT)
    part = lax.axis_index(TENSOR)
    toks, width = tokens.shape
    feats = width * L * C
    full = -(-feats // 128) * 128
    n_exp = Y * H * X
    per = n_exp // (L * C)

    gates = gate_codes.astype(f32)
    gates = 2.5 * gates / jnp.sum(gates, axis=1, keepdims=True)
    own = part * per + jnp.arange(per, dtype=jnp.int32)
    table = jnp.sum(jnp.where(routes[:, :, None] == own, gates[:, :, None], 0.0), axis=1)
    high = table.astype(bf16)
    low = (table - high.astype(f32)).astype(bf16)
    sent = jnp.concatenate(
        [tokens, high, low, jnp.zeros((toks, 256 - width - 2 * per), bf16)], 1
    )
    got = lax.all_gather(turn(sent), Z, axis=0, tiled=False)
    got = got.reshape(H, L, toks, 256).transpose(2, 1, 0, 3)
    rows = jnp.concatenate(
        [
            got[..., :width].reshape(toks, feats),
            got[..., width : width + 2 * per].reshape(toks, 2 * n_exp),
            jnp.zeros((toks, full - feats - 2 * n_exp), bf16),
        ],
        1,
    )
    at = (feats - (full - 128) + 2 * per * (expert // per) + expert % per).reshape(1)

    w_gate, w_up, w_down = routed_gate[0], routed_up[0], routed_down[0]
    w_in = jnp.concatenate([w_gate, swap(w_gate), w_up, swap(w_up)], 1)
    w_in = jnp.pad(w_in, ((0, full - feats), (0, 0)))
    w_out = jnp.concatenate([w_down, swap(w_down)], 0)
    units = shared_gate.shape[1] // n_exp
    depth = shared_gate.shape[0]
    s = jnp.stack([shared_gate.T, shared_up.T, shared_down]).reshape(3, n_exp, units, depth)
    s = s.transpose(1, 0, 2, 3).reshape(n_exp, 3 * units, depth)
    s = lax.all_to_all(s, EXPERT, split_axis=0, concat_axis=0, tiled=True)
    s = s.transpose(1, 0, 2).reshape(3, units, feats)
    s = jnp.concatenate([s, swap(s), jnp.zeros((3, 16 - 2 * units, feats), bf16)], 1)
    s_in = jnp.pad(s[:2].reshape(32, feats), ((0, 0), (0, full - feats)))
    s_out = s[2]

    apply = lambda block: ffn(at, block, w_in, s_in, w_out, s_out)

    near = jnp.concatenate([rows, move(rows, 0, 1), move(rows, 0, -1), move(rows, 0, 2)], 0)
    m = near.shape[0] // 2
    prev, succ = move(near, 1, 1), move(near, 1, -1)
    far = jnp.concatenate([move(prev[:m], 1, 1), move(succ[m:], 1, -1)], 0)
    own_out, prev_out, succ_out, far_out = apply(near), apply(prev), apply(succ), apply(far)

    from_prev, from_succ = move(far_out[:m], 1, 1), move(far_out[m:], 1, -1)
    to_succ = jnp.concatenate([add(succ_out[:m], from_prev), succ_out[m:]], 0)
    to_prev = jnp.concatenate([prev_out[:m], add(prev_out[m:], from_succ)], 0)
    total = add(own_out, move(to_succ, 1, 1), move(to_prev, 1, -1))
    total = total.reshape(4, toks, feats)
    total = add(total[0], move(total[1], 0, -1), move(total[2], 0, 1), move(total[3], 0, 2))
    back = total.reshape(toks, L, H, width).transpose(2, 1, 0, 3).reshape(H * L, toks, width)
    back = lax.all_to_all(back, Z, split_axis=0, concat_axis=0, tiled=True)
    return turn(jnp.sum(back.astype(f32), axis=0).astype(bf16))


def solution(mesh):
    fine = Mesh(mesh.devices.reshape(Y, H, X, L, C), AXES)
    in_specs = (
        P(EXPERT, TENSOR),
        P(EXPERT, None),
        P(EXPERT, None),
        P(EXPERT, None, TENSOR),
        P(EXPERT, None, TENSOR),
        P(EXPERT, TENSOR, None),
        P(EXPERT, TENSOR),
        P(EXPERT, TENSOR),
        P(TENSOR, EXPERT),
    )
    return jax.shard_map(
        local, mesh=fine, in_specs=in_specs, out_specs=P(EXPERT, TENSOR), check_vma=False
    )
```

time: 346 us -> 295 us (0.85)
  starting transfers between devices: 154 us -> 113 us
  matrix products: 40.4 us -> 0 us
  Pallas kernels: 0 us -> 16.3 us
  waiting for transfers between devices: 38.9 us -> 51.3 us
  local copies, waits for them, and re-layouts: 38.3 us -> 46.5 us
  blocking collectives: 53.8 us -> 45.8 us
    dot_general x24 -> x0, matrix products: 40.4 us -> none  [the longest x8 19.5 us: apply(): return jnp.dot(both, w_out, preferred_element_type=f32).astype(bf16)]
    ppermute x6 -> x4, starting transfers between devices: 43.9 us -> 18.5 us  [swap(): return lax.ppermute(a, 'c', [(0, 1), (1, 0)])]
    ppermute x32 -> x16, starting transfers between devices: 98 us -> 80.7 us  [the longest x14 44.1 us: move(): return lax.ppermute(a, ('y', 'x', 'c'), pairs)]
    pallas_call x0 -> x4, Pallas kernels: none -> 16.3 us  [ffn(): pl.pallas_call(functools.partial(ffn_kernel, hid=hid, units=units), out_s...]
    all_to_all x1, waiting for transfers between devices: 0.01 us -> 8.61 us  [local(): s = lax.all_to_all(s, EXPERT, split_axis=0, concat_axis=0, tiled=True)]
    ppermute x4 -> x5, local copies, waits for them, and re-layouts: 6.37 us -> 13.9 us  [the longest x4 11.6 us: move(): return lax.ppermute(a, ('y', 'x', 'c'), pairs)]
    concatenate x12 -> x8, other arithmetic: 2.84 us -> 10 us  [the longest x1 3.56 us: local(): w_in = jnp.concatenate([w_gate, swap(w_gate), w_up, swap(w_up)], 1)]
    unnamed x70 -> x31, local copies, waits for them, and re-layouts: 5.84 us -> 12.1 us
  transfers between devices with their start and end apart: 39 -> 21, of which waited for: 10 -> 12; matrix products, arithmetic and copies ran while one was open for 24% -> 10% of each run, Pallas kernels for 0% -> 4%
where the time goes in v2:
time: 295 us; the launch traced here: 293 us
  starting transfers between devices  113 us (38%)
  waiting for transfers between devices  51.3 us (17%)
  local copies, waits for them, and re-layouts  46.5 us (16%)
  blocking collectives  45.8 us (16%)
  other arithmetic  19.5 us (7%)
  Pallas kernels  16.3 us (6%)
    ppermute x14, starting transfers between devices, move(): return lax.ppermute(a, ('y', 'x', 'c'), pairs)  44.1 us
    ppermute x14, waiting for transfers between devices, move(): return lax.ppermute(a, ('y', 'x', 'c'), pairs)  36.9 us
    ppermute x2, starting transfers between devices, turn(): lax.ppermute(a, ('h', 'c'), [(h * 2 + c, c * 2 + h) for h in range(2) for...  36.5 us
    all_gather x1, blocking collectives, local(): got = lax.all_gather(turn(sent), Z, axis=0, tiled=False)  23.9 us
    all_to_all x1, blocking collectives, local(): back = lax.all_to_all(back, Z, split_axis=0, concat_axis=0, tiled=True)  21.9 us
    ppermute x4, starting transfers between devices, swap(): return lax.ppermute(a, 'c', [(0, 1), (1, 0)])  18.5 us
    pallas_call x4, Pallas kernels, ffn(): pl.pallas_call(functools.partial(ffn_kernel, hid=hid, units=units), out_s...  16.3 us
    all_to_all x1, starting transfers between devices, local(): s = lax.all_to_all(s, EXPERT, split_axis=0, concat_axis=0, tiled=True)  14.3 us
  transfers between devices with their start and end apart: 21, of which 12 were waited for; matrix products, arithmetic and copies ran while one was open for 10% of the time, Pallas kernels for 4%

profile of v2, /device:TPU:1, one launch (start us, length us, event | category | flops | bytes accessed | tf_op | source)
XLA Modules:
  0.0 293.5 jit_solution(12880897858860707142)
XLA Ops:
  3.3 16.8 %collective-permute-start = (bf16[64,256]{1,0:T(8,128)(2,1)S(1)}, bf16[64,256]{1,0:T(8,128)(2,1)S(1)}, u32[]{:S(2)}, u32[]{:S(2)}) collective-permute-start(bf16[64,256]{1,0:T(8,128)(2,1)S(1)} %maximum_maximum_fusion.1), channel_id=1, source_target_pairs={{0,0},{1,64},{64,1},{65,65},{2,2},{3,66},{66,3},{67,67},{4,4},{5,6... | collective-permute-start | bytes 98312 | tf_op jit(solution)/shard_map/ppermute | solution.py:34
  21.8 23.9 %all-gather = bf16[1024,256]{1,0:T(8,128)(2,1)S(1)} all-gather(bf16[64,256]{1,0:T(8,128)(2,1)S(1)} %collective-permute-done), channel_id=2, replica_groups=mesh['y'=4,'h'=2,'x'=4,'l'=8,'c'=2] {'h','l'}, dimensions={0}, use_global_device_ids=true | all-gather | bytes 557056 | tf_op jit(solution)/shard_map/all_gather | solution.py:115
  47.9 4.7 %collective-permute-start.3 = (bf16[64,3712]{1,0:T(8,128)(2,1)S(1)}, bf16[64,3712]{1,0:T(8,128)(2,1)S(1)}, u32[]{:S(2)}, u32[]{:S(2)}) collective-permute-start(bf16[64,3712]{1,0:T(8,128)(2,1)S(1)} %concatenate.29), channel_id=1, source_target_pairs={{0,256},{1,33},{16,272},{17,49},{32,288},{33,1},{48,304},{49,17},{... | collective-permute-start | bytes 1425416 | tf_op jit(solution)/shard_map/ppermute | solution.py:26
  52.6 2.8 collective-permute-start.2
  55.3 2.5 collective-permute-start.1
  59.1 14.3 %all-to-all-start = ((bf16[32,12,113]{2,1,0:T(8,128)(2,1)}), bf16[32,12,113]{2,1,0:T(8,128)(2,1)S(1)}, u32[]{:S(2)}, u32[]{:S(2)}) async-start(bf16[32,12,113]{2,1,0:T(8,128)(2,1)} %copy.68), calls=%async_computation | async-start | bytes 262144 | tf_op jit(solution)/shard_map/all_to_all | solution.py:135
  74.6 3.1 %collective-permute-start.9 = (bf16[256,3712]{1,0:T(8,128)(2,1)S(1)}, bf16[256,3712]{1,0:T(8,128)(2,1)}, u32[]{:S(2)}, u32[]{:S(2)}) collective-permute-start(bf16[256,3712]{1,0:T(8,128)(2,1)S(1)} %pad_maximum_fusion.x_ref), channel_id=1, source_target_pairs={{0,16},{1,129},{16,32},{17,145},{32,48},{33,161},{48,0},{49,177},{... | collective-permute-start | bytes 5701640 | tf_op jit(solution)/shard_map/ppermute | solution.py:26
  77.7 3.4 %collective-permute-start.8 = (bf16[256,3712]{1,0:T(8,128)(2,1)S(1)}, bf16[256,3712]{1,0:T(8,128)(2,1)}, u32[]{:S(2)}, u32[]{:S(2)}) collective-permute-start(bf16[256,3712]{1,0:T(8,128)(2,1)S(1)} %pad_maximum_fusion.x_ref), channel_id=1, source_target_pairs={{0,48},{1,385},{16,0},{17,401},{32,16},{33,417},{48,32},{49,433},{... | collective-permute-start | bytes 5701640 | tf_op jit(solution)/shard_map/ppermute | solution.py:26
  81.1 8.6 %all-to-all-done = bf16[32,12,113]{2,1,0:T(8,128)(2,1)S(1)} async-done(((bf16[32,12,113]{2,1,0:T(8,128)(2,1)}), bf16[32,12,113]{2,1,0:T(8,128)(2,1)S(1)}, u32[]{:S(2)}, u32[]{:S(2)}) %all-to-all-start) | async-done | bytes 86816 | tf_op jit(solution)/shard_map/all_to_all | solution.py:135
  89.9 12.2 %collective-permute-start.6 = (bf16[3,4,3616]{2,1,0:T(4,128)(2,1)S(1)}, bf16[3,4,3616]{2,1,0:T(4,128)(2,1)S(1)}, u32[]{:S(2)}, u32[]{:S(2)}) collective-permute-start(bf16[3,4,3616]{2,1,0:T(4,128)(2,1)S(1)} %reshape.55), channel_id=1, source_target_pairs={{0,1},{1,0},{2,3},{3,2},{4,5},{5,4},{6,7},{7,6},{8,9},{9,8},{10,11... | collective-permute-start | bytes 260360 | tf_op jit(solution)/shard_map/ppermute | solution.py:30
  102.2 1.9 collective-permute-start.4
  104.1 2.4 collective-permute-start.5
  108.3 1.9 collective-permute-start.7
  110.4 2.6 collective-permute-done.7
  113.0 2.3 copy.72
  116.6 2.2 collective-permute-start.10
  120.1 4.2 %collective-permute-start.11 = (bf16[128,3712]{1,0:T(8,128)(2,1)S(1)}, bf16[128,3712]{1,0:T(8,128)(2,1)S(1)}, u32[]{:S(2)}, u32[]{:S(2)}) collective-permute-start(bf16[128,3712]{1,0:T(8,128)(2,1)S(1)} %slice.74), channel_id=1, source_target_pairs={{0,48},{1,385},{16,0},{17,401},{32,16},{33,417},{48,32},{49,433},{... | collective-permute-start | bytes 2850824 | tf_op jit(solution)/shard_map/ppermute | solution.py:26
  124.6 3.6 %fusion.6.w_ref = bf16[3712,512]{1,0:T(8,128)(2,1)S(1)} fusion(bf16[3616,128]{1,0:T(8,128)(2,1)} %collective-permute-done.5, bf16[3616,128]{1,0:T(8,128)(2,1)} %bitcast.5, bf16[3616,128]{1,0:T(8,128)(2,1)} %collective-permute-done.4, bf16[3616,128]{1,0:T(8,128)(2,1)} %bitcast.4), kind=kLoop, calls=%fused_computation.7 | loop fusion | flops 24707072 | bytes 7503872 | tf_op jit(solution)/shard_map/concatenate | solution.py:128
  128.1 4.5 %collective-permute-done.10 = bf16[128,3712]{1,0:T(8,128)(2,1)S(1)} collective-permute-done((bf16[128,3712]{1,0:T(8,128)(2,1)S(1)}, bf16[128,3712]{1,0:T(8,128)(2,1)S(1)}, u32[]{:S(2)}, u32[]{:S(2)}) %collective-permute-start.10) | collective-permute-done | bytes 950304 | tf_op jit(solution)/shard_map/ppermute | solution.py:26
  132.6 2.5 collective-permute-done.11
  135.2 3.3 %shard_map.93 = bf16[256,3616]{1,0:T(8,128)(2,1)S(1)} custom-call(s32[1]{0:T(128)} %bitcast.at_ref, bf16[256,3712]{1,0:T(8,128)(2,1)S(1)} %pad_maximum_fusion.2.x_ref, bf16[3712,512]{1,0:T(8,128)(2,1)S(1)} %fusion.6.w_ref, bf16[32,3712]{1,0:T(8,128)(2,1)S(1)} %pad.9.s_ref, bf16[256,3616]{1,0:T(8,128)(2,1)S(1)} %pad_maximum_fusion.1.d_ref, ...), custom_call_target="tpu_custom_call" | custom-call | flops 2407530496 | bytes 9404416 | tf_op jit(solution)/shard_map/pallas_call | solution.py:73
  139.6 2.2 copy.77
  141.8 5.2 %collective-permute-start.14 = (bf16[128,3616]{0,1:T(8,128)(2,1)}, bf16[128,3616]{0,1:T(8,128)(2,1)}, u32[]{:S(2)}, u32[]{:S(2)}) collective-permute-start(bf16[128,3616]{0,1:T(8,128)(2,1)} %copy.77), channel_id=1, source_target_pairs={{0,48},{1,385},{16,0},{17,401},{32,16},{33,417},{48,32},{49,433},{... | collective-permute-start | bytes 2777096 | tf_op jit(solution)/shard_map/ppermute | solution.py:26
  147.0 2.1 copy-done.1
  149.1 4.8 %shard_map.94 = bf16[256,3616]{1,0:T(8,128)(2,1)S(1)} custom-call(s32[1]{0:T(128)} %bitcast.at_ref, bf16[256,3712]{1,0:T(8,128)(2,1)} %collective-permute-done.9.x_ref, bf16[3712,512]{1,0:T(8,128)(2,1)S(1)} %copy-done.1, bf16[32,3712]{1,0:T(8,128)(2,1)S(1)} %pad.9.s_ref, bf16[256,3616]{1,0:T(8,128)(2,1)S(1)} %pad_maximum_fusion.1.d_ref, ...), custom_call_target="tpu_custom_call" | custom-call | flops 2407530496 | bytes 9404416 | tf_op jit(solution)/shard_map/pallas_call | solution.py:73
  155.3 4.8 %shard_map.92 = bf16[256,3616]{1,0:T(8,128)(2,1)S(1)} custom-call(s32[1]{0:T(128)} %bitcast.at_ref, bf16[256,3712]{1,0:T(8,128)(2,1)} %collective-permute-done.8.x_ref, bf16[3712,512]{1,0:T(8,128)(2,1)S(1)} %copy-done.1, bf16[32,3712]{1,0:T(8,128)(2,1)S(1)} %pad.9.s_ref, bf16[256,3616]{1,0:T(8,128)(2,1)S(1)} %pad_maximum_fusion.1.d_ref, ...), custom_call_target="tpu_custom_call" | custom-call | flops 2407530496 | bytes 9404416 | tf_op jit(solution)/shard_map/pallas_call | solution.py:73
  166.2 2.4 add_convert_fusion.1
  168.6 10.1 %collective-permute-done.12 = bf16[128,3616]{0,1:T(8,128)(2,1)} collective-permute-done((bf16[128,3616]{0,1:T(8,128)(2,1)}, bf16[128,3616]{0,1:T(8,128)(2,1)}, u32[]{:S(2)}, u32[]{:S(2)}) %collective-permute-start.12) | collective-permute-done | bytes 925728 | tf_op jit(solution)/shard_map/ppermute | solution.py:26
  178.7 2.3 copy.74
  184.1 4.0 %copy.75 = bf16[256,3616]{0,1:T(8,128)(2,1)} copy(bf16[256,3616]{1,0:T(8,128)(2,1)} %pad_maximum_fusion.3) | data formatting | bytes 3702784 | tf_op jit(solution)/shard_map/concatenate | solution.py:150
  190.0 2.6 pad_maximum_fusion.4
  192.6 3.9 %copy.79 = bf16[256,3616]{0,1:T(8,128)(2,1)} copy(bf16[256,3616]{1,0:T(8,128)(2,1)} %pad_maximum_fusion.4) | data formatting | bytes 3702784 | tf_op jit(solution)/shard_map/concatenate | solution.py:151
  196.5 4.6 %collective-permute-start.15 = (bf16[256,3616]{0,1:T(8,128)(2,1)}, bf16[256,3616]{0,1:T(8,128)(2,1)}, u32[]{:S(2)}, u32[]{:S(2)}) collective-permute-start(bf16[256,3616]{0,1:T(8,128)(2,1)} %copy.79), channel_id=1, source_target_pairs={{0,48},{1,385},{16,0},{17,401},{32,16},{33,417},{48,32},{49,433},{... | collective-permute-start | bytes 5554184 | tf_op jit(solution)/shard_map/ppermute | solution.py:26
  201.1 2.1 copy-done.2
  204.7 3.3 %shard_map.91 = bf16[256,3616]{1,0:T(8,128)(2,1)S(1)} custom-call(s32[1]{0:T(128)} %bitcast.at_ref, bf16[256,3712]{1,0:T(8,128)(2,1)S(1)} %copy-done.5, bf16[3712,512]{1,0:T(8,128)(2,1)S(1)} %copy-done.2, bf16[32,3712]{1,0:T(8,128)(2,1)S(1)} %pad.9.s_ref, bf16[256,3616]{1,0:T(8,128)(2,1)S(1)} %pad_maximum_fusion.1.d_ref, ...), custom_call_target="tpu_custom_call" | custom-call | flops 2407530496 | bytes 9404416 | tf_op jit(solution)/shard_map/pallas_call | solution.py:73
  209.3 4.8 %collective-permute-done.13 = bf16[256,3616]{0,1:T(8,128)(2,1)} collective-permute-done((bf16[256,3616]{0,1:T(8,128)(2,1)}, bf16[256,3616]{0,1:T(8,128)(2,1)}, u32[]{:S(2)}, u32[]{:S(2)}) %collective-permute-start.13) | collective-permute-done | bytes 1851424 | tf_op jit(solution)/shard_map/ppermute | solution.py:26
  214.1 3.9 %copy.76 = bf16[256,3616]{1,0:T(8,128)(2,1)} copy(bf16[256,3616]{0,1:T(8,128)(2,1)} %collective-permute-done.13) | data formatting | bytes 3702784 | tf_op jit(solution)/shard_map/ppermute | solution.py:26
  218.0 3.7 %collective-permute-done.15 = bf16[256,3616]{0,1:T(8,128)(2,1)} collective-permute-done((bf16[256,3616]{0,1:T(8,128)(2,1)}, bf16[256,3616]{0,1:T(8,128)(2,1)}, u32[]{:S(2)}, u32[]{:S(2)}) %collective-permute-start.15) | collective-permute-done | bytes 1851424 | tf_op jit(solution)/shard_map/ppermute | solution.py:26
  221.7 3.9 %copy.80 = bf16[256,3616]{1,0:T(8,128)(2,1)} copy(bf16[256,3616]{0,1:T(8,128)(2,1)} %collective-permute-done.15) | data formatting | bytes 3702784 | tf_op jit(solution)/shard_map/ppermute | solution.py:26
  225.6 2.8 add_convert_fusion
  228.4 2.7 collective-permute-start.16
  231.1 3.1 %collective-permute-start.18 = (bf16[64,3616]{1,0:T(8,128)(2,1)S(1)}, bf16[64,3616]{1,0:T(8,128)(2,1)S(1)}, u32[]{:S(2)}, u32[]{:S(2)}) collective-permute-start(bf16[64,3616]{1,0:T(8,128)(2,1)S(1)} %get-tuple-element.8), channel_id=1, source_target_pairs={{0,256},{1,33},{16,272},{17,49},{32,288},{33,1},{48,304},{49,17},{... | collective-permute-start | bytes 1388552 | tf_op jit(solution)/shard_map/ppermute | solution.py:26
  234.2 1.9 collective-permute-start.17
  236.1 2.0 collective-permute-done.16
  238.1 4.2 %collective-permute-done.18 = bf16[64,3616]{1,0:T(8,128)(2,1)S(1)} collective-permute-done((bf16[64,3616]{1,0:T(8,128)(2,1)S(1)}, bf16[64,3616]{1,0:T(8,128)(2,1)S(1)}, u32[]{:S(2)}, u32[]{:S(2)}) %collective-permute-start.18) | collective-permute-done | bytes 462880 | tf_op jit(solution)/shard_map/ppermute | solution.py:26
  242.4 5.0 %collective-permute-done.17 = bf16[64,3616]{1,0:T(8,128)(2,1)S(1)} collective-permute-done((bf16[64,3616]{1,0:T(8,128)(2,1)S(1)}, bf16[64,3616]{1,0:T(8,128)(2,1)S(1)}, u32[]{:S(2)}, u32[]{:S(2)}) %collective-permute-start.17) | collective-permute-done | bytes 462880 | tf_op jit(solution)/shard_map/ppermute | solution.py:26
  249.5 21.9 %all_to_all.10 = bf16[16,64,226]{2,1,0:T(8,128)(2,1)S(1)} all-to-all(bf16[16,64,226]{2,1,0:T(8,128)(2,1)S(1)} %bitcast.29), channel_id=1, replica_groups=mesh['y'=4,'h'=2,'x'=4,'l'=8,'c'=2] {'h','l'}, dimensions={0} | all-to-all | bytes 925696 | tf_op jit(solution)/shard_map/all_to_all | solution.py:156
  271.5 19.7 %collective-permute-start.19 = (bf16[64,226]{1,0:T(8,128)(2,1)S(1)}, bf16[64,226]{1,0:T(8,128)(2,1)S(1)}, u32[]{:S(2)}, u32[]{:S(2)}) collective-permute-start(bf16[64,226]{1,0:T(8,128)(2,1)S(1)} %reduce_sum.32), channel_id=1, source_target_pairs={{0,0},{1,64},{64,1},{65,65},{2,2},{3,66},{66,3},{67,67},{4,4},{5,6... | collective-permute-start | bytes 86792 | tf_op jit(solution)/shard_map/ppermute | solution.py:34
  (90 shorter events, 35.2 us)
Async XLA Ops:
  3.3 18.4 %collective-permute-start = (bf16[64,256]{1,0:T(8,128)(2,1)S(1)}, bf16[64,256]{1,0:T(8,128)(2,1)S(1)}, u32[]{:S(2)}, u32[]{:S(2)}) collective-permute-start(bf16[64,256]{1,0:T(8,128)(2,1)S(1)} %maximum_maximum_fusion.1), channel_id=1, source_target_pairs={{0,0},{1,64},{64,1},{65,65},{2,2},{3,66},{66,3},{67,67},{4,4},{5,6... | collective-permute-start | bytes 98312 | tf_op jit(solution)/shard_map/ppermute | solution.py:34
  46.2 11.6 %copy-start.10 = (bf16[113,128]{1,0:T(8,128)(2,1)S(1)}, bf16[113,128]{1,0:T(8,128)(2,1)}, u32[]{:S(2)}) copy-start(bf16[113,128]{1,0:T(8,128)(2,1)} %param.15) | copy-start | bytes 86788
  46.3 11.7 %copy-start.11 = (bf16[113,128]{1,0:T(8,128)(2,1)S(1)}, bf16[113,128]{1,0:T(8,128)(2,1)}, u32[]{:S(2)}) copy-start(bf16[113,128]{1,0:T(8,128)(2,1)} %param.16) | copy-start | bytes 86788
  46.3 11.9 %copy-start.12 = (bf16[128,113]{0,1:T(8,128)(2,1)S(1)}, bf16[128,113]{0,1:T(8,128)(2,1)}, u32[]{:S(2)}) copy-start(bf16[128,113]{0,1:T(8,128)(2,1)} %param.17) | copy-start | bytes 86788
  47.9 25.5 %collective-permute-start.3 = (bf16[64,3712]{1,0:T(8,128)(2,1)S(1)}, bf16[64,3712]{1,0:T(8,128)(2,1)S(1)}, u32[]{:S(2)}, u32[]{:S(2)}) collective-permute-start(bf16[64,3712]{1,0:T(8,128)(2,1)S(1)} %concatenate.29), channel_id=1, source_target_pairs={{0,256},{1,33},{16,272},{17,49},{32,288},{33,1},{48,304},{49,17},{... | collective-permute-start | bytes 1425416 | tf_op jit(solution)/shard_map/ppermute | solution.py:26
  52.6 20.8 %collective-permute-start.2 = (bf16[64,3712]{1,0:T(8,128)(2,1)S(1)}, bf16[64,3712]{1,0:T(8,128)(2,1)S(1)}, u32[]{:S(2)}, u32[]{:S(2)}) collective-permute-start(bf16[64,3712]{1,0:T(8,128)(2,1)S(1)} %concatenate.29), channel_id=1, source_target_pairs={{0,384},{1,49},{16,400},{17,1},{32,416},{33,17},{48,432},{49,33},{... | collective-permute-start | bytes 1425416 | tf_op jit(solution)/shard_map/ppermute | solution.py:26
  55.3 18.0 %collective-permute-start.1 = (bf16[64,3712]{1,0:T(8,128)(2,1)S(1)}, bf16[64,3712]{1,0:T(8,128)(2,1)}, u32[]{:S(2)}, u32[]{:S(2)}) collective-permute-start(bf16[64,3712]{1,0:T(8,128)(2,1)S(1)} %concatenate.29), channel_id=1, source_target_pairs={{0,128},{1,17},{16,144},{17,33},{32,160},{33,49},{48,176},{49,1},{... | collective-permute-start | bytes 1425416 | tf_op jit(solution)/shard_map/ppermute | solution.py:26
  59.1 30.6 %all-to-all-start = ((bf16[32,12,113]{2,1,0:T(8,128)(2,1)}), bf16[32,12,113]{2,1,0:T(8,128)(2,1)S(1)}, u32[]{:S(2)}, u32[]{:S(2)}) async-start(bf16[32,12,113]{2,1,0:T(8,128)(2,1)} %copy.68), calls=%async_computation | async-start | bytes 262144 | tf_op jit(solution)/shard_map/all_to_all | solution.py:135
  74.5 35.9 %copy-start.4 = (bf16[256,3712]{1,0:T(8,128)(2,1)}, bf16[256,3712]{1,0:T(8,128)(2,1)S(1)}, u32[]{:S(2)}) copy-start(bf16[256,3712]{1,0:T(8,128)(2,1)S(1)} %pad_maximum_fusion.x_ref) | copy-start | bytes 5701636
  74.6 40.7 %collective-permute-start.9 = (bf16[256,3712]{1,0:T(8,128)(2,1)S(1)}, bf16[256,3712]{1,0:T(8,128)(2,1)}, u32[]{:S(2)}, u32[]{:S(2)}) collective-permute-start(bf16[256,3712]{1,0:T(8,128)(2,1)S(1)} %pad_maximum_fusion.x_ref), channel_id=1, source_target_pairs={{0,16},{1,129},{16,32},{17,145},{32,48},{33,161},{48,0},{49,177},{... | collective-permute-start | bytes 5701640 | tf_op jit(solution)/shard_map/ppermute | solution.py:26
  77.7 41.2 %collective-permute-start.8 = (bf16[256,3712]{1,0:T(8,128)(2,1)S(1)}, bf16[256,3712]{1,0:T(8,128)(2,1)}, u32[]{:S(2)}, u32[]{:S(2)}) collective-permute-start(bf16[256,3712]{1,0:T(8,128)(2,1)S(1)} %pad_maximum_fusion.x_ref), channel_id=1, source_target_pairs={{0,48},{1,385},{16,0},{17,401},{32,16},{33,417},{48,32},{49,433},{... | collective-permute-start | bytes 5701640 | tf_op jit(solution)/shard_map/ppermute | solution.py:26
  89.9 18.3 %collective-permute-start.6 = (bf16[3,4,3616]{2,1,0:T(4,128)(2,1)S(1)}, bf16[3,4,3616]{2,1,0:T(4,128)(2,1)S(1)}, u32[]{:S(2)}, u32[]{:S(2)}) collective-permute-start(bf16[3,4,3616]{2,1,0:T(4,128)(2,1)S(1)} %reshape.55), channel_id=1, source_target_pairs={{0,1},{1,0},{2,3},{3,2},{4,5},{5,4},{6,7},{7,6},{8,9},{9,8},{10,11... | collective-permute-start | bytes 260360 | tf_op jit(solution)/shard_map/ppermute | solution.py:30
  102.2 22.4 %collective-permute-start.4 = (bf16[3616,128]{1,0:T(8,128)(2,1)}, bf16[3616,128]{1,0:T(8,128)(2,1)}, u32[]{:S(2)}, u32[]{:S(2)}) collective-permute-start(bf16[3616,128]{1,0:T(8,128)(2,1)} %bitcast.4), channel_id=1, source_target_pairs={{0,1},{1,0},{2,3},{3,2},{4,5},{5,4},{6,7},{7,6},{8,9},{9,8},{10,11... | collective-permute-start | bytes 2777096 | tf_op jit(solution)/shard_map/ppermute | solution.py:30
  104.1 20.4 %collective-permute-start.5 = (bf16[3616,128]{1,0:T(8,128)(2,1)}, bf16[3616,128]{1,0:T(8,128)(2,1)}, u32[]{:S(2)}, u32[]{:S(2)}) collective-permute-start(bf16[3616,128]{1,0:T(8,128)(2,1)} %bitcast.5), channel_id=1, source_target_pairs={{0,1},{1,0},{2,3},{3,2},{4,5},{5,4},{6,7},{7,6},{8,9},{9,8},{10,11... | collective-permute-start | bytes 2777096 | tf_op jit(solution)/shard_map/ppermute | solution.py:30
  108.3 4.7 %collective-permute-start.7 = (bf16[128,3616]{0,1:T(8,128)(2,1)}, bf16[128,3616]{0,1:T(8,128)(2,1)}, u32[]{:S(2)}, u32[]{:S(2)}) collective-permute-start(bf16[128,3616]{0,1:T(8,128)(2,1)} %bitcast.31), channel_id=1, source_target_pairs={{0,1},{1,0},{2,3},{3,2},{4,5},{5,4},{6,7},{7,6},{8,9},{9,8},{10,11... | collective-permute-start | bytes 2777096 | tf_op jit(solution)/shard_map/ppermute | solution.py:30
  115.3 9.1 %copy-start.9 = (bf16[128,3616]{1,0:T(8,128)(2,1)S(1)}, bf16[128,3616]{1,0:T(8,128)(2,1)}, u32[]{:S(2)}) copy-start(bf16[128,3616]{1,0:T(8,128)(2,1)} %copy.72) | copy-start | bytes 2777092
  116.6 16.0 %collective-permute-start.10 = (bf16[128,3712]{1,0:T(8,128)(2,1)S(1)}, bf16[128,3712]{1,0:T(8,128)(2,1)S(1)}, u32[]{:S(2)}, u32[]{:S(2)}) collective-permute-start(bf16[128,3712]{1,0:T(8,128)(2,1)S(1)} %slice.73), channel_id=1, source_target_pairs={{0,16},{1,129},{16,32},{17,145},{32,48},{33,161},{48,0},{49,177},{... | collective-permute-start | bytes 2850824 | tf_op jit(solution)/shard_map/ppermute | solution.py:26
  120.1 14.9 %collective-permute-start.11 = (bf16[128,3712]{1,0:T(8,128)(2,1)S(1)}, bf16[128,3712]{1,0:T(8,128)(2,1)S(1)}, u32[]{:S(2)}, u32[]{:S(2)}) collective-permute-start(bf16[128,3712]{1,0:T(8,128)(2,1)S(1)} %slice.74), channel_id=1, source_target_pairs={{0,48},{1,385},{16,0},{17,401},{32,16},{33,417},{48,32},{49,433},{... | collective-permute-start | bytes 2850824 | tf_op jit(solution)/shard_map/ppermute | solution.py:26
  128.1 7.1 %copy-start = (bf16[3712,512]{1,0:T(8,128)(2,1)}, bf16[3712,512]{1,0:T(8,128)(2,1)S(1)}, u32[]{:S(2)}) copy-start(bf16[3712,512]{1,0:T(8,128)(2,1)S(1)} %fusion.6.w_ref) | copy-start | bytes 11403268
  141.8 22.8 %collective-permute-start.14 = (bf16[128,3616]{0,1:T(8,128)(2,1)}, bf16[128,3616]{0,1:T(8,128)(2,1)}, u32[]{:S(2)}, u32[]{:S(2)}) collective-permute-start(bf16[128,3616]{0,1:T(8,128)(2,1)} %copy.77), channel_id=1, source_target_pairs={{0,48},{1,385},{16,0},{17,401},{32,16},{33,417},{48,32},{49,433},{... | collective-permute-start | bytes 2777096 | tf_op jit(solution)/shard_map/ppermute | solution.py:26
  147.0 2.1 copy-start.1
  154.0 1.3 copy-start.6
  160.1 1.2 copy-start.3
  162.7 16.0 %collective-permute-start.12 = (bf16[128,3616]{0,1:T(8,128)(2,1)}, bf16[128,3616]{0,1:T(8,128)(2,1)}, u32[]{:S(2)}, u32[]{:S(2)}) collective-permute-start(bf16[128,3616]{0,1:T(8,128)(2,1)} %copy.73), channel_id=1, source_target_pairs={{0,16},{1,129},{16,32},{17,145},{32,48},{33,161},{48,0},{49,177},{... | collective-permute-start | bytes 2777096 | tf_op jit(solution)/shard_map/ppermute | solution.py:26
  168.6 14.1 %slice-start = ((bf16[256,3616]{1,0:T(8,128)(2,1)}), bf16[128,3616]{1,0:T(8,128)(2,1)S(1)}, s32[]{:S(2)}) async-start(bf16[256,3616]{1,0:T(8,128)(2,1)} %copy-done.3), calls=%async_computation.2 | async-start | bytes 1900544 | tf_op jit(solution)/shard_map/slice | solution.py:150
  184.1 5.9 %slice-start.1 = ((bf16[256,3616]{1,0:T(8,128)(2,1)}), bf16[128,3616]{1,0:T(8,128)(2,1)S(1)}, s32[]{:S(2)}) async-start(bf16[256,3616]{1,0:T(8,128)(2,1)} %copy-done.6), calls=%async_computation.3 | async-start | bytes 1900544 | tf_op jit(solution)/shard_map/slice | solution.py:151
  188.1 26.0 %collective-permute-start.13 = (bf16[256,3616]{0,1:T(8,128)(2,1)}, bf16[256,3616]{0,1:T(8,128)(2,1)}, u32[]{:S(2)}, u32[]{:S(2)}) collective-permute-start(bf16[256,3616]{0,1:T(8,128)(2,1)} %copy.75), channel_id=1, source_target_pairs={{0,16},{1,129},{16,32},{17,145},{32,48},{33,161},{48,0},{49,177},{... | collective-permute-start | bytes 5554184 | tf_op jit(solution)/shard_map/ppermute | solution.py:26
  196.5 25.2 %collective-permute-start.15 = (bf16[256,3616]{0,1:T(8,128)(2,1)}, bf16[256,3616]{0,1:T(8,128)(2,1)}, u32[]{:S(2)}, u32[]{:S(2)}) collective-permute-start(bf16[256,3616]{0,1:T(8,128)(2,1)} %copy.79), channel_id=1, source_target_pairs={{0,48},{1,385},{16,0},{17,401},{32,16},{33,417},{48,32},{49,433},{... | collective-permute-start | bytes 5554184 | tf_op jit(solution)/shard_map/ppermute | solution.py:26
  201.1 2.1 copy-start.2
  203.1 1.5 copy-start.5
  208.0 1.3 copy-start.7
  218.0 7.6 %copy-start.8 = (bf16[256,3616]{1,0:T(8,128)(2,1)S(1)}, bf16[256,3616]{1,0:T(8,128)(2,1)}, u32[]{:S(2)}) copy-start(bf16[256,3616]{1,0:T(8,128)(2,1)} %copy-done.7) | copy-start | bytes 5554180
  228.4 9.7 %collective-permute-start.16 = (bf16[64,3616]{1,0:T(8,128)(2,1)S(1)}, bf16[64,3616]{1,0:T(8,128)(2,1)S(1)}, u32[]{:S(2)}, u32[]{:S(2)}) collective-permute-start(bf16[64,3616]{1,0:T(8,128)(2,1)S(1)} %get-tuple-element.7), channel_id=1, source_target_pairs={{0,384},{1,49},{16,400},{17,1},{32,416},{33,17},{48,432},{49,33},{... | collective-permute-start | bytes 1388552 | tf_op jit(solution)/shard_map/ppermute | solution.py:26
  231.1 11.2 %collective-permute-start.18 = (bf16[64,3616]{1,0:T(8,128)(2,1)S(1)}, bf16[64,3616]{1,0:T(8,128)(2,1)S(1)}, u32[]{:S(2)}, u32[]{:S(2)}) collective-permute-start(bf16[64,3616]{1,0:T(8,128)(2,1)S(1)} %get-tuple-element.8), channel_id=1, source_target_pairs={{0,256},{1,33},{16,272},{17,49},{32,288},{33,1},{48,304},{49,17},{... | collective-permute-start | bytes 1388552 | tf_op jit(solution)/shard_map/ppermute | solution.py:26
  234.2 13.2 %collective-permute-start.17 = (bf16[64,3616]{1,0:T(8,128)(2,1)S(1)}, bf16[64,3616]{1,0:T(8,128)(2,1)S(1)}, u32[]{:S(2)}, u32[]{:S(2)}) collective-permute-start(bf16[64,3616]{1,0:T(8,128)(2,1)S(1)} %get-tuple-element.9), channel_id=1, source_target_pairs={{0,128},{1,17},{16,144},{17,33},{32,160},{33,49},{48,176},{49,1},{... | collective-permute-start | bytes 1388552 | tf_op jit(solution)/shard_map/ppermute | solution.py:26
  271.5 21.4 %collective-permute-start.19 = (bf16[64,226]{1,0:T(8,128)(2,1)S(1)}, bf16[64,226]{1,0:T(8,128)(2,1)S(1)}, u32[]{:S(2)}, u32[]{:S(2)}) collective-permute-start(bf16[64,226]{1,0:T(8,128)(2,1)S(1)} %reduce_sum.32), channel_id=1, source_target_pairs={{0,0},{1,64},{64,1},{65,65},{2,2},{3,66},{66,3},{67,67},{4,4},{5,6... | collective-permute-start | bytes 86792 | tf_op jit(solution)/shard_map/ppermute | solution.py:34

commit v3 on v2

--- a/solution.py
+++ b/solution.py
@@ -41,47 +41,45 @@
     return total.astype(bf16)
 
 
-def ffn_kernel(at_ref, x_ref, w_ref, s_ref, d_ref, sd_ref, o_ref, *, hid, units):
-    width = x_ref.shape[1]
-    tail = x_ref[:, width - 128 :].astype(f32)
+def ffn_kernel(at_ref, *refs, hid, parts):
+    w_ref, d_ref = refs[parts : parts + 2]
+    o_refs = refs[parts + 2 :]
+    x = jnp.concatenate([r[...] for r in refs[:parts]], 0)
+    width = x.shape[1]
+    tail = x[:, width - 128 :].astype(f32)
     lane = lax.broadcasted_iota(jnp.int32, tail.shape, 1)
     at = at_ref[0]
     weight = jnp.sum(
         jnp.where((lane == at) | (lane == at + 2), tail, 0.0), axis=1, keepdims=True
     )
-    x = x_ref[...]
     acts = jnp.dot(x, w_ref[...], preferred_element_type=f32)
     gate, up = acts[:, :hid], acts[:, hid:]
     hidden = (gate / (1.0 + jnp.exp(-gate)) * up * weight).astype(bf16)
-    nt = (((1,), (1,)), ((), ()))
-    s_gate = lax.dot_general(x, s_ref[:units], nt, preferred_element_type=f32)
-    s_up = lax.dot_general(x, s_ref[units:], nt, preferred_element_type=f32)
-    s_hidden = (s_gate / (1.0 + jnp.exp(-s_gate)) * s_up).astype(bf16)
-    cols = o_ref.shape[1]
-    for lo in range(0, cols, 512):
-        hi = min(lo + 512, cols)
-        o_ref[:, lo:hi] = (
-            jnp.dot(hidden, d_ref[:, lo:hi], preferred_element_type=f32)
-            + jnp.dot(s_hidden, sd_ref[:, lo:hi], preferred_element_type=f32)
-        ).astype(bf16)
+    rows = x.shape[0] // parts
+    for lo in range(0, width, 512):
+        hi = min(lo + 512, width)
+        out = jnp.dot(hidden, d_ref[:, lo:hi], preferred_element_type=f32).astype(bf16)
+        for i, o_ref in enumerate(o_refs):
+            o_ref[:, lo:hi] = out[i * rows : (i + 1) * rows]
 
 
-def ffn(at, x, w_in, s_in, w_out, s_out):
-    rows, width = x.shape
-    hid, units, cols = w_in.shape[1] // 2, s_in.shape[0] // 2, w_out.shape[1]
+def ffn(at, xs, w_in, w_out):
+    parts = len(xs)
+    rows, width = xs[0].shape
+    hid = w_in.shape[1] // 2
     whole = pl.BlockSpec(memory_space=pltpu.VMEM)
     return pl.pallas_call(
-        functools.partial(ffn_kernel, hid=hid, units=units),
-        out_shape=jax.ShapeDtypeStruct((rows, cols), bf16),
-        in_specs=[pl.BlockSpec(memory_space=pltpu.SMEM)] + [whole] * 5,
-        out_specs=whole,
+        functools.partial(ffn_kernel, hid=hid, parts=parts),
+        out_shape=[jax.ShapeDtypeStruct((rows, width), bf16)] * parts,
+        in_specs=[pl.BlockSpec(memory_space=pltpu.SMEM)] + [whole] * (parts + 2),
+        out_specs=[whole] * parts,
         compiler_params=pltpu.CompilerParams(vmem_limit_bytes=40 * 1024 * 1024),
         cost_estimate=pl.CostEstimate(
-            flops=2 * rows * (width * 3 * hid + 2 * hid * cols),
-            bytes_accessed=2 * (rows * (width + cols) + width * 2 * hid + hid * cols),
-            transcendentals=rows * hid,
+            flops=2 * parts * rows * width * 3 * hid,
+            bytes_accessed=2 * (2 * parts * rows * width + 3 * width * hid),
+            transcendentals=parts * rows * hid,
         ),
-    )(at, x, w_in, s_in, w_out, s_out)
+    )(at, *xs, w_in, w_out)
 
 
 def local(
@@ -128,30 +126,35 @@
     w_in = jnp.concatenate([w_gate, swap(w_gate), w_up, swap(w_up)], 1)
     w_in = jnp.pad(w_in, ((0, full - feats), (0, 0)))
     w_out = jnp.concatenate([w_down, swap(w_down)], 0)
-    units = shared_gate.shape[1] // n_exp
+    w_out = jnp.pad(w_out, ((0, 0), (0, full - feats)))
+
     depth = shared_gate.shape[0]
-    s = jnp.stack([shared_gate.T, shared_up.T, shared_down]).reshape(3, n_exp, units, depth)
-    s = s.transpose(1, 0, 2, 3).reshape(n_exp, 3 * units, depth)
-    s = lax.all_to_all(s, EXPERT, split_axis=0, concat_axis=0, tiled=True)
-    s = s.transpose(1, 0, 2).reshape(3, units, feats)
-    s = jnp.concatenate([s, swap(s), jnp.zeros((3, 16 - 2 * units, feats), bf16)], 1)
-    s_in = jnp.pad(s[:2].reshape(32, feats), ((0, 0), (0, full - feats)))
-    s_out = s[2]
-
-    apply = lambda block: ffn(at, block, w_in, s_in, w_out, s_out)
+    s = jnp.concatenate([shared_gate, shared_up, shared_down.T], 0)
+    s = jnp.pad(s, ((0, -s.shape[0] % 16), (0, 0)))
+    s = lax.all_gather(turn(s), ("y", "c", "x"), axis=0, tiled=False)
+    s_gate, s_up, s_down = (
+        s[:, i * depth : (i + 1) * depth].reshape(feats, s.shape[2]) for i in range(3)
+    )
+    s_gate = jnp.dot(rows[:, :feats], s_gate, preferred_element_type=f32)
+    s_up = jnp.dot(rows[:, :feats], s_up, preferred_element_type=f32)
+    s_hidden = (jax.nn.silu(s_gate) * s_up).astype(bf16)
+    shared = lax.dot_general(s_hidden, s_down, (((1,), (1,)), ((), ())), preferred_element_type=f32)
 
     near = jnp.concatenate([rows, move(rows, 0, 1), move(rows, 0, -1), move(rows, 0, 2)], 0)
     m = near.shape[0] // 2
     prev, succ = move(near, 1, 1), move(near, 1, -1)
-    far = jnp.concatenate([move(prev[:m], 1, 1), move(succ[m:], 1, -1)], 0)
-    own_out, prev_out, succ_out, far_out = apply(near), apply(prev), apply(succ), apply(far)
+    far = [move(prev[:m], 1, 1), move(succ[m:], 1, -1)]
+    far_lo, far_hi = ffn(at, far, w_in, w_out)
+    (prev_out,), (succ_out,) = ffn(at, [prev], w_in, w_out), ffn(at, [succ], w_in, w_out)
+    (own_out,) = ffn(at, [near], w_in, w_out)
 
-    from_prev, from_succ = move(far_out[:m], 1, 1), move(far_out[m:], 1, -1)
-    to_succ = jnp.concatenate([add(succ_out[:m], from_prev), succ_out[m:]], 0)
-    to_prev = jnp.concatenate([prev_out[:m], add(prev_out[m:], from_succ)], 0)
+    from_prev, from_succ = move(far_lo, 1, 1), move(far_hi, 1, -1)
+    to_succ = succ_out.at[:m].set(add(succ_out[:m], from_prev))
+    to_prev = prev_out.at[m:].set(add(prev_out[m:], from_succ))
     total = add(own_out, move(to_succ, 1, 1), move(to_prev, 1, -1))
-    total = total.reshape(4, toks, feats)
-    total = add(total[0], move(total[1], 0, -1), move(total[2], 0, 1), move(total[3], 0, 2))
+    total = total.reshape(4, toks, full)
+    total = [total[0], move(total[1], 0, -1), move(total[2], 0, 1), move(total[3], 0, 2)]
+    total = add(shared, *[t[:, :feats] for t in total])
     back = total.reshape(toks, L, H, width).transpose(2, 1, 0, 3).reshape(H * L, toks, width)
     back = lax.all_to_all(back, Z, split_axis=0, concat_axis=0, tiled=True)
     return turn(jnp.sum(back.astype(f32), axis=0).astype(bf16))

time: 295 us -> 302 us (1.024)
  local copies, waits for them, and re-layouts: 46.5 us -> 25 us
  blocking collectives: 45.8 us -> 63.2 us
  between operations: 0.66 us -> 13.9 us
  other arithmetic: 19.5 us -> 9.6 us
  starting transfers between devices: 113 us -> 122 us
  Pallas kernels: 16.3 us -> 11.6 us
  matrix products: 0 us -> 4.17 us
    all_to_all x1, blocking collectives: 21.9 us -> 39.3 us  [local(): back = lax.all_to_all(back, Z, split_axis=0, concat_axis=0, tiled=True)]
    ppermute x2 -> x3, starting transfers between devices: 36.5 us -> 51.7 us  [turn(): lax.ppermute(a, ('h', 'c'), [(h * 2 + c, c * 2 + h) for h in range(2) for...]
    all_to_all x1 -> x0, starting transfers between devices: 14.3 us -> none  [local(): s = lax.all_to_all(s, EXPERT, split_axis=0, concat_axis=0, tiled=True)]
    ppermute x4 -> x0, local copies, waits for them, and re-layouts: 11.6 us -> none  [move(): return lax.ppermute(a, ('y', 'x', 'c'), pairs)]
    all_to_all x1 -> x0, waiting for transfers between devices: 8.61 us -> none  [local(): s = lax.all_to_all(s, EXPERT, split_axis=0, concat_axis=0, tiled=True)]
    concatenate x3 -> x0, local copies, waits for them, and re-layouts: 7.9 us -> none  [the longest x1 3.96 us: local(): to_succ = jnp.concatenate([add(succ_out[:m], from_prev), succ_out[m:]], 0)]
    ppermute x14, waiting for transfers between devices: 36.9 us -> 44.7 us  [move(): return lax.ppermute(a, ('y', 'x', 'c'), pairs)]
    unnamed x31 -> x22, local copies, waits for them, and re-layouts: 12.1 us -> 4.96 us
  transfers between devices with their start and end apart: 21 -> 21, of which waited for: 12 -> 12; matrix products, arithmetic and copies ran while one was open for 10% -> 8% of each run, Pallas kernels for 4% -> 3%
where the time goes in v3:
time: 302 us; the launch traced here: 300 us
  starting transfers between devices  122 us (40%)
  blocking collectives  63.2 us (21%)
  waiting for transfers between devices  50.4 us (17%)
  local copies, waits for them, and re-layouts  25 us (8%)
  between operations  13.9 us (5%)
  Pallas kernels  11.6 us (4%)
  other arithmetic  9.6 us (3%)
  matrix products  4.17 us (1%)
    ppermute x3, starting transfers between devices, turn(): lax.ppermute(a, ('h', 'c'), [(h * 2 + c, c * 2 + h) for h in range(2) for...  51.7 us
    ppermute x14, starting transfers between devices, move(): return lax.ppermute(a, ('y', 'x', 'c'), pairs)  45.5 us
    ppermute x14, waiting for transfers between devices, move(): return lax.ppermute(a, ('y', 'x', 'c'), pairs)  44.7 us
    all_to_all x1, blocking collectives, local(): back = lax.all_to_all(back, Z, split_axis=0, concat_axis=0, tiled=True)  39.3 us
    ppermute x3, starting transfers between devices, swap(): return lax.ppermute(a, 'c', [(0, 1), (1, 0)])  25.3 us
    all_gather x1, blocking collectives, local(): got = lax.all_gather(turn(sent), Z, axis=0, tiled=False)  23.9 us
    pallas_call x4, Pallas kernels, ffn(): pl.pallas_call(functools.partial(ffn_kernel, hid=hid, parts=parts), out_s...  11.6 us
  transfers between devices with their start and end apart: 21, of which 12 were waited for; matrix products, arithmetic and copies ran while one was open for 8% of the time, Pallas kernels for 3%

profile of v3, /device:TPU:1, one launch (start us, length us, event | category | flops | bytes accessed | tf_op | source)
XLA Modules:
  0.0 300.3 jit_solution(12079801252023845811)
XLA Ops:
  9.9 16.8 %collective-permute-start = (bf16[64,256]{1,0:T(8,128)(2,1)S(1)}, bf16[64,256]{1,0:T(8,128)(2,1)S(1)}, u32[]{:S(2)}, u32[]{:S(2)}) collective-permute-start(bf16[64,256]{1,0:T(8,128)(2,1)S(1)} %maximum_maximum_fusion), channel_id=1, source_target_pairs={{0,0},{1,64},{64,1},{65,65},{2,2},{3,66},{66,3},{67,67},{4,4},{5,6... | collective-permute-start | bytes 98312 | tf_op jit(solution)/shard_map/ppermute | solution.py:34
  26.7 1.6 collective-permute-done
  28.3 23.9 %all-gather = bf16[1024,256]{1,0:T(8,128)(2,1)S(1)} all-gather(bf16[64,256]{1,0:T(8,128)(2,1)S(1)} %collective-permute-done), channel_id=2, replica_groups=mesh['y'=4,'h'=2,'x'=4,'l'=8,'c'=2] {'h','l'}, dimensions={0}, use_global_device_ids=true | all-gather | bytes 557056 | tf_op jit(solution)/shard_map/all_gather | solution.py:113
  54.4 3.1 %collective-permute-start.2 = (bf16[64,3712]{1,0:T(8,128)(2,1)S(1)}, bf16[64,3712]{1,0:T(8,128)(2,1)S(1)}, u32[]{:S(2)}, u32[]{:S(2)}) collective-permute-start(bf16[64,3712]{1,0:T(8,128)(2,1)S(1)} %concatenate.24), channel_id=1, source_target_pairs={{0,128},{1,17},{16,144},{17,33},{32,160},{33,49},{48,176},{49,1},{... | collective-permute-start | bytes 1425416 | tf_op jit(solution)/shard_map/ppermute | solution.py:26
  57.5 3.4 %collective-permute-start.3 = (bf16[64,3712]{1,0:T(8,128)(2,1)S(1)}, bf16[64,3712]{1,0:T(8,128)(2,1)S(1)}, u32[]{:S(2)}, u32[]{:S(2)}) collective-permute-start(bf16[64,3712]{1,0:T(8,128)(2,1)S(1)} %concatenate.24), channel_id=1, source_target_pairs={{0,384},{1,49},{16,400},{17,1},{32,416},{33,17},{48,432},{49,33},{... | collective-permute-start | bytes 1425416 | tf_op jit(solution)/shard_map/ppermute | solution.py:26
  60.9 3.4 %collective-permute-start.4 = (bf16[64,3712]{1,0:T(8,128)(2,1)S(1)}, bf16[64,3712]{1,0:T(8,128)(2,1)S(1)}, u32[]{:S(2)}, u32[]{:S(2)}) collective-permute-start(bf16[64,3712]{1,0:T(8,128)(2,1)S(1)} %concatenate.24), channel_id=1, source_target_pairs={{0,256},{1,33},{16,272},{17,49},{32,288},{33,1},{48,304},{49,17},{... | collective-permute-start | bytes 1425416 | tf_op jit(solution)/shard_map/ppermute | solution.py:26
  65.0 1.9 collective-permute-done.3
  66.9 4.9 %collective-permute-done.4 = bf16[64,3712]{1,0:T(8,128)(2,1)S(1)} collective-permute-done((bf16[64,3712]{1,0:T(8,128)(2,1)S(1)}, bf16[64,3712]{1,0:T(8,128)(2,1)S(1)}, u32[]{:S(2)}, u32[]{:S(2)}) %collective-permute-start.4) | collective-permute-done | bytes 475168 | tf_op jit(solution)/shard_map/ppermute | solution.py:26
  72.0 3.2 %collective-permute-start.9 = (bf16[256,3712]{1,0:T(8,128)(2,1)S(1)}, bf16[256,3712]{1,0:T(8,128)(2,1)}, u32[]{:S(2)}, u32[]{:S(2)}) collective-permute-start(bf16[256,3712]{1,0:T(8,128)(2,1)S(1)} %pad_maximum_fusion.refs_0_), channel_id=1, source_target_pairs={{0,16},{1,129},{16,32},{17,145},{32,48},{33,161},{48,0},{49,177},{... | collective-permute-start | bytes 5701640 | tf_op jit(solution)/shard_map/ppermute | solution.py:26
  75.2 3.4 %collective-permute-start.8 = (bf16[256,3712]{1,0:T(8,128)(2,1)S(1)}, bf16[256,3712]{1,0:T(8,128)(2,1)}, u32[]{:S(2)}, u32[]{:S(2)}) collective-permute-start(bf16[256,3712]{1,0:T(8,128)(2,1)S(1)} %pad_maximum_fusion.refs_0_), channel_id=1, source_target_pairs={{0,48},{1,385},{16,0},{17,401},{32,16},{33,417},{48,32},{49,433},{... | collective-permute-start | bytes 5701640 | tf_op jit(solution)/shard_map/ppermute | solution.py:26
  78.5 20.9 %collective-permute-start.7 = (bf16[128,3616]{0,1:T(8,128)(2,1)}, bf16[128,3616]{0,1:T(8,128)(2,1)}, u32[]{:S(2)}, u32[]{:S(2)}) collective-permute-start(bf16[128,3616]{0,1:T(8,128)(2,1)} %bitcast.9), channel_id=1, source_target_pairs={{0,1},{1,0},{2,3},{3,2},{4,5},{5,4},{6,7},{7,6},{8,9},{9,8},{10,11... | collective-permute-start | bytes 2777096 | tf_op jit(solution)/shard_map/ppermute | solution.py:30
  99.5 1.9 collective-permute-start.5
  101.4 2.4 collective-permute-start.6
  103.8 1.6 copy.35
  105.5 2.3 copy.37
  107.7 1.3 slice.110
  109.1 3.9 %collective-permute-start.10 = (bf16[128,3712]{1,0:T(8,128)(2,1)S(1)}, bf16[128,3712]{1,0:T(8,128)(2,1)S(1)}, u32[]{:S(2)}, u32[]{:S(2)}) collective-permute-start(bf16[128,3712]{1,0:T(8,128)(2,1)S(1)} %slice.110), channel_id=1, source_target_pairs={{0,16},{1,129},{16,32},{17,145},{32,48},{33,161},{48,0},{49,177},{... | collective-permute-start | bytes 2850824 | tf_op jit(solution)/shard_map/ppermute | solution.py:26
  114.3 2.6 collective-permute-start.11
  117.0 3.6 %fusion.10.refs_1_.refs_2_ = bf16[3712,512]{1,0:T(8,128)(2,1)S(1)} fusion(bf16[3616,128]{1,0:T(8,128)(2,1)} %collective-permute-done.6, bf16[3616,128]{1,0:T(8,128)(2,1)} %bitcast.7, bf16[3616,128]{1,0:T(8,128)(2,1)} %collective-permute-done.5, bf16[3616,128]{1,0:T(8,128)(2,1)} %bitcast.6), kind=kLoop, calls=%fused_computation.12 | loop fusion | flops 24707072 | bytes 7503872 | tf_op jit(solution)/shard_map/concatenate | solution.py:126
  120.6 4.2 %collective-permute-done.10.refs_0_ = bf16[128,3712]{1,0:T(8,128)(2,1)S(1)} collective-permute-done((bf16[128,3712]{1,0:T(8,128)(2,1)S(1)}, bf16[128,3712]{1,0:T(8,128)(2,1)S(1)}, u32[]{:S(2)}, u32[]{:S(2)}) %collective-permute-start.10) | collective-permute-done | bytes 950304 | tf_op jit(solution)/shard_map/ppermute | solution.py:26
  124.8 4.3 %collective-permute-done.11.refs_1_ = bf16[128,3712]{1,0:T(8,128)(2,1)S(1)} collective-permute-done((bf16[128,3712]{1,0:T(8,128)(2,1)S(1)}, bf16[128,3712]{1,0:T(8,128)(2,1)S(1)}, u32[]{:S(2)}, u32[]{:S(2)}) %collective-permute-start.11) | collective-permute-done | bytes 950304 | tf_op jit(solution)/shard_map/ppermute | solution.py:26
  129.1 2.8 shard_map.93
  131.9 1.9 collective-permute-start.12
  133.9 15.2 %collective-permute-start.1 = (bf16[352,128]{1,0:T(8,128)(2,1)S(1)}, bf16[352,128]{1,0:T(8,128)(2,1)S(1)}, u32[]{:S(2)}, u32[]{:S(2)}) collective-permute-start(bf16[352,128]{1,0:T(8,128)(2,1)S(1)} %fusion.21), channel_id=1, source_target_pairs={{0,0},{1,64},{64,1},{65,65},{2,2},{3,66},{66,3},{67,67},{4,4},{5,6... | collective-permute-start | bytes 270344 | tf_op jit(solution)/shard_map/ppermute | solution.py:34
  149.1 2.3 collective-permute-done.1
  152.1 2.1 copy-done.1
  154.1 3.5 %shard_map.92 = bf16[256,3712]{1,0:T(8,128)(2,1)S(1)} custom-call(s32[1]{0:T(128)} %bitcast.4.at_ref, bf16[256,3712]{1,0:T(8,128)(2,1)} %collective-permute-done.8.refs_0_, bf16[3712,512]{1,0:T(8,128)(2,1)S(1)} %copy-done.1, bf16[256,3712]{1,0:T(8,128)(2,1)S(1)} %fusion.13.refs_2_.refs_3_), custom_call_target="tpu_custom_call" | custom-call | flops 1459617792 | bytes 9502720 | tf_op jit(solution)/shard_map/pallas_call | solution.py:71
  157.7 3.4 %shard_map.94 = bf16[256,3712]{1,0:T(8,128)(2,1)S(1)} custom-call(s32[1]{0:T(128)} %bitcast.4.at_ref, bf16[256,3712]{1,0:T(8,128)(2,1)} %collective-permute-done.9.refs_0_, bf16[3712,512]{1,0:T(8,128)(2,1)S(1)} %copy-done.2, bf16[256,3712]{1,0:T(8,128)(2,1)S(1)} %fusion.13.refs_2_.refs_3_), custom_call_target="tpu_custom_call" | custom-call | flops 1459617792 | bytes 9502720 | tf_op jit(solution)/shard_map/pallas_call | solution.py:71
  161.1 3.7 %collective-permute-start.14 = (bf16[128,3712]{1,0:T(8,128)(2,1)S(1)}, bf16[128,3712]{1,0:T(8,128)(2,1)S(1)}, u32[]{:S(2)}, u32[]{:S(2)}) collective-permute-start(bf16[128,3712]{1,0:T(8,128)(2,1)S(1)} %get-tuple-element.32), channel_id=1, source_target_pairs={{0,48},{1,385},{16,0},{17,401},{32,16},{33,417},{48,32},{49,433},{... | collective-permute-start | bytes 2850824 | tf_op jit(solution)/shard_map/ppermute | solution.py:26
  164.7 1.5 fusion.15
  166.2 2.1 collective-permute-start.13
  168.3 7.6 %collective-permute-done.14 = bf16[128,3712]{1,0:T(8,128)(2,1)S(1)} collective-permute-done((bf16[128,3712]{1,0:T(8,128)(2,1)S(1)}, bf16[128,3712]{1,0:T(8,128)(2,1)S(1)}, u32[]{:S(2)}, u32[]{:S(2)}) %collective-permute-start.14) | collective-permute-done | bytes 950304 | tf_op jit(solution)/shard_map/ppermute | solution.py:26
  176.3 5.4 %collective-permute-start.15 = (bf16[256,3712]{1,0:T(8,128)(2,1)S(1)}, bf16[256,3712]{1,0:T(8,128)(2,1)S(1)}, u32[]{:S(2)}, u32[]{:S(2)}) collective-permute-start(bf16[256,3712]{1,0:T(8,128)(2,1)S(1)} %fusion.16), channel_id=1, source_target_pairs={{0,48},{1,385},{16,0},{17,401},{32,16},{33,417},{48,32},{49,433},{... | collective-permute-start | bytes 5701640 | tf_op jit(solution)/shard_map/ppermute | solution.py:26
  181.7 1.8 shard_map.91
  183.6 10.2 %collective-permute-done.13 = bf16[256,3712]{1,0:T(8,128)(2,1)S(1)} collective-permute-done((bf16[256,3712]{1,0:T(8,128)(2,1)S(1)}, bf16[256,3712]{1,0:T(8,128)(2,1)S(1)}, u32[]{:S(2)}, u32[]{:S(2)}) %collective-permute-start.13) | collective-permute-done | bytes 1900576 | tf_op jit(solution)/shard_map/ppermute | solution.py:26
  193.7 10.9 %collective-permute-done.15 = bf16[256,3712]{1,0:T(8,128)(2,1)S(1)} collective-permute-done((bf16[256,3712]{1,0:T(8,128)(2,1)S(1)}, bf16[256,3712]{1,0:T(8,128)(2,1)S(1)}, u32[]{:S(2)}, u32[]{:S(2)}) %collective-permute-start.15) | collective-permute-done | bytes 1900576 | tf_op jit(solution)/shard_map/ppermute | solution.py:26
  206.6 2.2 collective-permute-start.16
  208.8 3.1 %collective-permute-start.17 = (bf16[64,3712]{1,0:T(8,128)(2,1)}, bf16[64,3712]{1,0:T(8,128)(2,1)}, u32[]{:S(2)}, u32[]{:S(2)}) collective-permute-start(bf16[64,3712]{1,0:T(8,128)(2,1)} %get-tuple-element.40), channel_id=1, source_target_pairs={{0,128},{1,17},{16,144},{17,33},{32,160},{33,49},{48,176},{49,1},{... | collective-permute-start | bytes 1425416 | tf_op jit(solution)/shard_map/ppermute | solution.py:26
  211.9 4.2 %collective-permute-start.18 = (bf16[64,3712]{1,0:T(8,128)(2,1)}, bf16[64,3712]{1,0:T(8,128)(2,1)}, u32[]{:S(2)}, u32[]{:S(2)}) collective-permute-start(bf16[64,3712]{1,0:T(8,128)(2,1)} %get-tuple-element.39), channel_id=1, source_target_pairs={{0,256},{1,33},{16,272},{17,49},{32,288},{33,1},{48,304},{49,17},{... | collective-permute-start | bytes 1425416 | tf_op jit(solution)/shard_map/ppermute | solution.py:26
  216.2 4.0 %fusion.29 = (bf16[32,113,128]{2,1,0:T(8,128)(2,1)}, bf16[32,113,128]{2,1,0:T(8,128)(2,1)S(1)}, bf16[32,113,128]{2,1,0:T(8,128)(2,1)}) fusion(bf16[32,352,128]{2,1,0:T(8,128)(2,1)} %bitcast.21), kind=kLoop, calls=%fused_computation.44 | loop fusion | bytes 5554176 | tf_op jit(solution)/shard_map/slice | solution.py:136
  220.3 2.3 reshape.94
  222.5 2.3 reshape.95
  226.1 1.5 fusion.31
  227.6 2.7 fusion.7
  230.3 1.7 reshape.99
  232.1 39.3 %all_to_all.5 = bf16[16,64,226]{2,1,0:T(8,128)(2,1)S(1)} all-to-all(bf16[16,64,226]{2,1,0:T(8,128)(2,1)S(1)} %bitcast.23), channel_id=1, replica_groups=mesh['y'=4,'h'=2,'x'=4,'l'=8,'c'=2] {'h','l'}, dimensions={0} | all-to-all | bytes 925696 | tf_op jit(solution)/shard_map/all_to_all | solution.py:159
  271.5 19.7 %collective-permute-start.19 = (bf16[64,226]{1,0:T(8,128)(2,1)S(1)}, bf16[64,226]{1,0:T(8,128)(2,1)S(1)}, u32[]{:S(2)}, u32[]{:S(2)}) collective-permute-start(bf16[64,226]{1,0:T(8,128)(2,1)S(1)} %reduce_sum.32), channel_id=1, source_target_pairs={{0,0},{1,64},{64,1},{65,65},{2,2},{3,66},{66,3},{67,67},{4,4},{5,6... | collective-permute-start | bytes 86792 | tf_op jit(solution)/shard_map/ppermute | solution.py:34
  291.2 1.7 collective-permute-done.19
  (61 shorter events, 13.0 us)
Async XLA Ops:
  6.5 209.7 %all-gather.4.cloned.1.call-start = ((), (), s32[]{:S(2)}) async-start(), calls=%async_computation.1 | async-start | bytes 2973696 | tf_op jit(solution)/shard_map/all_gather | solution.py:134
  9.9 18.4 %collective-permute-start = (bf16[64,256]{1,0:T(8,128)(2,1)S(1)}, bf16[64,256]{1,0:T(8,128)(2,1)S(1)}, u32[]{:S(2)}, u32[]{:S(2)}) collective-permute-start(bf16[64,256]{1,0:T(8,128)(2,1)S(1)} %maximum_maximum_fusion), channel_id=1, source_target_pairs={{0,0},{1,64},{64,1},{65,65},{2,2},{3,66},{66,3},{67,67},{4,4},{5,6... | collective-permute-start | bytes 98312 | tf_op jit(solution)/shard_map/ppermute | solution.py:34
  54.4 10.6 %collective-permute-start.2 = (bf16[64,3712]{1,0:T(8,128)(2,1)S(1)}, bf16[64,3712]{1,0:T(8,128)(2,1)S(1)}, u32[]{:S(2)}, u32[]{:S(2)}) collective-permute-start(bf16[64,3712]{1,0:T(8,128)(2,1)S(1)} %concatenate.24), channel_id=1, source_target_pairs={{0,128},{1,17},{16,144},{17,33},{32,160},{33,49},{48,176},{49,1},{... | collective-permute-start | bytes 1425416 | tf_op jit(solution)/shard_map/ppermute | solution.py:26
  57.5 9.4 %collective-permute-start.3 = (bf16[64,3712]{1,0:T(8,128)(2,1)S(1)}, bf16[64,3712]{1,0:T(8,128)(2,1)S(1)}, u32[]{:S(2)}, u32[]{:S(2)}) collective-permute-start(bf16[64,3712]{1,0:T(8,128)(2,1)S(1)} %concatenate.24), channel_id=1, source_target_pairs={{0,384},{1,49},{16,400},{17,1},{32,416},{33,17},{48,432},{49,33},{... | collective-permute-start | bytes 1425416 | tf_op jit(solution)/shard_map/ppermute | solution.py:26
  60.9 10.9 %collective-permute-start.4 = (bf16[64,3712]{1,0:T(8,128)(2,1)S(1)}, bf16[64,3712]{1,0:T(8,128)(2,1)S(1)}, u32[]{:S(2)}, u32[]{:S(2)}) collective-permute-start(bf16[64,3712]{1,0:T(8,128)(2,1)S(1)} %concatenate.24), channel_id=1, source_target_pairs={{0,256},{1,33},{16,272},{17,49},{32,288},{33,1},{48,304},{49,17},{... | collective-permute-start | bytes 1425416 | tf_op jit(solution)/shard_map/ppermute | solution.py:26
  71.9 35.8 %copy-start.3 = (bf16[256,3712]{1,0:T(8,128)(2,1)}, bf16[256,3712]{1,0:T(8,128)(2,1)S(1)}, u32[]{:S(2)}) copy-start(bf16[256,3712]{1,0:T(8,128)(2,1)S(1)} %pad_maximum_fusion.refs_0_) | copy-start | bytes 5701636
  72.0 35.8 %collective-permute-start.9 = (bf16[256,3712]{1,0:T(8,128)(2,1)S(1)}, bf16[256,3712]{1,0:T(8,128)(2,1)}, u32[]{:S(2)}, u32[]{:S(2)}) collective-permute-start(bf16[256,3712]{1,0:T(8,128)(2,1)S(1)} %pad_maximum_fusion.refs_0_), channel_id=1, source_target_pairs={{0,16},{1,129},{16,32},{17,145},{32,48},{33,161},{48,0},{49,177},{... | collective-permute-start | bytes 5701640 | tf_op jit(solution)/shard_map/ppermute | solution.py:26
  75.2 37.8 %collective-permute-start.8 = (bf16[256,3712]{1,0:T(8,128)(2,1)S(1)}, bf16[256,3712]{1,0:T(8,128)(2,1)}, u32[]{:S(2)}, u32[]{:S(2)}) collective-permute-start(bf16[256,3712]{1,0:T(8,128)(2,1)S(1)} %pad_maximum_fusion.refs_0_), channel_id=1, source_target_pairs={{0,48},{1,385},{16,0},{17,401},{32,16},{33,417},{48,32},{49,433},{... | collective-permute-start | bytes 5701640 | tf_op jit(solution)/shard_map/ppermute | solution.py:26
  78.5 26.9 %collective-permute-start.7 = (bf16[128,3616]{0,1:T(8,128)(2,1)}, bf16[128,3616]{0,1:T(8,128)(2,1)}, u32[]{:S(2)}, u32[]{:S(2)}) collective-permute-start(bf16[128,3616]{0,1:T(8,128)(2,1)} %bitcast.9), channel_id=1, source_target_pairs={{0,1},{1,0},{2,3},{3,2},{4,5},{5,4},{6,7},{7,6},{8,9},{9,8},{10,11... | collective-permute-start | bytes 2777096 | tf_op jit(solution)/shard_map/ppermute | solution.py:30
  99.5 17.6 %collective-permute-start.5 = (bf16[3616,128]{1,0:T(8,128)(2,1)}, bf16[3616,128]{1,0:T(8,128)(2,1)}, u32[]{:S(2)}, u32[]{:S(2)}) collective-permute-start(bf16[3616,128]{1,0:T(8,128)(2,1)} %bitcast.6), channel_id=1, source_target_pairs={{0,1},{1,0},{2,3},{3,2},{4,5},{5,4},{6,7},{7,6},{8,9},{9,8},{10,11... | collective-permute-start | bytes 2777096 | tf_op jit(solution)/shard_map/ppermute | solution.py:30
  101.4 15.6 %collective-permute-start.6 = (bf16[3616,128]{1,0:T(8,128)(2,1)}, bf16[3616,128]{1,0:T(8,128)(2,1)}, u32[]{:S(2)}, u32[]{:S(2)}) collective-permute-start(bf16[3616,128]{1,0:T(8,128)(2,1)} %bitcast.7), channel_id=1, source_target_pairs={{0,1},{1,0},{2,3},{3,2},{4,5},{5,4},{6,7},{7,6},{8,9},{9,8},{10,11... | collective-permute-start | bytes 2777096 | tf_op jit(solution)/shard_map/ppermute | solution.py:30
  107.7 9.1 %copy-start.5 = (bf16[128,3616]{1,0:T(8,128)(2,1)S(1)}, bf16[128,3616]{1,0:T(8,128)(2,1)}, u32[]{:S(2)}) copy-start(bf16[128,3616]{1,0:T(8,128)(2,1)} %copy.37) | copy-start | bytes 2777092
  109.1 15.7 %collective-permute-start.10 = (bf16[128,3712]{1,0:T(8,128)(2,1)S(1)}, bf16[128,3712]{1,0:T(8,128)(2,1)S(1)}, u32[]{:S(2)}, u32[]{:S(2)}) collective-permute-start(bf16[128,3712]{1,0:T(8,128)(2,1)S(1)} %slice.110), channel_id=1, source_target_pairs={{0,16},{1,129},{16,32},{17,145},{32,48},{33,161},{48,0},{49,177},{... | collective-permute-start | bytes 2850824 | tf_op jit(solution)/shard_map/ppermute | solution.py:26
  114.3 14.8 %collective-permute-start.11 = (bf16[128,3712]{1,0:T(8,128)(2,1)S(1)}, bf16[128,3712]{1,0:T(8,128)(2,1)S(1)}, u32[]{:S(2)}, u32[]{:S(2)}) collective-permute-start(bf16[128,3712]{1,0:T(8,128)(2,1)S(1)} %slice.111), channel_id=1, source_target_pairs={{0,48},{1,385},{16,0},{17,401},{32,16},{33,417},{48,32},{49,433},{... | collective-permute-start | bytes 2850824 | tf_op jit(solution)/shard_map/ppermute | solution.py:26
  120.6 11.3 %copy-start = (bf16[3712,512]{1,0:T(8,128)(2,1)}, bf16[3712,512]{1,0:T(8,128)(2,1)S(1)}, u32[]{:S(2)}) copy-start(bf16[3712,512]{1,0:T(8,128)(2,1)S(1)} %fusion.10.refs_1_.refs_2_) | copy-start | bytes 11403268
  129.1 4.8 %copy-start.7 = (bf16[128,113]{0,1:T(8,128)(2,1)S(1)}, bf16[128,113]{0,1:T(8,128)(2,1)}, u32[]{:S(2)}) copy-start(bf16[128,113]{0,1:T(8,128)(2,1)} %param.21) | copy-start | bytes 86788
  129.1 4.8 %copy-start.8 = (bf16[113,128]{1,0:T(8,128)(2,1)S(1)}, bf16[113,128]{1,0:T(8,128)(2,1)}, u32[]{:S(2)}) copy-start(bf16[113,128]{1,0:T(8,128)(2,1)} %param.20) | copy-start | bytes 86788
  129.1 4.8 %copy-start.9 = (bf16[113,128]{1,0:T(8,128)(2,1)S(1)}, bf16[113,128]{1,0:T(8,128)(2,1)}, u32[]{:S(2)}) copy-start(bf16[113,128]{1,0:T(8,128)(2,1)} %param.19) | copy-start | bytes 86788
  131.9 32.8 %collective-permute-start.12 = (bf16[128,3712]{1,0:T(8,128)(2,1)}, bf16[128,3712]{1,0:T(8,128)(2,1)}, u32[]{:S(2)}, u32[]{:S(2)}) collective-permute-start(bf16[128,3712]{1,0:T(8,128)(2,1)} %get-tuple-element.31), channel_id=1, source_target_pairs={{0,16},{1,129},{16,32},{17,145},{32,48},{33,161},{48,0},{49,177},{... | collective-permute-start | bytes 2850824 | tf_op jit(solution)/shard_map/ppermute | solution.py:26
  133.9 17.5 %collective-permute-start.1 = (bf16[352,128]{1,0:T(8,128)(2,1)S(1)}, bf16[352,128]{1,0:T(8,128)(2,1)S(1)}, u32[]{:S(2)}, u32[]{:S(2)}) collective-permute-start(bf16[352,128]{1,0:T(8,128)(2,1)S(1)} %fusion.21), channel_id=1, source_target_pairs={{0,0},{1,64},{64,1},{65,65},{2,2},{3,66},{66,3},{67,67},{4,4},{5,6... | collective-permute-start | bytes 270344 | tf_op jit(solution)/shard_map/ppermute | solution.py:34
  151.4 0.6 copy-start.6
  152.1 2.1 copy-start.1
  154.1 3.5 %copy-start.2 = (bf16[3712,512]{1,0:T(8,128)(2,1)S(1)}, bf16[3712,512]{1,0:T(8,128)(2,1)}, u32[]{:S(2)}) copy-start(bf16[3712,512]{1,0:T(8,128)(2,1)} %copy-done) | copy-start | bytes 11403268
  161.1 14.9 %collective-permute-start.14 = (bf16[128,3712]{1,0:T(8,128)(2,1)S(1)}, bf16[128,3712]{1,0:T(8,128)(2,1)S(1)}, u32[]{:S(2)}, u32[]{:S(2)}) collective-permute-start(bf16[128,3712]{1,0:T(8,128)(2,1)S(1)} %get-tuple-element.32), channel_id=1, source_target_pairs={{0,48},{1,385},{16,0},{17,401},{32,16},{33,417},{48,32},{49,433},{... | collective-permute-start | bytes 2850824 | tf_op jit(solution)/shard_map/ppermute | solution.py:26
  166.2 15.5 %copy-start.4 = (bf16[256,3712]{1,0:T(8,128)(2,1)S(1)}, bf16[256,3712]{1,0:T(8,128)(2,1)}, u32[]{:S(2)}) copy-start(bf16[256,3712]{1,0:T(8,128)(2,1)} %copy-done.3) | copy-start | bytes 5701636
  166.2 27.5 %collective-permute-start.13 = (bf16[256,3712]{1,0:T(8,128)(2,1)S(1)}, bf16[256,3712]{1,0:T(8,128)(2,1)S(1)}, u32[]{:S(2)}, u32[]{:S(2)}) collective-permute-start(bf16[256,3712]{1,0:T(8,128)(2,1)S(1)} %fusion.15), channel_id=1, source_target_pairs={{0,16},{1,129},{16,32},{17,145},{32,48},{33,161},{48,0},{49,177},{... | collective-permute-start | bytes 5701640 | tf_op jit(solution)/shard_map/ppermute | solution.py:26
  176.3 28.4 %collective-permute-start.15 = (bf16[256,3712]{1,0:T(8,128)(2,1)S(1)}, bf16[256,3712]{1,0:T(8,128)(2,1)S(1)}, u32[]{:S(2)}, u32[]{:S(2)}) collective-permute-start(bf16[256,3712]{1,0:T(8,128)(2,1)S(1)} %fusion.16), channel_id=1, source_target_pairs={{0,48},{1,385},{16,0},{17,401},{32,16},{33,417},{48,32},{49,433},{... | collective-permute-start | bytes 5701640 | tf_op jit(solution)/shard_map/ppermute | solution.py:26
  206.6 21.0 %collective-permute-start.16 = (bf16[64,3712]{1,0:T(8,128)(2,1)}, bf16[64,3712]{1,0:T(8,128)(2,1)}, u32[]{:S(2)}, u32[]{:S(2)}) collective-permute-start(bf16[64,3712]{1,0:T(8,128)(2,1)} %get-tuple-element.38), channel_id=1, source_target_pairs={{0,384},{1,49},{16,400},{17,1},{32,416},{33,17},{48,432},{49,33},{... | collective-permute-start | bytes 1425416 | tf_op jit(solution)/shard_map/ppermute | solution.py:26
  208.8 18.8 %collective-permute-start.17 = (bf16[64,3712]{1,0:T(8,128)(2,1)}, bf16[64,3712]{1,0:T(8,128)(2,1)}, u32[]{:S(2)}, u32[]{:S(2)}) collective-permute-start(bf16[64,3712]{1,0:T(8,128)(2,1)} %get-tuple-element.40), channel_id=1, source_target_pairs={{0,128},{1,17},{16,144},{17,33},{32,160},{33,49},{48,176},{49,1},{... | collective-permute-start | bytes 1425416 | tf_op jit(solution)/shard_map/ppermute | solution.py:26
  211.9 15.7 %collective-permute-start.18 = (bf16[64,3712]{1,0:T(8,128)(2,1)}, bf16[64,3712]{1,0:T(8,128)(2,1)}, u32[]{:S(2)}, u32[]{:S(2)}) collective-permute-start(bf16[64,3712]{1,0:T(8,128)(2,1)} %get-tuple-element.39), channel_id=1, source_target_pairs={{0,256},{1,33},{16,272},{17,49},{32,288},{33,1},{48,304},{49,17},{... | collective-permute-start | bytes 1425416 | tf_op jit(solution)/shard_map/ppermute | solution.py:26
  271.5 21.4 %collective-permute-start.19 = (bf16[64,226]{1,0:T(8,128)(2,1)S(1)}, bf16[64,226]{1,0:T(8,128)(2,1)S(1)}, u32[]{:S(2)}, u32[]{:S(2)}) collective-permute-start(bf16[64,226]{1,0:T(8,128)(2,1)S(1)} %reduce_sum.32), channel_id=1, source_target_pairs={{0,0},{1,64},{64,1},{65,65},{2,2},{3,66},{66,3},{67,67},{4,4},{5,6... | collective-permute-start | bytes 86792 | tf_op jit(solution)/shard_map/ppermute | solution.py:34
Sparse Core Ops, SparseCore 0:
  152.2 63.9 all-gather.3

commit v4 on v3

--- a/solution.py
+++ b/solution.py
@@ -95,6 +95,7 @@
 ):
     expert = lax.axis_index(EXPERT)
     part = lax.axis_index(TENSOR)
+    core = lax.axis_index("c")
     toks, width = tokens.shape
     feats = width * L * C
     full = -(-feats // 128) * 128
@@ -107,11 +108,19 @@
     table = jnp.sum(jnp.where(routes[:, :, None] == own, gates[:, :, None], 0.0), axis=1)
     high = table.astype(bf16)
     low = (table - high.astype(f32)).astype(bf16)
+    sent = jnp.concatenate([high, low, jnp.zeros((toks, 256 - width - 2 * per), bf16)], 1)
+    sent = jnp.concatenate([tokens, sent], 1)
+    half = toks // C
     sent = jnp.concatenate(
-        [tokens, high, low, jnp.zeros((toks, 256 - width - 2 * per), bf16)], 1
-    )
-    got = lax.all_gather(turn(sent), Z, axis=0, tiled=False)
-    got = got.reshape(H, L, toks, 256).transpose(2, 1, 0, 3)
+        [
+            lax.dynamic_slice_in_dim(sent, core * half, half, 0),
+            swap(lax.dynamic_slice_in_dim(sent, (1 - core) * half, half, 0)),
+        ],
+        1,
+    )
+    got = lax.all_gather(sent, Z, axis=0, tiled=False)
+    got = got.reshape(H, L, half, C, 256)
+    got = jnp.where(core == 0, got, got[:, :, :, ::-1]).transpose(0, 2, 1, 3, 4)
     rows = jnp.concatenate(
         [
             got[..., :width].reshape(toks, feats),
@@ -131,7 +140,8 @@
     depth = shared_gate.shape[0]
     s = jnp.concatenate([shared_gate, shared_up, shared_down.T], 0)
     s = jnp.pad(s, ((0, -s.shape[0] % 16), (0, 0)))
-    s = lax.all_gather(turn(s), ("y", "c", "x"), axis=0, tiled=False)
+    rows, s = lax.optimization_barrier((rows, turn(s)))
+    s = lax.all_gather(s, ("y", "c", "x"), axis=0, tiled=False)
     s_gate, s_up, s_down = (
         s[:, i * depth : (i + 1) * depth].reshape(feats, s.shape[2]) for i in range(3)
     )
@@ -140,24 +150,37 @@
     s_hidden = (jax.nn.silu(s_gate) * s_up).astype(bf16)
     shared = lax.dot_general(s_hidden, s_down, (((1,), (1,)), ((), ())), preferred_element_type=f32)
 
-    near = jnp.concatenate([rows, move(rows, 0, 1), move(rows, 0, -1), move(rows, 0, 2)], 0)
-    m = near.shape[0] // 2
-    prev, succ = move(near, 1, 1), move(near, 1, -1)
-    far = [move(prev[:m], 1, 1), move(succ[m:], 1, -1)]
-    far_lo, far_hi = ffn(at, far, w_in, w_out)
-    (prev_out,), (succ_out,) = ffn(at, [prev], w_in, w_out), ffn(at, [succ], w_in, w_out)
-    (own_out,) = ffn(at, [near], w_in, w_out)
+    apply = lambda *blocks: ffn(at, blocks, w_in, w_out)
+    lo = jnp.concatenate([rows, move(rows, 0, 1)], 0)
+    hi = jnp.concatenate([move(rows, 0, -1), move(rows, 0, 2)], 0)
+    prev_lo, succ_hi = move(lo, 1, 1), move(hi, 1, -1)
+    prev_hi, succ_lo = move(hi, 1, 1), move(lo, 1, -1)
+    far_lo, far_hi = apply(move(prev_lo, 1, 1), move(succ_hi, 1, -1))
 
     from_prev, from_succ = move(far_lo, 1, 1), move(far_hi, 1, -1)
-    to_succ = succ_out.at[:m].set(add(succ_out[:m], from_prev))
-    to_prev = prev_out.at[m:].set(add(prev_out[m:], from_succ))
-    total = add(own_out, move(to_succ, 1, 1), move(to_prev, 1, -1))
-    total = total.reshape(4, toks, full)
-    total = [total[0], move(total[1], 0, -1), move(total[2], 0, 1), move(total[3], 0, 2)]
+    prev_lo, prev_hi = apply(prev_lo, prev_hi)
+    succ_lo, succ_hi = apply(succ_lo, succ_hi)
+    prev_lo, succ_hi = move(prev_lo, 1, -1), move(succ_hi, 1, 1)
+    lo, hi, shared = lax.optimization_barrier((lo, hi, shared))
+    own_lo, own_hi = apply(lo, hi)
+    prev_hi = move(add(prev_hi, from_succ), 1, -1)
+    succ_lo = move(add(succ_lo, from_prev), 1, 1)
+    los, his = (own_lo, prev_lo, succ_lo), (own_hi, prev_hi, succ_hi)
+    total = [t[:toks] for t in los]
+    total.append(move(add(*[t[toks:] for t in los]), 0, -1))
+    total.append(move(add(*[t[:toks] for t in his]), 0, 1))
+    total.append(move(add(*[t[toks:] for t in his]), 0, 2))
     total = add(shared, *[t[:, :feats] for t in total])
-    back = total.reshape(toks, L, H, width).transpose(2, 1, 0, 3).reshape(H * L, toks, width)
+
+    back = total.reshape(H, half, L, C, width).transpose(0, 2, 3, 1, 4)
+    back = jnp.where(core == 0, back, back[:, :, ::-1])
+    back = back.reshape(H * L, C * half, width)
     back = lax.all_to_all(back, Z, split_axis=0, concat_axis=0, tiled=True)
-    return turn(jnp.sum(back.astype(f32), axis=0).astype(bf16))
+    done = jnp.sum(back.astype(f32), axis=0).astype(bf16)
+    keep, take = done[:half], swap(done[half:])
+    return jnp.where(
+        core == 0, jnp.concatenate([keep, take], 0), jnp.concatenate([take, keep], 0)
+    )
 
 
 def solution(mesh):

time: 302 us -> 276 us (0.914)
  starting transfers between devices: 122 us -> 103 us
  blocking collectives: 63.2 us -> 50.5 us
  waiting for transfers between devices: 50.4 us -> 41.7 us
  other arithmetic: 9.6 us -> 17.6 us
  local copies, waits for them, and re-layouts: 25 us -> 29.7 us
    ppermute x3 -> x1, starting transfers between devices: 51.7 us -> 9.97 us  [turn(): lax.ppermute(a, ('h', 'c'), [(h * 2 + c, c * 2 + h) for h in range(2) for...]
    ppermute x14 -> x18, starting transfers between devices: 45.5 us -> 58.9 us  [move(): return lax.ppermute(a, ('y', 'x', 'c'), pairs)]
    all_to_all x1, blocking collectives: 39.3 us -> 26.3 us  [local(): back = lax.all_to_all(back, Z, split_axis=0, concat_axis=0, tiled=True)]
    ppermute x3 -> x5, starting transfers between devices: 25.3 us -> 34.6 us  [swap(): return lax.ppermute(a, 'c', [(0, 1), (1, 0)])]
    convert_element_type x1 -> x5, other arithmetic: 0.8 us -> 7.22 us  [add(): return total.astype(bf16)]
    ppermute x3 -> x1, waiting for transfers between devices: 5.56 us -> 0.01 us  [turn(): lax.ppermute(a, ('h', 'c'), [(h * 2 + c, c * 2 + h) for h in range(2) for...]
    ppermute x14 -> x18, waiting for transfers between devices: 44.7 us -> 40.8 us  [move(): return lax.ppermute(a, ('y', 'x', 'c'), pairs)]
    slice x3 -> x1, local copies, waits for them, and re-layouts: 3.73 us -> 0.01 us  [local(): keep, take = (done[:half], swap(done[half:]))]
  transfers between devices with their start and end apart: 21 -> 25, of which waited for: 12 -> 6; matrix products, arithmetic and copies ran while one was open for 8% -> 15% of each run, Pallas kernels for 3% -> 5%
where the time goes in v4:
time: 276 us; the launch traced here: 275 us
  starting transfers between devices  103 us (37%)
  blocking collectives  50.5 us (18%)
  waiting for transfers between devices  41.7 us (15%)
  local copies, waits for them, and re-layouts  29.7 us (11%)
  other arithmetic  17.6 us (6%)
  between operations  14 us (5%)
  Pallas kernels  13.1 us (5%)
  matrix products  4.62 us (2%)
    ppermute x18, starting transfers between devices, move(): return lax.ppermute(a, ('y', 'x', 'c'), pairs)  58.9 us
    ppermute x18, waiting for transfers between devices, move(): return lax.ppermute(a, ('y', 'x', 'c'), pairs)  40.8 us
    ppermute x5, starting transfers between devices, swap(): return lax.ppermute(a, 'c', [(0, 1), (1, 0)])  34.6 us
    all_to_all x1, blocking collectives, local(): back = lax.all_to_all(back, Z, split_axis=0, concat_axis=0, tiled=True)  26.3 us
    all_gather x1, blocking collectives, local(): got = lax.all_gather(sent, Z, axis=0, tiled=False)  24.2 us
    pallas_call x4, Pallas kernels, ffn(): pl.pallas_call(functools.partial(ffn_kernel, hid=hid, parts=parts), out_s...  13.1 us
    ppermute x1, starting transfers between devices, turn(): lax.ppermute(a, ('h', 'c'), [(h * 2 + c, c * 2 + h) for h in range(2) for...  9.97 us
    convert_element_type x5, other arithmetic, add(): return total.astype(bf16)  7.22 us
  transfers between devices with their start and end apart: 25, of which 6 were waited for; matrix products, arithmetic and copies ran while one was open for 15% of the time, Pallas kernels for 5%

profile of v4, /device:TPU:1, one launch (start us, length us, event | category | flops | bytes accessed | tf_op | source)
XLA Modules:
  0.0 274.7 jit_solution(11942912458650450245)
XLA Ops:
  9.9 8.8 %collective-permute-start = (bf16[32,256]{1,0:T(8,128)(2,1)S(1)}, bf16[32,256]{1,0:T(8,128)(2,1)S(1)}, u32[]{:S(2)}, u32[]{:S(2)}) collective-permute-start(bf16[32,256]{1,0:T(8,128)(2,1)S(1)} %get-tuple-element.41), channel_id=1, source_target_pairs={{0,1},{1,0},{2,3},{3,2},{4,5},{5,4},{6,7},{7,6},{8,9},{9,8},{10,11... | collective-permute-start | bytes 49160 | tf_op jit(solution)/shard_map/ppermute | solution.py:30
  19.5 10.0 %collective-permute-start.1 = (bf16[352,128]{1,0:T(8,128)(2,1)S(1)}, bf16[352,128]{1,0:T(8,128)(2,1)S(1)}, u32[]{:S(2)}, u32[]{:S(2)}) collective-permute-start(bf16[352,128]{1,0:T(8,128)(2,1)S(1)} %fusion.21), channel_id=1, source_target_pairs={{0,0},{1,64},{64,1},{65,65},{2,2},{3,66},{66,3},{67,67},{4,4},{5,6... | collective-permute-start | bytes 270344 | tf_op jit(solution)/shard_map/ppermute | solution.py:34
  29.5 24.2 %all-gather = bf16[512,512]{1,0:T(8,128)(2,1)S(1)} all-gather(bf16[32,512]{1,0:T(8,128)(2,1)S(1)} %pad_maximum_fusion), channel_id=2, replica_groups=mesh['y'=4,'h'=2,'x'=4,'l'=8,'c'=2] {'h','l'}, dimensions={0}, use_global_device_ids=true | all-gather | bytes 557056 | tf_op jit(solution)/shard_map/all_gather | solution.py:121
  55.4 2.3 fusion.9
  61.7 3.8 %collective-permute-start.2 = (bf16[64,3712]{1,0:T(8,128)(2,1)S(1)}, bf16[64,3712]{1,0:T(8,128)(2,1)}, u32[]{:S(2)}, u32[]{:S(2)}) collective-permute-start(bf16[64,3712]{1,0:T(8,128)(2,1)S(1)} %concatenate.32), channel_id=1, source_target_pairs={{0,128},{1,17},{16,144},{17,33},{32,160},{33,49},{48,176},{49,1},{... | collective-permute-start | bytes 1425416 | tf_op jit(solution)/shard_map/ppermute | solution.py:26
  65.5 4.4 %collective-permute-start.4 = (bf16[64,3712]{1,0:T(8,128)(2,1)S(1)}, bf16[64,3712]{1,0:T(8,128)(2,1)}, u32[]{:S(2)}, u32[]{:S(2)}) collective-permute-start(bf16[64,3712]{1,0:T(8,128)(2,1)S(1)} %concatenate.32), channel_id=1, source_target_pairs={{0,256},{1,33},{16,272},{17,49},{32,288},{33,1},{48,304},{49,17},{... | collective-permute-start | bytes 1425416 | tf_op jit(solution)/shard_map/ppermute | solution.py:26
  69.8 3.1 %collective-permute-start.3 = (bf16[64,3712]{1,0:T(8,128)(2,1)S(1)}, bf16[64,3712]{1,0:T(8,128)(2,1)}, u32[]{:S(2)}, u32[]{:S(2)}) collective-permute-start(bf16[64,3712]{1,0:T(8,128)(2,1)S(1)} %concatenate.32), channel_id=1, source_target_pairs={{0,384},{1,49},{16,400},{17,1},{32,416},{33,17},{48,432},{49,33},{... | collective-permute-start | bytes 1425416 | tf_op jit(solution)/shard_map/ppermute | solution.py:26
  74.1 3.3 %collective-permute-start.8 = (bf16[128,3712]{1,0:T(8,128)(2,1)S(1)}, bf16[128,3712]{1,0:T(8,128)(2,1)}, u32[]{:S(2)}, u32[]{:S(2)}) collective-permute-start(bf16[128,3712]{1,0:T(8,128)(2,1)S(1)} %constant_dynamic-update-slice_fusion.refs_0_), channel_id=1, source_target_pairs={{0,16},{1,129},{16,32},{17,145},{32,48},{33,161},{48,0},{49,177},{... | collective-permute-start | bytes 2850824 | tf_op jit(solution)/shard_map/ppermute | solution.py:26
  77.3 3.4 %collective-permute-done.3 = bf16[64,3712]{1,0:T(8,128)(2,1)} collective-permute-done((bf16[64,3712]{1,0:T(8,128)(2,1)S(1)}, bf16[64,3712]{1,0:T(8,128)(2,1)}, u32[]{:S(2)}, u32[]{:S(2)}) %collective-permute-start.3) | collective-permute-done | bytes 475168 | tf_op jit(solution)/shard_map/ppermute | solution.py:26
  80.7 1.9 constant_dynamic-update-slice_fusion.3
  82.6 1.8 constant_dynamic-update-slice_fusion.2.refs_1_
  84.4 4.8 %collective-permute-start.12 = (bf16[128,3712]{1,0:T(8,128)(2,1)}, bf16[128,3712]{1,0:T(8,128)(2,1)}, u32[]{:S(2)}, u32[]{:S(2)}) collective-permute-start(bf16[128,3712]{1,0:T(8,128)(2,1)} %constant_dynamic-update-slice_fusion.2.refs_1_), channel_id=1, source_target_pairs={{0,48},{1,385},{16,0},{17,401},{32,16},{33,417},{48,32},{49,433},{... | collective-permute-start | bytes 2850824 | tf_op jit(solution)/shard_map/ppermute | solution.py:26
  89.3 10.8 %collective-permute-start.7 = (bf16[128,3616]{0,1:T(8,128)(2,1)}, bf16[128,3616]{0,1:T(8,128)(2,1)}, u32[]{:S(2)}, u32[]{:S(2)}) collective-permute-start(bf16[128,3616]{0,1:T(8,128)(2,1)} %bitcast.22), channel_id=1, source_target_pairs={{0,1},{1,0},{2,3},{3,2},{4,5},{5,4},{6,7},{7,6},{8,9},{9,8},{10,11... | collective-permute-start | bytes 2777096 | tf_op jit(solution)/shard_map/ppermute | solution.py:30
  100.0 1.9 collective-permute-start.5
  102.0 2.4 collective-permute-start.6
  104.4 2.3 copy.39
  106.7 2.1 collective-permute-start.11
  108.8 2.3 copy.41
  111.1 3.3 %collective-permute-start.9 = (bf16[128,3712]{1,0:T(8,128)(2,1)}, bf16[128,3712]{1,0:T(8,128)(2,1)S(1)}, u32[]{:S(2)}, u32[]{:S(2)}) collective-permute-start(bf16[128,3712]{1,0:T(8,128)(2,1)} %constant_dynamic-update-slice_fusion.2.refs_1_), channel_id=1, source_target_pairs={{0,16},{1,129},{16,32},{17,145},{32,48},{33,161},{48,0},{49,177},{... | collective-permute-start | bytes 2850824 | tf_op jit(solution)/shard_map/ppermute | solution.py:26
  114.4 2.1 collective-permute-start.13
  116.4 4.4 %collective-permute-start.14 = (bf16[128,3712]{1,0:T(8,128)(2,1)}, bf16[128,3712]{1,0:T(8,128)(2,1)S(1)}, u32[]{:S(2)}, u32[]{:S(2)}) collective-permute-start(bf16[128,3712]{1,0:T(8,128)(2,1)} %collective-permute-done.12.refs_1_), channel_id=1, source_target_pairs={{0,48},{1,385},{16,0},{17,401},{32,16},{33,417},{48,32},{49,433},{... | collective-permute-start | bytes 2850824 | tf_op jit(solution)/shard_map/ppermute | solution.py:26
  120.9 3.3 %fusion.6.refs_2_ = bf16[3712,512]{1,0:T(8,128)(2,1)S(1)} fusion(bf16[3616,128]{1,0:T(8,128)(2,1)} %collective-permute-done.6, bf16[3616,128]{1,0:T(8,128)(2,1)S(1)} %bitcast.24, bf16[3616,128]{1,0:T(8,128)(2,1)} %collective-permute-done.5, bf16[3616,128]{1,0:T(8,128)(2,1)S(1)} %bitcast.26), kind=kLoop, calls=%fused_computation.8 | loop fusion | flops 24707072 | bytes 7503872 | tf_op jit(solution)/shard_map/concatenate | solution.py:135
  124.4 19.0 %collective-permute-done.13.refs_0_ = bf16[128,3712]{1,0:T(8,128)(2,1)S(1)} collective-permute-done((bf16[128,3712]{1,0:T(8,128)(2,1)}, bf16[128,3712]{1,0:T(8,128)(2,1)S(1)}, u32[]{:S(2)}, u32[]{:S(2)}) %collective-permute-start.13) | collective-permute-done | bytes 950304 | tf_op jit(solution)/shard_map/ppermute | solution.py:26
  143.4 1.8 shard_map.94
  145.3 1.9 collective-permute-start.15
  147.2 3.9 %shard_map.92 = (bf16[128,3712]{1,0:T(8,128)(2,1)}, bf16[128,3712]{1,0:T(8,128)(2,1)S(1)}) custom-call(s32[1]{0:T(128)} %bitcast.3.at_ref, bf16[128,3712]{1,0:T(8,128)(2,1)} %collective-permute-done.8.refs_0_, bf16[128,3712]{1,0:T(8,128)(2,1)S(1)} %collective-permute-done.9.refs_1_, bf16[3712,512]{1,0:T(8,128)(2,1)S(1)} %fusion.6.refs_2_, ...), custom_call_target="tpu_custom_call" | custom-call | flops 1459617792 | bytes 9502720 | tf_op jit(solution)/shard_map/pallas_call | solution.py:71
  151.1 4.7 %collective-permute-start.10 = (bf16[128,3712]{1,0:T(8,128)(2,1)}, bf16[128,3712]{1,0:T(8,128)(2,1)}, u32[]{:S(2)}, u32[]{:S(2)}) collective-permute-start(bf16[128,3712]{1,0:T(8,128)(2,1)} %get-tuple-element.24), channel_id=1, source_target_pairs={{0,48},{1,385},{16,0},{17,401},{32,16},{33,417},{48,32},{49,433},{... | collective-permute-start | bytes 2850824 | tf_op jit(solution)/shard_map/ppermute | solution.py:26
  155.9 4.3 %shard_map.93 = (bf16[128,3712]{1,0:T(8,128)(2,1)S(1)}, bf16[128,3712]{1,0:T(8,128)(2,1)}) custom-call(s32[1]{0:T(128)} %bitcast.3.at_ref, bf16[128,3712]{1,0:T(8,128)(2,1)} %collective-permute-done.11.refs_0_, bf16[128,3712]{1,0:T(8,128)(2,1)} %collective-permute-done.12.refs_1_, bf16[3712,512]{1,0:T(8,128)(2,1)S(1)} %fusion.6.refs_2_, ...), custom_call_target="tpu_custom_call" | custom-call | flops 1459617792 | bytes 9502720 | tf_op jit(solution)/shard_map/pallas_call | solution.py:71
  160.2 1.9 collective-permute-start.20
  162.1 4.6 %collective-permute-start.18 = (bf16[128,3712]{1,0:T(8,128)(2,1)S(1)}, bf16[128,3712]{1,0:T(8,128)(2,1)S(1)}, u32[]{:S(2)}, u32[]{:S(2)}) collective-permute-start(bf16[128,3712]{1,0:T(8,128)(2,1)S(1)} %get-tuple-element.29), channel_id=1, source_target_pairs={{0,48},{1,385},{16,0},{17,401},{32,16},{33,417},{48,32},{49,433},{... | collective-permute-start | bytes 2850824 | tf_op jit(solution)/shard_map/ppermute | solution.py:26
  167.9 1.9 collective-permute-start.16
  169.8 7.5 %collective-permute-done.18 = bf16[128,3712]{1,0:T(8,128)(2,1)S(1)} collective-permute-done((bf16[128,3712]{1,0:T(8,128)(2,1)S(1)}, bf16[128,3712]{1,0:T(8,128)(2,1)S(1)}, u32[]{:S(2)}, u32[]{:S(2)}) %collective-permute-start.18) | collective-permute-done | bytes 950304 | tf_op jit(solution)/shard_map/ppermute | solution.py:26
  178.6 5.4 %collective-permute-start.19 = (bf16[128,3712]{1,0:T(8,128)(2,1)}, bf16[128,3712]{1,0:T(8,128)(2,1)}, u32[]{:S(2)}, u32[]{:S(2)}) collective-permute-start(bf16[128,3712]{1,0:T(8,128)(2,1)} %add_convert_fusion), channel_id=1, source_target_pairs={{0,48},{1,385},{16,0},{17,401},{32,16},{33,417},{48,32},{49,433},{... | collective-permute-start | bytes 2850824 | tf_op jit(solution)/shard_map/ppermute | solution.py:26
  184.0 3.8 %fusion.29 = (bf16[32,113,128]{2,1,0:T(8,128)(2,1)}, bf16[32,113,128]{2,1,0:T(8,128)(2,1)}, bf16[32,113,128]{2,1,0:T(8,128)(2,1)}) fusion(bf16[32,352,128]{2,1,0:T(8,128)(2,1)} %bitcast.19), kind=kLoop, calls=%fused_computation.55 | loop fusion | bytes 5554176 | tf_op jit(solution)/shard_map/slice | solution.py:146
  187.8 2.3 reshape.37
  190.0 2.3 reshape.39
  192.3 2.3 reshape.38
  196.1 3.1 %fusion.12 = f32[64,3616]{1,0:T(8,128)} fusion(bf16[3616,128]{1,0:T(8,128)(2,1)} %reshape.39, bf16[3616,128]{1,0:T(8,128)(2,1)} %reshape.38, bf16[64,3712]{1,0:T(8,128)(2,1)S(1)} %concatenate.32, f32[64,128]{1,0:T(8,128)S(1)} %fusion.15), kind=kOutput, calls=%fused_computation.18 | convolution fusion | flops 118538240 | bytes 3284992 | tf_op jit(solution)/shard_map/dot_general | solution.py:151
  199.3 2.1 copy-done.1
  201.3 3.0 %shard_map.91 = (bf16[128,3712]{1,0:T(8,128)(2,1)S(1)}, bf16[128,3712]{1,0:T(8,128)(2,1)S(1)}) custom-call(s32[1]{0:T(128)} %bitcast.3.at_ref, bf16[128,3712]{1,0:T(8,128)(2,1)S(1)} %constant_dynamic-update-slice_fusion.refs_0_, bf16[128,3712]{1,0:T(8,128)(2,1)} %constant_dynamic-update-slice_fusion.2.refs_1_, bf16[3712,512]{1,0:T(8,128)(2,1)S(1)} %copy-done.1, ...), custom_call_target="tpu_custom_call" | custom-call | flops 1459617792 | bytes 9502720 | tf_op jit(solution)/shard_map/pallas_call | solution.py:71
  205.8 2.1 collective-permute-start.17
  207.9 1.8 add_convert_fusion.4
  209.7 3.2 %collective-permute-start.21 = (bf16[64,3712]{1,0:T(8,128)(2,1)S(1)}, bf16[64,3712]{1,0:T(8,128)(2,1)S(1)}, u32[]{:S(2)}, u32[]{:S(2)}) collective-permute-start(bf16[64,3712]{1,0:T(8,128)(2,1)S(1)} %get-tuple-element.36), channel_id=1, source_target_pairs={{0,128},{1,17},{16,144},{17,33},{32,160},{33,49},{48,176},{49,1},{... | collective-permute-start | bytes 1425416 | tf_op jit(solution)/shard_map/ppermute | solution.py:26
  213.0 1.9 collective-permute-start.22
  215.5 10.2 %collective-permute-done.21 = bf16[64,3712]{1,0:T(8,128)(2,1)S(1)} collective-permute-done((bf16[64,3712]{1,0:T(8,128)(2,1)S(1)}, bf16[64,3712]{1,0:T(8,128)(2,1)S(1)}, u32[]{:S(2)}, u32[]{:S(2)}) %collective-permute-start.21) | collective-permute-done | bytes 475168 | tf_op jit(solution)/shard_map/ppermute | solution.py:26
  227.4 1.7 reshape.41
  229.3 26.3 %all_to_all.5 = bf16[16,64,226]{2,1,0:T(8,128)(2,1)S(1)} all-to-all(bf16[16,64,226]{2,1,0:T(8,128)(2,1)S(1)} %bitcast.21), channel_id=1, replica_groups=mesh['y'=4,'h'=2,'x'=4,'l'=8,'c'=2] {'h','l'}, dimensions={0} | all-to-all | bytes 925696 | tf_op jit(solution)/shard_map/all_to_all | solution.py:178
  255.7 10.7 %collective-permute-start.23 = (bf16[32,226]{1,0:T(8,128)(2,1)S(1)}, bf16[32,226]{1,0:T(8,128)(2,1)S(1)}, u32[]{:S(2)}, u32[]{:S(2)}) collective-permute-start(bf16[32,226]{1,0:T(8,128)(2,1)S(1)} %get-tuple-element.39), channel_id=1, source_target_pairs={{0,1},{1,0},{2,3},{3,2},{4,5},{5,4},{6,7},{7,6},{8,9},{9,8},{10,11... | collective-permute-start | bytes 43400 | tf_op jit(solution)/shard_map/ppermute | solution.py:30
  (74 shorter events, 20.5 us)
Async XLA Ops:
  6.5 177.5 %all-gather.4.cloned.1.call-start = ((), (), s32[]{:S(2)}) async-start(), calls=%async_computation.1 | async-start | bytes 2973696 | tf_op jit(solution)/shard_map/all_gather | solution.py:144
  9.9 19.6 %collective-permute-start = (bf16[32,256]{1,0:T(8,128)(2,1)S(1)}, bf16[32,256]{1,0:T(8,128)(2,1)S(1)}, u32[]{:S(2)}, u32[]{:S(2)}) collective-permute-start(bf16[32,256]{1,0:T(8,128)(2,1)S(1)} %get-tuple-element.41), channel_id=1, source_target_pairs={{0,1},{1,0},{2,3},{3,2},{4,5},{5,4},{6,7},{7,6},{8,9},{9,8},{10,11... | collective-permute-start | bytes 49160 | tf_op jit(solution)/shard_map/ppermute | solution.py:30
  19.5 42.1 %collective-permute-start.1 = (bf16[352,128]{1,0:T(8,128)(2,1)S(1)}, bf16[352,128]{1,0:T(8,128)(2,1)S(1)}, u32[]{:S(2)}, u32[]{:S(2)}) collective-permute-start(bf16[352,128]{1,0:T(8,128)(2,1)S(1)} %fusion.21), channel_id=1, source_target_pairs={{0,0},{1,64},{64,1},{65,65},{2,2},{3,66},{66,3},{67,67},{4,4},{5,6... | collective-permute-start | bytes 270344 | tf_op jit(solution)/shard_map/ppermute | solution.py:34
  61.6 11.3 %copy-start.7 = (bf16[352,128]{1,0:T(8,128)(2,1)}, bf16[352,128]{1,0:T(8,128)(2,1)S(1)}, u32[]{:S(2)}) copy-start(bf16[352,128]{1,0:T(8,128)(2,1)S(1)} %collective-permute-done.1) | copy-start | bytes 270340
  61.6 59.3 %copy-start.5 = (bf16[1,3616,128]{2,1,0:T(8,128)(2,1)S(1)}, bf16[1,3616,128]{2,1,0:T(8,128)(2,1)}, u32[]{:S(2)}) copy-start(bf16[1,3616,128]{2,1,0:T(8,128)(2,1)} %param.13) | copy-start | bytes 2777092
  61.6 59.3 %copy-start.6 = (bf16[1,3616,128]{2,1,0:T(8,128)(2,1)S(1)}, bf16[1,3616,128]{2,1,0:T(8,128)(2,1)}, u32[]{:S(2)}) copy-start(bf16[1,3616,128]{2,1,0:T(8,128)(2,1)} %param.12) | copy-start | bytes 2777092
  61.7 11.3 %collective-permute-start.2 = (bf16[64,3712]{1,0:T(8,128)(2,1)S(1)}, bf16[64,3712]{1,0:T(8,128)(2,1)}, u32[]{:S(2)}, u32[]{:S(2)}) collective-permute-start(bf16[64,3712]{1,0:T(8,128)(2,1)S(1)} %concatenate.32), channel_id=1, source_target_pairs={{0,128},{1,17},{16,144},{17,33},{32,160},{33,49},{48,176},{49,1},{... | collective-permute-start | bytes 1425416 | tf_op jit(solution)/shard_map/ppermute | solution.py:26
  65.5 17.1 %collective-permute-start.4 = (bf16[64,3712]{1,0:T(8,128)(2,1)S(1)}, bf16[64,3712]{1,0:T(8,128)(2,1)}, u32[]{:S(2)}, u32[]{:S(2)}) collective-permute-start(bf16[64,3712]{1,0:T(8,128)(2,1)S(1)} %concatenate.32), channel_id=1, source_target_pairs={{0,256},{1,33},{16,272},{17,49},{32,288},{33,1},{48,304},{49,17},{... | collective-permute-start | bytes 1425416 | tf_op jit(solution)/shard_map/ppermute | solution.py:26
  69.8 10.9 %collective-permute-start.3 = (bf16[64,3712]{1,0:T(8,128)(2,1)S(1)}, bf16[64,3712]{1,0:T(8,128)(2,1)}, u32[]{:S(2)}, u32[]{:S(2)}) collective-permute-start(bf16[64,3712]{1,0:T(8,128)(2,1)S(1)} %concatenate.32), channel_id=1, source_target_pairs={{0,384},{1,49},{16,400},{17,1},{32,416},{33,17},{48,432},{49,33},{... | collective-permute-start | bytes 1425416 | tf_op jit(solution)/shard_map/ppermute | solution.py:26
  74.1 40.3 %collective-permute-start.8 = (bf16[128,3712]{1,0:T(8,128)(2,1)S(1)}, bf16[128,3712]{1,0:T(8,128)(2,1)}, u32[]{:S(2)}, u32[]{:S(2)}) collective-permute-start(bf16[128,3712]{1,0:T(8,128)(2,1)S(1)} %constant_dynamic-update-slice_fusion.refs_0_), channel_id=1, source_target_pairs={{0,16},{1,129},{16,32},{17,145},{32,48},{33,161},{48,0},{49,177},{... | collective-permute-start | bytes 2850824 | tf_op jit(solution)/shard_map/ppermute | solution.py:26
  84.4 32.0 %collective-permute-start.12 = (bf16[128,3712]{1,0:T(8,128)(2,1)}, bf16[128,3712]{1,0:T(8,128)(2,1)}, u32[]{:S(2)}, u32[]{:S(2)}) collective-permute-start(bf16[128,3712]{1,0:T(8,128)(2,1)} %constant_dynamic-update-slice_fusion.2.refs_1_), channel_id=1, source_target_pairs={{0,48},{1,385},{16,0},{17,401},{32,16},{33,417},{48,32},{49,433},{... | collective-permute-start | bytes 2850824 | tf_op jit(solution)/shard_map/ppermute | solution.py:26
  89.3 17.4 %collective-permute-start.7 = (bf16[128,3616]{0,1:T(8,128)(2,1)}, bf16[128,3616]{0,1:T(8,128)(2,1)}, u32[]{:S(2)}, u32[]{:S(2)}) collective-permute-start(bf16[128,3616]{0,1:T(8,128)(2,1)} %bitcast.22), channel_id=1, source_target_pairs={{0,1},{1,0},{2,3},{3,2},{4,5},{5,4},{6,7},{7,6},{8,9},{9,8},{10,11... | collective-permute-start | bytes 2777096 | tf_op jit(solution)/shard_map/ppermute | solution.py:30
  100.0 11.0 %collective-permute-start.5 = (bf16[3616,128]{1,0:T(8,128)(2,1)}, bf16[3616,128]{1,0:T(8,128)(2,1)}, u32[]{:S(2)}, u32[]{:S(2)}) collective-permute-start(bf16[3616,128]{1,0:T(8,128)(2,1)} %bitcast.25), channel_id=1, source_target_pairs={{0,1},{1,0},{2,3},{3,2},{4,5},{5,4},{6,7},{7,6},{8,9},{9,8},{10,11... | collective-permute-start | bytes 2777096 | tf_op jit(solution)/shard_map/ppermute | solution.py:30
  102.0 18.9 %collective-permute-start.6 = (bf16[3616,128]{1,0:T(8,128)(2,1)}, bf16[3616,128]{1,0:T(8,128)(2,1)}, u32[]{:S(2)}, u32[]{:S(2)}) collective-permute-start(bf16[3616,128]{1,0:T(8,128)(2,1)} %bitcast.23), channel_id=1, source_target_pairs={{0,1},{1,0},{2,3},{3,2},{4,5},{5,4},{6,7},{7,6},{8,9},{9,8},{10,11... | collective-permute-start | bytes 2777096 | tf_op jit(solution)/shard_map/ppermute | solution.py:30
  106.7 49.2 %collective-permute-start.11 = (bf16[128,3712]{1,0:T(8,128)(2,1)S(1)}, bf16[128,3712]{1,0:T(8,128)(2,1)}, u32[]{:S(2)}, u32[]{:S(2)}) collective-permute-start(bf16[128,3712]{1,0:T(8,128)(2,1)S(1)} %constant_dynamic-update-slice_fusion.refs_0_), channel_id=1, source_target_pairs={{0,48},{1,385},{16,0},{17,401},{32,16},{33,417},{48,32},{49,433},{... | collective-permute-start | bytes 2850824 | tf_op jit(solution)/shard_map/ppermute | solution.py:26
  111.1 13.2 %copy-start.2 = (bf16[1,128,3616]{2,1,0:T(8,128)(2,1)S(1)}, bf16[1,128,3616]{2,1,0:T(8,128)(2,1)}, u32[]{:S(2)}) copy-start(bf16[1,128,3616]{2,1,0:T(8,128)(2,1)} %copy.39) | copy-start | bytes 2777092
  111.1 13.2 %copy-start.4 = (bf16[128,3616]{1,0:T(8,128)(2,1)S(1)}, bf16[128,3616]{1,0:T(8,128)(2,1)}, u32[]{:S(2)}) copy-start(bf16[128,3616]{1,0:T(8,128)(2,1)} %copy.41) | copy-start | bytes 2777092
  111.1 36.1 %collective-permute-start.9 = (bf16[128,3712]{1,0:T(8,128)(2,1)}, bf16[128,3712]{1,0:T(8,128)(2,1)S(1)}, u32[]{:S(2)}, u32[]{:S(2)}) collective-permute-start(bf16[128,3712]{1,0:T(8,128)(2,1)} %constant_dynamic-update-slice_fusion.2.refs_1_), channel_id=1, source_target_pairs={{0,16},{1,129},{16,32},{17,145},{32,48},{33,161},{48,0},{49,177},{... | collective-permute-start | bytes 2850824 | tf_op jit(solution)/shard_map/ppermute | solution.py:26
  114.4 29.0 %collective-permute-start.13 = (bf16[128,3712]{1,0:T(8,128)(2,1)}, bf16[128,3712]{1,0:T(8,128)(2,1)S(1)}, u32[]{:S(2)}, u32[]{:S(2)}) collective-permute-start(bf16[128,3712]{1,0:T(8,128)(2,1)} %collective-permute-done.8.refs_0_), channel_id=1, source_target_pairs={{0,16},{1,129},{16,32},{17,145},{32,48},{33,161},{48,0},{49,177},{... | collective-permute-start | bytes 2850824 | tf_op jit(solution)/shard_map/ppermute | solution.py:26
  116.4 27.0 %collective-permute-start.14 = (bf16[128,3712]{1,0:T(8,128)(2,1)}, bf16[128,3712]{1,0:T(8,128)(2,1)S(1)}, u32[]{:S(2)}, u32[]{:S(2)}) collective-permute-start(bf16[128,3712]{1,0:T(8,128)(2,1)} %collective-permute-done.12.refs_1_), channel_id=1, source_target_pairs={{0,48},{1,385},{16,0},{17,401},{32,16},{33,417},{48,32},{49,433},{... | collective-permute-start | bytes 2850824 | tf_op jit(solution)/shard_map/ppermute | solution.py:26
  124.2 31.7 %copy-start = (bf16[3712,512]{1,0:T(8,128)(2,1)}, bf16[3712,512]{1,0:T(8,128)(2,1)S(1)}, u32[]{:S(2)}) copy-start(bf16[3712,512]{1,0:T(8,128)(2,1)S(1)} %fusion.6.refs_2_) | copy-start | bytes 11403268
  145.3 21.5 %collective-permute-start.15 = (bf16[128,3712]{1,0:T(8,128)(2,1)S(1)}, bf16[128,3712]{1,0:T(8,128)(2,1)S(1)}, u32[]{:S(2)}, u32[]{:S(2)}) collective-permute-start(bf16[128,3712]{1,0:T(8,128)(2,1)S(1)} %get-tuple-element.26), channel_id=1, source_target_pairs={{0,16},{1,129},{16,32},{17,145},{32,48},{33,161},{48,0},{49,177},{... | collective-permute-start | bytes 2850824 | tf_op jit(solution)/shard_map/ppermute | solution.py:26
  151.1 53.3 %collective-permute-start.10 = (bf16[128,3712]{1,0:T(8,128)(2,1)}, bf16[128,3712]{1,0:T(8,128)(2,1)}, u32[]{:S(2)}, u32[]{:S(2)}) collective-permute-start(bf16[128,3712]{1,0:T(8,128)(2,1)} %get-tuple-element.24), channel_id=1, source_target_pairs={{0,48},{1,385},{16,0},{17,401},{32,16},{33,417},{48,32},{49,433},{... | collective-permute-start | bytes 2850824 | tf_op jit(solution)/shard_map/ppermute | solution.py:26
  160.2 47.7 %collective-permute-start.20 = (bf16[128,3712]{1,0:T(8,128)(2,1)}, bf16[128,3712]{1,0:T(8,128)(2,1)}, u32[]{:S(2)}, u32[]{:S(2)}) collective-permute-start(bf16[128,3712]{1,0:T(8,128)(2,1)} %get-tuple-element.30), channel_id=1, source_target_pairs={{0,16},{1,129},{16,32},{17,145},{32,48},{33,161},{48,0},{49,177},{... | collective-permute-start | bytes 2850824 | tf_op jit(solution)/shard_map/ppermute | solution.py:26
  162.1 15.2 %collective-permute-start.18 = (bf16[128,3712]{1,0:T(8,128)(2,1)S(1)}, bf16[128,3712]{1,0:T(8,128)(2,1)S(1)}, u32[]{:S(2)}, u32[]{:S(2)}) collective-permute-start(bf16[128,3712]{1,0:T(8,128)(2,1)S(1)} %get-tuple-element.29), channel_id=1, source_target_pairs={{0,48},{1,385},{16,0},{17,401},{32,16},{33,417},{48,32},{49,433},{... | collective-permute-start | bytes 2850824 | tf_op jit(solution)/shard_map/ppermute | solution.py:26
  167.9 36.5 %collective-permute-start.16 = (bf16[128,3712]{1,0:T(8,128)(2,1)}, bf16[128,3712]{1,0:T(8,128)(2,1)}, u32[]{:S(2)}, u32[]{:S(2)}) collective-permute-start(bf16[128,3712]{1,0:T(8,128)(2,1)} %add_convert_fusion.1), channel_id=1, source_target_pairs={{0,16},{1,129},{16,32},{17,145},{32,48},{33,161},{48,0},{49,177},{... | collective-permute-start | bytes 2850824 | tf_op jit(solution)/shard_map/ppermute | solution.py:26
  178.6 29.3 %collective-permute-start.19 = (bf16[128,3712]{1,0:T(8,128)(2,1)}, bf16[128,3712]{1,0:T(8,128)(2,1)}, u32[]{:S(2)}, u32[]{:S(2)}) collective-permute-start(bf16[128,3712]{1,0:T(8,128)(2,1)} %add_convert_fusion), channel_id=1, source_target_pairs={{0,48},{1,385},{16,0},{17,401},{32,16},{33,417},{48,32},{49,433},{... | collective-permute-start | bytes 2850824 | tf_op jit(solution)/shard_map/ppermute | solution.py:26
  199.3 2.1 copy-start.1
  204.4 21.3 %copy-start.3 = (f32[64,3616]{1,0:T(8,128)S(1)}, f32[64,3616]{1,0:T(8,128)}, u32[]{:S(2)}) copy-start(f32[64,3616]{1,0:T(8,128)} %fusion.12) | copy-start | bytes 2777092
  205.8 9.7 %collective-permute-start.17 = (bf16[64,3712]{1,0:T(8,128)(2,1)S(1)}, bf16[64,3712]{1,0:T(8,128)(2,1)S(1)}, u32[]{:S(2)}, u32[]{:S(2)}) collective-permute-start(bf16[64,3712]{1,0:T(8,128)(2,1)S(1)} %add_convert_fusion.5), channel_id=1, source_target_pairs={{0,384},{1,49},{16,400},{17,1},{32,416},{33,17},{48,432},{49,33},{... | collective-permute-start | bytes 1425416 | tf_op jit(solution)/shard_map/ppermute | solution.py:26
  209.7 16.0 %collective-permute-start.21 = (bf16[64,3712]{1,0:T(8,128)(2,1)S(1)}, bf16[64,3712]{1,0:T(8,128)(2,1)S(1)}, u32[]{:S(2)}, u32[]{:S(2)}) collective-permute-start(bf16[64,3712]{1,0:T(8,128)(2,1)S(1)} %get-tuple-element.36), channel_id=1, source_target_pairs={{0,128},{1,17},{16,144},{17,33},{32,160},{33,49},{48,176},{49,1},{... | collective-permute-start | bytes 1425416 | tf_op jit(solution)/shard_map/ppermute | solution.py:26
  213.0 12.8 %collective-permute-start.22 = (bf16[64,3712]{1,0:T(8,128)(2,1)S(1)}, bf16[64,3712]{1,0:T(8,128)(2,1)S(1)}, u32[]{:S(2)}, u32[]{:S(2)}) collective-permute-start(bf16[64,3712]{1,0:T(8,128)(2,1)S(1)} %get-tuple-element.37), channel_id=1, source_target_pairs={{0,256},{1,33},{16,272},{17,49},{32,288},{33,1},{48,304},{49,17},{... | collective-permute-start | bytes 1425416 | tf_op jit(solution)/shard_map/ppermute | solution.py:26
  255.7 11.5 %collective-permute-start.23 = (bf16[32,226]{1,0:T(8,128)(2,1)S(1)}, bf16[32,226]{1,0:T(8,128)(2,1)S(1)}, u32[]{:S(2)}, u32[]{:S(2)}) collective-permute-start(bf16[32,226]{1,0:T(8,128)(2,1)S(1)} %get-tuple-element.39), channel_id=1, source_target_pairs={{0,1},{1,0},{2,3},{3,2},{4,5},{5,4},{6,7},{7,6},{8,9},{9,8},{10,11... | collective-permute-start | bytes 43400 | tf_op jit(solution)/shard_map/ppermute | solution.py:30
Sparse Core Ops, SparseCore 0:
  73.1 58.5 all-gather.3

commit v5 on v4

--- a/solution.py
+++ b/solution.py
@@ -28,6 +28,14 @@
 
 def swap(a):
     return lax.ppermute(a, "c", [(0, 1), (1, 0)])
+
+
+def spread(a):
+    groups = [[(y * X + x) * C for y in range(Y)] for x in range(X)]
+    groups += [[(y * X + x) * C + 1 for x in range(X)] for y in range(Y)]
+    return lax.all_to_all(
+        a, ("y", "x", "c"), 0, 0, axis_index_groups=groups, tiled=True
+    )
 
 
 def turn(a):
@@ -151,25 +159,27 @@
     shared = lax.dot_general(s_hidden, s_down, (((1,), (1,)), ((), ())), preferred_element_type=f32)
 
     apply = lambda *blocks: ffn(at, blocks, w_in, w_out)
-    lo = jnp.concatenate([rows, move(rows, 0, 1)], 0)
-    hi = jnp.concatenate([move(rows, 0, -1), move(rows, 0, 2)], 0)
+    order = lax.optimization_barrier
+    near = spread(jnp.concatenate([rows] * 4, 0))
+    lo, hi = near[: 2 * toks], near[2 * toks :]
     prev_lo, succ_hi = move(lo, 1, 1), move(hi, 1, -1)
+    far = move(prev_lo, 1, 1), move(succ_hi, 1, -1)
+    prev_lo, succ_hi = apply(prev_lo, succ_hi)
+    lo, hi, prev_lo, succ_hi = order((lo, hi, prev_lo, succ_hi))
     prev_hi, succ_lo = move(hi, 1, 1), move(lo, 1, -1)
-    far_lo, far_hi = apply(move(prev_lo, 1, 1), move(succ_hi, 1, -1))
-
+    back_p, back_s = move(prev_lo, 1, -1), move(succ_hi, 1, 1)
+    far_lo, far_hi = apply(*far)
+
+    far_lo, far_hi, prev_hi, succ_lo = order((far_lo, far_hi, prev_hi, succ_lo))
     from_prev, from_succ = move(far_lo, 1, 1), move(far_hi, 1, -1)
-    prev_lo, prev_hi = apply(prev_lo, prev_hi)
-    succ_lo, succ_hi = apply(succ_lo, succ_hi)
-    prev_lo, succ_hi = move(prev_lo, 1, -1), move(succ_hi, 1, 1)
-    lo, hi, shared = lax.optimization_barrier((lo, hi, shared))
+    prev_hi, succ_lo = apply(prev_hi, succ_lo)
+    lo, hi, shared, prev_hi, succ_lo = order((lo, hi, shared, prev_hi, succ_lo))
     own_lo, own_hi = apply(lo, hi)
     prev_hi = move(add(prev_hi, from_succ), 1, -1)
     succ_lo = move(add(succ_lo, from_prev), 1, 1)
-    los, his = (own_lo, prev_lo, succ_lo), (own_hi, prev_hi, succ_hi)
-    total = [t[:toks] for t in los]
-    total.append(move(add(*[t[toks:] for t in los]), 0, -1))
-    total.append(move(add(*[t[:toks] for t in his]), 0, 1))
-    total.append(move(add(*[t[toks:] for t in his]), 0, 2))
+    total = jnp.concatenate([add(own_lo, back_p, succ_lo), add(own_hi, back_s, prev_hi)], 0)
+    total = spread(total)
+    total = [total[i * toks : (i + 1) * toks] for i in range(4)]
     total = add(shared, *[t[:, :feats] for t in total])
 
     back = total.reshape(H, half, L, C, width).transpose(0, 2, 3, 1, 4)

time: 276 us -> 250 us (0.906)
  waiting for transfers between devices: 41.7 us -> 24 us
  starting transfers between devices: 103 us -> 87.1 us
  blocking collectives: 50.5 us -> 64.5 us
  local copies, waits for them, and re-layouts: 29.7 us -> 25 us
  Pallas kernels: 13.1 us -> 9.87 us
    ppermute x18 -> x12, starting transfers between devices: 58.9 us -> 37.4 us  [move(): return lax.ppermute(a, ('y', 'x', 'c'), pairs)]
    all_to_all x0 -> x1, blocking collectives: none -> 18.2 us  [spread(): lax.all_to_all(a, ('y', 'x', 'c'), 0, 0, axis_index_groups=groups, tiled=...]
    ppermute x18 -> x12, waiting for transfers between devices: 40.8 us -> 23.2 us  [move(): return lax.ppermute(a, ('y', 'x', 'c'), pairs)]
    all_to_all x0 -> x1, starting transfers between devices: none -> 4.69 us  [spread(): lax.all_to_all(a, ('y', 'x', 'c'), 0, 0, axis_index_groups=groups, tiled=...]
    all_to_all x1, blocking collectives: 26.3 us -> 22.2 us  [local(): back = lax.all_to_all(back, Z, split_axis=0, concat_axis=0, tiled=True)]
    pallas_call x4, Pallas kernels: 13.1 us -> 9.87 us  [ffn(): pl.pallas_call(functools.partial(ffn_kernel, hid=hid, parts=parts), out_s...]
    concatenate x2 -> x0, local copies, waits for them, and re-layouts: 2.9 us -> none  [the longest x1 1.84 us: local(): hi = jnp.concatenate([move(rows, 0, -1), move(rows, 0, 2)], 0)]
    unnamed x19 -> x29, local copies, waits for them, and re-layouts: 6.25 us -> 4.37 us
  transfers between devices with their start and end apart: 25 -> 20, of which waited for: 6 -> 6; matrix products, arithmetic and copies ran while one was open for 15% -> 15% of each run, Pallas kernels for 5% -> 4%
where the time goes in v5:
time: 250 us; the launch traced here: 248 us
  starting transfers between devices  87.1 us (35%)
  blocking collectives  64.5 us (26%)
  local copies, waits for them, and re-layouts  25 us (10%)
  waiting for transfers between devices  24 us (10%)
  other arithmetic  18.6 us (7%)
  between operations  14 us (6%)
  Pallas kernels  9.87 us (4%)
  matrix products  4.61 us (2%)
    ppermute x12, starting transfers between devices, move(): return lax.ppermute(a, ('y', 'x', 'c'), pairs)  37.4 us
    ppermute x5, starting transfers between devices, swap(): return lax.ppermute(a, 'c', [(0, 1), (1, 0)])  35.1 us
    all_gather x1, blocking collectives, local(): got = lax.all_gather(sent, Z, axis=0, tiled=False)  24.2 us
    ppermute x12, waiting for transfers between devices, move(): return lax.ppermute(a, ('y', 'x', 'c'), pairs)  23.2 us
    all_to_all x1, blocking collectives, local(): back = lax.all_to_all(back, Z, split_axis=0, concat_axis=0, tiled=True)  22.2 us
    all_to_all x1, blocking collectives, spread(): lax.all_to_all(a, ('y', 'x', 'c'), 0, 0, axis_index_groups=groups, tiled=...  18.2 us
    ppermute x1, starting transfers between devices, turn(): lax.ppermute(a, ('h', 'c'), [(h * 2 + c, c * 2 + h) for h in range(2) for...  9.97 us
    pallas_call x4, Pallas kernels, ffn(): pl.pallas_call(functools.partial(ffn_kernel, hid=hid, parts=parts), out_s...  9.87 us
  transfers between devices with their start and end apart: 20, of which 6 were waited for; matrix products, arithmetic and copies ran while one was open for 15% of the time, Pallas kernels for 4%

profile of v5, /device:TPU:1, one launch (start us, length us, event | category | flops | bytes accessed | tf_op | source)
XLA Modules:
  0.0 247.8 jit_solution(2828871634055385479)
XLA Ops:
  9.9 8.8 %collective-permute-start = (bf16[32,256]{1,0:T(8,128)(2,1)S(1)}, bf16[32,256]{1,0:T(8,128)(2,1)S(1)}, u32[]{:S(2)}, u32[]{:S(2)}) collective-permute-start(bf16[32,256]{1,0:T(8,128)(2,1)S(1)} %get-tuple-element.61), channel_id=1, source_target_pairs={{0,1},{1,0},{2,3},{3,2},{4,5},{5,4},{6,7},{7,6},{8,9},{9,8},{10,11... | collective-permute-start | bytes 49160 | tf_op jit(solution)/shard_map/ppermute | solution.py:30
  19.5 10.0 %collective-permute-start.1 = (bf16[352,128]{1,0:T(8,128)(2,1)S(1)}, bf16[352,128]{1,0:T(8,128)(2,1)S(1)}, u32[]{:S(2)}, u32[]{:S(2)}) collective-permute-start(bf16[352,128]{1,0:T(8,128)(2,1)S(1)} %fusion.21), channel_id=1, source_target_pairs={{0,0},{1,64},{64,1},{65,65},{2,2},{3,66},{66,3},{67,67},{4,4},{5,6... | collective-permute-start | bytes 270344 | tf_op jit(solution)/shard_map/ppermute | solution.py:42
  29.5 24.2 %all-gather = bf16[512,512]{1,0:T(8,128)(2,1)S(1)} all-gather(bf16[32,512]{1,0:T(8,128)(2,1)S(1)} %pad_maximum_fusion.2), channel_id=2, replica_groups=mesh['y'=4,'h'=2,'x'=4,'l'=8,'c'=2] {'h','l'}, dimensions={0}, use_global_device_ids=true | all-gather | bytes 557056 | tf_op jit(solution)/shard_map/all_gather | solution.py:129
  53.8 1.5 copy.34
  55.4 2.3 fusion.9
  59.0 1.6 copy.35
  62.3 1.4 pad_maximum_fusion
  63.7 4.7 %all-to-all-start = ((bf16[4,64,3712]{2,1,0:T(8,128)(2,1)}), bf16[4,64,3712]{2,1,0:T(8,128)(2,1)S(1)}, u32[]{:S(2)}, u32[]{:S(2)}) async-start(bf16[4,64,3712]{2,1,0:T(8,128)(2,1)} %bitcast.29), calls=%async_computation | async-start | bytes 3801088 | tf_op jit(solution)/shard_map/all_to_all | solution.py:36
  68.4 7.9 %collective-permute-start.6 = (bf16[128,3616]{0,1:T(8,128)(2,1)S(1)}, bf16[128,3616]{0,1:T(8,128)(2,1)}, u32[]{:S(2)}, u32[]{:S(2)}) collective-permute-start(bf16[128,3616]{0,1:T(8,128)(2,1)S(1)} %bitcast.36), channel_id=1, source_target_pairs={{0,1},{1,0},{2,3},{3,2},{4,5},{5,4},{6,7},{7,6},{8,9},{9,8},{10,11... | collective-permute-start | bytes 2777096 | tf_op jit(solution)/shard_map/ppermute | solution.py:30
  76.3 1.9 collective-permute-start.4
  78.2 2.4 collective-permute-start.5
  80.6 1.8 copy.37
  82.4 2.2 copy.39
  84.8 3.9 %collective-permute-start.2 = (bf16[128,3712]{1,0:T(8,128)(2,1)S(1)}, bf16[128,3712]{1,0:T(8,128)(2,1)S(1)}, u32[]{:S(2)}, u32[]{:S(2)}) collective-permute-start(bf16[128,3712]{1,0:T(8,128)(2,1)S(1)} %bitcast.26), channel_id=1, source_target_pairs={{0,16},{1,129},{16,32},{17,145},{32,48},{33,161},{48,0},{49,177},{... | collective-permute-start | bytes 2850824 | tf_op jit(solution)/shard_map/ppermute | solution.py:26
  88.8 3.1 %collective-permute-start.3 = (bf16[128,3712]{1,0:T(8,128)(2,1)S(1)}, bf16[128,3712]{1,0:T(8,128)(2,1)S(1)}, u32[]{:S(2)}, u32[]{:S(2)}) collective-permute-start(bf16[128,3712]{1,0:T(8,128)(2,1)S(1)} %bitcast.23), channel_id=1, source_target_pairs={{0,48},{1,385},{16,0},{17,401},{32,16},{33,417},{48,32},{49,433},{... | collective-permute-start | bytes 2850824 | tf_op jit(solution)/shard_map/ppermute | solution.py:26
  92.1 3.3 %fusion.6.refs_2_ = bf16[3712,512]{1,0:T(8,128)(2,1)S(1)} fusion(bf16[3616,128]{1,0:T(8,128)(2,1)} %collective-permute-done.5, bf16[3616,128]{1,0:T(8,128)(2,1)S(1)} %bitcast.38, bf16[3616,128]{1,0:T(8,128)(2,1)} %collective-permute-done.4, bf16[3616,128]{1,0:T(8,128)(2,1)S(1)} %bitcast.40), kind=kLoop, calls=%fused_computation.8 | loop fusion | flops 24707072 | bytes 7503872 | tf_op jit(solution)/shard_map/concatenate | solution.py:143
  95.4 6.1 %collective-permute-done.2.refs_0_ = bf16[128,3712]{1,0:T(8,128)(2,1)S(1)} collective-permute-done((bf16[128,3712]{1,0:T(8,128)(2,1)S(1)}, bf16[128,3712]{1,0:T(8,128)(2,1)S(1)}, u32[]{:S(2)}, u32[]{:S(2)}) %collective-permute-start.2) | collective-permute-done | bytes 950304 | tf_op jit(solution)/shard_map/ppermute | solution.py:26
  101.5 2.4 collective-permute-start.7
  103.9 4.1 %collective-permute-start.8 = (bf16[128,3712]{1,0:T(8,128)(2,1)S(1)}, bf16[128,3712]{1,0:T(8,128)(2,1)S(1)}, u32[]{:S(2)}, u32[]{:S(2)}) collective-permute-start(bf16[128,3712]{1,0:T(8,128)(2,1)S(1)} %collective-permute-done.3.refs_1_), channel_id=1, source_target_pairs={{0,48},{1,385},{16,0},{17,401},{32,16},{33,417},{48,32},{49,433},{... | collective-permute-start | bytes 2850824 | tf_op jit(solution)/shard_map/ppermute | solution.py:26
  108.0 3.1 %shard_map.91 = (bf16[128,3712]{1,0:T(8,128)(2,1)}, bf16[128,3712]{1,0:T(8,128)(2,1)}) custom-call(s32[1]{0:T(128)} %bitcast.5.at_ref, bf16[128,3712]{1,0:T(8,128)(2,1)S(1)} %collective-permute-done.2.refs_0_, bf16[128,3712]{1,0:T(8,128)(2,1)S(1)} %collective-permute-done.3.refs_1_, bf16[3712,512]{1,0:T(8,128)(2,1)S(1)} %fusion.6.refs_2_, ...), custom_call_target="tpu_custom_call" | custom-call | flops 1459617792 | bytes 9502720 | tf_op jit(solution)/shard_map/pallas_call | solution.py:79
  111.1 2.1 collective-permute-start.10
  113.3 3.1 %collective-permute-start.9 = (bf16[128,3712]{1,0:T(8,128)(2,1)S(1)}, bf16[128,3712]{1,0:T(8,128)(2,1)S(1)}, u32[]{:S(2)}, u32[]{:S(2)}) collective-permute-start(bf16[128,3712]{1,0:T(8,128)(2,1)S(1)} %bitcast.24), channel_id=1, source_target_pairs={{0,16},{1,129},{16,32},{17,145},{32,48},{33,161},{48,0},{49,177},{... | collective-permute-start | bytes 2850824 | tf_op jit(solution)/shard_map/ppermute | solution.py:26
  116.4 3.4 %collective-permute-start.11 = (bf16[128,3712]{1,0:T(8,128)(2,1)}, bf16[128,3712]{1,0:T(8,128)(2,1)}, u32[]{:S(2)}, u32[]{:S(2)}) collective-permute-start(bf16[128,3712]{1,0:T(8,128)(2,1)} %get-tuple-element.44), channel_id=1, source_target_pairs={{0,48},{1,385},{16,0},{17,401},{32,16},{33,417},{48,32},{49,433},{... | collective-permute-start | bytes 2850824 | tf_op jit(solution)/shard_map/ppermute | solution.py:26
  119.8 3.5 %collective-permute-done.7.refs_0_ = bf16[128,3712]{1,0:T(8,128)(2,1)S(1)} collective-permute-done((bf16[128,3712]{1,0:T(8,128)(2,1)S(1)}, bf16[128,3712]{1,0:T(8,128)(2,1)S(1)}, u32[]{:S(2)}, u32[]{:S(2)}) %collective-permute-start.7) | collective-permute-done | bytes 950304 | tf_op jit(solution)/shard_map/ppermute | solution.py:26
  123.3 1.9 collective-permute-start.14
  125.2 3.1 %shard_map.92 = (bf16[128,3712]{1,0:T(8,128)(2,1)}, bf16[128,3712]{1,0:T(8,128)(2,1)}) custom-call(s32[1]{0:T(128)} %bitcast.5.at_ref, bf16[128,3712]{1,0:T(8,128)(2,1)S(1)} %collective-permute-done.7.refs_0_, bf16[128,3712]{1,0:T(8,128)(2,1)S(1)} %collective-permute-done.8.refs_1_, bf16[3712,512]{1,0:T(8,128)(2,1)S(1)} %fusion.6.refs_2_, ...), custom_call_target="tpu_custom_call" | custom-call | flops 1459617792 | bytes 9502720 | tf_op jit(solution)/shard_map/pallas_call | solution.py:79
  128.3 6.4 %collective-permute-done.10.refs_1_ = bf16[128,3712]{1,0:T(8,128)(2,1)S(1)} collective-permute-done((bf16[128,3712]{1,0:T(8,128)(2,1)S(1)}, bf16[128,3712]{1,0:T(8,128)(2,1)S(1)}, u32[]{:S(2)}, u32[]{:S(2)}) %collective-permute-start.10) | collective-permute-done | bytes 950304 | tf_op jit(solution)/shard_map/ppermute | solution.py:26
  134.7 2.7 %collective-permute-start.12 = (bf16[128,3712]{1,0:T(8,128)(2,1)}, bf16[128,3712]{1,0:T(8,128)(2,1)}, u32[]{:S(2)}, u32[]{:S(2)}) collective-permute-start(bf16[128,3712]{1,0:T(8,128)(2,1)} %get-tuple-element.46), channel_id=1, source_target_pairs={{0,16},{1,129},{16,32},{17,145},{32,48},{33,161},{48,0},{49,177},{... | collective-permute-start | bytes 2850824 | tf_op jit(solution)/shard_map/ppermute | solution.py:26
  137.4 3.9 %collective-permute-start.15 = (bf16[128,3712]{1,0:T(8,128)(2,1)}, bf16[128,3712]{1,0:T(8,128)(2,1)}, u32[]{:S(2)}, u32[]{:S(2)}) collective-permute-start(bf16[128,3712]{1,0:T(8,128)(2,1)} %get-tuple-element.50), channel_id=1, source_target_pairs={{0,48},{1,385},{16,0},{17,401},{32,16},{33,417},{48,32},{49,433},{... | collective-permute-start | bytes 2850824 | tf_op jit(solution)/shard_map/ppermute | solution.py:26
  141.4 1.8 shard_map.93
  145.1 3.7 %fusion.29 = (bf16[32,113,128]{2,1,0:T(8,128)(2,1)}, bf16[32,113,128]{2,1,0:T(8,128)(2,1)}, bf16[32,113,128]{2,1,0:T(8,128)(2,1)}) fusion(bf16[32,352,128]{2,1,0:T(8,128)(2,1)} %bitcast.33), kind=kLoop, calls=%fused_computation.52 | loop fusion | bytes 5554176 | tf_op jit(solution)/shard_map/slice | solution.py:154
  148.9 2.3 reshape.44
  151.2 2.3 reshape.46
  153.4 2.3 reshape.45
  155.8 1.5 fusion.15
  157.3 3.1 %fusion.12 = f32[64,3616]{1,0:T(8,128)} fusion(bf16[3616,128]{1,0:T(8,128)(2,1)} %reshape.46, bf16[3616,128]{1,0:T(8,128)(2,1)} %reshape.45, bf16[64,3712]{1,0:T(8,128)(2,1)S(1)} %concatenate.32, f32[64,128]{1,0:T(8,128)S(1)} %fusion.15), kind=kOutput, calls=%fused_computation.22 | convolution fusion | flops 118538240 | bytes 3284992 | tf_op jit(solution)/shard_map/dot_general | solution.py:159
  160.4 1.8 add_convert_fusion.3
  162.2 2.1 collective-permute-start.13
  164.3 1.4 add_convert_fusion.1
  165.8 4.6 %collective-permute-start.16 = (bf16[128,3712]{1,0:T(8,128)(2,1)S(1)}, bf16[128,3712]{1,0:T(8,128)(2,1)S(1)}, u32[]{:S(2)}, u32[]{:S(2)}) collective-permute-start(bf16[128,3712]{1,0:T(8,128)(2,1)S(1)} %add_convert_fusion.1), channel_id=1, source_target_pairs={{0,48},{1,385},{16,0},{17,401},{32,16},{33,417},{48,32},{49,433},{... | collective-permute-start | bytes 2850824 | tf_op jit(solution)/shard_map/ppermute | solution.py:26
  170.4 1.8 shard_map.94
  172.2 6.2 %collective-permute-done.13 = bf16[128,3712]{1,0:T(8,128)(2,1)S(1)} collective-permute-done((bf16[128,3712]{1,0:T(8,128)(2,1)S(1)}, bf16[128,3712]{1,0:T(8,128)(2,1)S(1)}, u32[]{:S(2)}, u32[]{:S(2)}) %collective-permute-start.13) | collective-permute-done | bytes 950304 | tf_op jit(solution)/shard_map/ppermute | solution.py:26
  178.4 1.6 add_convert_fusion.2
  181.0 1.6 add_convert_fusion
  182.7 18.2 %all_to_all.26 = bf16[4,64,3712]{2,1,0:T(8,128)(2,1)S(1)} all-to-all(bf16[4,64,3712]{2,1,0:T(8,128)(2,1)S(1)} %bitcast.30), channel_id=1, replica_groups={{0,128,256,384},{16,144,272,400},{32,160,288,416},{48,176,304,432},{1,1..., dimensions={0} | all-to-all | bytes 3801088 | tf_op jit(solution)/shard_map/all_to_all | solution.py:36
  201.2 1.7 reshape.47
  203.1 22.2 %all_to_all.27 = bf16[16,64,226]{2,1,0:T(8,128)(2,1)S(1)} all-to-all(bf16[16,64,226]{2,1,0:T(8,128)(2,1)S(1)} %bitcast.35), channel_id=1, replica_groups=mesh['y'=4,'h'=2,'x'=4,'l'=8,'c'=2] {'h','l'}, dimensions={0} | all-to-all | bytes 925696 | tf_op jit(solution)/shard_map/all_to_all | solution.py:188
  225.4 14.1 %collective-permute-start.17 = (bf16[32,226]{1,0:T(8,128)(2,1)S(1)}, bf16[32,226]{1,0:T(8,128)(2,1)S(1)}, u32[]{:S(2)}, u32[]{:S(2)}) collective-permute-start(bf16[32,226]{1,0:T(8,128)(2,1)S(1)} %get-tuple-element.59), channel_id=1, source_target_pairs={{0,1},{1,0},{2,3},{3,2},{4,5},{5,4},{6,7},{7,6},{8,9},{9,8},{10,11... | collective-permute-start | bytes 43400 | tf_op jit(solution)/shard_map/ppermute | solution.py:30
  (76 shorter events, 12.9 us)
Async XLA Ops:
  6.5 138.6 %all-gather.4.cloned.1.call-start = ((), (), s32[]{:S(2)}) async-start(), calls=%async_computation.3 | async-start | bytes 2973696 | tf_op jit(solution)/shard_map/all_gather | solution.py:152
  9.9 19.6 %collective-permute-start = (bf16[32,256]{1,0:T(8,128)(2,1)S(1)}, bf16[32,256]{1,0:T(8,128)(2,1)S(1)}, u32[]{:S(2)}, u32[]{:S(2)}) collective-permute-start(bf16[32,256]{1,0:T(8,128)(2,1)S(1)} %get-tuple-element.61), channel_id=1, source_target_pairs={{0,1},{1,0},{2,3},{3,2},{4,5},{5,4},{6,7},{7,6},{8,9},{9,8},{10,11... | collective-permute-start | bytes 49160 | tf_op jit(solution)/shard_map/ppermute | solution.py:30
  19.5 42.1 %collective-permute-start.1 = (bf16[352,128]{1,0:T(8,128)(2,1)S(1)}, bf16[352,128]{1,0:T(8,128)(2,1)S(1)}, u32[]{:S(2)}, u32[]{:S(2)}) collective-permute-start(bf16[352,128]{1,0:T(8,128)(2,1)S(1)} %fusion.21), channel_id=1, source_target_pairs={{0,0},{1,64},{64,1},{65,65},{2,2},{3,66},{66,3},{67,67},{4,4},{5,6... | collective-permute-start | bytes 270344 | tf_op jit(solution)/shard_map/ppermute | solution.py:42
  61.6 0.6 copy-start.13
  63.7 4.7 %copy-start.10 = (bf16[1,128,3616]{1,2,0:T(8,128)(2,1)S(1)}, bf16[1,128,3616]{1,2,0:T(8,128)(2,1)}, u32[]{:S(2)}) copy-start(bf16[1,128,3616]{1,2,0:T(8,128)(2,1)} %param.14) | copy-start | bytes 2777092
  63.7 21.0 %all-to-all-start = ((bf16[4,64,3712]{2,1,0:T(8,128)(2,1)}), bf16[4,64,3712]{2,1,0:T(8,128)(2,1)S(1)}, u32[]{:S(2)}, u32[]{:S(2)}) async-start(bf16[4,64,3712]{2,1,0:T(8,128)(2,1)} %bitcast.29), calls=%async_computation | async-start | bytes 3801088 | tf_op jit(solution)/shard_map/all_to_all | solution.py:36
  68.4 14.0 %collective-permute-start.6 = (bf16[128,3616]{0,1:T(8,128)(2,1)S(1)}, bf16[128,3616]{0,1:T(8,128)(2,1)}, u32[]{:S(2)}, u32[]{:S(2)}) collective-permute-start(bf16[128,3616]{0,1:T(8,128)(2,1)S(1)} %bitcast.36), channel_id=1, source_target_pairs={{0,1},{1,0},{2,3},{3,2},{4,5},{5,4},{6,7},{7,6},{8,9},{9,8},{10,11... | collective-permute-start | bytes 2777096 | tf_op jit(solution)/shard_map/ppermute | solution.py:30
  76.3 15.8 %collective-permute-start.4 = (bf16[3616,128]{1,0:T(8,128)(2,1)}, bf16[3616,128]{1,0:T(8,128)(2,1)}, u32[]{:S(2)}, u32[]{:S(2)}) collective-permute-start(bf16[3616,128]{1,0:T(8,128)(2,1)} %bitcast.39), channel_id=1, source_target_pairs={{0,1},{1,0},{2,3},{3,2},{4,5},{5,4},{6,7},{7,6},{8,9},{9,8},{10,11... | collective-permute-start | bytes 2777096 | tf_op jit(solution)/shard_map/ppermute | solution.py:30
  78.2 13.9 %collective-permute-start.5 = (bf16[3616,128]{1,0:T(8,128)(2,1)}, bf16[3616,128]{1,0:T(8,128)(2,1)}, u32[]{:S(2)}, u32[]{:S(2)}) collective-permute-start(bf16[3616,128]{1,0:T(8,128)(2,1)} %bitcast.37), channel_id=1, source_target_pairs={{0,1},{1,0},{2,3},{3,2},{4,5},{5,4},{6,7},{7,6},{8,9},{9,8},{10,11... | collective-permute-start | bytes 2777096 | tf_op jit(solution)/shard_map/ppermute | solution.py:30
  84.7 7.2 %copy-start.8 = (bf16[1,128,3616]{2,1,0:T(8,128)(2,1)S(1)}, bf16[1,128,3616]{2,1,0:T(8,128)(2,1)}, u32[]{:S(2)}) copy-start(bf16[1,128,3616]{2,1,0:T(8,128)(2,1)} %copy.37) | copy-start | bytes 2777092
  84.7 7.3 %copy-start.9 = (bf16[128,3616]{1,0:T(8,128)(2,1)S(1)}, bf16[128,3616]{1,0:T(8,128)(2,1)}, u32[]{:S(2)}) copy-start(bf16[128,3616]{1,0:T(8,128)(2,1)} %copy.39) | copy-start | bytes 2777092
  84.8 26.3 %copy-start.2 = (bf16[2,64,3712]{2,1,0:T(8,128)(2,1)}, bf16[2,64,3712]{2,1,0:T(8,128)(2,1)S(1)}, u32[]{:S(2)}) copy-start(bf16[2,64,3712]{2,1,0:T(8,128)(2,1)S(1)} %get-tuple-element.57) | copy-start | bytes 2850820
  84.8 7.3 %copy-start.11 = (bf16[1,3616,128]{2,1,0:T(8,128)(2,1)S(1)}, bf16[1,3616,128]{2,1,0:T(8,128)(2,1)}, u32[]{:S(2)}) copy-start(bf16[1,3616,128]{2,1,0:T(8,128)(2,1)} %param.13) | copy-start | bytes 2777092
  84.8 7.3 %copy-start.12 = (bf16[1,3616,128]{2,1,0:T(8,128)(2,1)S(1)}, bf16[1,3616,128]{2,1,0:T(8,128)(2,1)}, u32[]{:S(2)}) copy-start(bf16[1,3616,128]{2,1,0:T(8,128)(2,1)} %param.12) | copy-start | bytes 2777092
  84.8 16.7 %collective-permute-start.2 = (bf16[128,3712]{1,0:T(8,128)(2,1)S(1)}, bf16[128,3712]{1,0:T(8,128)(2,1)S(1)}, u32[]{:S(2)}, u32[]{:S(2)}) collective-permute-start(bf16[128,3712]{1,0:T(8,128)(2,1)S(1)} %bitcast.26), channel_id=1, source_target_pairs={{0,16},{1,129},{16,32},{17,145},{32,48},{33,161},{48,0},{49,177},{... | collective-permute-start | bytes 2850824 | tf_op jit(solution)/shard_map/ppermute | solution.py:26
  88.8 15.1 %collective-permute-start.3 = (bf16[128,3712]{1,0:T(8,128)(2,1)S(1)}, bf16[128,3712]{1,0:T(8,128)(2,1)S(1)}, u32[]{:S(2)}, u32[]{:S(2)}) collective-permute-start(bf16[128,3712]{1,0:T(8,128)(2,1)S(1)} %bitcast.23), channel_id=1, source_target_pairs={{0,48},{1,385},{16,0},{17,401},{32,16},{33,417},{48,32},{49,433},{... | collective-permute-start | bytes 2850824 | tf_op jit(solution)/shard_map/ppermute | solution.py:26
  95.4 45.9 %copy-start = (bf16[3712,512]{1,0:T(8,128)(2,1)}, bf16[3712,512]{1,0:T(8,128)(2,1)S(1)}, u32[]{:S(2)}) copy-start(bf16[3712,512]{1,0:T(8,128)(2,1)S(1)} %fusion.6.refs_2_) | copy-start | bytes 11403268
  101.5 21.8 %collective-permute-start.7 = (bf16[128,3712]{1,0:T(8,128)(2,1)S(1)}, bf16[128,3712]{1,0:T(8,128)(2,1)S(1)}, u32[]{:S(2)}, u32[]{:S(2)}) collective-permute-start(bf16[128,3712]{1,0:T(8,128)(2,1)S(1)} %collective-permute-done.2.refs_0_), channel_id=1, source_target_pairs={{0,16},{1,129},{16,32},{17,145},{32,48},{33,161},{48,0},{49,177},{... | collective-permute-start | bytes 2850824 | tf_op jit(solution)/shard_map/ppermute | solution.py:26
  103.9 21.3 %collective-permute-start.8 = (bf16[128,3712]{1,0:T(8,128)(2,1)S(1)}, bf16[128,3712]{1,0:T(8,128)(2,1)S(1)}, u32[]{:S(2)}, u32[]{:S(2)}) collective-permute-start(bf16[128,3712]{1,0:T(8,128)(2,1)S(1)} %collective-permute-done.3.refs_1_), channel_id=1, source_target_pairs={{0,48},{1,385},{16,0},{17,401},{32,16},{33,417},{48,32},{49,433},{... | collective-permute-start | bytes 2850824 | tf_op jit(solution)/shard_map/ppermute | solution.py:26
  111.1 23.5 %collective-permute-start.10 = (bf16[128,3712]{1,0:T(8,128)(2,1)S(1)}, bf16[128,3712]{1,0:T(8,128)(2,1)S(1)}, u32[]{:S(2)}, u32[]{:S(2)}) collective-permute-start(bf16[128,3712]{1,0:T(8,128)(2,1)S(1)} %bitcast.27), channel_id=1, source_target_pairs={{0,48},{1,385},{16,0},{17,401},{32,16},{33,417},{48,32},{49,433},{... | collective-permute-start | bytes 2850824 | tf_op jit(solution)/shard_map/ppermute | solution.py:26
  113.3 21.4 %collective-permute-start.9 = (bf16[128,3712]{1,0:T(8,128)(2,1)S(1)}, bf16[128,3712]{1,0:T(8,128)(2,1)S(1)}, u32[]{:S(2)}, u32[]{:S(2)}) collective-permute-start(bf16[128,3712]{1,0:T(8,128)(2,1)S(1)} %bitcast.24), channel_id=1, source_target_pairs={{0,16},{1,129},{16,32},{17,145},{32,48},{33,161},{48,0},{49,177},{... | collective-permute-start | bytes 2850824 | tf_op jit(solution)/shard_map/ppermute | solution.py:26
  116.4 55.8 %collective-permute-start.11 = (bf16[128,3712]{1,0:T(8,128)(2,1)}, bf16[128,3712]{1,0:T(8,128)(2,1)}, u32[]{:S(2)}, u32[]{:S(2)}) collective-permute-start(bf16[128,3712]{1,0:T(8,128)(2,1)} %get-tuple-element.44), channel_id=1, source_target_pairs={{0,48},{1,385},{16,0},{17,401},{32,16},{33,417},{48,32},{49,433},{... | collective-permute-start | bytes 2850824 | tf_op jit(solution)/shard_map/ppermute | solution.py:26
  123.3 56.6 %collective-permute-start.14 = (bf16[128,3712]{1,0:T(8,128)(2,1)}, bf16[128,3712]{1,0:T(8,128)(2,1)}, u32[]{:S(2)}, u32[]{:S(2)}) collective-permute-start(bf16[128,3712]{1,0:T(8,128)(2,1)} %get-tuple-element.48), channel_id=1, source_target_pairs={{0,16},{1,129},{16,32},{17,145},{32,48},{33,161},{48,0},{49,177},{... | collective-permute-start | bytes 2850824 | tf_op jit(solution)/shard_map/ppermute | solution.py:26
  134.7 25.7 %collective-permute-start.12 = (bf16[128,3712]{1,0:T(8,128)(2,1)}, bf16[128,3712]{1,0:T(8,128)(2,1)}, u32[]{:S(2)}, u32[]{:S(2)}) collective-permute-start(bf16[128,3712]{1,0:T(8,128)(2,1)} %get-tuple-element.46), channel_id=1, source_target_pairs={{0,16},{1,129},{16,32},{17,145},{32,48},{33,161},{48,0},{49,177},{... | collective-permute-start | bytes 2850824 | tf_op jit(solution)/shard_map/ppermute | solution.py:26
  137.4 26.9 %collective-permute-start.15 = (bf16[128,3712]{1,0:T(8,128)(2,1)}, bf16[128,3712]{1,0:T(8,128)(2,1)}, u32[]{:S(2)}, u32[]{:S(2)}) collective-permute-start(bf16[128,3712]{1,0:T(8,128)(2,1)} %get-tuple-element.50), channel_id=1, source_target_pairs={{0,48},{1,385},{16,0},{17,401},{32,16},{33,417},{48,32},{49,433},{... | collective-permute-start | bytes 2850824 | tf_op jit(solution)/shard_map/ppermute | solution.py:26
  143.2 1.0 copy-start.4
  144.2 0.9 copy-start.6
  160.4 3.9 %copy-start.5 = (bf16[128,3712]{1,0:T(8,128)(2,1)S(1)}, bf16[128,3712]{1,0:T(8,128)(2,1)}, u32[]{:S(2)}) copy-start(bf16[128,3712]{1,0:T(8,128)(2,1)} %copy-done.4) | copy-start | bytes 2850820
  160.4 10.0 %copy-start.1 = (bf16[3712,512]{1,0:T(8,128)(2,1)S(1)}, bf16[3712,512]{1,0:T(8,128)(2,1)}, u32[]{:S(2)}) copy-start(bf16[3712,512]{1,0:T(8,128)(2,1)} %copy-done) | copy-start | bytes 11403268
  162.2 8.1 %copy-start.3 = (bf16[2,64,3712]{2,1,0:T(8,128)(2,1)S(1)}, bf16[2,64,3712]{2,1,0:T(8,128)(2,1)}, u32[]{:S(2)}) copy-start(bf16[2,64,3712]{2,1,0:T(8,128)(2,1)} %copy-done.2) | copy-start | bytes 2850820
  162.2 16.1 %collective-permute-start.13 = (bf16[128,3712]{1,0:T(8,128)(2,1)S(1)}, bf16[128,3712]{1,0:T(8,128)(2,1)S(1)}, u32[]{:S(2)}, u32[]{:S(2)}) collective-permute-start(bf16[128,3712]{1,0:T(8,128)(2,1)S(1)} %add_convert_fusion.3), channel_id=1, source_target_pairs={{0,16},{1,129},{16,32},{17,145},{32,48},{33,161},{48,0},{49,177},{... | collective-permute-start | bytes 2850824 | tf_op jit(solution)/shard_map/ppermute | solution.py:26
  165.8 15.2 %collective-permute-start.16 = (bf16[128,3712]{1,0:T(8,128)(2,1)S(1)}, bf16[128,3712]{1,0:T(8,128)(2,1)S(1)}, u32[]{:S(2)}, u32[]{:S(2)}) collective-permute-start(bf16[128,3712]{1,0:T(8,128)(2,1)S(1)} %add_convert_fusion.1), channel_id=1, source_target_pairs={{0,48},{1,385},{16,0},{17,401},{32,16},{33,417},{48,32},{49,433},{... | collective-permute-start | bytes 2850824 | tf_op jit(solution)/shard_map/ppermute | solution.py:26
  182.7 18.2 %copy-start.7 = (f32[64,3616]{1,0:T(8,128)S(1)}, f32[64,3616]{1,0:T(8,128)}, u32[]{:S(2)}) copy-start(f32[64,3616]{1,0:T(8,128)} %fusion.12) | copy-start | bytes 2777092
  225.4 14.9 %collective-permute-start.17 = (bf16[32,226]{1,0:T(8,128)(2,1)S(1)}, bf16[32,226]{1,0:T(8,128)(2,1)S(1)}, u32[]{:S(2)}, u32[]{:S(2)}) collective-permute-start(bf16[32,226]{1,0:T(8,128)(2,1)S(1)} %get-tuple-element.59), channel_id=1, source_target_pairs={{0,1},{1,0},{2,3},{3,2},{4,5},{5,4},{6,7},{7,6},{8,9},{9,8},{10,11... | collective-permute-start | bytes 43400 | tf_op jit(solution)/shard_map/ppermute | solution.py:30
Sparse Core Ops, SparseCore 0:
  62.4 60.5 all-gather.3

commit v6 on v5

--- a/solution.py
+++ b/solution.py
@@ -36,10 +36,6 @@
     return lax.all_to_all(
         a, ("y", "x", "c"), 0, 0, axis_index_groups=groups, tiled=True
     )
-
-
-def turn(a):
-    return lax.ppermute(a, ("h", "c"), [(h * 2 + c, c * 2 + h) for h in range(2) for c in range(2)])
 
 
 def add(*terms):
@@ -90,6 +86,78 @@
     )(at, *xs, w_in, w_out)
 
 
+def rows_kernel(core_ref, got_ref, o_ref, *, width, extra):
+    core = core_ref[0]
+    half = got_ref.shape[1]
+    for h in range(H):
+        own, other, pieces = [], [], []
+        for block in range(L):
+            v = got_ref[h * L + block]
+            own.append(v[:, :256].astype(f32))
+            other.append(v[:, 256:].astype(f32))
+        for block in range(L):
+            pieces.append(jnp.where(core == 0, own[block], other[block]))
+            pieces.append(jnp.where(core == 0, other[block], own[block]))
+        feats = width * len(pieces)
+        used = feats + extra * len(pieces)
+        row = jnp.concatenate(
+            [p[:, :width] for p in pieces]
+            + [p[:, width : width + extra] for p in pieces]
+            + [jnp.zeros((half, o_ref.shape[1] - used), f32)],
+            1,
+        ).astype(bf16)
+        for copy in range(o_ref.shape[0] // (H * half)):
+            at = (copy * H + h) * half
+            o_ref[at : at + half, :] = row
+
+
+def assemble(core, got, width, extra, full):
+    return pl.pallas_call(
+        functools.partial(rows_kernel, width=width, extra=extra),
+        out_shape=jax.ShapeDtypeStruct((4 * H * got.shape[1], full), bf16),
+        in_specs=[
+            pl.BlockSpec(memory_space=pltpu.SMEM),
+            pl.BlockSpec(memory_space=pltpu.VMEM),
+        ],
+        out_specs=pl.BlockSpec(memory_space=pltpu.VMEM),
+        compiler_params=pltpu.CompilerParams(vmem_limit_bytes=32 * 1024 * 1024),
+        cost_estimate=pl.CostEstimate(flops=0, bytes_accessed=3_000_000, transcendentals=0),
+    )(core.reshape(1), got)
+
+
+def shared_kernel(x_ref, s_ref, o_ref, *, depth):
+    count = s_ref.shape[0]
+    gate = jnp.zeros((x_ref.shape[0], 128), f32)
+    up = gate
+    for e in range(count):
+        x = x_ref[:, e * depth : e * depth + 128]
+        gate += jnp.dot(x, s_ref[e, :128, :], preferred_element_type=f32)
+        up += jnp.dot(x, s_ref[e, 128:256, :], preferred_element_type=f32)
+    hidden = (gate / (1.0 + jnp.exp(-gate)) * up).astype(bf16)
+    outs = []
+    for e in range(count):
+        out = lax.dot_general(
+            hidden, s_ref[e, 256:384, :], (((1,), (1,)), ((), ())), preferred_element_type=f32
+        )
+        outs.append(out[:, :depth])
+    o_ref[...] = jnp.concatenate(outs, 1)
+
+
+def shared_expert(x, s, depth):
+    rows, count = x.shape[0], s.shape[0]
+    whole = pl.BlockSpec(memory_space=pltpu.VMEM)
+    return pl.pallas_call(
+        functools.partial(shared_kernel, depth=depth),
+        out_shape=jax.ShapeDtypeStruct((rows, count * depth), f32),
+        in_specs=[whole] * 2,
+        out_specs=whole,
+        compiler_params=pltpu.CompilerParams(vmem_limit_bytes=32 * 1024 * 1024),
+        cost_estimate=pl.CostEstimate(
+            flops=6 * rows * count * 128 * 128, bytes_accessed=6_000_000, transcendentals=rows * 128
+        ),
+    )(x, s)
+
+
 def local(
     tokens,
     gate_codes,
@@ -104,6 +172,7 @@
     expert = lax.axis_index(EXPERT)
     part = lax.axis_index(TENSOR)
     core = lax.axis_index("c")
+    order = lax.optimization_barrier
     toks, width = tokens.shape
     feats = width * L * C
     full = -(-feats // 128) * 128
@@ -126,17 +195,13 @@
         ],
         1,
     )
+    s = jnp.stack([shared_gate, shared_up, shared_down.T])
+    depth = s.shape[1]
+    s = jnp.pad(s, ((0, 0), (0, 128 - depth), (0, 0))).reshape(384, 128)
+    sent, s = order((sent, s))
+    s = lax.all_gather(s, EXPERT, axis=0, tiled=False)
     got = lax.all_gather(sent, Z, axis=0, tiled=False)
-    got = got.reshape(H, L, half, C, 256)
-    got = jnp.where(core == 0, got, got[:, :, :, ::-1]).transpose(0, 2, 1, 3, 4)
-    rows = jnp.concatenate(
-        [
-            got[..., :width].reshape(toks, feats),
-            got[..., width : width + 2 * per].reshape(toks, 2 * n_exp),
-            jnp.zeros((toks, full - feats - 2 * n_exp), bf16),
-        ],
-        1,
-    )
+    copies = assemble(core, got, width, 2 * per, full)
     at = (feats - (full - 128) + 2 * per * (expert // per) + expert % per).reshape(1)
 
     w_gate, w_up, w_down = routed_gate[0], routed_up[0], routed_down[0]
@@ -145,38 +210,32 @@
     w_out = jnp.concatenate([w_down, swap(w_down)], 0)
     w_out = jnp.pad(w_out, ((0, 0), (0, full - feats)))
 
-    depth = shared_gate.shape[0]
-    s = jnp.concatenate([shared_gate, shared_up, shared_down.T], 0)
-    s = jnp.pad(s, ((0, -s.shape[0] % 16), (0, 0)))
-    rows, s = lax.optimization_barrier((rows, turn(s)))
-    s = lax.all_gather(s, ("y", "c", "x"), axis=0, tiled=False)
-    s_gate, s_up, s_down = (
-        s[:, i * depth : (i + 1) * depth].reshape(feats, s.shape[2]) for i in range(3)
-    )
-    s_gate = jnp.dot(rows[:, :feats], s_gate, preferred_element_type=f32)
-    s_up = jnp.dot(rows[:, :feats], s_up, preferred_element_type=f32)
-    s_hidden = (jax.nn.silu(s_gate) * s_up).astype(bf16)
-    shared = lax.dot_general(s_hidden, s_down, (((1,), (1,)), ((), ())), preferred_element_type=f32)
-
     apply = lambda *blocks: ffn(at, blocks, w_in, w_out)
-    order = lax.optimization_barrier
-    near = spread(jnp.concatenate([rows] * 4, 0))
+    held = lax.dynamic_slice_in_dim(copies, lax.axis_index("h") * half, half, 0)
+    near, held = order((spread(copies), jnp.concatenate([held, swap(held)], 0)))
     lo, hi = near[: 2 * toks], near[2 * toks :]
     prev_lo, succ_hi = move(lo, 1, 1), move(hi, 1, -1)
-    far = move(prev_lo, 1, 1), move(succ_hi, 1, -1)
+    far_lo, far_hi, s = order((move(prev_lo, 1, 1), move(succ_hi, 1, -1), s))
     prev_lo, succ_hi = apply(prev_lo, succ_hi)
     lo, hi, prev_lo, succ_hi = order((lo, hi, prev_lo, succ_hi))
     prev_hi, succ_lo = move(hi, 1, 1), move(lo, 1, -1)
     back_p, back_s = move(prev_lo, 1, -1), move(succ_hi, 1, 1)
-    far_lo, far_hi = apply(*far)
+    far_lo, far_hi = apply(far_lo, far_hi)
 
     far_lo, far_hi, prev_hi, succ_lo = order((far_lo, far_hi, prev_hi, succ_lo))
     from_prev, from_succ = move(far_lo, 1, 1), move(far_hi, 1, -1)
     prev_hi, succ_lo = apply(prev_hi, succ_lo)
-    lo, hi, shared, prev_hi, succ_lo = order((lo, hi, shared, prev_hi, succ_lo))
+    prev_hi, succ_lo, s = order((prev_hi, succ_lo, s))
+    out = shared_expert(held, s, depth)
+    prev_hi, succ_lo = add(prev_hi, from_succ), add(succ_lo, from_prev)
+    prev_hi, succ_lo, lo, hi, out, back_p, back_s = order(
+        (prev_hi, succ_lo, lo, hi, out, back_p, back_s)
+    )
+    prev_hi, succ_lo = move(prev_hi, 1, -1), move(succ_lo, 1, 1)
     own_lo, own_hi = apply(lo, hi)
-    prev_hi = move(add(prev_hi, from_succ), 1, -1)
-    succ_lo = move(add(succ_lo, from_prev), 1, 1)
+    out = out[:half] + swap(out[half:].astype(bf16)).astype(f32)
+    here = jnp.arange(H * half, dtype=jnp.int32)[:, None] // half == lax.axis_index("h")
+    shared = jnp.where(here, jnp.concatenate([out] * H, 0), 0.0)
     total = jnp.concatenate([add(own_lo, back_p, succ_lo), add(own_hi, back_s, prev_hi)], 0)
     total = spread(total)
     total = [total[i * toks : (i + 1) * toks] for i in range(4)]

time: 250 us -> 290 us (1.16)
  waiting for transfers between devices: 24 us -> 93.3 us
  blocking collectives: 64.5 us -> 49.4 us
  local copies, waits for them, and re-layouts: 25 us -> 17 us
  other arithmetic: 18.6 us -> 13 us
  matrix products: 4.61 us -> 0 us
  Pallas kernels: 9.87 us -> 13.4 us
    all_gather x1, waiting for transfers between devices: 0.01 us -> 48 us  [local(): s = lax.all_gather(s, EXPERT, axis=0, tiled=False)]
    all_to_all x1 -> x0, blocking collectives: 18.2 us -> none  [spread(): lax.all_to_all(a, ('y', 'x', 'c'), 0, 0, axis_index_groups=groups, tiled=...]
    ppermute x12, waiting for transfers between devices: 23.2 us -> 36.9 us  [move(): return lax.ppermute(a, ('y', 'x', 'c'), pairs)]
    ppermute x1 -> x0, starting transfers between devices: 9.97 us -> none  [turn(): lax.ppermute(a, ('h', 'c'), [(h * 2 + c, c * 2 + h) for h in range(2) for...]
    reshape x8 -> x0, local copies, waits for them, and re-layouts: 9.42 us -> none  [the longest x3 6.86 us: local(): s[:, i * depth:(i + 1) * depth].reshape(feats, s.shape[2])]
    slice x4 -> x1, local copies, waits for them, and re-layouts: 6.6 us -> 0.03 us  [local(): out = out[:half] + swap(out[half:].astype(bf16)).astype(f32)]
    all_to_all x1 -> x2, waiting for transfers between devices: 0.01 us -> 6.36 us  [spread(): lax.all_to_all(a, ('y', 'x', 'c'), 0, 0, axis_index_groups=groups, tiled=...]
    ppermute x5 -> x7, starting transfers between devices: 35.1 us -> 41.5 us  [swap(): return lax.ppermute(a, 'c', [(0, 1), (1, 0)])]
  transfers between devices with their start and end apart: 20 -> 22, of which waited for: 6 -> 10; matrix products, arithmetic and copies ran while one was open for 15% -> 5% of each run, Pallas kernels for 4% -> 5%
where the time goes in v6:
time: 290 us; the launch traced here: 289 us
  waiting for transfers between devices  93.3 us (32%)
  starting transfers between devices  89 us (31%)
  blocking collectives  49.4 us (17%)
  local copies, waits for them, and re-layouts  17 us (6%)
  between operations  13.9 us (5%)
  Pallas kernels  13.4 us (5%)
  other arithmetic  13 us (4%)
    all_gather x1, waiting for transfers between devices, local(): s = lax.all_gather(s, EXPERT, axis=0, tiled=False)  48 us
    ppermute x7, starting transfers between devices, swap(): return lax.ppermute(a, 'c', [(0, 1), (1, 0)])  41.5 us
    ppermute x12, starting transfers between devices, move(): return lax.ppermute(a, ('y', 'x', 'c'), pairs)  40 us
    ppermute x12, waiting for transfers between devices, move(): return lax.ppermute(a, ('y', 'x', 'c'), pairs)  36.9 us
    all_gather x1, blocking collectives, local(): got = lax.all_gather(sent, Z, axis=0, tiled=False)  27.4 us
    all_to_all x1, blocking collectives, local(): back = lax.all_to_all(back, Z, split_axis=0, concat_axis=0, tiled=True)  22 us
    unnamed x33, local copies, waits for them, and re-layouts  10.5 us
    pallas_call x4, Pallas kernels, ffn(): pl.pallas_call(functools.partial(ffn_kernel, hid=hid, parts=parts), out_s...  10.2 us
  transfers between devices with their start and end apart: 22, of which 10 were waited for; matrix products, arithmetic and copies ran while one was open for 5% of the time, Pallas kernels for 5%

profile of v6, /device:TPU:1, one launch (start us, length us, event | category | flops | bytes accessed | tf_op | source)
XLA Modules:
  0.0 288.9 jit_solution(4437031947950265697)
XLA Ops:
  9.9 8.8 %collective-permute-start = (bf16[32,256]{1,0:T(8,128)(2,1)S(1)}, bf16[32,256]{1,0:T(8,128)(2,1)S(1)}, u32[]{:S(2)}, u32[]{:S(2)}) collective-permute-start(bf16[32,256]{1,0:T(8,128)(2,1)S(1)} %get-tuple-element.78), channel_id=1, source_target_pairs={{0,1},{1,0},{2,3},{3,2},{4,5},{5,4},{6,7},{7,6},{8,9},{9,8},{10,11... | collective-permute-start | bytes 49160 | tf_op jit(solution)/shard_map/ppermute | solution.py:30
  18.7 1.4 fusion.19
  20.2 27.4 %all-gather = bf16[512,512]{1,0:T(8,128)(2,1)S(1)} all-gather(bf16[32,512]{1,0:T(8,128)(2,1)S(1)} %pad_maximum_fusion.2), channel_id=2, replica_groups=mesh['y'=4,'h'=2,'x'=4,'l'=8,'c'=2] {'h','l'}, dimensions={0}, use_global_device_ids=true | all-gather | bytes 557056 | tf_op jit(solution)/shard_map/all_gather | solution.py:203
  47.5 1.6 shard_map.91
  49.1 3.8 %all-to-all-start = ((bf16[4,64,3712]{2,1,0:T(8,128)(2,1)}), bf16[4,64,3712]{2,1,0:T(8,128)(2,1)S(1)}, u32[]{:S(2)}, u32[]{:S(2)}) async-start(bf16[4,64,3712]{2,1,0:T(8,128)(2,1)} %bitcast.8), calls=%async_computation | async-start | bytes 3801088 | tf_op jit(solution)/shard_map/all_to_all | solution.py:36
  52.9 8.6 %collective-permute-start.8 = (bf16[128,3616]{0,1:T(8,128)(2,1)}, bf16[128,3616]{0,1:T(8,128)(2,1)}, u32[]{:S(2)}, u32[]{:S(2)}) collective-permute-start(bf16[128,3616]{0,1:T(8,128)(2,1)} %bitcast.14), channel_id=1, source_target_pairs={{0,1},{1,0},{2,3},{3,2},{4,5},{5,4},{6,7},{7,6},{8,9},{9,8},{10,11... | collective-permute-start | bytes 2777096 | tf_op jit(solution)/shard_map/ppermute | solution.py:30
  62.5 1.9 collective-permute-start.1
  64.5 2.4 collective-permute-start.6
  66.9 1.9 collective-permute-start.7
  68.8 2.2 copy.25
  71.1 2.3 copy.27
  73.4 1.1 fusion.21
  74.5 4.8 %collective-permute-start.4 = (bf16[128,3712]{1,0:T(8,128)(2,1)S(1)}, bf16[128,3712]{1,0:T(8,128)(2,1)S(1)}, u32[]{:S(2)}, u32[]{:S(2)}) collective-permute-start(bf16[128,3712]{1,0:T(8,128)(2,1)S(1)} %get-tuple-element.64.refs_1_), channel_id=1, source_target_pairs={{0,48},{1,385},{16,0},{17,401},{32,16},{33,417},{48,32},{49,433},{... | collective-permute-start | bytes 2850824 | tf_op jit(solution)/shard_map/ppermute | solution.py:26
  79.4 1.9 collective-permute-start.2
  81.5 3.6 %fusion.6.refs_2_ = bf16[3712,512]{1,0:T(8,128)(2,1)S(1)} fusion(bf16[3616,128]{1,0:T(8,128)(2,1)} %collective-permute-done.7, bf16[3616,128]{1,0:T(8,128)(2,1)} %bitcast.12, bf16[3616,128]{1,0:T(8,128)(2,1)} %collective-permute-done.6, bf16[3616,128]{1,0:T(8,128)(2,1)} %bitcast.11), kind=kLoop, calls=%fused_computation.7 | loop fusion | flops 24707072 | bytes 7503872 | tf_op jit(solution)/shard_map/concatenate | solution.py:208
  85.1 7.3 %collective-permute-done.4.refs_1_ = bf16[128,3712]{1,0:T(8,128)(2,1)S(1)} collective-permute-done((bf16[128,3712]{1,0:T(8,128)(2,1)S(1)}, bf16[128,3712]{1,0:T(8,128)(2,1)S(1)}, u32[]{:S(2)}, u32[]{:S(2)}) %collective-permute-start.4) | collective-permute-done | bytes 950304 | tf_op jit(solution)/shard_map/ppermute | solution.py:26
  92.4 5.4 %collective-permute-start.5 = (bf16[128,3712]{1,0:T(8,128)(2,1)S(1)}, bf16[128,3712]{1,0:T(8,128)(2,1)S(1)}, u32[]{:S(2)}, u32[]{:S(2)}) collective-permute-start(bf16[128,3712]{1,0:T(8,128)(2,1)S(1)} %collective-permute-done.4.refs_1_), channel_id=1, source_target_pairs={{0,48},{1,385},{16,0},{17,401},{32,16},{33,417},{48,32},{49,433},{... | collective-permute-start | bytes 2850824 | tf_op jit(solution)/shard_map/ppermute | solution.py:26
  97.8 1.9 collective-permute-start.3
  99.7 1.8 shard_map.93
  103.5 1.9 collective-permute-start.9
  105.4 4.6 %collective-permute-start.10 = (bf16[128,3712]{1,0:T(8,128)(2,1)}, bf16[128,3712]{1,0:T(8,128)(2,1)}, u32[]{:S(2)}, u32[]{:S(2)}) collective-permute-start(bf16[128,3712]{1,0:T(8,128)(2,1)} %get-tuple-element.63.refs_0_), channel_id=1, source_target_pairs={{0,48},{1,385},{16,0},{17,401},{32,16},{33,417},{48,32},{49,433},{... | collective-permute-start | bytes 2850824 | tf_op jit(solution)/shard_map/ppermute | solution.py:26
  110.0 1.3 collective-permute-done.5.refs_1_
  112.2 4.5 %collective-permute-done.3.refs_0_ = bf16[128,3712]{1,0:T(8,128)(2,1)S(1)} collective-permute-done((bf16[128,3712]{1,0:T(8,128)(2,1)S(1)}, bf16[128,3712]{1,0:T(8,128)(2,1)S(1)}, u32[]{:S(2)}, u32[]{:S(2)}) %collective-permute-start.3) | collective-permute-done | bytes 950304 | tf_op jit(solution)/shard_map/ppermute | solution.py:26
  116.7 1.0 copy-done.8
  117.7 48.0 %all-gather.4.cloned.1.call-done = bf16[12288,128]{1,0:T(8,128)(2,1)} async-done(((bf16[384,128]{1,0:T(8,128)(2,1)}), bf16[12288,128]{1,0:T(8,128)(2,1)}) %all-gather.4.cloned.1.call-update) | async-done | bytes 3145744 | tf_op jit(solution)/shard_map/all_gather | solution.py:202
  165.7 2.1 copy-done.1
  167.7 1.2 copy-done.7
  168.9 1.2 copy-done.9
  170.1 1.8 shard_map.92
  172.0 5.5 %collective-permute-start.11 = (bf16[128,3712]{1,0:T(8,128)(2,1)S(1)}, bf16[128,3712]{1,0:T(8,128)(2,1)S(1)}, u32[]{:S(2)}, u32[]{:S(2)}) collective-permute-start(bf16[128,3712]{1,0:T(8,128)(2,1)S(1)} %get-tuple-element.55), channel_id=1, source_target_pairs={{0,48},{1,385},{16,0},{17,401},{32,16},{33,417},{48,32},{49,433},{... | collective-permute-start | bytes 2850824 | tf_op jit(solution)/shard_map/ppermute | solution.py:26
  177.5 3.1 %collective-permute-start.13 = (bf16[128,3712]{1,0:T(8,128)(2,1)S(1)}, bf16[128,3712]{1,0:T(8,128)(2,1)S(1)}, u32[]{:S(2)}, u32[]{:S(2)}) collective-permute-start(bf16[128,3712]{1,0:T(8,128)(2,1)S(1)} %copy-done.13), channel_id=1, source_target_pairs={{0,48},{1,385},{16,0},{17,401},{32,16},{33,417},{48,32},{49,433},{... | collective-permute-start | bytes 2850824 | tf_op jit(solution)/shard_map/ppermute | solution.py:26
  180.6 2.2 collective-permute-start.14
  182.9 3.5 %shard_map.94 = (bf16[128,3712]{1,0:T(8,128)(2,1)S(1)}, bf16[128,3712]{1,0:T(8,128)(2,1)S(1)}) custom-call(s32[1]{0:T(128)} %bitcast.at_ref, bf16[128,3712]{1,0:T(8,128)(2,1)} %collective-permute-done.9.refs_0_, bf16[128,3712]{1,0:T(8,128)(2,1)} %collective-permute-done.10.refs_1_, bf16[3712,512]{1,0:T(8,128)(2,1)S(1)} %copy-done.2, ...), custom_call_target="tpu_custom_call" | custom-call | flops 1459617792 | bytes 9502720 | tf_op jit(solution)/shard_map/pallas_call | solution.py:75
  186.3 1.9 collective-permute-start.12
  188.3 1.6 shard_map.95
  190.2 16.7 %collective-permute-done.12 = bf16[128,3712]{1,0:T(8,128)(2,1)S(1)} collective-permute-done((bf16[128,3712]{1,0:T(8,128)(2,1)S(1)}, bf16[128,3712]{1,0:T(8,128)(2,1)S(1)}, u32[]{:S(2)}, u32[]{:S(2)}) %collective-permute-start.12) | collective-permute-done | bytes 950304 | tf_op jit(solution)/shard_map/ppermute | solution.py:26
  207.1 1.9 collective-permute-start.16
  209.0 4.8 %collective-permute-start.17 = (bf16[128,3712]{1,0:T(8,128)(2,1)S(1)}, bf16[128,3712]{1,0:T(8,128)(2,1)S(1)}, u32[]{:S(2)}, u32[]{:S(2)}) collective-permute-start(bf16[128,3712]{1,0:T(8,128)(2,1)S(1)} %add_convert_fusion.3), channel_id=1, source_target_pairs={{0,48},{1,385},{16,0},{17,401},{32,16},{33,417},{48,32},{49,433},{... | collective-permute-start | bytes 2850824 | tf_op jit(solution)/shard_map/ppermute | solution.py:26
  213.8 3.0 %shard_map.96 = (bf16[128,3712]{1,0:T(8,128)(2,1)S(1)}, bf16[128,3712]{1,0:T(8,128)(2,1)S(1)}) custom-call(s32[1]{0:T(128)} %bitcast.at_ref, bf16[128,3712]{1,0:T(8,128)(2,1)} %get-tuple-element.63.refs_0_, bf16[128,3712]{1,0:T(8,128)(2,1)S(1)} %get-tuple-element.64.refs_1_, bf16[3712,512]{1,0:T(8,128)(2,1)S(1)} %copy-done.2, ...), custom_call_target="tpu_custom_call" | custom-call | flops 1459617792 | bytes 9502720 | tf_op jit(solution)/shard_map/pallas_call | solution.py:75
  216.8 6.3 %collective-permute-done.16 = bf16[128,3712]{1,0:T(8,128)(2,1)S(1)} collective-permute-done((bf16[128,3712]{1,0:T(8,128)(2,1)S(1)}, bf16[128,3712]{1,0:T(8,128)(2,1)S(1)}, u32[]{:S(2)}, u32[]{:S(2)}) %collective-permute-start.16) | collective-permute-done | bytes 950304 | tf_op jit(solution)/shard_map/ppermute | solution.py:26
  224.6 1.4 pad_maximum_fusion
  226.0 3.7 %all-to-all-start.1 = ((bf16[4,64,3712]{2,1,0:T(8,128)(2,1)}), bf16[4,64,3712]{2,1,0:T(8,128)(2,1)S(1)}, u32[]{:S(2)}, u32[]{:S(2)}) async-start(bf16[4,64,3712]{2,1,0:T(8,128)(2,1)} %bitcast.26), calls=%async_computation.1 | async-start | bytes 3801088 | tf_op jit(solution)/shard_map/all_to_all | solution.py:36
  229.8 5.9 %collective-permute-start.15 = (bf16[32,3616]{1,0:T(8,128)(2,1)S(1)}, bf16[32,3616]{1,0:T(8,128)(2,1)}, u32[]{:S(2)}, u32[]{:S(2)}) collective-permute-start(bf16[32,3616]{1,0:T(8,128)(2,1)S(1)} %slice.62), channel_id=1, source_target_pairs={{0,1},{1,0},{2,3},{3,2},{4,5},{5,4},{6,7},{7,6},{8,9},{9,8},{10,11... | collective-permute-start | bytes 694280 | tf_op jit(solution)/shard_map/ppermute | solution.py:30
  235.8 1.2 collective-permute-done.15
  238.0 6.4 %all-to-all-done.1 = bf16[4,64,3712]{2,1,0:T(8,128)(2,1)S(1)} async-done(((bf16[4,64,3712]{2,1,0:T(8,128)(2,1)}), bf16[4,64,3712]{2,1,0:T(8,128)(2,1)S(1)}, u32[]{:S(2)}, u32[]{:S(2)}) %all-to-all-start.1) | async-done | bytes 1900576 | tf_op jit(solution)/shard_map/all_to_all | solution.py:36
  244.7 1.7 reshape.68
  246.7 22.0 %all_to_all.29 = bf16[16,64,226]{2,1,0:T(8,128)(2,1)S(1)} all-to-all(bf16[16,64,226]{2,1,0:T(8,128)(2,1)S(1)} %bitcast.29), channel_id=1, replica_groups=mesh['y'=4,'h'=2,'x'=4,'l'=8,'c'=2] {'h','l'}, dimensions={0} | all-to-all | bytes 925696 | tf_op jit(solution)/shard_map/all_to_all | solution.py:247
  268.8 11.9 %collective-permute-start.18 = (bf16[32,226]{1,0:T(8,128)(2,1)S(1)}, bf16[32,226]{1,0:T(8,128)(2,1)S(1)}, u32[]{:S(2)}, u32[]{:S(2)}) collective-permute-start(bf16[32,226]{1,0:T(8,128)(2,1)S(1)} %get-tuple-element.76), channel_id=1, source_target_pairs={{0,1},{1,0},{2,3},{3,2},{4,5},{5,4},{6,7},{7,6},{8,9},{9,8},{10,11... | collective-permute-start | bytes 43400 | tf_op jit(solution)/shard_map/ppermute | solution.py:30
  (72 shorter events, 12.6 us)
Async XLA Ops:
  6.5 159.1 %all-gather.4.cloned.1.call-start = ((), (), s32[]{:S(2)}) async-start(), calls=%async_computation.3 | async-start | bytes 3244032 | tf_op jit(solution)/shard_map/all_gather | solution.py:202
  9.9 10.2 %collective-permute-start = (bf16[32,256]{1,0:T(8,128)(2,1)S(1)}, bf16[32,256]{1,0:T(8,128)(2,1)S(1)}, u32[]{:S(2)}, u32[]{:S(2)}) collective-permute-start(bf16[32,256]{1,0:T(8,128)(2,1)S(1)} %get-tuple-element.78), channel_id=1, source_target_pairs={{0,1},{1,0},{2,3},{3,2},{4,5},{5,4},{6,7},{7,6},{8,9},{9,8},{10,11... | collective-permute-start | bytes 49160 | tf_op jit(solution)/shard_map/ppermute | solution.py:30
  49.1 24.2 %all-to-all-start = ((bf16[4,64,3712]{2,1,0:T(8,128)(2,1)}), bf16[4,64,3712]{2,1,0:T(8,128)(2,1)S(1)}, u32[]{:S(2)}, u32[]{:S(2)}) async-start(bf16[4,64,3712]{2,1,0:T(8,128)(2,1)} %bitcast.8), calls=%async_computation | async-start | bytes 3801088 | tf_op jit(solution)/shard_map/all_to_all | solution.py:36
  52.9 18.2 %collective-permute-start.8 = (bf16[128,3616]{0,1:T(8,128)(2,1)}, bf16[128,3616]{0,1:T(8,128)(2,1)}, u32[]{:S(2)}, u32[]{:S(2)}) collective-permute-start(bf16[128,3616]{0,1:T(8,128)(2,1)} %bitcast.14), channel_id=1, source_target_pairs={{0,1},{1,0},{2,3},{3,2},{4,5},{5,4},{6,7},{7,6},{8,9},{9,8},{10,11... | collective-permute-start | bytes 2777096 | tf_op jit(solution)/shard_map/ppermute | solution.py:30
  62.5 8.5 %collective-permute-start.1 = (bf16[32,3712]{1,0:T(8,128)(2,1)S(1)}, bf16[32,3712]{1,0:T(8,128)(2,1)S(1)}, u32[]{:S(2)}, u32[]{:S(2)}) collective-permute-start(bf16[32,3712]{1,0:T(8,128)(2,1)S(1)} %constant_dynamic-slice_fusion), channel_id=1, source_target_pairs={{0,1},{1,0},{2,3},{3,2},{4,5},{5,4},{6,7},{7,6},{8,9},{9,8},{10,11... | collective-permute-start | bytes 712712 | tf_op jit(solution)/shard_map/ppermute | solution.py:30
  64.5 17.0 %collective-permute-start.6 = (bf16[3616,128]{1,0:T(8,128)(2,1)}, bf16[3616,128]{1,0:T(8,128)(2,1)}, u32[]{:S(2)}, u32[]{:S(2)}) collective-permute-start(bf16[3616,128]{1,0:T(8,128)(2,1)} %bitcast.11), channel_id=1, source_target_pairs={{0,1},{1,0},{2,3},{3,2},{4,5},{5,4},{6,7},{7,6},{8,9},{9,8},{10,11... | collective-permute-start | bytes 2777096 | tf_op jit(solution)/shard_map/ppermute | solution.py:30
  66.9 14.6 %collective-permute-start.7 = (bf16[3616,128]{1,0:T(8,128)(2,1)}, bf16[3616,128]{1,0:T(8,128)(2,1)}, u32[]{:S(2)}, u32[]{:S(2)}) collective-permute-start(bf16[3616,128]{1,0:T(8,128)(2,1)} %bitcast.12), channel_id=1, source_target_pairs={{0,1},{1,0},{2,3},{3,2},{4,5},{5,4},{6,7},{7,6},{8,9},{9,8},{10,11... | collective-permute-start | bytes 2777096 | tf_op jit(solution)/shard_map/ppermute | solution.py:30
  73.4 7.9 %copy-start.14 = (bf16[1,128,3616]{2,1,0:T(8,128)(2,1)S(1)}, bf16[1,128,3616]{2,1,0:T(8,128)(2,1)}, u32[]{:S(2)}) copy-start(bf16[1,128,3616]{2,1,0:T(8,128)(2,1)} %copy.25) | copy-start | bytes 2777092
  73.4 7.9 %copy-start.15 = (bf16[128,3616]{1,0:T(8,128)(2,1)S(1)}, bf16[128,3616]{1,0:T(8,128)(2,1)}, u32[]{:S(2)}) copy-start(bf16[128,3616]{1,0:T(8,128)(2,1)} %copy.27) | copy-start | bytes 2777092
  74.5 17.8 %collective-permute-start.4 = (bf16[128,3712]{1,0:T(8,128)(2,1)S(1)}, bf16[128,3712]{1,0:T(8,128)(2,1)S(1)}, u32[]{:S(2)}, u32[]{:S(2)}) collective-permute-start(bf16[128,3712]{1,0:T(8,128)(2,1)S(1)} %get-tuple-element.64.refs_1_), channel_id=1, source_target_pairs={{0,48},{1,385},{16,0},{17,401},{32,16},{33,417},{48,32},{49,433},{... | collective-permute-start | bytes 2850824 | tf_op jit(solution)/shard_map/ppermute | solution.py:26
  79.4 18.4 %collective-permute-start.2 = (bf16[128,3712]{1,0:T(8,128)(2,1)}, bf16[128,3712]{1,0:T(8,128)(2,1)S(1)}, u32[]{:S(2)}, u32[]{:S(2)}) collective-permute-start(bf16[128,3712]{1,0:T(8,128)(2,1)} %get-tuple-element.63.refs_0_), channel_id=1, source_target_pairs={{0,16},{1,129},{16,32},{17,145},{32,48},{33,161},{48,0},{49,177},{... | collective-permute-start | bytes 2850824 | tf_op jit(solution)/shard_map/ppermute | solution.py:26
  85.1 16.5 %copy-start = (bf16[3712,512]{1,0:T(8,128)(2,1)}, bf16[3712,512]{1,0:T(8,128)(2,1)S(1)}, u32[]{:S(2)}) copy-start(bf16[3712,512]{1,0:T(8,128)(2,1)S(1)} %fusion.6.refs_2_) | copy-start | bytes 11403268
  92.4 18.9 %collective-permute-start.5 = (bf16[128,3712]{1,0:T(8,128)(2,1)S(1)}, bf16[128,3712]{1,0:T(8,128)(2,1)S(1)}, u32[]{:S(2)}, u32[]{:S(2)}) collective-permute-start(bf16[128,3712]{1,0:T(8,128)(2,1)S(1)} %collective-permute-done.4.refs_1_), channel_id=1, source_target_pairs={{0,48},{1,385},{16,0},{17,401},{32,16},{33,417},{48,32},{49,433},{... | collective-permute-start | bytes 2850824 | tf_op jit(solution)/shard_map/ppermute | solution.py:26
  97.8 18.9 %collective-permute-start.3 = (bf16[128,3712]{1,0:T(8,128)(2,1)S(1)}, bf16[128,3712]{1,0:T(8,128)(2,1)S(1)}, u32[]{:S(2)}, u32[]{:S(2)}) collective-permute-start(bf16[128,3712]{1,0:T(8,128)(2,1)S(1)} %collective-permute-done.2.refs_0_), channel_id=1, source_target_pairs={{0,16},{1,129},{16,32},{17,145},{32,48},{33,161},{48,0},{49,177},{... | collective-permute-start | bytes 2850824 | tf_op jit(solution)/shard_map/ppermute | solution.py:26
  101.6 0.9 copy-start.10
  102.5 0.9 copy-start.12
  103.5 68.5 %collective-permute-start.9 = (bf16[128,3712]{1,0:T(8,128)(2,1)S(1)}, bf16[128,3712]{1,0:T(8,128)(2,1)}, u32[]{:S(2)}, u32[]{:S(2)}) collective-permute-start(bf16[128,3712]{1,0:T(8,128)(2,1)S(1)} %get-tuple-element.64.refs_1_), channel_id=1, source_target_pairs={{0,16},{1,129},{16,32},{17,145},{32,48},{33,161},{48,0},{49,177},{... | collective-permute-start | bytes 2850824 | tf_op jit(solution)/shard_map/ppermute | solution.py:26
  105.4 66.6 %collective-permute-start.10 = (bf16[128,3712]{1,0:T(8,128)(2,1)}, bf16[128,3712]{1,0:T(8,128)(2,1)}, u32[]{:S(2)}, u32[]{:S(2)}) collective-permute-start(bf16[128,3712]{1,0:T(8,128)(2,1)} %get-tuple-element.63.refs_0_), channel_id=1, source_target_pairs={{0,48},{1,385},{16,0},{17,401},{32,16},{33,417},{48,32},{49,433},{... | collective-permute-start | bytes 2850824 | tf_op jit(solution)/shard_map/ppermute | solution.py:26
  111.3 0.9 copy-start.6
  116.7 1.0 copy-start.8
  165.7 2.1 copy-start.1
  167.7 1.2 copy-start.7
  168.9 1.2 copy-start.9
  170.1 7.4 %copy-start.13 = (bf16[128,3712]{1,0:T(8,128)(2,1)S(1)}, bf16[128,3712]{1,0:T(8,128)(2,1)}, u32[]{:S(2)}) copy-start(bf16[128,3712]{1,0:T(8,128)(2,1)} %copy-done.12) | copy-start | bytes 2850820
  170.1 10.5 %copy-start.11 = (bf16[128,3712]{1,0:T(8,128)(2,1)S(1)}, bf16[128,3712]{1,0:T(8,128)(2,1)}, u32[]{:S(2)}) copy-start(bf16[128,3712]{1,0:T(8,128)(2,1)} %copy-done.10) | copy-start | bytes 2850820
  170.1 12.7 %copy-start.2 = (bf16[3712,512]{1,0:T(8,128)(2,1)S(1)}, bf16[3712,512]{1,0:T(8,128)(2,1)}, u32[]{:S(2)}) copy-start(bf16[3712,512]{1,0:T(8,128)(2,1)} %copy-done) | copy-start | bytes 11403268
  172.0 17.9 %collective-permute-start.11 = (bf16[128,3712]{1,0:T(8,128)(2,1)S(1)}, bf16[128,3712]{1,0:T(8,128)(2,1)S(1)}, u32[]{:S(2)}, u32[]{:S(2)}) collective-permute-start(bf16[128,3712]{1,0:T(8,128)(2,1)S(1)} %get-tuple-element.55), channel_id=1, source_target_pairs={{0,48},{1,385},{16,0},{17,401},{32,16},{33,417},{48,32},{49,433},{... | collective-permute-start | bytes 2850824 | tf_op jit(solution)/shard_map/ppermute | solution.py:26
  177.5 29.5 %collective-permute-start.13 = (bf16[128,3712]{1,0:T(8,128)(2,1)S(1)}, bf16[128,3712]{1,0:T(8,128)(2,1)S(1)}, u32[]{:S(2)}, u32[]{:S(2)}) collective-permute-start(bf16[128,3712]{1,0:T(8,128)(2,1)S(1)} %copy-done.13), channel_id=1, source_target_pairs={{0,48},{1,385},{16,0},{17,401},{32,16},{33,417},{48,32},{49,433},{... | collective-permute-start | bytes 2850824 | tf_op jit(solution)/shard_map/ppermute | solution.py:26
  180.6 26.4 %collective-permute-start.14 = (bf16[128,3712]{1,0:T(8,128)(2,1)S(1)}, bf16[128,3712]{1,0:T(8,128)(2,1)S(1)}, u32[]{:S(2)}, u32[]{:S(2)}) collective-permute-start(bf16[128,3712]{1,0:T(8,128)(2,1)S(1)} %copy-done.11), channel_id=1, source_target_pairs={{0,16},{1,129},{16,32},{17,145},{32,48},{33,161},{48,0},{49,177},{... | collective-permute-start | bytes 2850824 | tf_op jit(solution)/shard_map/ppermute | solution.py:26
  182.9 5.4 %copy-start.3 = (bf16[12288,128]{1,0:T(8,128)(2,1)S(1)}, bf16[12288,128]{1,0:T(8,128)(2,1)}, u32[]{:S(2)}) copy-start(bf16[12288,128]{1,0:T(8,128)(2,1)} %all-gather.4.cloned.1.call-done) | copy-start | bytes 9437188
  186.3 20.5 %collective-permute-start.12 = (bf16[128,3712]{1,0:T(8,128)(2,1)S(1)}, bf16[128,3712]{1,0:T(8,128)(2,1)S(1)}, u32[]{:S(2)}, u32[]{:S(2)}) collective-permute-start(bf16[128,3712]{1,0:T(8,128)(2,1)S(1)} %get-tuple-element.57), channel_id=1, source_target_pairs={{0,16},{1,129},{16,32},{17,145},{32,48},{33,161},{48,0},{49,177},{... | collective-permute-start | bytes 2850824 | tf_op jit(solution)/shard_map/ppermute | solution.py:26
  189.9 17.1 %copy-start.4 = (f32[64,3616]{1,0:T(8,128)}, f32[64,3616]{1,0:T(8,128)S(1)}, u32[]{:S(2)}) copy-start(f32[64,3616]{1,0:T(8,128)S(1)} %shard_map.95) | copy-start | bytes 2777092
  207.1 16.0 %collective-permute-start.16 = (bf16[128,3712]{1,0:T(8,128)(2,1)S(1)}, bf16[128,3712]{1,0:T(8,128)(2,1)S(1)}, u32[]{:S(2)}, u32[]{:S(2)}) collective-permute-start(bf16[128,3712]{1,0:T(8,128)(2,1)S(1)} %add_convert_fusion.2), channel_id=1, source_target_pairs={{0,16},{1,129},{16,32},{17,145},{32,48},{33,161},{48,0},{49,177},{... | collective-permute-start | bytes 2850824 | tf_op jit(solution)/shard_map/ppermute | solution.py:26
  209.0 15.2 %collective-permute-start.17 = (bf16[128,3712]{1,0:T(8,128)(2,1)S(1)}, bf16[128,3712]{1,0:T(8,128)(2,1)S(1)}, u32[]{:S(2)}, u32[]{:S(2)}) collective-permute-start(bf16[128,3712]{1,0:T(8,128)(2,1)S(1)} %add_convert_fusion.3), channel_id=1, source_target_pairs={{0,48},{1,385},{16,0},{17,401},{32,16},{33,417},{48,32},{49,433},{... | collective-permute-start | bytes 2850824 | tf_op jit(solution)/shard_map/ppermute | solution.py:26
  226.0 3.7 %copy-start.5 = (f32[64,3616]{1,0:T(8,128)S(1)}, f32[64,3616]{1,0:T(8,128)}, u32[]{:S(2)}) copy-start(f32[64,3616]{1,0:T(8,128)} %copy-done.4) | copy-start | bytes 2777092
  226.0 18.3 %all-to-all-start.1 = ((bf16[4,64,3712]{2,1,0:T(8,128)(2,1)}), bf16[4,64,3712]{2,1,0:T(8,128)(2,1)S(1)}, u32[]{:S(2)}, u32[]{:S(2)}) async-start(bf16[4,64,3712]{2,1,0:T(8,128)(2,1)} %bitcast.26), calls=%async_computation.1 | async-start | bytes 3801088 | tf_op jit(solution)/shard_map/all_to_all | solution.py:36
  229.8 7.2 %collective-permute-start.15 = (bf16[32,3616]{1,0:T(8,128)(2,1)S(1)}, bf16[32,3616]{1,0:T(8,128)(2,1)}, u32[]{:S(2)}, u32[]{:S(2)}) collective-permute-start(bf16[32,3616]{1,0:T(8,128)(2,1)S(1)} %slice.62), channel_id=1, source_target_pairs={{0,1},{1,0},{2,3},{3,2},{4,5},{5,4},{6,7},{7,6},{8,9},{9,8},{10,11... | collective-permute-start | bytes 694280 | tf_op jit(solution)/shard_map/ppermute | solution.py:30
  268.8 12.7 %collective-permute-start.18 = (bf16[32,226]{1,0:T(8,128)(2,1)S(1)}, bf16[32,226]{1,0:T(8,128)(2,1)S(1)}, u32[]{:S(2)}, u32[]{:S(2)}) collective-permute-start(bf16[32,226]{1,0:T(8,128)(2,1)S(1)} %get-tuple-element.76), channel_id=1, source_target_pairs={{0,1},{1,0},{2,3},{3,2},{4,5},{5,4},{6,7},{7,6},{8,9},{9,8},{10,11... | collective-permute-start | bytes 43400 | tf_op jit(solution)/shard_map/ppermute | solution.py:30
Sparse Core Ops, SparseCore 0:
  20.3 145.3 all-gather.3

commit v7 on v6

--- a/solution.py
+++ b/solution.py
@@ -129,15 +129,16 @@
     count = s_ref.shape[0]
     gate = jnp.zeros((x_ref.shape[0], 128), f32)
     up = gate
+    at = [(e // X % H * Y + e // X // H) * X + e % X for e in range(count)]
     for e in range(count):
         x = x_ref[:, e * depth : e * depth + 128]
-        gate += jnp.dot(x, s_ref[e, :128, :], preferred_element_type=f32)
-        up += jnp.dot(x, s_ref[e, 128:256, :], preferred_element_type=f32)
+        gate += jnp.dot(x, s_ref[at[e], :128, :], preferred_element_type=f32)
+        up += jnp.dot(x, s_ref[at[e], 128:256, :], preferred_element_type=f32)
     hidden = (gate / (1.0 + jnp.exp(-gate)) * up).astype(bf16)
     outs = []
     for e in range(count):
         out = lax.dot_general(
-            hidden, s_ref[e, 256:384, :], (((1,), (1,)), ((), ())), preferred_element_type=f32
+            hidden, s_ref[at[e], 256:384, :], (((1,), (1,)), ((), ())), preferred_element_type=f32
         )
         outs.append(out[:, :depth])
     o_ref[...] = jnp.concatenate(outs, 1)
@@ -199,7 +200,7 @@
     depth = s.shape[1]
     s = jnp.pad(s, ((0, 0), (0, 128 - depth), (0, 0))).reshape(384, 128)
     sent, s = order((sent, s))
-    s = lax.all_gather(s, EXPERT, axis=0, tiled=False)
+    s = lax.all_gather(s, ("h", "y", "x"), axis=0, tiled=False)
     got = lax.all_gather(sent, Z, axis=0, tiled=False)
     copies = assemble(core, got, width, 2 * per, full)
     at = (feats - (full - 128) + 2 * per * (expert // per) + expert % per).reshape(1)
@@ -215,7 +216,7 @@
     near, held = order((spread(copies), jnp.concatenate([held, swap(held)], 0)))
     lo, hi = near[: 2 * toks], near[2 * toks :]
     prev_lo, succ_hi = move(lo, 1, 1), move(hi, 1, -1)
-    far_lo, far_hi, s = order((move(prev_lo, 1, 1), move(succ_hi, 1, -1), s))
+    far_lo, far_hi = move(prev_lo, 1, 1), move(succ_hi, 1, -1)
     prev_lo, succ_hi = apply(prev_lo, succ_hi)
     lo, hi, prev_lo, succ_hi = order((lo, hi, prev_lo, succ_hi))
     prev_hi, succ_lo = move(hi, 1, 1), move(lo, 1, -1)

time: 290 us -> 261 us (0.900)
  waiting for transfers between devices: 93.3 us -> 62.5 us
  other arithmetic: 13 us -> 18.4 us
  local copies, waits for them, and re-layouts: 17 us -> 11.7 us
  blocking collectives: 49.4 us -> 54 us
    all_gather x1, waiting for transfers between devices: 48 us -> 25 us  [local(): s = lax.all_gather(s, ('h', 'y', 'x'), axis=0, tiled=False)]
    ppermute x12, waiting for transfers between devices: 36.9 us -> 28.4 us  [move(): return lax.ppermute(a, ('y', 'x', 'c'), pairs)]
    convert_element_type x5, other arithmetic: 1.53 us -> 6.91 us  [add(): return total.astype(bf16)]
    all_to_all x1, blocking collectives: 22 us -> 26.6 us  [local(): back = lax.all_to_all(back, Z, split_axis=0, concat_axis=0, tiled=True)]
    unnamed x33 -> x27, local copies, waits for them, and re-layouts: 10.5 us -> 6.15 us
  transfers between devices with their start and end apart: 22 -> 22, of which waited for: 10 -> 9; matrix products, arithmetic and copies ran while one was open for 5% -> 6% of each run, Pallas kernels for 5% -> 5%
where the time goes in v7:
time: 261 us; the launch traced here: 260 us
  starting transfers between devices  86.4 us (33%)
  waiting for transfers between devices  62.5 us (24%)
  blocking collectives  54 us (21%)
  other arithmetic  18.4 us (7%)
  between operations  13.9 us (5%)
  Pallas kernels  13.2 us (5%)
  local copies, waits for them, and re-layouts  11.7 us (4%)
    ppermute x7, starting transfers between devices, swap(): return lax.ppermute(a, 'c', [(0, 1), (1, 0)])  40.1 us
    ppermute x12, starting transfers between devices, move(): return lax.ppermute(a, ('y', 'x', 'c'), pairs)  38.9 us
    ppermute x12, waiting for transfers between devices, move(): return lax.ppermute(a, ('y', 'x', 'c'), pairs)  28.4 us
    all_gather x1, blocking collectives, local(): got = lax.all_gather(sent, Z, axis=0, tiled=False)  27.4 us
    all_to_all x1, blocking collectives, local(): back = lax.all_to_all(back, Z, split_axis=0, concat_axis=0, tiled=True)  26.6 us
    all_gather x1, waiting for transfers between devices, local(): s = lax.all_gather(s, ('h', 'y', 'x'), axis=0, tiled=False)  25 us
    pallas_call x4, Pallas kernels, ffn(): pl.pallas_call(functools.partial(ffn_kernel, hid=hid, parts=parts), out_s...  9.94 us
    all_to_all x2, starting transfers between devices, spread(): lax.all_to_all(a, ('y', 'x', 'c'), 0, 0, axis_index_groups=groups, tiled=...  7.51 us
  transfers between devices with their start and end apart: 22, of which 9 were waited for; matrix products, arithmetic and copies ran while one was open for 6% of the time, Pallas kernels for 5%

profile of v7, /device:TPU:1, one launch (start us, length us, event | category | flops | bytes accessed | tf_op | source)
XLA Modules:
  0.0 260.1 jit_solution(2207503112355606983)
XLA Ops:
  9.9 8.8 %collective-permute-start = (bf16[32,256]{1,0:T(8,128)(2,1)S(1)}, bf16[32,256]{1,0:T(8,128)(2,1)S(1)}, u32[]{:S(2)}, u32[]{:S(2)}) collective-permute-start(bf16[32,256]{1,0:T(8,128)(2,1)S(1)} %get-tuple-element.72), channel_id=1, source_target_pairs={{0,1},{1,0},{2,3},{3,2},{4,5},{5,4},{6,7},{7,6},{8,9},{9,8},{10,11... | collective-permute-start | bytes 49160 | tf_op jit(solution)/shard_map/ppermute | solution.py:30
  18.7 1.4 fusion.19
  20.1 27.4 %all-gather = bf16[512,512]{1,0:T(8,128)(2,1)S(1)} all-gather(bf16[32,512]{1,0:T(8,128)(2,1)S(1)} %pad_maximum_fusion.2), channel_id=2, replica_groups=mesh['y'=4,'h'=2,'x'=4,'l'=8,'c'=2] {'h','l'}, dimensions={0}, use_global_device_ids=true | all-gather | bytes 557056 | tf_op jit(solution)/shard_map/all_gather | solution.py:204
  47.5 1.6 shard_map.91
  49.1 3.8 %all-to-all-start = ((bf16[4,64,3712]{2,1,0:T(8,128)(2,1)}), bf16[4,64,3712]{2,1,0:T(8,128)(2,1)S(1)}, u32[]{:S(2)}, u32[]{:S(2)}) async-start(bf16[4,64,3712]{2,1,0:T(8,128)(2,1)} %bitcast.8), calls=%async_computation | async-start | bytes 3801088 | tf_op jit(solution)/shard_map/all_to_all | solution.py:36
  52.9 8.6 %collective-permute-start.8 = (bf16[128,3616]{0,1:T(8,128)(2,1)}, bf16[128,3616]{0,1:T(8,128)(2,1)}, u32[]{:S(2)}, u32[]{:S(2)}) collective-permute-start(bf16[128,3616]{0,1:T(8,128)(2,1)} %bitcast.13), channel_id=1, source_target_pairs={{0,1},{1,0},{2,3},{3,2},{4,5},{5,4},{6,7},{7,6},{8,9},{9,8},{10,11... | collective-permute-start | bytes 2777096 | tf_op jit(solution)/shard_map/ppermute | solution.py:30
  62.5 1.9 collective-permute-start.1
  64.4 2.4 collective-permute-start.6
  66.9 1.9 collective-permute-start.7
  68.8 2.3 copy.25
  71.2 2.3 copy.27
  73.6 3.8 %collective-permute-start.2 = (bf16[128,3712]{1,0:T(8,128)(2,1)S(1)}, bf16[128,3712]{1,0:T(8,128)(2,1)S(1)}, u32[]{:S(2)}, u32[]{:S(2)}) collective-permute-start(bf16[128,3712]{1,0:T(8,128)(2,1)S(1)} %get-tuple-element.57.refs_0_), channel_id=1, source_target_pairs={{0,16},{1,129},{16,32},{17,145},{32,48},{33,161},{48,0},{49,177},{... | collective-permute-start | bytes 2850824 | tf_op jit(solution)/shard_map/ppermute | solution.py:26
  77.4 3.1 %collective-permute-start.4 = (bf16[128,3712]{1,0:T(8,128)(2,1)S(1)}, bf16[128,3712]{1,0:T(8,128)(2,1)S(1)}, u32[]{:S(2)}, u32[]{:S(2)}) collective-permute-start(bf16[128,3712]{1,0:T(8,128)(2,1)S(1)} %get-tuple-element.58.refs_1_), channel_id=1, source_target_pairs={{0,48},{1,385},{16,0},{17,401},{32,16},{33,417},{48,32},{49,433},{... | collective-permute-start | bytes 2850824 | tf_op jit(solution)/shard_map/ppermute | solution.py:26
  80.7 3.6 %fusion.6.refs_2_ = bf16[3712,512]{1,0:T(8,128)(2,1)S(1)} fusion(bf16[3616,128]{1,0:T(8,128)(2,1)} %collective-permute-done.7, bf16[3616,128]{1,0:T(8,128)(2,1)} %bitcast.11, bf16[3616,128]{1,0:T(8,128)(2,1)} %collective-permute-done.6, bf16[3616,128]{1,0:T(8,128)(2,1)} %bitcast.10), kind=kLoop, calls=%fused_computation.7 | loop fusion | flops 24707072 | bytes 7503872 | tf_op jit(solution)/shard_map/concatenate | solution.py:209
  84.3 6.8 %collective-permute-done.2.refs_0_ = bf16[128,3712]{1,0:T(8,128)(2,1)S(1)} collective-permute-done((bf16[128,3712]{1,0:T(8,128)(2,1)S(1)}, bf16[128,3712]{1,0:T(8,128)(2,1)S(1)}, u32[]{:S(2)}, u32[]{:S(2)}) %collective-permute-start.2) | collective-permute-done | bytes 950304 | tf_op jit(solution)/shard_map/ppermute | solution.py:26
  91.1 2.0 collective-permute-start.3
  93.1 1.4 collective-permute-done.4.refs_1_
  94.5 4.2 %collective-permute-start.5 = (bf16[128,3712]{1,0:T(8,128)(2,1)S(1)}, bf16[128,3712]{1,0:T(8,128)(2,1)S(1)}, u32[]{:S(2)}, u32[]{:S(2)}) collective-permute-start(bf16[128,3712]{1,0:T(8,128)(2,1)S(1)} %collective-permute-done.4.refs_1_), channel_id=1, source_target_pairs={{0,48},{1,385},{16,0},{17,401},{32,16},{33,417},{48,32},{49,433},{... | collective-permute-start | bytes 2850824 | tf_op jit(solution)/shard_map/ppermute | solution.py:26
  98.7 3.1 %shard_map.93 = (bf16[128,3712]{1,0:T(8,128)(2,1)}, bf16[128,3712]{1,0:T(8,128)(2,1)}) custom-call(s32[1]{0:T(128)} %bitcast.at_ref, bf16[128,3712]{1,0:T(8,128)(2,1)S(1)} %collective-permute-done.2.refs_0_, bf16[128,3712]{1,0:T(8,128)(2,1)S(1)} %collective-permute-done.4.refs_1_, bf16[3712,512]{1,0:T(8,128)(2,1)S(1)} %fusion.6.refs_2_, ...), custom_call_target="tpu_custom_call" | custom-call | flops 1459617792 | bytes 9502720 | tf_op jit(solution)/shard_map/pallas_call | solution.py:75
  101.8 2.3 collective-permute-start.10
  104.1 3.0 %collective-permute-start.9 = (bf16[128,3712]{1,0:T(8,128)(2,1)S(1)}, bf16[128,3712]{1,0:T(8,128)(2,1)S(1)}, u32[]{:S(2)}, u32[]{:S(2)}) collective-permute-start(bf16[128,3712]{1,0:T(8,128)(2,1)S(1)} %get-tuple-element.58.refs_1_), channel_id=1, source_target_pairs={{0,16},{1,129},{16,32},{17,145},{32,48},{33,161},{48,0},{49,177},{... | collective-permute-start | bytes 2850824 | tf_op jit(solution)/shard_map/ppermute | solution.py:26
  107.1 5.0 %collective-permute-done.5.refs_1_ = bf16[128,3712]{1,0:T(8,128)(2,1)S(1)} collective-permute-done((bf16[128,3712]{1,0:T(8,128)(2,1)S(1)}, bf16[128,3712]{1,0:T(8,128)(2,1)S(1)}, u32[]{:S(2)}, u32[]{:S(2)}) %collective-permute-start.5) | collective-permute-done | bytes 950304 | tf_op jit(solution)/shard_map/ppermute | solution.py:26
  112.2 3.1 %shard_map.92 = (bf16[128,3712]{1,0:T(8,128)(2,1)}, bf16[128,3712]{1,0:T(8,128)(2,1)}) custom-call(s32[1]{0:T(128)} %bitcast.at_ref, bf16[128,3712]{1,0:T(8,128)(2,1)S(1)} %collective-permute-done.3.refs_0_, bf16[128,3712]{1,0:T(8,128)(2,1)S(1)} %collective-permute-done.5.refs_1_, bf16[3712,512]{1,0:T(8,128)(2,1)S(1)} %fusion.6.refs_2_, ...), custom_call_target="tpu_custom_call" | custom-call | flops 1459617792 | bytes 9502720 | tf_op jit(solution)/shard_map/pallas_call | solution.py:75
  115.3 7.8 %collective-permute-done.10.refs_1_ = bf16[128,3712]{1,0:T(8,128)(2,1)S(1)} collective-permute-done((bf16[128,3712]{1,0:T(8,128)(2,1)S(1)}, bf16[128,3712]{1,0:T(8,128)(2,1)S(1)}, u32[]{:S(2)}, u32[]{:S(2)}) %collective-permute-start.10) | collective-permute-done | bytes 950304 | tf_op jit(solution)/shard_map/ppermute | solution.py:26
  123.0 3.3 %collective-permute-start.12 = (bf16[128,3712]{1,0:T(8,128)(2,1)}, bf16[128,3712]{1,0:T(8,128)(2,1)}, u32[]{:S(2)}, u32[]{:S(2)}) collective-permute-start(bf16[128,3712]{1,0:T(8,128)(2,1)} %get-tuple-element.51), channel_id=1, source_target_pairs={{0,16},{1,129},{16,32},{17,145},{32,48},{33,161},{48,0},{49,177},{... | collective-permute-start | bytes 2850824 | tf_op jit(solution)/shard_map/ppermute | solution.py:26
  126.3 4.1 %collective-permute-start.13 = (bf16[128,3712]{1,0:T(8,128)(2,1)}, bf16[128,3712]{1,0:T(8,128)(2,1)}, u32[]{:S(2)}, u32[]{:S(2)}) collective-permute-start(bf16[128,3712]{1,0:T(8,128)(2,1)} %get-tuple-element.54), channel_id=1, source_target_pairs={{0,48},{1,385},{16,0},{17,401},{32,16},{33,417},{48,32},{49,433},{... | collective-permute-start | bytes 2850824 | tf_op jit(solution)/shard_map/ppermute | solution.py:26
  130.4 1.9 collective-permute-start.14
  132.3 4.6 %collective-permute-start.11 = (bf16[128,3712]{1,0:T(8,128)(2,1)}, bf16[128,3712]{1,0:T(8,128)(2,1)}, u32[]{:S(2)}, u32[]{:S(2)}) collective-permute-start(bf16[128,3712]{1,0:T(8,128)(2,1)} %get-tuple-element.49), channel_id=1, source_target_pairs={{0,48},{1,385},{16,0},{17,401},{32,16},{33,417},{48,32},{49,433},{... | collective-permute-start | bytes 2850824 | tf_op jit(solution)/shard_map/ppermute | solution.py:26
  136.9 1.8 shard_map.94
  140.7 25.0 %all-gather.4.cloned.1.call-done = bf16[12288,128]{1,0:T(8,128)(2,1)} async-done(((bf16[384,128]{1,0:T(8,128)(2,1)}), bf16[12288,128]{1,0:T(8,128)(2,1)}) %all-gather.4.cloned.1.call-update) | async-done | bytes 3145744 | tf_op jit(solution)/shard_map/all_gather | solution.py:203
  165.7 1.9 copy-done.4
  167.6 1.6 shard_map.95
  169.3 1.8 add_convert_fusion.2
  171.1 1.7 add_convert_fusion.3
  172.8 2.8 %collective-permute-start.16 = (bf16[128,3712]{1,0:T(8,128)(2,1)S(1)}, bf16[128,3712]{1,0:T(8,128)(2,1)S(1)}, u32[]{:S(2)}, u32[]{:S(2)}) collective-permute-start(bf16[128,3712]{1,0:T(8,128)(2,1)S(1)} %add_convert_fusion.2), channel_id=1, source_target_pairs={{0,16},{1,129},{16,32},{17,145},{32,48},{33,161},{48,0},{49,177},{... | collective-permute-start | bytes 2850824 | tf_op jit(solution)/shard_map/ppermute | solution.py:26
  175.6 3.9 %collective-permute-start.17 = (bf16[128,3712]{1,0:T(8,128)(2,1)S(1)}, bf16[128,3712]{1,0:T(8,128)(2,1)S(1)}, u32[]{:S(2)}, u32[]{:S(2)}) collective-permute-start(bf16[128,3712]{1,0:T(8,128)(2,1)S(1)} %add_convert_fusion.3), channel_id=1, source_target_pairs={{0,48},{1,385},{16,0},{17,401},{32,16},{33,417},{48,32},{49,433},{... | collective-permute-start | bytes 2850824 | tf_op jit(solution)/shard_map/ppermute | solution.py:26
  179.5 1.8 shard_map.96
  181.4 7.4 %collective-permute-done.16 = bf16[128,3712]{1,0:T(8,128)(2,1)S(1)} collective-permute-done((bf16[128,3712]{1,0:T(8,128)(2,1)S(1)}, bf16[128,3712]{1,0:T(8,128)(2,1)S(1)}, u32[]{:S(2)}, u32[]{:S(2)}) %collective-permute-start.16) | collective-permute-done | bytes 950304 | tf_op jit(solution)/shard_map/ppermute | solution.py:26
  188.8 1.6 add_convert_fusion.1
  190.4 1.6 add_convert_fusion
  191.9 1.4 pad_maximum_fusion
  193.3 3.7 %all-to-all-start.1 = ((bf16[4,64,3712]{2,1,0:T(8,128)(2,1)}), bf16[4,64,3712]{2,1,0:T(8,128)(2,1)S(1)}, u32[]{:S(2)}, u32[]{:S(2)}) async-start(bf16[4,64,3712]{2,1,0:T(8,128)(2,1)} %bitcast.26), calls=%async_computation.1 | async-start | bytes 3801088 | tf_op jit(solution)/shard_map/all_to_all | solution.py:36
  197.1 5.3 %collective-permute-start.15 = (bf16[32,3616]{1,0:T(8,128)(2,1)S(1)}, bf16[32,3616]{1,0:T(8,128)(2,1)}, u32[]{:S(2)}, u32[]{:S(2)}) collective-permute-start(bf16[32,3616]{1,0:T(8,128)(2,1)S(1)} %slice.62), channel_id=1, source_target_pairs={{0,1},{1,0},{2,3},{3,2},{4,5},{5,4},{6,7},{7,6},{8,9},{9,8},{10,11... | collective-permute-start | bytes 694280 | tf_op jit(solution)/shard_map/ppermute | solution.py:30
  202.4 1.2 collective-permute-done.15
  204.6 7.0 %all-to-all-done.1 = bf16[4,64,3712]{2,1,0:T(8,128)(2,1)S(1)} async-done(((bf16[4,64,3712]{2,1,0:T(8,128)(2,1)}), bf16[4,64,3712]{2,1,0:T(8,128)(2,1)S(1)}, u32[]{:S(2)}, u32[]{:S(2)}) %all-to-all-start.1) | async-done | bytes 1900576 | tf_op jit(solution)/shard_map/all_to_all | solution.py:36
  212.0 1.7 reshape.68
  214.0 26.6 %all_to_all.29 = bf16[16,64,226]{2,1,0:T(8,128)(2,1)S(1)} all-to-all(bf16[16,64,226]{2,1,0:T(8,128)(2,1)S(1)} %bitcast.29), channel_id=1, replica_groups=mesh['y'=4,'h'=2,'x'=4,'l'=8,'c'=2] {'h','l'}, dimensions={0} | all-to-all | bytes 925696 | tf_op jit(solution)/shard_map/all_to_all | solution.py:248
  240.7 11.1 %collective-permute-start.18 = (bf16[32,226]{1,0:T(8,128)(2,1)S(1)}, bf16[32,226]{1,0:T(8,128)(2,1)S(1)}, u32[]{:S(2)}, u32[]{:S(2)}) collective-permute-start(bf16[32,226]{1,0:T(8,128)(2,1)S(1)} %get-tuple-element.70), channel_id=1, source_target_pairs={{0,1},{1,0},{2,3},{3,2},{4,5},{5,4},{6,7},{7,6},{8,9},{9,8},{10,11... | collective-permute-start | bytes 43400 | tf_op jit(solution)/shard_map/ppermute | solution.py:30
  (66 shorter events, 9.8 us)
Async XLA Ops:
  6.5 159.2 %all-gather.4.cloned.1.call-start = ((), (), s32[]{:S(2)}) async-start(), calls=%async_computation.3 | async-start | bytes 3244032 | tf_op jit(solution)/shard_map/all_gather | solution.py:203
  9.9 10.2 %collective-permute-start = (bf16[32,256]{1,0:T(8,128)(2,1)S(1)}, bf16[32,256]{1,0:T(8,128)(2,1)S(1)}, u32[]{:S(2)}, u32[]{:S(2)}) collective-permute-start(bf16[32,256]{1,0:T(8,128)(2,1)S(1)} %get-tuple-element.72), channel_id=1, source_target_pairs={{0,1},{1,0},{2,3},{3,2},{4,5},{5,4},{6,7},{7,6},{8,9},{9,8},{10,11... | collective-permute-start | bytes 49160 | tf_op jit(solution)/shard_map/ppermute | solution.py:30
  49.1 24.3 %all-to-all-start = ((bf16[4,64,3712]{2,1,0:T(8,128)(2,1)}), bf16[4,64,3712]{2,1,0:T(8,128)(2,1)S(1)}, u32[]{:S(2)}, u32[]{:S(2)}) async-start(bf16[4,64,3712]{2,1,0:T(8,128)(2,1)} %bitcast.8), calls=%async_computation | async-start | bytes 3801088 | tf_op jit(solution)/shard_map/all_to_all | solution.py:36
  52.9 18.3 %collective-permute-start.8 = (bf16[128,3616]{0,1:T(8,128)(2,1)}, bf16[128,3616]{0,1:T(8,128)(2,1)}, u32[]{:S(2)}, u32[]{:S(2)}) collective-permute-start(bf16[128,3616]{0,1:T(8,128)(2,1)} %bitcast.13), channel_id=1, source_target_pairs={{0,1},{1,0},{2,3},{3,2},{4,5},{5,4},{6,7},{7,6},{8,9},{9,8},{10,11... | collective-permute-start | bytes 2777096 | tf_op jit(solution)/shard_map/ppermute | solution.py:30
  62.5 8.6 %collective-permute-start.1 = (bf16[32,3712]{1,0:T(8,128)(2,1)S(1)}, bf16[32,3712]{1,0:T(8,128)(2,1)S(1)}, u32[]{:S(2)}, u32[]{:S(2)}) collective-permute-start(bf16[32,3712]{1,0:T(8,128)(2,1)S(1)} %constant_dynamic-slice_fusion), channel_id=1, source_target_pairs={{0,1},{1,0},{2,3},{3,2},{4,5},{5,4},{6,7},{7,6},{8,9},{9,8},{10,11... | collective-permute-start | bytes 712712 | tf_op jit(solution)/shard_map/ppermute | solution.py:30
  64.4 16.3 %collective-permute-start.6 = (bf16[3616,128]{1,0:T(8,128)(2,1)}, bf16[3616,128]{1,0:T(8,128)(2,1)}, u32[]{:S(2)}, u32[]{:S(2)}) collective-permute-start(bf16[3616,128]{1,0:T(8,128)(2,1)} %bitcast.10), channel_id=1, source_target_pairs={{0,1},{1,0},{2,3},{3,2},{4,5},{5,4},{6,7},{7,6},{8,9},{9,8},{10,11... | collective-permute-start | bytes 2777096 | tf_op jit(solution)/shard_map/ppermute | solution.py:30
  66.9 13.9 %collective-permute-start.7 = (bf16[3616,128]{1,0:T(8,128)(2,1)}, bf16[3616,128]{1,0:T(8,128)(2,1)}, u32[]{:S(2)}, u32[]{:S(2)}) collective-permute-start(bf16[3616,128]{1,0:T(8,128)(2,1)} %bitcast.11), channel_id=1, source_target_pairs={{0,1},{1,0},{2,3},{3,2},{4,5},{5,4},{6,7},{7,6},{8,9},{9,8},{10,11... | collective-permute-start | bytes 2777096 | tf_op jit(solution)/shard_map/ppermute | solution.py:30
  73.5 7.1 %copy-start.11 = (bf16[1,128,3616]{2,1,0:T(8,128)(2,1)S(1)}, bf16[1,128,3616]{2,1,0:T(8,128)(2,1)}, u32[]{:S(2)}) copy-start(bf16[1,128,3616]{2,1,0:T(8,128)(2,1)} %copy.25) | copy-start | bytes 2777092
  73.5 7.1 %copy-start.12 = (bf16[128,3616]{1,0:T(8,128)(2,1)S(1)}, bf16[128,3616]{1,0:T(8,128)(2,1)}, u32[]{:S(2)}) copy-start(bf16[128,3616]{1,0:T(8,128)(2,1)} %copy.27) | copy-start | bytes 2777092
  73.6 28.2 %copy-start.2 = (bf16[128,3712]{1,0:T(8,128)(2,1)}, bf16[128,3712]{1,0:T(8,128)(2,1)S(1)}, u32[]{:S(2)}) copy-start(bf16[128,3712]{1,0:T(8,128)(2,1)S(1)} %get-tuple-element.57.refs_0_) | copy-start | bytes 2850820
  73.6 17.5 %collective-permute-start.2 = (bf16[128,3712]{1,0:T(8,128)(2,1)S(1)}, bf16[128,3712]{1,0:T(8,128)(2,1)S(1)}, u32[]{:S(2)}, u32[]{:S(2)}) collective-permute-start(bf16[128,3712]{1,0:T(8,128)(2,1)S(1)} %get-tuple-element.57.refs_0_), channel_id=1, source_target_pairs={{0,16},{1,129},{16,32},{17,145},{32,48},{33,161},{48,0},{49,177},{... | collective-permute-start | bytes 2850824 | tf_op jit(solution)/shard_map/ppermute | solution.py:26
  77.4 17.1 %collective-permute-start.4 = (bf16[128,3712]{1,0:T(8,128)(2,1)S(1)}, bf16[128,3712]{1,0:T(8,128)(2,1)S(1)}, u32[]{:S(2)}, u32[]{:S(2)}) collective-permute-start(bf16[128,3712]{1,0:T(8,128)(2,1)S(1)} %get-tuple-element.58.refs_1_), channel_id=1, source_target_pairs={{0,48},{1,385},{16,0},{17,401},{32,16},{33,417},{48,32},{49,433},{... | collective-permute-start | bytes 2850824 | tf_op jit(solution)/shard_map/ppermute | solution.py:26
  84.3 52.6 %copy-start = (bf16[3712,512]{1,0:T(8,128)(2,1)}, bf16[3712,512]{1,0:T(8,128)(2,1)S(1)}, u32[]{:S(2)}) copy-start(bf16[3712,512]{1,0:T(8,128)(2,1)S(1)} %fusion.6.refs_2_) | copy-start | bytes 11403268
  91.1 16.0 %collective-permute-start.3 = (bf16[128,3712]{1,0:T(8,128)(2,1)S(1)}, bf16[128,3712]{1,0:T(8,128)(2,1)S(1)}, u32[]{:S(2)}, u32[]{:S(2)}) collective-permute-start(bf16[128,3712]{1,0:T(8,128)(2,1)S(1)} %collective-permute-done.2.refs_0_), channel_id=1, source_target_pairs={{0,16},{1,129},{16,32},{17,145},{32,48},{33,161},{48,0},{49,177},{... | collective-permute-start | bytes 2850824 | tf_op jit(solution)/shard_map/ppermute | solution.py:26
  94.5 17.7 %collective-permute-start.5 = (bf16[128,3712]{1,0:T(8,128)(2,1)S(1)}, bf16[128,3712]{1,0:T(8,128)(2,1)S(1)}, u32[]{:S(2)}, u32[]{:S(2)}) collective-permute-start(bf16[128,3712]{1,0:T(8,128)(2,1)S(1)} %collective-permute-done.4.refs_1_), channel_id=1, source_target_pairs={{0,48},{1,385},{16,0},{17,401},{32,16},{33,417},{48,32},{49,433},{... | collective-permute-start | bytes 2850824 | tf_op jit(solution)/shard_map/ppermute | solution.py:26
  101.8 21.2 %collective-permute-start.10 = (bf16[128,3712]{1,0:T(8,128)(2,1)S(1)}, bf16[128,3712]{1,0:T(8,128)(2,1)S(1)}, u32[]{:S(2)}, u32[]{:S(2)}) collective-permute-start(bf16[128,3712]{1,0:T(8,128)(2,1)S(1)} %get-tuple-element.57.refs_0_), channel_id=1, source_target_pairs={{0,48},{1,385},{16,0},{17,401},{32,16},{33,417},{48,32},{49,433},{... | collective-permute-start | bytes 2850824 | tf_op jit(solution)/shard_map/ppermute | solution.py:26
  104.1 18.9 %collective-permute-start.9 = (bf16[128,3712]{1,0:T(8,128)(2,1)S(1)}, bf16[128,3712]{1,0:T(8,128)(2,1)S(1)}, u32[]{:S(2)}, u32[]{:S(2)}) collective-permute-start(bf16[128,3712]{1,0:T(8,128)(2,1)S(1)} %get-tuple-element.58.refs_1_), channel_id=1, source_target_pairs={{0,16},{1,129},{16,32},{17,145},{32,48},{33,161},{48,0},{49,177},{... | collective-permute-start | bytes 2850824 | tf_op jit(solution)/shard_map/ppermute | solution.py:26
  123.0 46.2 %collective-permute-start.12 = (bf16[128,3712]{1,0:T(8,128)(2,1)}, bf16[128,3712]{1,0:T(8,128)(2,1)}, u32[]{:S(2)}, u32[]{:S(2)}) collective-permute-start(bf16[128,3712]{1,0:T(8,128)(2,1)} %get-tuple-element.51), channel_id=1, source_target_pairs={{0,16},{1,129},{16,32},{17,145},{32,48},{33,161},{48,0},{49,177},{... | collective-permute-start | bytes 2850824 | tf_op jit(solution)/shard_map/ppermute | solution.py:26
  126.3 46.4 %collective-permute-start.13 = (bf16[128,3712]{1,0:T(8,128)(2,1)}, bf16[128,3712]{1,0:T(8,128)(2,1)}, u32[]{:S(2)}, u32[]{:S(2)}) collective-permute-start(bf16[128,3712]{1,0:T(8,128)(2,1)} %get-tuple-element.54), channel_id=1, source_target_pairs={{0,48},{1,385},{16,0},{17,401},{32,16},{33,417},{48,32},{49,433},{... | collective-permute-start | bytes 2850824 | tf_op jit(solution)/shard_map/ppermute | solution.py:26
  130.4 42.4 %collective-permute-start.14 = (bf16[128,3712]{1,0:T(8,128)(2,1)}, bf16[128,3712]{1,0:T(8,128)(2,1)}, u32[]{:S(2)}, u32[]{:S(2)}) collective-permute-start(bf16[128,3712]{1,0:T(8,128)(2,1)} %get-tuple-element.55), channel_id=1, source_target_pairs={{0,16},{1,129},{16,32},{17,145},{32,48},{33,161},{48,0},{49,177},{... | collective-permute-start | bytes 2850824 | tf_op jit(solution)/shard_map/ppermute | solution.py:26
  132.3 38.7 %collective-permute-start.11 = (bf16[128,3712]{1,0:T(8,128)(2,1)}, bf16[128,3712]{1,0:T(8,128)(2,1)}, u32[]{:S(2)}, u32[]{:S(2)}) collective-permute-start(bf16[128,3712]{1,0:T(8,128)(2,1)} %get-tuple-element.49), channel_id=1, source_target_pairs={{0,48},{1,385},{16,0},{17,401},{32,16},{33,417},{48,32},{49,433},{... | collective-permute-start | bytes 2850824 | tf_op jit(solution)/shard_map/ppermute | solution.py:26
  138.8 1.0 copy-start.7
  139.7 0.9 copy-start.9
  165.7 1.9 copy-start.4
  167.6 1.7 copy-start.10
  169.2 3.5 %copy-start.5 = (f32[64,3616]{1,0:T(8,128)}, f32[64,3616]{1,0:T(8,128)S(1)}, u32[]{:S(2)}) copy-start(f32[64,3616]{1,0:T(8,128)S(1)} %shard_map.95) | copy-start | bytes 2777092
  169.2 1.8 copy-start.8
  169.3 10.2 %copy-start.1 = (bf16[3712,512]{1,0:T(8,128)(2,1)S(1)}, bf16[3712,512]{1,0:T(8,128)(2,1)}, u32[]{:S(2)}) copy-start(bf16[3712,512]{1,0:T(8,128)(2,1)} %copy-done) | copy-start | bytes 11403268
  171.1 8.4 %copy-start.3 = (bf16[128,3712]{1,0:T(8,128)(2,1)S(1)}, bf16[128,3712]{1,0:T(8,128)(2,1)}, u32[]{:S(2)}) copy-start(bf16[128,3712]{1,0:T(8,128)(2,1)} %copy-done.2) | copy-start | bytes 2850820
  172.8 16.0 %collective-permute-start.16 = (bf16[128,3712]{1,0:T(8,128)(2,1)S(1)}, bf16[128,3712]{1,0:T(8,128)(2,1)S(1)}, u32[]{:S(2)}, u32[]{:S(2)}) collective-permute-start(bf16[128,3712]{1,0:T(8,128)(2,1)S(1)} %add_convert_fusion.2), channel_id=1, source_target_pairs={{0,16},{1,129},{16,32},{17,145},{32,48},{33,161},{48,0},{49,177},{... | collective-permute-start | bytes 2850824 | tf_op jit(solution)/shard_map/ppermute | solution.py:26
  175.6 14.8 %collective-permute-start.17 = (bf16[128,3712]{1,0:T(8,128)(2,1)S(1)}, bf16[128,3712]{1,0:T(8,128)(2,1)S(1)}, u32[]{:S(2)}, u32[]{:S(2)}) collective-permute-start(bf16[128,3712]{1,0:T(8,128)(2,1)S(1)} %add_convert_fusion.3), channel_id=1, source_target_pairs={{0,48},{1,385},{16,0},{17,401},{32,16},{33,417},{48,32},{49,433},{... | collective-permute-start | bytes 2850824 | tf_op jit(solution)/shard_map/ppermute | solution.py:26
  193.3 3.7 %copy-start.6 = (f32[64,3616]{1,0:T(8,128)S(1)}, f32[64,3616]{1,0:T(8,128)}, u32[]{:S(2)}) copy-start(f32[64,3616]{1,0:T(8,128)} %copy-done.5) | copy-start | bytes 2777092
  193.3 18.3 %all-to-all-start.1 = ((bf16[4,64,3712]{2,1,0:T(8,128)(2,1)}), bf16[4,64,3712]{2,1,0:T(8,128)(2,1)S(1)}, u32[]{:S(2)}, u32[]{:S(2)}) async-start(bf16[4,64,3712]{2,1,0:T(8,128)(2,1)} %bitcast.26), calls=%async_computation.1 | async-start | bytes 3801088 | tf_op jit(solution)/shard_map/all_to_all | solution.py:36
  197.1 6.6 %collective-permute-start.15 = (bf16[32,3616]{1,0:T(8,128)(2,1)S(1)}, bf16[32,3616]{1,0:T(8,128)(2,1)}, u32[]{:S(2)}, u32[]{:S(2)}) collective-permute-start(bf16[32,3616]{1,0:T(8,128)(2,1)S(1)} %slice.62), channel_id=1, source_target_pairs={{0,1},{1,0},{2,3},{3,2},{4,5},{5,4},{6,7},{7,6},{8,9},{9,8},{10,11... | collective-permute-start | bytes 694280 | tf_op jit(solution)/shard_map/ppermute | solution.py:30
  240.7 11.9 %collective-permute-start.18 = (bf16[32,226]{1,0:T(8,128)(2,1)S(1)}, bf16[32,226]{1,0:T(8,128)(2,1)S(1)}, u32[]{:S(2)}, u32[]{:S(2)}) collective-permute-start(bf16[32,226]{1,0:T(8,128)(2,1)S(1)} %get-tuple-element.70), channel_id=1, source_target_pairs={{0,1},{1,0},{2,3},{3,2},{4,5},{5,4},{6,7},{7,6},{8,9},{9,8},{10,11... | collective-permute-start | bytes 43400 | tf_op jit(solution)/shard_map/ppermute | solution.py:30
Sparse Core Ops, SparseCore 0:
  20.3 145.4 all-gather.3

commit v8 on v6

--- a/solution.py
+++ b/solution.py
@@ -36,6 +36,10 @@
     return lax.all_to_all(
         a, ("y", "x", "c"), 0, 0, axis_index_groups=groups, tiled=True
     )
+
+
+def turn(a):
+    return lax.ppermute(a, ("h", "c"), [(h * 2 + c, c * 2 + h) for h in range(2) for c in range(2)])
 
 
 def add(*terms):
@@ -198,9 +202,9 @@
     s = jnp.stack([shared_gate, shared_up, shared_down.T])
     depth = s.shape[1]
     s = jnp.pad(s, ((0, 0), (0, 128 - depth), (0, 0))).reshape(384, 128)
-    sent, s = order((sent, s))
-    s = lax.all_gather(s, EXPERT, axis=0, tiled=False)
     got = lax.all_gather(sent, Z, axis=0, tiled=False)
+    got, s = order((got, s))
+    s = turn(s)
     copies = assemble(core, got, width, 2 * per, full)
     at = (feats - (full - 128) + 2 * per * (expert // per) + expert % per).reshape(1)
 
@@ -211,11 +215,11 @@
     w_out = jnp.pad(w_out, ((0, 0), (0, full - feats)))
 
     apply = lambda *blocks: ffn(at, blocks, w_in, w_out)
-    held = lax.dynamic_slice_in_dim(copies, lax.axis_index("h") * half, half, 0)
-    near, held = order((spread(copies), jnp.concatenate([held, swap(held)], 0)))
+    near, s = order((spread(copies), s))
+    s = lax.all_gather(s, ("y", "c", "x"), axis=0, tiled=False)
     lo, hi = near[: 2 * toks], near[2 * toks :]
     prev_lo, succ_hi = move(lo, 1, 1), move(hi, 1, -1)
-    far_lo, far_hi, s = order((move(prev_lo, 1, 1), move(succ_hi, 1, -1), s))
+    far_lo, far_hi = move(prev_lo, 1, 1), move(succ_hi, 1, -1)
     prev_lo, succ_hi = apply(prev_lo, succ_hi)
     lo, hi, prev_lo, succ_hi = order((lo, hi, prev_lo, succ_hi))
     prev_hi, succ_lo = move(hi, 1, 1), move(lo, 1, -1)
@@ -226,20 +230,17 @@
     from_prev, from_succ = move(far_lo, 1, 1), move(far_hi, 1, -1)
     prev_hi, succ_lo = apply(prev_hi, succ_lo)
     prev_hi, succ_lo, s = order((prev_hi, succ_lo, s))
-    out = shared_expert(held, s, depth)
+    out = shared_expert(copies[:toks], s, depth)
     prev_hi, succ_lo = add(prev_hi, from_succ), add(succ_lo, from_prev)
     prev_hi, succ_lo, lo, hi, out, back_p, back_s = order(
         (prev_hi, succ_lo, lo, hi, out, back_p, back_s)
     )
     prev_hi, succ_lo = move(prev_hi, 1, -1), move(succ_lo, 1, 1)
     own_lo, own_hi = apply(lo, hi)
-    out = out[:half] + swap(out[half:].astype(bf16)).astype(f32)
-    here = jnp.arange(H * half, dtype=jnp.int32)[:, None] // half == lax.axis_index("h")
-    shared = jnp.where(here, jnp.concatenate([out] * H, 0), 0.0)
     total = jnp.concatenate([add(own_lo, back_p, succ_lo), add(own_hi, back_s, prev_hi)], 0)
     total = spread(total)
     total = [total[i * toks : (i + 1) * toks] for i in range(4)]
-    total = add(shared, *[t[:, :feats] for t in total])
+    total = add(out, *[t[:, :feats] for t in total])
 
     back = total.reshape(H, half, L, C, width).transpose(0, 2, 3, 1, 4)
     back = jnp.where(core == 0, back, back[:, :, ::-1])

time: 290 us -> 261 us (0.900)
  waiting for transfers between devices: 93.3 us -> 60.8 us
  local copies, waits for them, and re-layouts: 17 us -> 11.7 us
  blocking collectives: 49.4 us -> 53.4 us
  other arithmetic: 13 us -> 16.1 us
    all_gather x1, waiting for transfers between devices: 48 us -> 0.01 us  [local(): s = lax.all_gather(s, ('y', 'c', 'x'), axis=0, tiled=False)]
    ppermute x0 -> x1, starting transfers between devices: none -> 14.9 us  [turn(): lax.ppermute(a, ('h', 'c'), [(h * 2 + c, c * 2 + h) for h in range(2) for...]
    ppermute x7 -> x5, starting transfers between devices: 41.5 us -> 32.6 us  [swap(): return lax.ppermute(a, 'c', [(0, 1), (1, 0)])]
    all_to_all x2, waiting for transfers between devices: 6.36 us -> 14.3 us  [spread(): lax.all_to_all(a, ('y', 'x', 'c'), 0, 0, axis_index_groups=groups, tiled=...]
    ppermute x12, waiting for transfers between devices: 36.9 us -> 43.4 us  [move(): return lax.ppermute(a, ('y', 'x', 'c'), pairs)]
    all_to_all x1, blocking collectives: 22 us -> 27.3 us  [local(): back = lax.all_to_all(back, Z, split_axis=0, concat_axis=0, tiled=True)]
    ppermute x12, starting transfers between devices: 40 us -> 35 us  [move(): return lax.ppermute(a, ('y', 'x', 'c'), pairs)]
    convert_element_type x5, other arithmetic: 1.53 us -> 6.3 us  [add(): return total.astype(bf16)]
  transfers between devices with their start and end apart: 22 -> 21, of which waited for: 10 -> 8; matrix products, arithmetic and copies ran while one was open for 5% -> 5% of each run, Pallas kernels for 5% -> 4%
where the time goes in v8:
time: 261 us; the launch traced here: 259 us
  starting transfers between devices  90.1 us (35%)
  waiting for transfers between devices  60.8 us (23%)
  blocking collectives  53.4 us (20%)
  other arithmetic  16.1 us (6%)
  between operations  13.9 us (5%)
  Pallas kernels  13.1 us (5%)
  local copies, waits for them, and re-layouts  11.7 us (4%)
    ppermute x12, waiting for transfers between devices, move(): return lax.ppermute(a, ('y', 'x', 'c'), pairs)  43.4 us
    ppermute x12, starting transfers between devices, move(): return lax.ppermute(a, ('y', 'x', 'c'), pairs)  35 us
    ppermute x5, starting transfers between devices, swap(): return lax.ppermute(a, 'c', [(0, 1), (1, 0)])  32.6 us
    all_to_all x1, blocking collectives, local(): back = lax.all_to_all(back, Z, split_axis=0, concat_axis=0, tiled=True)  27.3 us
    all_gather x1, blocking collectives, local(): got = lax.all_gather(sent, Z, axis=0, tiled=False)  26.1 us
    ppermute x1, starting transfers between devices, turn(): lax.ppermute(a, ('h', 'c'), [(h * 2 + c, c * 2 + h) for h in range(2) for...  14.9 us
    all_to_all x2, waiting for transfers between devices, spread(): lax.all_to_all(a, ('y', 'x', 'c'), 0, 0, axis_index_groups=groups, tiled=...  14.3 us
    pallas_call x4, Pallas kernels, ffn(): pl.pallas_call(functools.partial(ffn_kernel, hid=hid, parts=parts), out_s...  9.88 us
  transfers between devices with their start and end apart: 21, of which 8 were waited for; matrix products, arithmetic and copies ran while one was open for 5% of the time, Pallas kernels for 4%

profile of v8, /device:TPU:1, one launch (start us, length us, event | category | flops | bytes accessed | tf_op | source)
XLA Modules:
  0.0 259.2 jit_solution(17688293757509669144)
XLA Ops:
  9.9 8.8 %collective-permute-start = (bf16[32,256]{1,0:T(8,128)(2,1)S(1)}, bf16[32,256]{1,0:T(8,128)(2,1)S(1)}, u32[]{:S(2)}, u32[]{:S(2)}) collective-permute-start(bf16[32,256]{1,0:T(8,128)(2,1)S(1)} %get-tuple-element.72), channel_id=1, source_target_pairs={{0,1},{1,0},{2,3},{3,2},{4,5},{5,4},{6,7},{7,6},{8,9},{9,8},{10,11... | collective-permute-start | bytes 49160 | tf_op jit(solution)/shard_map/ppermute | solution.py:30
  19.5 26.1 %all-gather = bf16[512,512]{1,0:T(8,128)(2,1)S(1)} all-gather(bf16[32,512]{1,0:T(8,128)(2,1)S(1)} %pad_maximum_fusion.1), channel_id=2, replica_groups=mesh['y'=4,'h'=2,'x'=4,'l'=8,'c'=2] {'h','l'}, dimensions={0}, use_global_device_ids=true | all-gather | bytes 557056 | tf_op jit(solution)/shard_map/all_gather | solution.py:205
  45.6 1.7 shard_map.91
  47.3 4.0 %all-to-all-start = ((bf16[4,64,3712]{2,1,0:T(8,128)(2,1)}), bf16[4,64,3712]{2,1,0:T(8,128)(2,1)S(1)}, u32[]{:S(2)}, u32[]{:S(2)}) async-start(bf16[4,64,3712]{2,1,0:T(8,128)(2,1)} %bitcast.8), calls=%async_computation | async-start | bytes 3801088 | tf_op jit(solution)/shard_map/all_to_all | solution.py:36
  51.3 14.9 %collective-permute-start.1 = (bf16[384,128]{1,0:T(8,128)(2,1)S(1)}, bf16[384,128]{1,0:T(8,128)(2,1)S(1)}, u32[]{:S(2)}, u32[]{:S(2)}) collective-permute-start(bf16[384,128]{1,0:T(8,128)(2,1)S(1)} %bitcast.30), channel_id=1, source_target_pairs={{0,0},{1,64},{64,1},{65,65},{2,2},{3,66},{66,3},{67,67},{4,4},{5,6... | collective-permute-start | bytes 294920 | tf_op jit(solution)/shard_map/ppermute | solution.py:42
  66.1 2.3 collective-permute-done.1
  69.1 7.1 %collective-permute-start.8 = (bf16[128,3616]{0,1:T(8,128)(2,1)}, bf16[128,3616]{0,1:T(8,128)(2,1)}, u32[]{:S(2)}, u32[]{:S(2)}) collective-permute-start(bf16[128,3616]{0,1:T(8,128)(2,1)} %bitcast.13), channel_id=1, source_target_pairs={{0,1},{1,0},{2,3},{3,2},{4,5},{5,4},{6,7},{7,6},{8,9},{9,8},{10,11... | collective-permute-start | bytes 2777096 | tf_op jit(solution)/shard_map/ppermute | solution.py:30
  76.2 1.9 collective-permute-start.6
  78.1 2.4 collective-permute-start.7
  80.6 1.6 copy.25
  82.2 2.3 copy.27
  84.6 2.9 %collective-permute-start.4 = (bf16[128,3712]{1,0:T(8,128)(2,1)S(1)}, bf16[128,3712]{1,0:T(8,128)(2,1)S(1)}, u32[]{:S(2)}, u32[]{:S(2)}) collective-permute-start(bf16[128,3712]{1,0:T(8,128)(2,1)S(1)} %get-tuple-element.58.refs_1_), channel_id=1, source_target_pairs={{0,48},{1,385},{16,0},{17,401},{32,16},{33,417},{48,32},{49,433},{... | collective-permute-start | bytes 2850824 | tf_op jit(solution)/shard_map/ppermute | solution.py:26
  87.5 2.5 collective-permute-start.2
  90.2 3.6 %fusion.6.refs_2_ = bf16[3712,512]{1,0:T(8,128)(2,1)S(1)} fusion(bf16[3616,128]{1,0:T(8,128)(2,1)} %collective-permute-done.7, bf16[3616,128]{1,0:T(8,128)(2,1)} %bitcast.11, bf16[3616,128]{1,0:T(8,128)(2,1)} %collective-permute-done.6, bf16[3616,128]{1,0:T(8,128)(2,1)} %bitcast.10), kind=kLoop, calls=%fused_computation.7 | loop fusion | flops 24707072 | bytes 7503872 | tf_op jit(solution)/shard_map/concatenate | solution.py:212
  93.8 7.3 %collective-permute-done.4.refs_1_ = bf16[128,3712]{1,0:T(8,128)(2,1)S(1)} collective-permute-done((bf16[128,3712]{1,0:T(8,128)(2,1)S(1)}, bf16[128,3712]{1,0:T(8,128)(2,1)S(1)}, u32[]{:S(2)}, u32[]{:S(2)}) %collective-permute-start.4) | collective-permute-done | bytes 950304 | tf_op jit(solution)/shard_map/ppermute | solution.py:26
  101.1 4.0 %collective-permute-start.5 = (bf16[128,3712]{1,0:T(8,128)(2,1)S(1)}, bf16[128,3712]{1,0:T(8,128)(2,1)S(1)}, u32[]{:S(2)}, u32[]{:S(2)}) collective-permute-start(bf16[128,3712]{1,0:T(8,128)(2,1)S(1)} %collective-permute-done.4.refs_1_), channel_id=1, source_target_pairs={{0,48},{1,385},{16,0},{17,401},{32,16},{33,417},{48,32},{49,433},{... | collective-permute-start | bytes 2850824 | tf_op jit(solution)/shard_map/ppermute | solution.py:26
  105.1 1.9 collective-permute-start.3
  107.0 3.1 %shard_map.93 = (bf16[128,3712]{1,0:T(8,128)(2,1)}, bf16[128,3712]{1,0:T(8,128)(2,1)}) custom-call(s32[1]{0:T(128)} %bitcast.at_ref, bf16[128,3712]{1,0:T(8,128)(2,1)S(1)} %collective-permute-done.2.refs_0_, bf16[128,3712]{1,0:T(8,128)(2,1)S(1)} %collective-permute-done.4.refs_1_, bf16[3712,512]{1,0:T(8,128)(2,1)S(1)} %fusion.6.refs_2_, ...), custom_call_target="tpu_custom_call" | custom-call | flops 1459617792 | bytes 9502720 | tf_op jit(solution)/shard_map/pallas_call | solution.py:79
  110.2 1.9 collective-permute-start.9
  112.1 4.6 %collective-permute-start.10 = (bf16[128,3712]{1,0:T(8,128)(2,1)S(1)}, bf16[128,3712]{1,0:T(8,128)(2,1)S(1)}, u32[]{:S(2)}, u32[]{:S(2)}) collective-permute-start(bf16[128,3712]{1,0:T(8,128)(2,1)S(1)} %get-tuple-element.57.refs_0_), channel_id=1, source_target_pairs={{0,48},{1,385},{16,0},{17,401},{32,16},{33,417},{48,32},{49,433},{... | collective-permute-start | bytes 2850824 | tf_op jit(solution)/shard_map/ppermute | solution.py:26
  116.7 7.1 %collective-permute-done.3.refs_0_ = bf16[128,3712]{1,0:T(8,128)(2,1)S(1)} collective-permute-done((bf16[128,3712]{1,0:T(8,128)(2,1)S(1)}, bf16[128,3712]{1,0:T(8,128)(2,1)S(1)}, u32[]{:S(2)}, u32[]{:S(2)}) %collective-permute-start.3) | collective-permute-done | bytes 950304 | tf_op jit(solution)/shard_map/ppermute | solution.py:26
  123.7 3.1 %shard_map.92 = (bf16[128,3712]{1,0:T(8,128)(2,1)}, bf16[128,3712]{1,0:T(8,128)(2,1)}) custom-call(s32[1]{0:T(128)} %bitcast.at_ref, bf16[128,3712]{1,0:T(8,128)(2,1)S(1)} %collective-permute-done.3.refs_0_, bf16[128,3712]{1,0:T(8,128)(2,1)S(1)} %collective-permute-done.5.refs_1_, bf16[3712,512]{1,0:T(8,128)(2,1)S(1)} %fusion.6.refs_2_, ...), custom_call_target="tpu_custom_call" | custom-call | flops 1459617792 | bytes 9502720 | tf_op jit(solution)/shard_map/pallas_call | solution.py:79
  126.8 10.8 %collective-permute-done.9.refs_0_ = bf16[128,3712]{1,0:T(8,128)(2,1)S(1)} collective-permute-done((bf16[128,3712]{1,0:T(8,128)(2,1)S(1)}, bf16[128,3712]{1,0:T(8,128)(2,1)S(1)}, u32[]{:S(2)}, u32[]{:S(2)}) %collective-permute-start.9) | collective-permute-done | bytes 950304 | tf_op jit(solution)/shard_map/ppermute | solution.py:26
  137.6 1.9 collective-permute-start.11
  139.5 1.1 slice.44.x_ref
  140.6 1.9 collective-permute-start.13
  142.5 3.4 %collective-permute-start.14 = (bf16[128,3712]{1,0:T(8,128)(2,1)}, bf16[128,3712]{1,0:T(8,128)(2,1)}, u32[]{:S(2)}, u32[]{:S(2)}) collective-permute-start(bf16[128,3712]{1,0:T(8,128)(2,1)} %get-tuple-element.55), channel_id=1, source_target_pairs={{0,16},{1,129},{16,32},{17,145},{32,48},{33,161},{48,0},{49,177},{... | collective-permute-start | bytes 2850824 | tf_op jit(solution)/shard_map/ppermute | solution.py:26
  145.9 3.4 %collective-permute-start.12 = (bf16[128,3712]{1,0:T(8,128)(2,1)}, bf16[128,3712]{1,0:T(8,128)(2,1)}, u32[]{:S(2)}, u32[]{:S(2)}) collective-permute-start(bf16[128,3712]{1,0:T(8,128)(2,1)} %get-tuple-element.52), channel_id=1, source_target_pairs={{0,16},{1,129},{16,32},{17,145},{32,48},{33,161},{48,0},{49,177},{... | collective-permute-start | bytes 2850824 | tf_op jit(solution)/shard_map/ppermute | solution.py:26
  149.3 1.8 shard_map.94
  151.1 0.9 copy-done.7
  152.1 1.0 copy-done.9
  153.1 1.9 copy-done.6
  155.0 1.6 shard_map.95
  156.6 1.6 add_convert_fusion.3
  158.2 10.8 %collective-permute-done.12 = bf16[128,3712]{1,0:T(8,128)(2,1)} collective-permute-done((bf16[128,3712]{1,0:T(8,128)(2,1)}, bf16[128,3712]{1,0:T(8,128)(2,1)}, u32[]{:S(2)}, u32[]{:S(2)}) %collective-permute-start.12) | collective-permute-done | bytes 950304 | tf_op jit(solution)/shard_map/ppermute | solution.py:26
  169.0 1.4 add_convert_fusion.2
  170.5 2.2 collective-permute-start.15
  172.6 4.5 %collective-permute-start.16 = (bf16[128,3712]{1,0:T(8,128)(2,1)S(1)}, bf16[128,3712]{1,0:T(8,128)(2,1)S(1)}, u32[]{:S(2)}, u32[]{:S(2)}) collective-permute-start(bf16[128,3712]{1,0:T(8,128)(2,1)S(1)} %add_convert_fusion.3), channel_id=1, source_target_pairs={{0,48},{1,385},{16,0},{17,401},{32,16},{33,417},{48,32},{49,433},{... | collective-permute-start | bytes 2850824 | tf_op jit(solution)/shard_map/ppermute | solution.py:26
  177.2 1.8 shard_map.96
  179.0 7.4 %collective-permute-done.15 = bf16[128,3712]{1,0:T(8,128)(2,1)S(1)} collective-permute-done((bf16[128,3712]{1,0:T(8,128)(2,1)S(1)}, bf16[128,3712]{1,0:T(8,128)(2,1)S(1)}, u32[]{:S(2)}, u32[]{:S(2)}) %collective-permute-start.15) | collective-permute-done | bytes 950304 | tf_op jit(solution)/shard_map/ppermute | solution.py:26
  186.5 1.5 add_convert_fusion.1
  188.0 1.5 add_convert_fusion
  189.5 1.4 pad_maximum_fusion
  190.9 3.6 %all-to-all-start.1 = ((bf16[4,64,3712]{2,1,0:T(8,128)(2,1)}), bf16[4,64,3712]{2,1,0:T(8,128)(2,1)S(1)}, u32[]{:S(2)}, u32[]{:S(2)}) async-start(bf16[4,64,3712]{2,1,0:T(8,128)(2,1)} %bitcast.26), calls=%async_computation.1 | async-start | bytes 3801088 | tf_op jit(solution)/shard_map/all_to_all | solution.py:36
  194.5 14.3 %all-to-all-done.1 = bf16[4,64,3712]{2,1,0:T(8,128)(2,1)S(1)} async-done(((bf16[4,64,3712]{2,1,0:T(8,128)(2,1)}), bf16[4,64,3712]{2,1,0:T(8,128)(2,1)S(1)}, u32[]{:S(2)}, u32[]{:S(2)}) %all-to-all-start.1) | async-done | bytes 1900576 | tf_op jit(solution)/shard_map/all_to_all | solution.py:36
  209.1 1.7 reshape.29
  211.1 27.3 %all_to_all.29 = bf16[16,64,226]{2,1,0:T(8,128)(2,1)S(1)} all-to-all(bf16[16,64,226]{2,1,0:T(8,128)(2,1)S(1)} %bitcast.29), channel_id=1, replica_groups=mesh['y'=4,'h'=2,'x'=4,'l'=8,'c'=2] {'h','l'}, dimensions={0} | all-to-all | bytes 925696 | tf_op jit(solution)/shard_map/all_to_all | solution.py:248
  238.4 12.4 %collective-permute-start.17 = (bf16[32,226]{1,0:T(8,128)(2,1)S(1)}, bf16[32,226]{1,0:T(8,128)(2,1)S(1)}, u32[]{:S(2)}, u32[]{:S(2)}) collective-permute-start(bf16[32,226]{1,0:T(8,128)(2,1)S(1)} %get-tuple-element.70), channel_id=1, source_target_pairs={{0,1},{1,0},{2,3},{3,2},{4,5},{5,4},{6,7},{7,6},{8,9},{9,8},{10,11... | collective-permute-start | bytes 43400 | tf_op jit(solution)/shard_map/ppermute | solution.py:30
  (60 shorter events, 7.3 us)
Async XLA Ops:
  9.9 9.6 %collective-permute-start = (bf16[32,256]{1,0:T(8,128)(2,1)S(1)}, bf16[32,256]{1,0:T(8,128)(2,1)S(1)}, u32[]{:S(2)}, u32[]{:S(2)}) collective-permute-start(bf16[32,256]{1,0:T(8,128)(2,1)S(1)} %get-tuple-element.72), channel_id=1, source_target_pairs={{0,1},{1,0},{2,3},{3,2},{4,5},{5,4},{6,7},{7,6},{8,9},{9,8},{10,11... | collective-permute-start | bytes 49160 | tf_op jit(solution)/shard_map/ppermute | solution.py:30
  47.3 21.2 %all-to-all-start = ((bf16[4,64,3712]{2,1,0:T(8,128)(2,1)}), bf16[4,64,3712]{2,1,0:T(8,128)(2,1)S(1)}, u32[]{:S(2)}, u32[]{:S(2)}) async-start(bf16[4,64,3712]{2,1,0:T(8,128)(2,1)} %bitcast.8), calls=%async_computation | async-start | bytes 3801088 | tf_op jit(solution)/shard_map/all_to_all | solution.py:36
  51.3 101.8 %all-gather.4.cloned.1.call-start = ((), (), s32[]{:S(2)}) async-start(), calls=%async_computation.3 | async-start | bytes 3244032 | tf_op jit(solution)/shard_map/all_gather | solution.py:219
  51.3 17.1 %collective-permute-start.1 = (bf16[384,128]{1,0:T(8,128)(2,1)S(1)}, bf16[384,128]{1,0:T(8,128)(2,1)S(1)}, u32[]{:S(2)}, u32[]{:S(2)}) collective-permute-start(bf16[384,128]{1,0:T(8,128)(2,1)S(1)} %bitcast.30), channel_id=1, source_target_pairs={{0,0},{1,64},{64,1},{65,65},{2,2},{3,66},{66,3},{67,67},{4,4},{5,6... | collective-permute-start | bytes 294920 | tf_op jit(solution)/shard_map/ppermute | solution.py:42
  68.4 0.6 copy-start.12
  69.1 13.1 %collective-permute-start.8 = (bf16[128,3616]{0,1:T(8,128)(2,1)}, bf16[128,3616]{0,1:T(8,128)(2,1)}, u32[]{:S(2)}, u32[]{:S(2)}) collective-permute-start(bf16[128,3616]{0,1:T(8,128)(2,1)} %bitcast.13), channel_id=1, source_target_pairs={{0,1},{1,0},{2,3},{3,2},{4,5},{5,4},{6,7},{7,6},{8,9},{9,8},{10,11... | collective-permute-start | bytes 2777096 | tf_op jit(solution)/shard_map/ppermute | solution.py:30
  76.2 14.0 %collective-permute-start.6 = (bf16[3616,128]{1,0:T(8,128)(2,1)}, bf16[3616,128]{1,0:T(8,128)(2,1)}, u32[]{:S(2)}, u32[]{:S(2)}) collective-permute-start(bf16[3616,128]{1,0:T(8,128)(2,1)} %bitcast.10), channel_id=1, source_target_pairs={{0,1},{1,0},{2,3},{3,2},{4,5},{5,4},{6,7},{7,6},{8,9},{9,8},{10,11... | collective-permute-start | bytes 2777096 | tf_op jit(solution)/shard_map/ppermute | solution.py:30
  78.1 12.1 %collective-permute-start.7 = (bf16[3616,128]{1,0:T(8,128)(2,1)}, bf16[3616,128]{1,0:T(8,128)(2,1)}, u32[]{:S(2)}, u32[]{:S(2)}) collective-permute-start(bf16[3616,128]{1,0:T(8,128)(2,1)} %bitcast.11), channel_id=1, source_target_pairs={{0,1},{1,0},{2,3},{3,2},{4,5},{5,4},{6,7},{7,6},{8,9},{9,8},{10,11... | collective-permute-start | bytes 2777096 | tf_op jit(solution)/shard_map/ppermute | solution.py:30
  84.5 5.6 %copy-start.11 = (bf16[128,3616]{1,0:T(8,128)(2,1)S(1)}, bf16[128,3616]{1,0:T(8,128)(2,1)}, u32[]{:S(2)}) copy-start(bf16[128,3616]{1,0:T(8,128)(2,1)} %copy.27) | copy-start | bytes 2777092
  84.6 25.6 %copy-start.2 = (bf16[128,3712]{1,0:T(8,128)(2,1)}, bf16[128,3712]{1,0:T(8,128)(2,1)S(1)}, u32[]{:S(2)}) copy-start(bf16[128,3712]{1,0:T(8,128)(2,1)S(1)} %get-tuple-element.58.refs_1_) | copy-start | bytes 2850820
  84.6 27.5 %copy-start.4 = (bf16[128,3712]{1,0:T(8,128)(2,1)}, bf16[128,3712]{1,0:T(8,128)(2,1)S(1)}, u32[]{:S(2)}) copy-start(bf16[128,3712]{1,0:T(8,128)(2,1)S(1)} %get-tuple-element.57.refs_0_) | copy-start | bytes 2850820
  84.6 16.5 %collective-permute-start.4 = (bf16[128,3712]{1,0:T(8,128)(2,1)S(1)}, bf16[128,3712]{1,0:T(8,128)(2,1)S(1)}, u32[]{:S(2)}, u32[]{:S(2)}) collective-permute-start(bf16[128,3712]{1,0:T(8,128)(2,1)S(1)} %get-tuple-element.58.refs_1_), channel_id=1, source_target_pairs={{0,48},{1,385},{16,0},{17,401},{32,16},{33,417},{48,32},{49,433},{... | collective-permute-start | bytes 2850824 | tf_op jit(solution)/shard_map/ppermute | solution.py:26
  87.5 17.6 %collective-permute-start.2 = (bf16[128,3712]{1,0:T(8,128)(2,1)S(1)}, bf16[128,3712]{1,0:T(8,128)(2,1)S(1)}, u32[]{:S(2)}, u32[]{:S(2)}) collective-permute-start(bf16[128,3712]{1,0:T(8,128)(2,1)S(1)} %get-tuple-element.57.refs_0_), channel_id=1, source_target_pairs={{0,16},{1,129},{16,32},{17,145},{32,48},{33,161},{48,0},{49,177},{... | collective-permute-start | bytes 2850824 | tf_op jit(solution)/shard_map/ppermute | solution.py:26
  93.8 55.5 %copy-start = (bf16[3712,512]{1,0:T(8,128)(2,1)}, bf16[3712,512]{1,0:T(8,128)(2,1)S(1)}, u32[]{:S(2)}) copy-start(bf16[3712,512]{1,0:T(8,128)(2,1)S(1)} %fusion.6.refs_2_) | copy-start | bytes 11403268
  101.1 15.6 %collective-permute-start.5 = (bf16[128,3712]{1,0:T(8,128)(2,1)S(1)}, bf16[128,3712]{1,0:T(8,128)(2,1)S(1)}, u32[]{:S(2)}, u32[]{:S(2)}) collective-permute-start(bf16[128,3712]{1,0:T(8,128)(2,1)S(1)} %collective-permute-done.4.refs_1_), channel_id=1, source_target_pairs={{0,48},{1,385},{16,0},{17,401},{32,16},{33,417},{48,32},{49,433},{... | collective-permute-start | bytes 2850824 | tf_op jit(solution)/shard_map/ppermute | solution.py:26
  105.1 18.6 %collective-permute-start.3 = (bf16[128,3712]{1,0:T(8,128)(2,1)S(1)}, bf16[128,3712]{1,0:T(8,128)(2,1)S(1)}, u32[]{:S(2)}, u32[]{:S(2)}) collective-permute-start(bf16[128,3712]{1,0:T(8,128)(2,1)S(1)} %collective-permute-done.2.refs_0_), channel_id=1, source_target_pairs={{0,16},{1,129},{16,32},{17,145},{32,48},{33,161},{48,0},{49,177},{... | collective-permute-start | bytes 2850824 | tf_op jit(solution)/shard_map/ppermute | solution.py:26
  110.2 27.4 %collective-permute-start.9 = (bf16[128,3712]{1,0:T(8,128)(2,1)S(1)}, bf16[128,3712]{1,0:T(8,128)(2,1)S(1)}, u32[]{:S(2)}, u32[]{:S(2)}) collective-permute-start(bf16[128,3712]{1,0:T(8,128)(2,1)S(1)} %get-tuple-element.58.refs_1_), channel_id=1, source_target_pairs={{0,16},{1,129},{16,32},{17,145},{32,48},{33,161},{48,0},{49,177},{... | collective-permute-start | bytes 2850824 | tf_op jit(solution)/shard_map/ppermute | solution.py:26
  112.1 25.5 %collective-permute-start.10 = (bf16[128,3712]{1,0:T(8,128)(2,1)S(1)}, bf16[128,3712]{1,0:T(8,128)(2,1)S(1)}, u32[]{:S(2)}, u32[]{:S(2)}) collective-permute-start(bf16[128,3712]{1,0:T(8,128)(2,1)S(1)} %get-tuple-element.57.refs_0_), channel_id=1, source_target_pairs={{0,48},{1,385},{16,0},{17,401},{32,16},{33,417},{48,32},{49,433},{... | collective-permute-start | bytes 2850824 | tf_op jit(solution)/shard_map/ppermute | solution.py:26
  137.6 19.0 %collective-permute-start.11 = (bf16[128,3712]{1,0:T(8,128)(2,1)}, bf16[128,3712]{1,0:T(8,128)(2,1)}, u32[]{:S(2)}, u32[]{:S(2)}) collective-permute-start(bf16[128,3712]{1,0:T(8,128)(2,1)} %get-tuple-element.50), channel_id=1, source_target_pairs={{0,48},{1,385},{16,0},{17,401},{32,16},{33,417},{48,32},{49,433},{... | collective-permute-start | bytes 2850824 | tf_op jit(solution)/shard_map/ppermute | solution.py:26
  140.6 29.8 %collective-permute-start.13 = (bf16[128,3712]{1,0:T(8,128)(2,1)}, bf16[128,3712]{1,0:T(8,128)(2,1)}, u32[]{:S(2)}, u32[]{:S(2)}) collective-permute-start(bf16[128,3712]{1,0:T(8,128)(2,1)} %get-tuple-element.54), channel_id=1, source_target_pairs={{0,48},{1,385},{16,0},{17,401},{32,16},{33,417},{48,32},{49,433},{... | collective-permute-start | bytes 2850824 | tf_op jit(solution)/shard_map/ppermute | solution.py:26
  142.5 27.9 %collective-permute-start.14 = (bf16[128,3712]{1,0:T(8,128)(2,1)}, bf16[128,3712]{1,0:T(8,128)(2,1)}, u32[]{:S(2)}, u32[]{:S(2)}) collective-permute-start(bf16[128,3712]{1,0:T(8,128)(2,1)} %get-tuple-element.55), channel_id=1, source_target_pairs={{0,16},{1,129},{16,32},{17,145},{32,48},{33,161},{48,0},{49,177},{... | collective-permute-start | bytes 2850824 | tf_op jit(solution)/shard_map/ppermute | solution.py:26
  145.9 23.1 %collective-permute-start.12 = (bf16[128,3712]{1,0:T(8,128)(2,1)}, bf16[128,3712]{1,0:T(8,128)(2,1)}, u32[]{:S(2)}, u32[]{:S(2)}) collective-permute-start(bf16[128,3712]{1,0:T(8,128)(2,1)} %get-tuple-element.52), channel_id=1, source_target_pairs={{0,16},{1,129},{16,32},{17,145},{32,48},{33,161},{48,0},{49,177},{... | collective-permute-start | bytes 2850824 | tf_op jit(solution)/shard_map/ppermute | solution.py:26
  151.1 0.9 copy-start.7
  152.1 1.0 copy-start.9
  153.1 1.9 copy-start.6
  155.0 1.6 copy-start.10
  155.0 14.1 %copy-start.8 = (bf16[128,3712]{1,0:T(8,128)(2,1)S(1)}, bf16[128,3712]{1,0:T(8,128)(2,1)}, u32[]{:S(2)}) copy-start(bf16[128,3712]{1,0:T(8,128)(2,1)} %copy-done.7) | copy-start | bytes 2850820
  156.6 20.6 %copy-start.1 = (bf16[3712,512]{1,0:T(8,128)(2,1)S(1)}, bf16[3712,512]{1,0:T(8,128)(2,1)}, u32[]{:S(2)}) copy-start(bf16[3712,512]{1,0:T(8,128)(2,1)} %copy-done) | copy-start | bytes 11403268
  158.2 19.0 %copy-start.3 = (bf16[128,3712]{1,0:T(8,128)(2,1)S(1)}, bf16[128,3712]{1,0:T(8,128)(2,1)}, u32[]{:S(2)}) copy-start(bf16[128,3712]{1,0:T(8,128)(2,1)} %copy-done.2) | copy-start | bytes 2850820
  158.2 19.0 %copy-start.5 = (bf16[128,3712]{1,0:T(8,128)(2,1)S(1)}, bf16[128,3712]{1,0:T(8,128)(2,1)}, u32[]{:S(2)}) copy-start(bf16[128,3712]{1,0:T(8,128)(2,1)} %copy-done.4) | copy-start | bytes 2850820
  170.5 16.0 %collective-permute-start.15 = (bf16[128,3712]{1,0:T(8,128)(2,1)S(1)}, bf16[128,3712]{1,0:T(8,128)(2,1)S(1)}, u32[]{:S(2)}, u32[]{:S(2)}) collective-permute-start(bf16[128,3712]{1,0:T(8,128)(2,1)S(1)} %add_convert_fusion.2), channel_id=1, source_target_pairs={{0,16},{1,129},{16,32},{17,145},{32,48},{33,161},{48,0},{49,177},{... | collective-permute-start | bytes 2850824 | tf_op jit(solution)/shard_map/ppermute | solution.py:26
  172.6 15.4 %collective-permute-start.16 = (bf16[128,3712]{1,0:T(8,128)(2,1)S(1)}, bf16[128,3712]{1,0:T(8,128)(2,1)S(1)}, u32[]{:S(2)}, u32[]{:S(2)}) collective-permute-start(bf16[128,3712]{1,0:T(8,128)(2,1)S(1)} %add_convert_fusion.3), channel_id=1, source_target_pairs={{0,48},{1,385},{16,0},{17,401},{32,16},{33,417},{48,32},{49,433},{... | collective-permute-start | bytes 2850824 | tf_op jit(solution)/shard_map/ppermute | solution.py:26
  190.9 17.9 %all-to-all-start.1 = ((bf16[4,64,3712]{2,1,0:T(8,128)(2,1)}), bf16[4,64,3712]{2,1,0:T(8,128)(2,1)S(1)}, u32[]{:S(2)}, u32[]{:S(2)}) async-start(bf16[4,64,3712]{2,1,0:T(8,128)(2,1)} %bitcast.26), calls=%async_computation.1 | async-start | bytes 3801088 | tf_op jit(solution)/shard_map/all_to_all | solution.py:36
  238.4 13.2 %collective-permute-start.17 = (bf16[32,226]{1,0:T(8,128)(2,1)S(1)}, bf16[32,226]{1,0:T(8,128)(2,1)S(1)}, u32[]{:S(2)}, u32[]{:S(2)}) collective-permute-start(bf16[32,226]{1,0:T(8,128)(2,1)S(1)} %get-tuple-element.70), channel_id=1, source_target_pairs={{0,1},{1,0},{2,3},{3,2},{4,5},{5,4},{6,7},{7,6},{8,9},{9,8},{10,11... | collective-permute-start | bytes 43400 | tf_op jit(solution)/shard_map/ppermute | solution.py:30
Sparse Core Ops, SparseCore 0:
  69.2 63.8 all-gather.3

commit v9 on v8

--- a/solution.py
+++ b/solution.py
@@ -203,9 +203,8 @@
     depth = s.shape[1]
     s = jnp.pad(s, ((0, 0), (0, 128 - depth), (0, 0))).reshape(384, 128)
     got = lax.all_gather(sent, Z, axis=0, tiled=False)
-    got, s = order((got, s))
-    s = turn(s)
-    copies = assemble(core, got, width, 2 * per, full)
+    copies, s = order((assemble(core, got, width, 2 * per, full), turn(s)))
+    s = lax.all_gather(s, ("y", "c", "x"), axis=0, tiled=False)
     at = (feats - (full - 128) + 2 * per * (expert // per) + expert % per).reshape(1)
 
     w_gate, w_up, w_down = routed_gate[0], routed_up[0], routed_down[0]
@@ -215,8 +214,7 @@
     w_out = jnp.pad(w_out, ((0, 0), (0, full - feats)))
 
     apply = lambda *blocks: ffn(at, blocks, w_in, w_out)
-    near, s = order((spread(copies), s))
-    s = lax.all_gather(s, ("y", "c", "x"), axis=0, tiled=False)
+    near = spread(copies)
     lo, hi = near[: 2 * toks], near[2 * toks :]
     prev_lo, succ_hi = move(lo, 1, 1), move(hi, 1, -1)
     far_lo, far_hi = move(prev_lo, 1, 1), move(succ_hi, 1, -1)

time: 261 us -> 252 us (0.966)
  blocking collectives: 53.4 us -> 47.1 us
  waiting for transfers between devices: 60.8 us -> 55.4 us
  starting transfers between devices: 90.1 us -> 93 us
    all_to_all x1, blocking collectives: 27.3 us -> 22.1 us  [local(): back = lax.all_to_all(back, Z, split_axis=0, concat_axis=0, tiled=True)]
    ppermute x1, starting transfers between devices: 14.9 us -> 9.97 us  [turn(): lax.ppermute(a, ('h', 'c'), [(h * 2 + c, c * 2 + h) for h in range(2) for...]
    ppermute x12, starting transfers between devices: 35 us -> 39.1 us  [move(): return lax.ppermute(a, ('y', 'x', 'c'), pairs)]
    ppermute x5, starting transfers between devices: 32.6 us -> 36.2 us  [swap(): return lax.ppermute(a, 'c', [(0, 1), (1, 0)])]
    ppermute x12, waiting for transfers between devices: 43.4 us -> 40.3 us  [move(): return lax.ppermute(a, ('y', 'x', 'c'), pairs)]
  transfers between devices with their start and end apart: 21 -> 21, of which waited for: 8 -> 9; matrix products, arithmetic and copies ran while one was open for 5% -> 6% of each run, Pallas kernels for 4% -> 5%
where the time goes in v9:
time: 252 us; the launch traced here: 250 us
  starting transfers between devices  93 us (37%)
  waiting for transfers between devices  55.4 us (22%)
  blocking collectives  47.1 us (19%)
  other arithmetic  16.1 us (6%)
  between operations  13.9 us (6%)
  Pallas kernels  13.1 us (5%)
  local copies, waits for them, and re-layouts  11.7 us (5%)
    ppermute x12, waiting for transfers between devices, move(): return lax.ppermute(a, ('y', 'x', 'c'), pairs)  40.3 us
    ppermute x12, starting transfers between devices, move(): return lax.ppermute(a, ('y', 'x', 'c'), pairs)  39.1 us
    ppermute x5, starting transfers between devices, swap(): return lax.ppermute(a, 'c', [(0, 1), (1, 0)])  36.2 us
    all_gather x1, blocking collectives, local(): got = lax.all_gather(sent, Z, axis=0, tiled=False)  25 us
    all_to_all x1, blocking collectives, local(): back = lax.all_to_all(back, Z, split_axis=0, concat_axis=0, tiled=True)  22.1 us
    all_to_all x2, waiting for transfers between devices, spread(): lax.all_to_all(a, ('y', 'x', 'c'), 0, 0, axis_index_groups=groups, tiled=...  14.3 us
    ppermute x1, starting transfers between devices, turn(): lax.ppermute(a, ('h', 'c'), [(h * 2 + c, c * 2 + h) for h in range(2) for...  9.97 us
    pallas_call x4, Pallas kernels, ffn(): pl.pallas_call(functools.partial(ffn_kernel, hid=hid, parts=parts), out_s...  9.88 us
  transfers between devices with their start and end apart: 21, of which 9 were waited for; matrix products, arithmetic and copies ran while one was open for 6% of the time, Pallas kernels for 5%

profile of v9, /device:TPU:1, one launch (start us, length us, event | category | flops | bytes accessed | tf_op | source)
XLA Modules:
  0.0 250.3 jit_solution(8232856075253900966)
XLA Ops:
  9.9 8.8 %collective-permute-start = (bf16[32,256]{1,0:T(8,128)(2,1)S(1)}, bf16[32,256]{1,0:T(8,128)(2,1)S(1)}, u32[]{:S(2)}, u32[]{:S(2)}) collective-permute-start(bf16[32,256]{1,0:T(8,128)(2,1)S(1)} %get-tuple-element.68), channel_id=1, source_target_pairs={{0,1},{1,0},{2,3},{3,2},{4,5},{5,4},{6,7},{7,6},{8,9},{9,8},{10,11... | collective-permute-start | bytes 49160 | tf_op jit(solution)/shard_map/ppermute | solution.py:30
  19.5 10.0 %collective-permute-start.1 = (bf16[384,128]{1,0:T(8,128)(2,1)S(1)}, bf16[384,128]{1,0:T(8,128)(2,1)S(1)}, u32[]{:S(2)}, u32[]{:S(2)}) collective-permute-start(bf16[384,128]{1,0:T(8,128)(2,1)S(1)} %bitcast.36), channel_id=1, source_target_pairs={{0,0},{1,64},{64,1},{65,65},{2,2},{3,66},{66,3},{67,67},{4,4},{5,6... | collective-permute-start | bytes 294920 | tf_op jit(solution)/shard_map/ppermute | solution.py:42
  29.5 25.0 %all-gather = bf16[512,512]{1,0:T(8,128)(2,1)S(1)} all-gather(bf16[32,512]{1,0:T(8,128)(2,1)S(1)} %pad_maximum_fusion.1), channel_id=2, replica_groups=mesh['y'=4,'h'=2,'x'=4,'l'=8,'c'=2] {'h','l'}, dimensions={0}, use_global_device_ids=true | all-gather | bytes 557056 | tf_op jit(solution)/shard_map/all_gather | solution.py:205
  54.5 1.7 shard_map.91
  56.8 4.2 %all-to-all-start = ((bf16[4,64,3712]{2,1,0:T(8,128)(2,1)}), bf16[4,64,3712]{2,1,0:T(8,128)(2,1)S(1)}, u32[]{:S(2)}, u32[]{:S(2)}) async-start(bf16[4,64,3712]{2,1,0:T(8,128)(2,1)} %bitcast.8), calls=%async_computation | async-start | bytes 3801088 | tf_op jit(solution)/shard_map/all_to_all | solution.py:36
  61.0 7.7 %collective-permute-start.8 = (bf16[128,3616]{0,1:T(8,128)(2,1)}, bf16[128,3616]{0,1:T(8,128)(2,1)}, u32[]{:S(2)}, u32[]{:S(2)}) collective-permute-start(bf16[128,3616]{0,1:T(8,128)(2,1)} %bitcast.14), channel_id=1, source_target_pairs={{0,1},{1,0},{2,3},{3,2},{4,5},{5,4},{6,7},{7,6},{8,9},{9,8},{10,11... | collective-permute-start | bytes 2777096 | tf_op jit(solution)/shard_map/ppermute | solution.py:30
  68.7 1.9 collective-permute-start.6
  70.6 2.4 collective-permute-start.7
  73.1 1.6 copy.25
  74.7 2.3 copy.27
  77.1 3.8 %collective-permute-start.2 = (bf16[128,3712]{1,0:T(8,128)(2,1)S(1)}, bf16[128,3712]{1,0:T(8,128)(2,1)S(1)}, u32[]{:S(2)}, u32[]{:S(2)}) collective-permute-start(bf16[128,3712]{1,0:T(8,128)(2,1)S(1)} %bitcast.26), channel_id=1, source_target_pairs={{0,16},{1,129},{16,32},{17,145},{32,48},{33,161},{48,0},{49,177},{... | collective-permute-start | bytes 2850824 | tf_op jit(solution)/shard_map/ppermute | solution.py:26
  80.9 3.1 %collective-permute-start.4 = (bf16[128,3712]{1,0:T(8,128)(2,1)S(1)}, bf16[128,3712]{1,0:T(8,128)(2,1)S(1)}, u32[]{:S(2)}, u32[]{:S(2)}) collective-permute-start(bf16[128,3712]{1,0:T(8,128)(2,1)S(1)} %bitcast.23), channel_id=1, source_target_pairs={{0,48},{1,385},{16,0},{17,401},{32,16},{33,417},{48,32},{49,433},{... | collective-permute-start | bytes 2850824 | tf_op jit(solution)/shard_map/ppermute | solution.py:26
  84.2 3.6 %fusion.6.refs_2_ = bf16[3712,512]{1,0:T(8,128)(2,1)S(1)} fusion(bf16[3616,128]{1,0:T(8,128)(2,1)} %collective-permute-done.7, bf16[3616,128]{1,0:T(8,128)(2,1)} %bitcast.12, bf16[3616,128]{1,0:T(8,128)(2,1)} %collective-permute-done.6, bf16[3616,128]{1,0:T(8,128)(2,1)} %bitcast.11), kind=kLoop, calls=%fused_computation.7 | loop fusion | flops 24707072 | bytes 7503872 | tf_op jit(solution)/shard_map/concatenate | solution.py:211
  87.8 6.2 %collective-permute-done.2.refs_0_ = bf16[128,3712]{1,0:T(8,128)(2,1)S(1)} collective-permute-done((bf16[128,3712]{1,0:T(8,128)(2,1)S(1)}, bf16[128,3712]{1,0:T(8,128)(2,1)S(1)}, u32[]{:S(2)}, u32[]{:S(2)}) %collective-permute-start.2) | collective-permute-done | bytes 950304 | tf_op jit(solution)/shard_map/ppermute | solution.py:26
  94.0 2.2 collective-permute-start.3
  96.2 4.3 %collective-permute-start.5 = (bf16[128,3712]{1,0:T(8,128)(2,1)S(1)}, bf16[128,3712]{1,0:T(8,128)(2,1)S(1)}, u32[]{:S(2)}, u32[]{:S(2)}) collective-permute-start(bf16[128,3712]{1,0:T(8,128)(2,1)S(1)} %collective-permute-done.4.refs_1_), channel_id=1, source_target_pairs={{0,48},{1,385},{16,0},{17,401},{32,16},{33,417},{48,32},{49,433},{... | collective-permute-start | bytes 2850824 | tf_op jit(solution)/shard_map/ppermute | solution.py:26
  100.5 3.1 %shard_map.93 = (bf16[128,3712]{1,0:T(8,128)(2,1)}, bf16[128,3712]{1,0:T(8,128)(2,1)}) custom-call(s32[1]{0:T(128)} %bitcast.at_ref, bf16[128,3712]{1,0:T(8,128)(2,1)S(1)} %collective-permute-done.2.refs_0_, bf16[128,3712]{1,0:T(8,128)(2,1)S(1)} %collective-permute-done.4.refs_1_, bf16[3712,512]{1,0:T(8,128)(2,1)S(1)} %fusion.6.refs_2_, ...), custom_call_target="tpu_custom_call" | custom-call | flops 1459617792 | bytes 9502720 | tf_op jit(solution)/shard_map/pallas_call | solution.py:79
  103.7 1.9 collective-permute-start.9
  105.6 4.6 %collective-permute-start.10 = (bf16[128,3712]{1,0:T(8,128)(2,1)S(1)}, bf16[128,3712]{1,0:T(8,128)(2,1)S(1)}, u32[]{:S(2)}, u32[]{:S(2)}) collective-permute-start(bf16[128,3712]{1,0:T(8,128)(2,1)S(1)} %bitcast.27), channel_id=1, source_target_pairs={{0,48},{1,385},{16,0},{17,401},{32,16},{33,417},{48,32},{49,433},{... | collective-permute-start | bytes 2850824 | tf_op jit(solution)/shard_map/ppermute | solution.py:26
  110.2 6.3 %collective-permute-done.3.refs_0_ = bf16[128,3712]{1,0:T(8,128)(2,1)S(1)} collective-permute-done((bf16[128,3712]{1,0:T(8,128)(2,1)S(1)}, bf16[128,3712]{1,0:T(8,128)(2,1)S(1)}, u32[]{:S(2)}, u32[]{:S(2)}) %collective-permute-start.3) | collective-permute-done | bytes 950304 | tf_op jit(solution)/shard_map/ppermute | solution.py:26
  116.4 1.0 collective-permute-done.5.refs_1_
  117.4 3.1 %shard_map.92 = (bf16[128,3712]{1,0:T(8,128)(2,1)}, bf16[128,3712]{1,0:T(8,128)(2,1)}) custom-call(s32[1]{0:T(128)} %bitcast.at_ref, bf16[128,3712]{1,0:T(8,128)(2,1)S(1)} %collective-permute-done.3.refs_0_, bf16[128,3712]{1,0:T(8,128)(2,1)S(1)} %collective-permute-done.5.refs_1_, bf16[3712,512]{1,0:T(8,128)(2,1)S(1)} %fusion.6.refs_2_, ...), custom_call_target="tpu_custom_call" | custom-call | flops 1459617792 | bytes 9502720 | tf_op jit(solution)/shard_map/pallas_call | solution.py:79
  120.5 6.0 %collective-permute-done.9.refs_0_ = bf16[128,3712]{1,0:T(8,128)(2,1)S(1)} collective-permute-done((bf16[128,3712]{1,0:T(8,128)(2,1)S(1)}, bf16[128,3712]{1,0:T(8,128)(2,1)S(1)}, u32[]{:S(2)}, u32[]{:S(2)}) %collective-permute-start.9) | collective-permute-done | bytes 950304 | tf_op jit(solution)/shard_map/ppermute | solution.py:26
  126.5 1.1 collective-permute-done.10.refs_1_
  127.6 5.3 %collective-permute-start.11 = (bf16[128,3712]{1,0:T(8,128)(2,1)}, bf16[128,3712]{1,0:T(8,128)(2,1)}, u32[]{:S(2)}, u32[]{:S(2)}) collective-permute-start(bf16[128,3712]{1,0:T(8,128)(2,1)} %get-tuple-element.46), channel_id=1, source_target_pairs={{0,48},{1,385},{16,0},{17,401},{32,16},{33,417},{48,32},{49,433},{... | collective-permute-start | bytes 2850824 | tf_op jit(solution)/shard_map/ppermute | solution.py:26
  132.9 1.1 slice.45.x_ref
  134.0 1.9 collective-permute-start.13
  135.9 3.4 %collective-permute-start.14 = (bf16[128,3712]{1,0:T(8,128)(2,1)}, bf16[128,3712]{1,0:T(8,128)(2,1)}, u32[]{:S(2)}, u32[]{:S(2)}) collective-permute-start(bf16[128,3712]{1,0:T(8,128)(2,1)} %get-tuple-element.51), channel_id=1, source_target_pairs={{0,16},{1,129},{16,32},{17,145},{32,48},{33,161},{48,0},{49,177},{... | collective-permute-start | bytes 2850824 | tf_op jit(solution)/shard_map/ppermute | solution.py:26
  139.3 1.9 collective-permute-start.12
  141.2 1.8 shard_map.94
  144.0 1.0 copy-done.9
  145.0 1.9 copy-done.6
  146.9 1.6 shard_map.95
  148.5 1.6 add_convert_fusion.3
  150.1 12.3 %collective-permute-done.12 = bf16[128,3712]{1,0:T(8,128)(2,1)} collective-permute-done((bf16[128,3712]{1,0:T(8,128)(2,1)}, bf16[128,3712]{1,0:T(8,128)(2,1)}, u32[]{:S(2)}, u32[]{:S(2)}) %collective-permute-start.12) | collective-permute-done | bytes 950304 | tf_op jit(solution)/shard_map/ppermute | solution.py:26
  162.4 1.4 add_convert_fusion.2
  163.8 2.2 collective-permute-start.15
  166.0 4.5 %collective-permute-start.16 = (bf16[128,3712]{1,0:T(8,128)(2,1)S(1)}, bf16[128,3712]{1,0:T(8,128)(2,1)S(1)}, u32[]{:S(2)}, u32[]{:S(2)}) collective-permute-start(bf16[128,3712]{1,0:T(8,128)(2,1)S(1)} %add_convert_fusion.3), channel_id=1, source_target_pairs={{0,48},{1,385},{16,0},{17,401},{32,16},{33,417},{48,32},{49,433},{... | collective-permute-start | bytes 2850824 | tf_op jit(solution)/shard_map/ppermute | solution.py:26
  170.6 1.8 shard_map.96
  172.4 7.4 %collective-permute-done.15 = bf16[128,3712]{1,0:T(8,128)(2,1)S(1)} collective-permute-done((bf16[128,3712]{1,0:T(8,128)(2,1)S(1)}, bf16[128,3712]{1,0:T(8,128)(2,1)S(1)}, u32[]{:S(2)}, u32[]{:S(2)}) %collective-permute-start.15) | collective-permute-done | bytes 950304 | tf_op jit(solution)/shard_map/ppermute | solution.py:26
  179.8 1.5 add_convert_fusion.1
  181.4 1.5 add_convert_fusion
  182.9 1.4 pad_maximum_fusion
  184.3 3.6 %all-to-all-start.1 = ((bf16[4,64,3712]{2,1,0:T(8,128)(2,1)}), bf16[4,64,3712]{2,1,0:T(8,128)(2,1)S(1)}, u32[]{:S(2)}, u32[]{:S(2)}) async-start(bf16[4,64,3712]{2,1,0:T(8,128)(2,1)} %bitcast.32), calls=%async_computation.1 | async-start | bytes 3801088 | tf_op jit(solution)/shard_map/all_to_all | solution.py:36
  187.9 14.3 %all-to-all-done.1 = bf16[4,64,3712]{2,1,0:T(8,128)(2,1)S(1)} async-done(((bf16[4,64,3712]{2,1,0:T(8,128)(2,1)}), bf16[4,64,3712]{2,1,0:T(8,128)(2,1)S(1)}, u32[]{:S(2)}, u32[]{:S(2)}) %all-to-all-start.1) | async-done | bytes 1900576 | tf_op jit(solution)/shard_map/all_to_all | solution.py:36
  202.5 1.7 reshape.31
  204.4 22.1 %all_to_all.26 = bf16[16,64,226]{2,1,0:T(8,128)(2,1)S(1)} all-to-all(bf16[16,64,226]{2,1,0:T(8,128)(2,1)S(1)} %bitcast.35), channel_id=1, replica_groups=mesh['y'=4,'h'=2,'x'=4,'l'=8,'c'=2] {'h','l'}, dimensions={0} | all-to-all | bytes 925696 | tf_op jit(solution)/shard_map/all_to_all | solution.py:246
  226.6 15.3 %collective-permute-start.17 = (bf16[32,226]{1,0:T(8,128)(2,1)S(1)}, bf16[32,226]{1,0:T(8,128)(2,1)S(1)}, u32[]{:S(2)}, u32[]{:S(2)}) collective-permute-start(bf16[32,226]{1,0:T(8,128)(2,1)S(1)} %get-tuple-element.66), channel_id=1, source_target_pairs={{0,1},{1,0},{2,3},{3,2},{4,5},{5,4},{6,7},{7,6},{8,9},{9,8},{10,11... | collective-permute-start | bytes 43400 | tf_op jit(solution)/shard_map/ppermute | solution.py:30
  (60 shorter events, 8.2 us)
Async XLA Ops:
  6.5 138.5 %all-gather.4.cloned.1.call-start = ((), (), s32[]{:S(2)}) async-start(), calls=%async_computation.3 | async-start | bytes 3244032 | tf_op jit(solution)/shard_map/all_gather | solution.py:207
  9.9 19.6 %collective-permute-start = (bf16[32,256]{1,0:T(8,128)(2,1)S(1)}, bf16[32,256]{1,0:T(8,128)(2,1)S(1)}, u32[]{:S(2)}, u32[]{:S(2)}) collective-permute-start(bf16[32,256]{1,0:T(8,128)(2,1)S(1)} %get-tuple-element.68), channel_id=1, source_target_pairs={{0,1},{1,0},{2,3},{3,2},{4,5},{5,4},{6,7},{7,6},{8,9},{9,8},{10,11... | collective-permute-start | bytes 49160 | tf_op jit(solution)/shard_map/ppermute | solution.py:30
  19.5 36.7 %collective-permute-start.1 = (bf16[384,128]{1,0:T(8,128)(2,1)S(1)}, bf16[384,128]{1,0:T(8,128)(2,1)S(1)}, u32[]{:S(2)}, u32[]{:S(2)}) collective-permute-start(bf16[384,128]{1,0:T(8,128)(2,1)S(1)} %bitcast.36), channel_id=1, source_target_pairs={{0,0},{1,64},{64,1},{65,65},{2,2},{3,66},{66,3},{67,67},{4,4},{5,6... | collective-permute-start | bytes 294920 | tf_op jit(solution)/shard_map/ppermute | solution.py:42
  56.2 0.6 copy-start.12
  56.8 20.2 %all-to-all-start = ((bf16[4,64,3712]{2,1,0:T(8,128)(2,1)}), bf16[4,64,3712]{2,1,0:T(8,128)(2,1)S(1)}, u32[]{:S(2)}, u32[]{:S(2)}) async-start(bf16[4,64,3712]{2,1,0:T(8,128)(2,1)} %bitcast.8), calls=%async_computation | async-start | bytes 3801088 | tf_op jit(solution)/shard_map/all_to_all | solution.py:36
  61.0 13.7 %collective-permute-start.8 = (bf16[128,3616]{0,1:T(8,128)(2,1)}, bf16[128,3616]{0,1:T(8,128)(2,1)}, u32[]{:S(2)}, u32[]{:S(2)}) collective-permute-start(bf16[128,3616]{0,1:T(8,128)(2,1)} %bitcast.14), channel_id=1, source_target_pairs={{0,1},{1,0},{2,3},{3,2},{4,5},{5,4},{6,7},{7,6},{8,9},{9,8},{10,11... | collective-permute-start | bytes 2777096 | tf_op jit(solution)/shard_map/ppermute | solution.py:30
  68.7 15.5 %collective-permute-start.6 = (bf16[3616,128]{1,0:T(8,128)(2,1)}, bf16[3616,128]{1,0:T(8,128)(2,1)}, u32[]{:S(2)}, u32[]{:S(2)}) collective-permute-start(bf16[3616,128]{1,0:T(8,128)(2,1)} %bitcast.11), channel_id=1, source_target_pairs={{0,1},{1,0},{2,3},{3,2},{4,5},{5,4},{6,7},{7,6},{8,9},{9,8},{10,11... | collective-permute-start | bytes 2777096 | tf_op jit(solution)/shard_map/ppermute | solution.py:30
  70.6 13.6 %collective-permute-start.7 = (bf16[3616,128]{1,0:T(8,128)(2,1)}, bf16[3616,128]{1,0:T(8,128)(2,1)}, u32[]{:S(2)}, u32[]{:S(2)}) collective-permute-start(bf16[3616,128]{1,0:T(8,128)(2,1)} %bitcast.12), channel_id=1, source_target_pairs={{0,1},{1,0},{2,3},{3,2},{4,5},{5,4},{6,7},{7,6},{8,9},{9,8},{10,11... | collective-permute-start | bytes 2777096 | tf_op jit(solution)/shard_map/ppermute | solution.py:30
  77.0 7.1 %copy-start.11 = (bf16[128,3616]{1,0:T(8,128)(2,1)S(1)}, bf16[128,3616]{1,0:T(8,128)(2,1)}, u32[]{:S(2)}) copy-start(bf16[128,3616]{1,0:T(8,128)(2,1)} %copy.27) | copy-start | bytes 2777092
  77.1 26.5 %copy-start.2 = (bf16[2,64,3712]{2,1,0:T(8,128)(2,1)}, bf16[2,64,3712]{2,1,0:T(8,128)(2,1)S(1)}, u32[]{:S(2)}) copy-start(bf16[2,64,3712]{2,1,0:T(8,128)(2,1)S(1)} %get-tuple-element.63) | copy-start | bytes 2850820
  77.1 28.5 %copy-start.4 = (bf16[2,64,3712]{2,1,0:T(8,128)(2,1)}, bf16[2,64,3712]{2,1,0:T(8,128)(2,1)S(1)}, u32[]{:S(2)}) copy-start(bf16[2,64,3712]{2,1,0:T(8,128)(2,1)S(1)} %get-tuple-element.64) | copy-start | bytes 2850820
  77.1 16.9 %collective-permute-start.2 = (bf16[128,3712]{1,0:T(8,128)(2,1)S(1)}, bf16[128,3712]{1,0:T(8,128)(2,1)S(1)}, u32[]{:S(2)}, u32[]{:S(2)}) collective-permute-start(bf16[128,3712]{1,0:T(8,128)(2,1)S(1)} %bitcast.26), channel_id=1, source_target_pairs={{0,16},{1,129},{16,32},{17,145},{32,48},{33,161},{48,0},{49,177},{... | collective-permute-start | bytes 2850824 | tf_op jit(solution)/shard_map/ppermute | solution.py:26
  80.9 15.3 %collective-permute-start.4 = (bf16[128,3712]{1,0:T(8,128)(2,1)S(1)}, bf16[128,3712]{1,0:T(8,128)(2,1)S(1)}, u32[]{:S(2)}, u32[]{:S(2)}) collective-permute-start(bf16[128,3712]{1,0:T(8,128)(2,1)S(1)} %bitcast.23), channel_id=1, source_target_pairs={{0,48},{1,385},{16,0},{17,401},{32,16},{33,417},{48,32},{49,433},{... | collective-permute-start | bytes 2850824 | tf_op jit(solution)/shard_map/ppermute | solution.py:26
  87.8 53.4 %copy-start = (bf16[3712,512]{1,0:T(8,128)(2,1)}, bf16[3712,512]{1,0:T(8,128)(2,1)S(1)}, u32[]{:S(2)}) copy-start(bf16[3712,512]{1,0:T(8,128)(2,1)S(1)} %fusion.6.refs_2_) | copy-start | bytes 11403268
  94.0 22.4 %collective-permute-start.3 = (bf16[128,3712]{1,0:T(8,128)(2,1)S(1)}, bf16[128,3712]{1,0:T(8,128)(2,1)S(1)}, u32[]{:S(2)}, u32[]{:S(2)}) collective-permute-start(bf16[128,3712]{1,0:T(8,128)(2,1)S(1)} %collective-permute-done.2.refs_0_), channel_id=1, source_target_pairs={{0,16},{1,129},{16,32},{17,145},{32,48},{33,161},{48,0},{49,177},{... | collective-permute-start | bytes 2850824 | tf_op jit(solution)/shard_map/ppermute | solution.py:26
  96.2 21.2 %collective-permute-start.5 = (bf16[128,3712]{1,0:T(8,128)(2,1)S(1)}, bf16[128,3712]{1,0:T(8,128)(2,1)S(1)}, u32[]{:S(2)}, u32[]{:S(2)}) collective-permute-start(bf16[128,3712]{1,0:T(8,128)(2,1)S(1)} %collective-permute-done.4.refs_1_), channel_id=1, source_target_pairs={{0,48},{1,385},{16,0},{17,401},{32,16},{33,417},{48,32},{49,433},{... | collective-permute-start | bytes 2850824 | tf_op jit(solution)/shard_map/ppermute | solution.py:26
  103.7 22.8 %collective-permute-start.9 = (bf16[128,3712]{1,0:T(8,128)(2,1)S(1)}, bf16[128,3712]{1,0:T(8,128)(2,1)S(1)}, u32[]{:S(2)}, u32[]{:S(2)}) collective-permute-start(bf16[128,3712]{1,0:T(8,128)(2,1)S(1)} %bitcast.24), channel_id=1, source_target_pairs={{0,16},{1,129},{16,32},{17,145},{32,48},{33,161},{48,0},{49,177},{... | collective-permute-start | bytes 2850824 | tf_op jit(solution)/shard_map/ppermute | solution.py:26
  105.6 22.0 %collective-permute-start.10 = (bf16[128,3712]{1,0:T(8,128)(2,1)S(1)}, bf16[128,3712]{1,0:T(8,128)(2,1)S(1)}, u32[]{:S(2)}, u32[]{:S(2)}) collective-permute-start(bf16[128,3712]{1,0:T(8,128)(2,1)S(1)} %bitcast.27), channel_id=1, source_target_pairs={{0,48},{1,385},{16,0},{17,401},{32,16},{33,417},{48,32},{49,433},{... | collective-permute-start | bytes 2850824 | tf_op jit(solution)/shard_map/ppermute | solution.py:26
  127.6 20.9 %collective-permute-start.11 = (bf16[128,3712]{1,0:T(8,128)(2,1)}, bf16[128,3712]{1,0:T(8,128)(2,1)}, u32[]{:S(2)}, u32[]{:S(2)}) collective-permute-start(bf16[128,3712]{1,0:T(8,128)(2,1)} %get-tuple-element.46), channel_id=1, source_target_pairs={{0,48},{1,385},{16,0},{17,401},{32,16},{33,417},{48,32},{49,433},{... | collective-permute-start | bytes 2850824 | tf_op jit(solution)/shard_map/ppermute | solution.py:26
  134.0 29.8 %collective-permute-start.13 = (bf16[128,3712]{1,0:T(8,128)(2,1)}, bf16[128,3712]{1,0:T(8,128)(2,1)}, u32[]{:S(2)}, u32[]{:S(2)}) collective-permute-start(bf16[128,3712]{1,0:T(8,128)(2,1)} %get-tuple-element.50), channel_id=1, source_target_pairs={{0,48},{1,385},{16,0},{17,401},{32,16},{33,417},{48,32},{49,433},{... | collective-permute-start | bytes 2850824 | tf_op jit(solution)/shard_map/ppermute | solution.py:26
  135.9 27.9 %collective-permute-start.14 = (bf16[128,3712]{1,0:T(8,128)(2,1)}, bf16[128,3712]{1,0:T(8,128)(2,1)}, u32[]{:S(2)}, u32[]{:S(2)}) collective-permute-start(bf16[128,3712]{1,0:T(8,128)(2,1)} %get-tuple-element.51), channel_id=1, source_target_pairs={{0,16},{1,129},{16,32},{17,145},{32,48},{33,161},{48,0},{49,177},{... | collective-permute-start | bytes 2850824 | tf_op jit(solution)/shard_map/ppermute | solution.py:26
  139.3 23.1 %collective-permute-start.12 = (bf16[128,3712]{1,0:T(8,128)(2,1)}, bf16[128,3712]{1,0:T(8,128)(2,1)}, u32[]{:S(2)}, u32[]{:S(2)}) collective-permute-start(bf16[128,3712]{1,0:T(8,128)(2,1)} %get-tuple-element.48), channel_id=1, source_target_pairs={{0,16},{1,129},{16,32},{17,145},{32,48},{33,161},{48,0},{49,177},{... | collective-permute-start | bytes 2850824 | tf_op jit(solution)/shard_map/ppermute | solution.py:26
  143.1 0.9 copy-start.7
  144.0 1.0 copy-start.9
  145.0 1.9 copy-start.6
  146.9 1.6 copy-start.10
  146.9 15.5 %copy-start.8 = (bf16[128,3712]{1,0:T(8,128)(2,1)S(1)}, bf16[128,3712]{1,0:T(8,128)(2,1)}, u32[]{:S(2)}) copy-start(bf16[128,3712]{1,0:T(8,128)(2,1)} %copy-done.7) | copy-start | bytes 2850820
  148.5 22.0 %copy-start.1 = (bf16[3712,512]{1,0:T(8,128)(2,1)S(1)}, bf16[3712,512]{1,0:T(8,128)(2,1)}, u32[]{:S(2)}) copy-start(bf16[3712,512]{1,0:T(8,128)(2,1)} %copy-done) | copy-start | bytes 11403268
  150.1 20.4 %copy-start.3 = (bf16[2,64,3712]{2,1,0:T(8,128)(2,1)S(1)}, bf16[2,64,3712]{2,1,0:T(8,128)(2,1)}, u32[]{:S(2)}) copy-start(bf16[2,64,3712]{2,1,0:T(8,128)(2,1)} %copy-done.2) | copy-start | bytes 2850820
  150.1 20.4 %copy-start.5 = (bf16[2,64,3712]{2,1,0:T(8,128)(2,1)S(1)}, bf16[2,64,3712]{2,1,0:T(8,128)(2,1)}, u32[]{:S(2)}) copy-start(bf16[2,64,3712]{2,1,0:T(8,128)(2,1)} %copy-done.4) | copy-start | bytes 2850820
  163.8 16.0 %collective-permute-start.15 = (bf16[128,3712]{1,0:T(8,128)(2,1)S(1)}, bf16[128,3712]{1,0:T(8,128)(2,1)S(1)}, u32[]{:S(2)}, u32[]{:S(2)}) collective-permute-start(bf16[128,3712]{1,0:T(8,128)(2,1)S(1)} %add_convert_fusion.2), channel_id=1, source_target_pairs={{0,16},{1,129},{16,32},{17,145},{32,48},{33,161},{48,0},{49,177},{... | collective-permute-start | bytes 2850824 | tf_op jit(solution)/shard_map/ppermute | solution.py:26
  166.0 15.4 %collective-permute-start.16 = (bf16[128,3712]{1,0:T(8,128)(2,1)S(1)}, bf16[128,3712]{1,0:T(8,128)(2,1)S(1)}, u32[]{:S(2)}, u32[]{:S(2)}) collective-permute-start(bf16[128,3712]{1,0:T(8,128)(2,1)S(1)} %add_convert_fusion.3), channel_id=1, source_target_pairs={{0,48},{1,385},{16,0},{17,401},{32,16},{33,417},{48,32},{49,433},{... | collective-permute-start | bytes 2850824 | tf_op jit(solution)/shard_map/ppermute | solution.py:26
  184.3 17.9 %all-to-all-start.1 = ((bf16[4,64,3712]{2,1,0:T(8,128)(2,1)}), bf16[4,64,3712]{2,1,0:T(8,128)(2,1)S(1)}, u32[]{:S(2)}, u32[]{:S(2)}) async-start(bf16[4,64,3712]{2,1,0:T(8,128)(2,1)} %bitcast.32), calls=%async_computation.1 | async-start | bytes 3801088 | tf_op jit(solution)/shard_map/all_to_all | solution.py:36
  226.6 16.2 %collective-permute-start.17 = (bf16[32,226]{1,0:T(8,128)(2,1)S(1)}, bf16[32,226]{1,0:T(8,128)(2,1)S(1)}, u32[]{:S(2)}, u32[]{:S(2)}) collective-permute-start(bf16[32,226]{1,0:T(8,128)(2,1)S(1)} %get-tuple-element.66), channel_id=1, source_target_pairs={{0,1},{1,0},{2,3},{3,2},{4,5},{5,4},{6,7},{7,6},{8,9},{9,8},{10,11... | collective-permute-start | bytes 43400 | tf_op jit(solution)/shard_map/ppermute | solution.py:30
Sparse Core Ops, SparseCore 0:
  56.9 61.0 all-gather.3

commit v10 on v9

--- a/solution.py
+++ b/solution.py
@@ -224,15 +224,13 @@
     back_p, back_s = move(prev_lo, 1, -1), move(succ_hi, 1, 1)
     far_lo, far_hi = apply(far_lo, far_hi)
 
-    far_lo, far_hi, prev_hi, succ_lo = order((far_lo, far_hi, prev_hi, succ_lo))
     from_prev, from_succ = move(far_lo, 1, 1), move(far_hi, 1, -1)
+    prev_hi, succ_lo, back_p, back_s, _ = order((prev_hi, succ_lo, back_p, back_s, far_lo))
     prev_hi, succ_lo = apply(prev_hi, succ_lo)
     prev_hi, succ_lo, s = order((prev_hi, succ_lo, s))
     out = shared_expert(copies[:toks], s, depth)
     prev_hi, succ_lo = add(prev_hi, from_succ), add(succ_lo, from_prev)
-    prev_hi, succ_lo, lo, hi, out, back_p, back_s = order(
-        (prev_hi, succ_lo, lo, hi, out, back_p, back_s)
-    )
+    prev_hi, succ_lo, lo, hi, out = order((prev_hi, succ_lo, lo, hi, out))
     prev_hi, succ_lo = move(prev_hi, 1, -1), move(succ_lo, 1, 1)
     own_lo, own_hi = apply(lo, hi)
     total = jnp.concatenate([add(own_lo, back_p, succ_lo), add(own_hi, back_s, prev_hi)], 0)

time: 252 us -> 243 us (0.964)
  waiting for transfers between devices: 55.4 us -> 37.3 us
  blocking collectives: 47.1 us -> 52.4 us
  Pallas kernels: 13.1 us -> 16 us
    ppermute x12, waiting for transfers between devices: 40.3 us -> 15.3 us  [move(): return lax.ppermute(a, ('y', 'x', 'c'), pairs)]
    all_to_all x2, waiting for transfers between devices: 14.3 us -> 21.1 us  [spread(): lax.all_to_all(a, ('y', 'x', 'c'), 0, 0, axis_index_groups=groups, tiled=...]
    all_to_all x1, blocking collectives: 22.1 us -> 27.4 us  [local(): back = lax.all_to_all(back, Z, split_axis=0, concat_axis=0, tiled=True)]
    ppermute x5, starting transfers between devices: 36.2 us -> 39 us  [swap(): return lax.ppermute(a, 'c', [(0, 1), (1, 0)])]
    pallas_call x4, Pallas kernels: 9.88 us -> 12.7 us  [ffn(): pl.pallas_call(functools.partial(ffn_kernel, hid=hid, parts=parts), out_s...]
    unnamed x27 -> x33, local copies, waits for them, and re-layouts: 6.08 us -> 6.78 us
  transfers between devices with their start and end apart: 21 -> 21, of which waited for: 9 -> 8; matrix products, arithmetic and copies ran while one was open for 6% -> 6% of each run, Pallas kernels for 5% -> 7%
where the time goes in v10:
time: 243 us; the launch traced here: 242 us
  starting transfers between devices  93.9 us (39%)
  blocking collectives  52.4 us (22%)
  waiting for transfers between devices  37.3 us (15%)
  Pallas kernels  16 us (7%)
  other arithmetic  15.1 us (6%)
  between operations  13.9 us (6%)
  local copies, waits for them, and re-layouts  13.3 us (5%)
    ppermute x5, starting transfers between devices, swap(): return lax.ppermute(a, 'c', [(0, 1), (1, 0)])  39 us
    ppermute x12, starting transfers between devices, move(): return lax.ppermute(a, ('y', 'x', 'c'), pairs)  37.2 us
    all_to_all x1, blocking collectives, local(): back = lax.all_to_all(back, Z, split_axis=0, concat_axis=0, tiled=True)  27.4 us
    all_gather x1, blocking collectives, local(): got = lax.all_gather(sent, Z, axis=0, tiled=False)  25 us
    all_to_all x2, waiting for transfers between devices, spread(): lax.all_to_all(a, ('y', 'x', 'c'), 0, 0, axis_index_groups=groups, tiled=...  21.1 us
    ppermute x12, waiting for transfers between devices, move(): return lax.ppermute(a, ('y', 'x', 'c'), pairs)  15.3 us
    pallas_call x4, Pallas kernels, ffn(): pl.pallas_call(functools.partial(ffn_kernel, hid=hid, parts=parts), out_s...  12.7 us
    ppermute x1, starting transfers between devices, turn(): lax.ppermute(a, ('h', 'c'), [(h * 2 + c, c * 2 + h) for h in range(2) for...  9.97 us
  transfers between devices with their start and end apart: 21, of which 8 were waited for; matrix products, arithmetic and copies ran while one was open for 6% of the time, Pallas kernels for 7%

profile of v10, /device:TPU:1, one launch (start us, length us, event | category | flops | bytes accessed | tf_op | source)
XLA Modules:
  0.0 241.9 jit_solution(12745906077372900363)
XLA Ops:
  9.0 0.8 maximum_maximum_fusion
  9.9 8.8 %collective-permute-start = (bf16[32,256]{1,0:T(8,128)(2,1)S(1)}, bf16[32,256]{1,0:T(8,128)(2,1)S(1)}, u32[]{:S(2)}, u32[]{:S(2)}) collective-permute-start(bf16[32,256]{1,0:T(8,128)(2,1)S(1)} %get-tuple-element.64), channel_id=1, source_target_pairs={{0,1},{1,0},{2,3},{3,2},{4,5},{5,4},{6,7},{7,6},{8,9},{9,8},{10,11... | collective-permute-start | bytes 49160 | tf_op jit(solution)/shard_map/ppermute | solution.py:30
  19.5 10.0 %collective-permute-start.1 = (bf16[384,128]{1,0:T(8,128)(2,1)S(1)}, bf16[384,128]{1,0:T(8,128)(2,1)S(1)}, u32[]{:S(2)}, u32[]{:S(2)}) collective-permute-start(bf16[384,128]{1,0:T(8,128)(2,1)S(1)} %bitcast.37), channel_id=1, source_target_pairs={{0,0},{1,64},{64,1},{65,65},{2,2},{3,66},{66,3},{67,67},{4,4},{5,6... | collective-permute-start | bytes 294920 | tf_op jit(solution)/shard_map/ppermute | solution.py:42
  29.5 25.0 %all-gather = bf16[512,512]{1,0:T(8,128)(2,1)S(1)} all-gather(bf16[32,512]{1,0:T(8,128)(2,1)S(1)} %pad_maximum_fusion.1), channel_id=2, replica_groups=mesh['y'=4,'h'=2,'x'=4,'l'=8,'c'=2] {'h','l'}, dimensions={0}, use_global_device_ids=true | all-gather | bytes 557056 | tf_op jit(solution)/shard_map/all_gather | solution.py:205
  54.5 1.7 shard_map.91
  56.8 4.2 %all-to-all-start = ((bf16[4,64,3712]{2,1,0:T(8,128)(2,1)}), bf16[4,64,3712]{2,1,0:T(8,128)(2,1)S(1)}, u32[]{:S(2)}, u32[]{:S(2)}) async-start(bf16[4,64,3712]{2,1,0:T(8,128)(2,1)} %bitcast.8), calls=%async_computation | async-start | bytes 3801088 | tf_op jit(solution)/shard_map/all_to_all | solution.py:36
  61.0 7.7 %collective-permute-start.6 = (bf16[128,3616]{0,1:T(8,128)(2,1)}, bf16[128,3616]{0,1:T(8,128)(2,1)}, u32[]{:S(2)}, u32[]{:S(2)}) collective-permute-start(bf16[128,3616]{0,1:T(8,128)(2,1)} %bitcast.14), channel_id=1, source_target_pairs={{0,1},{1,0},{2,3},{3,2},{4,5},{5,4},{6,7},{7,6},{8,9},{9,8},{10,11... | collective-permute-start | bytes 2777096 | tf_op jit(solution)/shard_map/ppermute | solution.py:30
  68.7 6.6 %all-to-all-done = bf16[4,64,3712]{2,1,0:T(8,128)(2,1)S(1)} async-done(((bf16[4,64,3712]{2,1,0:T(8,128)(2,1)}), bf16[4,64,3712]{2,1,0:T(8,128)(2,1)S(1)}, u32[]{:S(2)}, u32[]{:S(2)}) %all-to-all-start) | async-done | bytes 1900576 | tf_op jit(solution)/shard_map/all_to_all | solution.py:36
  75.3 1.1 fusion.15
  76.4 3.2 %collective-permute-start.2 = (bf16[128,3712]{1,0:T(8,128)(2,1)}, bf16[128,3712]{1,0:T(8,128)(2,1)}, u32[]{:S(2)}, u32[]{:S(2)}) collective-permute-start(bf16[128,3712]{1,0:T(8,128)(2,1)} %bitcast.9.refs_0_), channel_id=1, source_target_pairs={{0,16},{1,129},{16,32},{17,145},{32,48},{33,161},{48,0},{49,177},{... | collective-permute-start | bytes 2850824 | tf_op jit(solution)/shard_map/ppermute | solution.py:26
  79.6 3.7 %collective-permute-start.3 = (bf16[128,3712]{1,0:T(8,128)(2,1)S(1)}, bf16[128,3712]{1,0:T(8,128)(2,1)}, u32[]{:S(2)}, u32[]{:S(2)}) collective-permute-start(bf16[128,3712]{1,0:T(8,128)(2,1)S(1)} %bitcast.23), channel_id=1, source_target_pairs={{0,48},{1,385},{16,0},{17,401},{32,16},{33,417},{48,32},{49,433},{... | collective-permute-start | bytes 2850824 | tf_op jit(solution)/shard_map/ppermute | solution.py:26
  83.2 9.9 %collective-permute-start.4 = (bf16[3616,128]{1,0:T(8,128)(2,1)}, bf16[3616,128]{1,0:T(8,128)(2,1)}, u32[]{:S(2)}, u32[]{:S(2)}) collective-permute-start(bf16[3616,128]{1,0:T(8,128)(2,1)} %bitcast.35), channel_id=1, source_target_pairs={{0,1},{1,0},{2,3},{3,2},{4,5},{5,4},{6,7},{7,6},{8,9},{9,8},{10,11... | collective-permute-start | bytes 2777096 | tf_op jit(solution)/shard_map/ppermute | solution.py:30
  93.1 1.9 collective-permute-start.5
  95.1 2.3 copy.25
  97.3 2.3 copy.27
  99.6 1.8 fusion.9.refs_3_
  101.4 2.4 %collective-permute-start.11 = (bf16[128,3712]{1,0:T(8,128)(2,1)}, bf16[128,3712]{1,0:T(8,128)(2,1)S(1)}, u32[]{:S(2)}, u32[]{:S(2)}) collective-permute-start(bf16[128,3712]{1,0:T(8,128)(2,1)} %collective-permute-done.2.refs_0_), channel_id=1, source_target_pairs={{0,16},{1,129},{16,32},{17,145},{32,48},{33,161},{48,0},{49,177},{... | collective-permute-start | bytes 2850824 | tf_op jit(solution)/shard_map/ppermute | solution.py:26
  103.8 4.1 %collective-permute-start.12 = (bf16[128,3712]{1,0:T(8,128)(2,1)}, bf16[128,3712]{1,0:T(8,128)(2,1)S(1)}, u32[]{:S(2)}, u32[]{:S(2)}) collective-permute-start(bf16[128,3712]{1,0:T(8,128)(2,1)} %collective-permute-done.3.refs_1_), channel_id=1, source_target_pairs={{0,48},{1,385},{16,0},{17,401},{32,16},{33,417},{48,32},{49,433},{... | collective-permute-start | bytes 2850824 | tf_op jit(solution)/shard_map/ppermute | solution.py:26
  107.9 3.3 %fusion.6.refs_2_ = bf16[3712,512]{1,0:T(8,128)(2,1)S(1)} fusion(bf16[3616,128]{1,0:T(8,128)(2,1)} %collective-permute-done.5, bf16[3616,128]{1,0:T(8,128)(2,1)S(1)} %bitcast.34, bf16[3616,128]{1,0:T(8,128)(2,1)} %collective-permute-done.4, bf16[3616,128]{1,0:T(8,128)(2,1)S(1)} %bitcast.36), kind=kLoop, calls=%fused_computation.7 | loop fusion | flops 24707072 | bytes 7503872 | tf_op jit(solution)/shard_map/concatenate | solution.py:211
  111.3 4.7 %shard_map.92 = (bf16[128,3712]{1,0:T(8,128)(2,1)S(1)}, bf16[128,3712]{1,0:T(8,128)(2,1)S(1)}) custom-call(s32[1]{0:T(128)} %bitcast.at_ref, bf16[128,3712]{1,0:T(8,128)(2,1)} %collective-permute-done.2.refs_0_, bf16[128,3712]{1,0:T(8,128)(2,1)} %collective-permute-done.3.refs_1_, bf16[3712,512]{1,0:T(8,128)(2,1)S(1)} %fusion.6.refs_2_, ...), custom_call_target="tpu_custom_call" | custom-call | flops 1459617792 | bytes 9502720 | tf_op jit(solution)/shard_map/pallas_call | solution.py:79
  116.0 2.0 collective-permute-start.9
  118.0 3.3 %collective-permute-start.10 = (bf16[128,3712]{1,0:T(8,128)(2,1)S(1)}, bf16[128,3712]{1,0:T(8,128)(2,1)S(1)}, u32[]{:S(2)}, u32[]{:S(2)}) collective-permute-start(bf16[128,3712]{1,0:T(8,128)(2,1)S(1)} %get-tuple-element.37), channel_id=1, source_target_pairs={{0,16},{1,129},{16,32},{17,145},{32,48},{33,161},{48,0},{49,177},{... | collective-permute-start | bytes 2850824 | tf_op jit(solution)/shard_map/ppermute | solution.py:26
  121.3 1.9 collective-permute-start.7
  123.2 4.6 %collective-permute-start.8 = (bf16[128,3712]{1,0:T(8,128)(2,1)}, bf16[128,3712]{1,0:T(8,128)(2,1)S(1)}, u32[]{:S(2)}, u32[]{:S(2)}) collective-permute-start(bf16[128,3712]{1,0:T(8,128)(2,1)} %bitcast.9.refs_0_), channel_id=1, source_target_pairs={{0,48},{1,385},{16,0},{17,401},{32,16},{33,417},{48,32},{49,433},{... | collective-permute-start | bytes 2850824 | tf_op jit(solution)/shard_map/ppermute | solution.py:26
  127.8 3.1 %shard_map.93 = (bf16[128,3712]{1,0:T(8,128)(2,1)}, bf16[128,3712]{1,0:T(8,128)(2,1)}) custom-call(s32[1]{0:T(128)} %bitcast.at_ref, bf16[128,3712]{1,0:T(8,128)(2,1)S(1)} %collective-permute-done.11.refs_0_, bf16[128,3712]{1,0:T(8,128)(2,1)S(1)} %collective-permute-done.12.refs_1_, bf16[3712,512]{1,0:T(8,128)(2,1)S(1)} %fusion.6.refs_2_, ...), custom_call_target="tpu_custom_call" | custom-call | flops 1459617792 | bytes 9502720 | tf_op jit(solution)/shard_map/pallas_call | solution.py:79
  130.9 2.0 collective-permute-start.13
  132.9 1.1 slice.45.x_ref
  134.0 3.3 %collective-permute-start.14 = (bf16[128,3712]{1,0:T(8,128)(2,1)}, bf16[128,3712]{1,0:T(8,128)(2,1)}, u32[]{:S(2)}, u32[]{:S(2)}) collective-permute-start(bf16[128,3712]{1,0:T(8,128)(2,1)} %get-tuple-element.38), channel_id=1, source_target_pairs={{0,16},{1,129},{16,32},{17,145},{32,48},{33,161},{48,0},{49,177},{... | collective-permute-start | bytes 2850824 | tf_op jit(solution)/shard_map/ppermute | solution.py:26
  137.3 6.8 %collective-permute-done.7.refs_0_ = bf16[128,3712]{1,0:T(8,128)(2,1)S(1)} collective-permute-done((bf16[128,3712]{1,0:T(8,128)(2,1)S(1)}, bf16[128,3712]{1,0:T(8,128)(2,1)S(1)}, u32[]{:S(2)}, u32[]{:S(2)}) %collective-permute-start.7) | collective-permute-done | bytes 950304 | tf_op jit(solution)/shard_map/ppermute | solution.py:26
  144.2 1.8 shard_map.94
  146.0 1.0 copy-done.5
  147.0 0.9 copy-done.7
  148.0 1.9 copy-done.4
  149.8 1.6 shard_map.95
  151.5 1.0 collective-permute-done.13
  152.5 1.6 add_convert_fusion.3
  154.4 1.4 add_convert_fusion.2
  155.8 2.3 collective-permute-start.15
  158.1 4.5 %collective-permute-start.16 = (bf16[128,3712]{1,0:T(8,128)(2,1)S(1)}, bf16[128,3712]{1,0:T(8,128)(2,1)S(1)}, u32[]{:S(2)}, u32[]{:S(2)}) collective-permute-start(bf16[128,3712]{1,0:T(8,128)(2,1)S(1)} %add_convert_fusion.3), channel_id=1, source_target_pairs={{0,48},{1,385},{16,0},{17,401},{32,16},{33,417},{48,32},{49,433},{... | collective-permute-start | bytes 2850824 | tf_op jit(solution)/shard_map/ppermute | solution.py:26
  162.7 3.0 %shard_map.96 = (bf16[128,3712]{1,0:T(8,128)(2,1)S(1)}, bf16[128,3712]{1,0:T(8,128)(2,1)S(1)}) custom-call(s32[1]{0:T(128)} %bitcast.at_ref, bf16[128,3712]{1,0:T(8,128)(2,1)} %bitcast.9.refs_0_, bf16[128,3712]{1,0:T(8,128)(2,1)S(1)} %bitcast.25, bf16[3712,512]{1,0:T(8,128)(2,1)S(1)} %copy-done.1, bf16[256,3712]{1,0:T(8,128)(2,1)S(1)} %fusion.9.refs_3_), custom_call_target="tpu_custom_call" | custom-call | flops 1459617792 | bytes 9502720 | tf_op jit(solution)/shard_map/pallas_call | solution.py:79
  165.7 6.2 %collective-permute-done.15 = bf16[128,3712]{1,0:T(8,128)(2,1)S(1)} collective-permute-done((bf16[128,3712]{1,0:T(8,128)(2,1)S(1)}, bf16[128,3712]{1,0:T(8,128)(2,1)S(1)}, u32[]{:S(2)}, u32[]{:S(2)}) %collective-permute-start.15) | collective-permute-done | bytes 950304 | tf_op jit(solution)/shard_map/ppermute | solution.py:26
  172.3 0.8 collective-permute-done.16
  173.5 1.4 pad_maximum_fusion
  174.9 3.6 %all-to-all-start.1 = ((bf16[4,64,3712]{2,1,0:T(8,128)(2,1)}), bf16[4,64,3712]{2,1,0:T(8,128)(2,1)S(1)}, u32[]{:S(2)}, u32[]{:S(2)}) async-start(bf16[4,64,3712]{2,1,0:T(8,128)(2,1)} %bitcast.29), calls=%async_computation.1 | async-start | bytes 3801088 | tf_op jit(solution)/shard_map/all_to_all | solution.py:36
  178.5 14.6 %all-to-all-done.1 = bf16[4,64,3712]{2,1,0:T(8,128)(2,1)S(1)} async-done(((bf16[4,64,3712]{2,1,0:T(8,128)(2,1)}), bf16[4,64,3712]{2,1,0:T(8,128)(2,1)S(1)}, u32[]{:S(2)}, u32[]{:S(2)}) %all-to-all-start.1) | async-done | bytes 1900576 | tf_op jit(solution)/shard_map/all_to_all | solution.py:36
  193.4 1.7 reshape.31
  195.3 27.4 %all_to_all.26 = bf16[16,64,226]{2,1,0:T(8,128)(2,1)S(1)} all-to-all(bf16[16,64,226]{2,1,0:T(8,128)(2,1)S(1)} %bitcast.32), channel_id=1, replica_groups=mesh['y'=4,'h'=2,'x'=4,'l'=8,'c'=2] {'h','l'}, dimensions={0} | all-to-all | bytes 925696 | tf_op jit(solution)/shard_map/all_to_all | solution.py:244
  222.9 10.7 %collective-permute-start.17 = (bf16[32,226]{1,0:T(8,128)(2,1)S(1)}, bf16[32,226]{1,0:T(8,128)(2,1)S(1)}, u32[]{:S(2)}, u32[]{:S(2)}) collective-permute-start(bf16[32,226]{1,0:T(8,128)(2,1)S(1)} %get-tuple-element.62), channel_id=1, source_target_pairs={{0,1},{1,0},{2,3},{3,2},{4,5},{5,4},{6,7},{7,6},{8,9},{9,8},{10,11... | collective-permute-start | bytes 43400 | tf_op jit(solution)/shard_map/ppermute | solution.py:30
  (66 shorter events, 7.2 us)
Async XLA Ops:
  6.5 141.4 %all-gather.4.cloned.1.call-start = ((), (), s32[]{:S(2)}) async-start(), calls=%async_computation.3 | async-start | bytes 3244032 | tf_op jit(solution)/shard_map/all_gather | solution.py:207
  9.9 19.6 %collective-permute-start = (bf16[32,256]{1,0:T(8,128)(2,1)S(1)}, bf16[32,256]{1,0:T(8,128)(2,1)S(1)}, u32[]{:S(2)}, u32[]{:S(2)}) collective-permute-start(bf16[32,256]{1,0:T(8,128)(2,1)S(1)} %get-tuple-element.64), channel_id=1, source_target_pairs={{0,1},{1,0},{2,3},{3,2},{4,5},{5,4},{6,7},{7,6},{8,9},{9,8},{10,11... | collective-permute-start | bytes 49160 | tf_op jit(solution)/shard_map/ppermute | solution.py:30
  19.5 36.7 %collective-permute-start.1 = (bf16[384,128]{1,0:T(8,128)(2,1)S(1)}, bf16[384,128]{1,0:T(8,128)(2,1)S(1)}, u32[]{:S(2)}, u32[]{:S(2)}) collective-permute-start(bf16[384,128]{1,0:T(8,128)(2,1)S(1)} %bitcast.37), channel_id=1, source_target_pairs={{0,0},{1,64},{64,1},{65,65},{2,2},{3,66},{66,3},{67,67},{4,4},{5,6... | collective-permute-start | bytes 294920 | tf_op jit(solution)/shard_map/ppermute | solution.py:42
  56.2 0.6 copy-start.15
  56.8 18.5 %all-to-all-start = ((bf16[4,64,3712]{2,1,0:T(8,128)(2,1)}), bf16[4,64,3712]{2,1,0:T(8,128)(2,1)S(1)}, u32[]{:S(2)}, u32[]{:S(2)}) async-start(bf16[4,64,3712]{2,1,0:T(8,128)(2,1)} %bitcast.8), calls=%async_computation | async-start | bytes 3801088 | tf_op jit(solution)/shard_map/all_to_all | solution.py:36
  61.0 36.4 %collective-permute-start.6 = (bf16[128,3616]{0,1:T(8,128)(2,1)}, bf16[128,3616]{0,1:T(8,128)(2,1)}, u32[]{:S(2)}, u32[]{:S(2)}) collective-permute-start(bf16[128,3616]{0,1:T(8,128)(2,1)} %bitcast.14), channel_id=1, source_target_pairs={{0,1},{1,0},{2,3},{3,2},{4,5},{5,4},{6,7},{7,6},{8,9},{9,8},{10,11... | collective-permute-start | bytes 2777096 | tf_op jit(solution)/shard_map/ppermute | solution.py:30
  76.4 44.9 %copy-start.2 = (bf16[2,64,3712]{2,1,0:T(8,128)(2,1)}, bf16[2,64,3712]{2,1,0:T(8,128)(2,1)S(1)}, u32[]{:S(2)}) copy-start(bf16[2,64,3712]{2,1,0:T(8,128)(2,1)S(1)} %get-tuple-element.59) | copy-start | bytes 2850820
  76.4 25.0 %collective-permute-start.2 = (bf16[128,3712]{1,0:T(8,128)(2,1)}, bf16[128,3712]{1,0:T(8,128)(2,1)}, u32[]{:S(2)}, u32[]{:S(2)}) collective-permute-start(bf16[128,3712]{1,0:T(8,128)(2,1)} %bitcast.9.refs_0_), channel_id=1, source_target_pairs={{0,16},{1,129},{16,32},{17,145},{32,48},{33,161},{48,0},{49,177},{... | collective-permute-start | bytes 2850824 | tf_op jit(solution)/shard_map/ppermute | solution.py:26
  79.6 24.2 %collective-permute-start.3 = (bf16[128,3712]{1,0:T(8,128)(2,1)S(1)}, bf16[128,3712]{1,0:T(8,128)(2,1)}, u32[]{:S(2)}, u32[]{:S(2)}) collective-permute-start(bf16[128,3712]{1,0:T(8,128)(2,1)S(1)} %bitcast.23), channel_id=1, source_target_pairs={{0,48},{1,385},{16,0},{17,401},{32,16},{33,417},{48,32},{49,433},{... | collective-permute-start | bytes 2850824 | tf_op jit(solution)/shard_map/ppermute | solution.py:26
  83.2 24.7 %collective-permute-start.4 = (bf16[3616,128]{1,0:T(8,128)(2,1)}, bf16[3616,128]{1,0:T(8,128)(2,1)}, u32[]{:S(2)}, u32[]{:S(2)}) collective-permute-start(bf16[3616,128]{1,0:T(8,128)(2,1)} %bitcast.35), channel_id=1, source_target_pairs={{0,1},{1,0},{2,3},{3,2},{4,5},{5,4},{6,7},{7,6},{8,9},{9,8},{10,11... | collective-permute-start | bytes 2777096 | tf_op jit(solution)/shard_map/ppermute | solution.py:30
  93.1 14.8 %collective-permute-start.5 = (bf16[3616,128]{1,0:T(8,128)(2,1)}, bf16[3616,128]{1,0:T(8,128)(2,1)}, u32[]{:S(2)}, u32[]{:S(2)}) collective-permute-start(bf16[3616,128]{1,0:T(8,128)(2,1)} %bitcast.33), channel_id=1, source_target_pairs={{0,1},{1,0},{2,3},{3,2},{4,5},{5,4},{6,7},{7,6},{8,9},{9,8},{10,11... | collective-permute-start | bytes 2777096 | tf_op jit(solution)/shard_map/ppermute | solution.py:30
  99.6 8.3 %copy-start.13 = (bf16[1,3616,128]{2,1,0:T(8,128)(2,1)S(1)}, bf16[1,3616,128]{2,1,0:T(8,128)(2,1)}, u32[]{:S(2)}) copy-start(bf16[1,3616,128]{2,1,0:T(8,128)(2,1)} %param.13) | copy-start | bytes 2777092
  99.6 8.3 %copy-start.14 = (bf16[1,3616,128]{2,1,0:T(8,128)(2,1)S(1)}, bf16[1,3616,128]{2,1,0:T(8,128)(2,1)}, u32[]{:S(2)}) copy-start(bf16[1,3616,128]{2,1,0:T(8,128)(2,1)} %param.12) | copy-start | bytes 2777092
  101.4 21.8 %collective-permute-start.11 = (bf16[128,3712]{1,0:T(8,128)(2,1)}, bf16[128,3712]{1,0:T(8,128)(2,1)S(1)}, u32[]{:S(2)}, u32[]{:S(2)}) collective-permute-start(bf16[128,3712]{1,0:T(8,128)(2,1)} %collective-permute-done.2.refs_0_), channel_id=1, source_target_pairs={{0,16},{1,129},{16,32},{17,145},{32,48},{33,161},{48,0},{49,177},{... | collective-permute-start | bytes 2850824 | tf_op jit(solution)/shard_map/ppermute | solution.py:26
  103.8 24.0 %collective-permute-start.12 = (bf16[128,3712]{1,0:T(8,128)(2,1)}, bf16[128,3712]{1,0:T(8,128)(2,1)S(1)}, u32[]{:S(2)}, u32[]{:S(2)}) collective-permute-start(bf16[128,3712]{1,0:T(8,128)(2,1)} %collective-permute-done.3.refs_1_), channel_id=1, source_target_pairs={{0,48},{1,385},{16,0},{17,401},{32,16},{33,417},{48,32},{49,433},{... | collective-permute-start | bytes 2850824 | tf_op jit(solution)/shard_map/ppermute | solution.py:26
  111.2 32.9 %copy-start = (bf16[3712,512]{1,0:T(8,128)(2,1)}, bf16[3712,512]{1,0:T(8,128)(2,1)S(1)}, u32[]{:S(2)}) copy-start(bf16[3712,512]{1,0:T(8,128)(2,1)S(1)} %fusion.6.refs_2_) | copy-start | bytes 11403268
  116.0 18.0 %collective-permute-start.9 = (bf16[128,3712]{1,0:T(8,128)(2,1)S(1)}, bf16[128,3712]{1,0:T(8,128)(2,1)S(1)}, u32[]{:S(2)}, u32[]{:S(2)}) collective-permute-start(bf16[128,3712]{1,0:T(8,128)(2,1)S(1)} %get-tuple-element.36), channel_id=1, source_target_pairs={{0,48},{1,385},{16,0},{17,401},{32,16},{33,417},{48,32},{49,433},{... | collective-permute-start | bytes 2850824 | tf_op jit(solution)/shard_map/ppermute | solution.py:26
  118.0 19.4 %collective-permute-start.10 = (bf16[128,3712]{1,0:T(8,128)(2,1)S(1)}, bf16[128,3712]{1,0:T(8,128)(2,1)S(1)}, u32[]{:S(2)}, u32[]{:S(2)}) collective-permute-start(bf16[128,3712]{1,0:T(8,128)(2,1)S(1)} %get-tuple-element.37), channel_id=1, source_target_pairs={{0,16},{1,129},{16,32},{17,145},{32,48},{33,161},{48,0},{49,177},{... | collective-permute-start | bytes 2850824 | tf_op jit(solution)/shard_map/ppermute | solution.py:26
  121.3 22.9 %collective-permute-start.7 = (bf16[128,3712]{1,0:T(8,128)(2,1)S(1)}, bf16[128,3712]{1,0:T(8,128)(2,1)S(1)}, u32[]{:S(2)}, u32[]{:S(2)}) collective-permute-start(bf16[128,3712]{1,0:T(8,128)(2,1)S(1)} %bitcast.24), channel_id=1, source_target_pairs={{0,16},{1,129},{16,32},{17,145},{32,48},{33,161},{48,0},{49,177},{... | collective-permute-start | bytes 2850824 | tf_op jit(solution)/shard_map/ppermute | solution.py:26
  123.2 20.9 %collective-permute-start.8 = (bf16[128,3712]{1,0:T(8,128)(2,1)}, bf16[128,3712]{1,0:T(8,128)(2,1)S(1)}, u32[]{:S(2)}, u32[]{:S(2)}) collective-permute-start(bf16[128,3712]{1,0:T(8,128)(2,1)} %bitcast.9.refs_0_), channel_id=1, source_target_pairs={{0,48},{1,385},{16,0},{17,401},{32,16},{33,417},{48,32},{49,433},{... | collective-permute-start | bytes 2850824 | tf_op jit(solution)/shard_map/ppermute | solution.py:26
  130.9 21.6 %collective-permute-start.13 = (bf16[128,3712]{1,0:T(8,128)(2,1)}, bf16[128,3712]{1,0:T(8,128)(2,1)}, u32[]{:S(2)}, u32[]{:S(2)}) collective-permute-start(bf16[128,3712]{1,0:T(8,128)(2,1)} %get-tuple-element.45), channel_id=1, source_target_pairs={{0,48},{1,385},{16,0},{17,401},{32,16},{33,417},{48,32},{49,433},{... | collective-permute-start | bytes 2850824 | tf_op jit(solution)/shard_map/ppermute | solution.py:26
  134.0 10.2 %copy-start.11 = (bf16[128,3712]{1,0:T(8,128)(2,1)}, bf16[128,3712]{1,0:T(8,128)(2,1)S(1)}, u32[]{:S(2)}) copy-start(bf16[128,3712]{1,0:T(8,128)(2,1)S(1)} %collective-permute-done.9) | copy-start | bytes 2850820
  134.0 20.4 %collective-permute-start.14 = (bf16[128,3712]{1,0:T(8,128)(2,1)}, bf16[128,3712]{1,0:T(8,128)(2,1)}, u32[]{:S(2)}, u32[]{:S(2)}) collective-permute-start(bf16[128,3712]{1,0:T(8,128)(2,1)} %get-tuple-element.38), channel_id=1, source_target_pairs={{0,16},{1,129},{16,32},{17,145},{32,48},{33,161},{48,0},{49,177},{... | collective-permute-start | bytes 2850824 | tf_op jit(solution)/shard_map/ppermute | solution.py:26
  137.3 6.8 %copy-start.9 = (bf16[128,3712]{1,0:T(8,128)(2,1)}, bf16[128,3712]{1,0:T(8,128)(2,1)S(1)}, u32[]{:S(2)}) copy-start(bf16[128,3712]{1,0:T(8,128)(2,1)S(1)} %collective-permute-done.10) | copy-start | bytes 2850820
  146.0 1.0 copy-start.5
  147.0 0.9 copy-start.7
  148.0 1.9 copy-start.4
  149.8 2.7 %copy-start.8 = (bf16[128,3712]{1,0:T(8,128)(2,1)S(1)}, bf16[128,3712]{1,0:T(8,128)(2,1)}, u32[]{:S(2)}) copy-start(bf16[128,3712]{1,0:T(8,128)(2,1)} %copy-done.7) | copy-start | bytes 2850820
  151.5 3.0 %copy-start.6 = (bf16[128,3712]{1,0:T(8,128)(2,1)S(1)}, bf16[128,3712]{1,0:T(8,128)(2,1)}, u32[]{:S(2)}) copy-start(bf16[128,3712]{1,0:T(8,128)(2,1)} %copy-done.5) | copy-start | bytes 2850820
  152.5 10.2 %copy-start.1 = (bf16[3712,512]{1,0:T(8,128)(2,1)S(1)}, bf16[3712,512]{1,0:T(8,128)(2,1)}, u32[]{:S(2)}) copy-start(bf16[3712,512]{1,0:T(8,128)(2,1)} %copy-done) | copy-start | bytes 11403268
  154.1 8.6 %copy-start.3 = (bf16[2,64,3712]{2,1,0:T(8,128)(2,1)S(1)}, bf16[2,64,3712]{2,1,0:T(8,128)(2,1)}, u32[]{:S(2)}) copy-start(bf16[2,64,3712]{2,1,0:T(8,128)(2,1)} %copy-done.2) | copy-start | bytes 2850820
  155.8 16.1 %copy-start.12 = (bf16[128,3712]{1,0:T(8,128)(2,1)S(1)}, bf16[128,3712]{1,0:T(8,128)(2,1)}, u32[]{:S(2)}) copy-start(bf16[128,3712]{1,0:T(8,128)(2,1)} %copy-done.11) | copy-start | bytes 2850820
  155.8 16.1 %collective-permute-start.15 = (bf16[128,3712]{1,0:T(8,128)(2,1)S(1)}, bf16[128,3712]{1,0:T(8,128)(2,1)S(1)}, u32[]{:S(2)}, u32[]{:S(2)}) collective-permute-start(bf16[128,3712]{1,0:T(8,128)(2,1)S(1)} %add_convert_fusion.2), channel_id=1, source_target_pairs={{0,16},{1,129},{16,32},{17,145},{32,48},{33,161},{48,0},{49,177},{... | collective-permute-start | bytes 2850824 | tf_op jit(solution)/shard_map/ppermute | solution.py:26
  158.1 15.0 %collective-permute-start.16 = (bf16[128,3712]{1,0:T(8,128)(2,1)S(1)}, bf16[128,3712]{1,0:T(8,128)(2,1)S(1)}, u32[]{:S(2)}, u32[]{:S(2)}) collective-permute-start(bf16[128,3712]{1,0:T(8,128)(2,1)S(1)} %add_convert_fusion.3), channel_id=1, source_target_pairs={{0,48},{1,385},{16,0},{17,401},{32,16},{33,417},{48,32},{49,433},{... | collective-permute-start | bytes 2850824 | tf_op jit(solution)/shard_map/ppermute | solution.py:26
  172.0 1.2 copy-start.10
  174.9 18.2 %all-to-all-start.1 = ((bf16[4,64,3712]{2,1,0:T(8,128)(2,1)}), bf16[4,64,3712]{2,1,0:T(8,128)(2,1)S(1)}, u32[]{:S(2)}, u32[]{:S(2)}) async-start(bf16[4,64,3712]{2,1,0:T(8,128)(2,1)} %bitcast.29), calls=%async_computation.1 | async-start | bytes 3801088 | tf_op jit(solution)/shard_map/all_to_all | solution.py:36
  222.9 11.6 %collective-permute-start.17 = (bf16[32,226]{1,0:T(8,128)(2,1)S(1)}, bf16[32,226]{1,0:T(8,128)(2,1)S(1)}, u32[]{:S(2)}, u32[]{:S(2)}) collective-permute-start(bf16[32,226]{1,0:T(8,128)(2,1)S(1)} %get-tuple-element.62), channel_id=1, source_target_pairs={{0,1},{1,0},{2,3},{3,2},{4,5},{5,4},{6,7},{7,6},{8,9},{9,8},{10,11... | collective-permute-start | bytes 43400 | tf_op jit(solution)/shard_map/ppermute | solution.py:30
Sparse Core Ops, SparseCore 0:
  56.9 60.6 all-gather.3

commit v11 on v10

--- a/solution.py
+++ b/solution.py
@@ -207,14 +207,13 @@
     s = lax.all_gather(s, ("y", "c", "x"), axis=0, tiled=False)
     at = (feats - (full - 128) + 2 * per * (expert // per) + expert % per).reshape(1)
 
+    apply = lambda *blocks: ffn(at, blocks, w_in, w_out)
     w_gate, w_up, w_down = routed_gate[0], routed_up[0], routed_down[0]
-    w_in = jnp.concatenate([w_gate, swap(w_gate), w_up, swap(w_up)], 1)
+    near, o_gate, o_up, o_down = order((spread(copies), swap(w_gate), swap(w_up), swap(w_down)))
+    w_in = jnp.concatenate([w_gate, o_gate, w_up, o_up], 1)
     w_in = jnp.pad(w_in, ((0, full - feats), (0, 0)))
-    w_out = jnp.concatenate([w_down, swap(w_down)], 0)
+    w_out = jnp.concatenate([w_down, o_down], 0)
     w_out = jnp.pad(w_out, ((0, 0), (0, full - feats)))
-
-    apply = lambda *blocks: ffn(at, blocks, w_in, w_out)
-    near = spread(copies)
     lo, hi = near[: 2 * toks], near[2 * toks :]
     prev_lo, succ_hi = move(lo, 1, 1), move(hi, 1, -1)
     far_lo, far_hi = move(prev_lo, 1, 1), move(succ_hi, 1, -1)

time: 243 us -> 242 us (level)
  blocking collectives: 52.4 us -> 48 us
    ppermute x12, waiting for transfers between devices: 15.3 us -> 22.3 us  [move(): return lax.ppermute(a, ('y', 'x', 'c'), pairs)]
    all_to_all x2, waiting for transfers between devices: 21.1 us -> 14.3 us  [spread(): lax.all_to_all(a, ('y', 'x', 'c'), 0, 0, axis_index_groups=groups, tiled=...]
    all_to_all x1, blocking collectives: 27.4 us -> 23 us  [local(): back = lax.all_to_all(back, Z, split_axis=0, concat_axis=0, tiled=True)]
    ppermute x5, starting transfers between devices: 39 us -> 36.1 us  [swap(): return lax.ppermute(a, 'c', [(0, 1), (1, 0)])]
    unnamed x33 -> x43, local copies, waits for them, and re-layouts: 6.78 us -> 8.41 us
  transfers between devices with their start and end apart: 21 -> 21, of which waited for: 8 -> 10; matrix products, arithmetic and copies ran while one was open for 6% -> 6% of each run, Pallas kernels for 7% -> 7%
where the time goes in v11:
time: 242 us; the launch traced here: 239 us
  starting transfers between devices  93.8 us (39%)
  blocking collectives  48 us (20%)
  waiting for transfers between devices  38 us (16%)
  Pallas kernels  16 us (7%)
  local copies, waits for them, and re-layouts  14.9 us (6%)
  other arithmetic  14 us (6%)
  between operations  13.9 us (6%)
    ppermute x12, starting transfers between devices, move(): return lax.ppermute(a, ('y', 'x', 'c'), pairs)  39.6 us
    ppermute x5, starting transfers between devices, swap(): return lax.ppermute(a, 'c', [(0, 1), (1, 0)])  36.1 us
    all_gather x1, blocking collectives, local(): got = lax.all_gather(sent, Z, axis=0, tiled=False)  25 us
    all_to_all x1, blocking collectives, local(): back = lax.all_to_all(back, Z, split_axis=0, concat_axis=0, tiled=True)  23 us
    ppermute x12, waiting for transfers between devices, move(): return lax.ppermute(a, ('y', 'x', 'c'), pairs)  22.3 us
    all_to_all x2, waiting for transfers between devices, spread(): lax.all_to_all(a, ('y', 'x', 'c'), 0, 0, axis_index_groups=groups, tiled=...  14.3 us
    pallas_call x4, Pallas kernels, ffn(): pl.pallas_call(functools.partial(ffn_kernel, hid=hid, parts=parts), out_s...  12.7 us
    ppermute x1, starting transfers between devices, turn(): lax.ppermute(a, ('h', 'c'), [(h * 2 + c, c * 2 + h) for h in range(2) for...  9.97 us
  transfers between devices with their start and end apart: 21, of which 10 were waited for; matrix products, arithmetic and copies ran while one was open for 6% of the time, Pallas kernels for 7%

profile of v11, /device:TPU:1, one launch (start us, length us, event | category | flops | bytes accessed | tf_op | source)
XLA Modules:
  0.0 238.6 jit_solution(8515617514188612280)
XLA Ops:
  9.0 0.8 maximum_maximum_fusion
  9.9 8.8 %collective-permute-start = (bf16[32,256]{1,0:T(8,128)(2,1)S(1)}, bf16[32,256]{1,0:T(8,128)(2,1)S(1)}, u32[]{:S(2)}, u32[]{:S(2)}) collective-permute-start(bf16[32,256]{1,0:T(8,128)(2,1)S(1)} %get-tuple-element.72), channel_id=1, source_target_pairs={{0,1},{1,0},{2,3},{3,2},{4,5},{5,4},{6,7},{7,6},{8,9},{9,8},{10,11... | collective-permute-start | bytes 49160 | tf_op jit(solution)/shard_map/ppermute | solution.py:30
  19.5 10.0 %collective-permute-start.1 = (bf16[384,128]{1,0:T(8,128)(2,1)S(1)}, bf16[384,128]{1,0:T(8,128)(2,1)S(1)}, u32[]{:S(2)}, u32[]{:S(2)}) collective-permute-start(bf16[384,128]{1,0:T(8,128)(2,1)S(1)} %bitcast.35), channel_id=1, source_target_pairs={{0,0},{1,64},{64,1},{65,65},{2,2},{3,66},{66,3},{67,67},{4,4},{5,6... | collective-permute-start | bytes 294920 | tf_op jit(solution)/shard_map/ppermute | solution.py:42
  29.5 25.0 %all-gather = bf16[512,512]{1,0:T(8,128)(2,1)S(1)} all-gather(bf16[32,512]{1,0:T(8,128)(2,1)S(1)} %pad_maximum_fusion.1), channel_id=2, replica_groups=mesh['y'=4,'h'=2,'x'=4,'l'=8,'c'=2] {'h','l'}, dimensions={0}, use_global_device_ids=true | all-gather | bytes 557056 | tf_op jit(solution)/shard_map/all_gather | solution.py:205
  54.5 1.7 shard_map.91
  56.8 4.3 %all-to-all-start = ((bf16[4,64,3712]{2,1,0:T(8,128)(2,1)}), bf16[4,64,3712]{2,1,0:T(8,128)(2,1)S(1)}, u32[]{:S(2)}, u32[]{:S(2)}) async-start(bf16[4,64,3712]{2,1,0:T(8,128)(2,1)} %bitcast.8), calls=%async_computation | async-start | bytes 3801088 | tf_op jit(solution)/shard_map/all_to_all | solution.py:36
  61.1 7.7 %collective-permute-start.2 = (bf16[3616,128]{1,0:T(8,128)(2,1)}, bf16[3616,128]{1,0:T(8,128)(2,1)S(1)}, u32[]{:S(2)}, u32[]{:S(2)}) collective-permute-start(bf16[3616,128]{1,0:T(8,128)(2,1)} %bitcast.33), channel_id=1, source_target_pairs={{0,1},{1,0},{2,3},{3,2},{4,5},{5,4},{6,7},{7,6},{8,9},{9,8},{10,11... | collective-permute-start | bytes 2777096 | tf_op jit(solution)/shard_map/ppermute | solution.py:30
  68.8 1.9 collective-permute-start.3
  70.8 2.4 %collective-permute-start.4 = (bf16[128,3616]{0,1:T(8,128)(2,1)S(1)}, bf16[128,3616]{0,1:T(8,128)(2,1)}, u32[]{:S(2)}, u32[]{:S(2)}) collective-permute-start(bf16[128,3616]{0,1:T(8,128)(2,1)S(1)} %bitcast.30), channel_id=1, source_target_pairs={{0,1},{1,0},{2,3},{3,2},{4,5},{5,4},{6,7},{7,6},{8,9},{9,8},{10,11... | collective-permute-start | bytes 2777096 | tf_op jit(solution)/shard_map/ppermute | solution.py:30
  74.1 0.9 copy-done.18
  75.4 1.1 fusion.15
  76.5 4.9 %collective-permute-start.6 = (bf16[128,3712]{1,0:T(8,128)(2,1)S(1)}, bf16[128,3712]{1,0:T(8,128)(2,1)}, u32[]{:S(2)}, u32[]{:S(2)}) collective-permute-start(bf16[128,3712]{1,0:T(8,128)(2,1)S(1)} %get-tuple-element.58.refs_1_), channel_id=1, source_target_pairs={{0,48},{1,385},{16,0},{17,401},{32,16},{33,417},{48,32},{49,433},{... | collective-permute-start | bytes 2850824 | tf_op jit(solution)/shard_map/ppermute | solution.py:26
  81.4 1.9 collective-permute-start.5
  83.4 2.3 copy.25
  85.6 2.2 copy.27
  87.9 1.8 fusion.9.refs_3_
  89.7 3.0 %collective-permute-done.6.refs_1_ = bf16[128,3712]{1,0:T(8,128)(2,1)} collective-permute-done((bf16[128,3712]{1,0:T(8,128)(2,1)S(1)}, bf16[128,3712]{1,0:T(8,128)(2,1)}, u32[]{:S(2)}, u32[]{:S(2)}) %collective-permute-start.6) | collective-permute-done | bytes 950304 | tf_op jit(solution)/shard_map/ppermute | solution.py:26
  92.6 5.1 %collective-permute-start.12 = (bf16[128,3712]{1,0:T(8,128)(2,1)}, bf16[128,3712]{1,0:T(8,128)(2,1)S(1)}, u32[]{:S(2)}, u32[]{:S(2)}) collective-permute-start(bf16[128,3712]{1,0:T(8,128)(2,1)} %collective-permute-done.6.refs_1_), channel_id=1, source_target_pairs={{0,48},{1,385},{16,0},{17,401},{32,16},{33,417},{48,32},{49,433},{... | collective-permute-start | bytes 2850824 | tf_op jit(solution)/shard_map/ppermute | solution.py:26
  97.8 1.9 collective-permute-start.11
  99.7 2.2 fusion.6.refs_2_
  101.9 4.7 %shard_map.92 = (bf16[128,3712]{1,0:T(8,128)(2,1)S(1)}, bf16[128,3712]{1,0:T(8,128)(2,1)S(1)}) custom-call(s32[1]{0:T(128)} %bitcast.at_ref, bf16[128,3712]{1,0:T(8,128)(2,1)} %collective-permute-done.5.refs_0_, bf16[128,3712]{1,0:T(8,128)(2,1)} %collective-permute-done.6.refs_1_, bf16[3712,512]{1,0:T(8,128)(2,1)S(1)} %fusion.6.refs_2_, ...), custom_call_target="tpu_custom_call" | custom-call | flops 1459617792 | bytes 9502720 | tf_op jit(solution)/shard_map/pallas_call | solution.py:79
  106.6 4.6 %collective-permute-start.9 = (bf16[128,3712]{1,0:T(8,128)(2,1)S(1)}, bf16[128,3712]{1,0:T(8,128)(2,1)S(1)}, u32[]{:S(2)}, u32[]{:S(2)}) collective-permute-start(bf16[128,3712]{1,0:T(8,128)(2,1)S(1)} %get-tuple-element.44), channel_id=1, source_target_pairs={{0,48},{1,385},{16,0},{17,401},{32,16},{33,417},{48,32},{49,433},{... | collective-permute-start | bytes 2850824 | tf_op jit(solution)/shard_map/ppermute | solution.py:26
  111.2 1.9 collective-permute-start.10
  113.1 1.9 collective-permute-start.7
  115.1 5.2 %collective-permute-start.8 = (bf16[128,3712]{1,0:T(8,128)(2,1)}, bf16[128,3712]{1,0:T(8,128)(2,1)S(1)}, u32[]{:S(2)}, u32[]{:S(2)}) collective-permute-start(bf16[128,3712]{1,0:T(8,128)(2,1)} %get-tuple-element.57.refs_0_), channel_id=1, source_target_pairs={{0,48},{1,385},{16,0},{17,401},{32,16},{33,417},{48,32},{49,433},{... | collective-permute-start | bytes 2850824 | tf_op jit(solution)/shard_map/ppermute | solution.py:26
  120.3 3.2 %shard_map.93 = (bf16[128,3712]{1,0:T(8,128)(2,1)}, bf16[128,3712]{1,0:T(8,128)(2,1)}) custom-call(s32[1]{0:T(128)} %bitcast.at_ref, bf16[128,3712]{1,0:T(8,128)(2,1)S(1)} %collective-permute-done.11.refs_0_, bf16[128,3712]{1,0:T(8,128)(2,1)S(1)} %collective-permute-done.12.refs_1_, bf16[3712,512]{1,0:T(8,128)(2,1)S(1)} %fusion.6.refs_2_, ...), custom_call_target="tpu_custom_call" | custom-call | flops 1459617792 | bytes 9502720 | tf_op jit(solution)/shard_map/pallas_call | solution.py:79
  123.4 2.7 %collective-permute-start.13 = (bf16[128,3712]{1,0:T(8,128)(2,1)}, bf16[128,3712]{1,0:T(8,128)(2,1)}, u32[]{:S(2)}, u32[]{:S(2)}) collective-permute-start(bf16[128,3712]{1,0:T(8,128)(2,1)} %get-tuple-element.53), channel_id=1, source_target_pairs={{0,48},{1,385},{16,0},{17,401},{32,16},{33,417},{48,32},{49,433},{... | collective-permute-start | bytes 2850824 | tf_op jit(solution)/shard_map/ppermute | solution.py:26
  126.2 1.1 slice.37.x_ref
  127.3 2.6 %collective-permute-start.14 = (bf16[128,3712]{1,0:T(8,128)(2,1)}, bf16[128,3712]{1,0:T(8,128)(2,1)}, u32[]{:S(2)}, u32[]{:S(2)}) collective-permute-start(bf16[128,3712]{1,0:T(8,128)(2,1)} %get-tuple-element.46), channel_id=1, source_target_pairs={{0,16},{1,129},{16,32},{17,145},{32,48},{33,161},{48,0},{49,177},{... | collective-permute-start | bytes 2850824 | tf_op jit(solution)/shard_map/ppermute | solution.py:26
  130.5 10.2 %collective-permute-done.7.refs_0_ = bf16[128,3712]{1,0:T(8,128)(2,1)S(1)} collective-permute-done((bf16[128,3712]{1,0:T(8,128)(2,1)S(1)}, bf16[128,3712]{1,0:T(8,128)(2,1)S(1)}, u32[]{:S(2)}, u32[]{:S(2)}) %collective-permute-start.7) | collective-permute-done | bytes 950304 | tf_op jit(solution)/shard_map/ppermute | solution.py:26
  140.7 1.8 shard_map.94
  142.5 1.0 copy-done.5
  143.5 0.9 copy-done.7
  144.4 1.9 copy-done.4
  146.3 1.6 shard_map.95
  148.0 1.6 add_convert_fusion.3
  149.6 1.4 collective-permute-done.14
  150.9 1.4 add_convert_fusion.2
  152.4 2.1 collective-permute-start.15
  154.4 4.8 %collective-permute-start.16 = (bf16[128,3712]{1,0:T(8,128)(2,1)S(1)}, bf16[128,3712]{1,0:T(8,128)(2,1)S(1)}, u32[]{:S(2)}, u32[]{:S(2)}) collective-permute-start(bf16[128,3712]{1,0:T(8,128)(2,1)S(1)} %add_convert_fusion.3), channel_id=1, source_target_pairs={{0,48},{1,385},{16,0},{17,401},{32,16},{33,417},{48,32},{49,433},{... | collective-permute-start | bytes 2850824 | tf_op jit(solution)/shard_map/ppermute | solution.py:26
  159.2 3.0 %shard_map.96 = (bf16[128,3712]{1,0:T(8,128)(2,1)S(1)}, bf16[128,3712]{1,0:T(8,128)(2,1)S(1)}) custom-call(s32[1]{0:T(128)} %bitcast.at_ref, bf16[128,3712]{1,0:T(8,128)(2,1)} %get-tuple-element.57.refs_0_, bf16[128,3712]{1,0:T(8,128)(2,1)S(1)} %copy-done.3, bf16[3712,512]{1,0:T(8,128)(2,1)S(1)} %copy-done.1, bf16[256,3712]{1,0:T(8,128)(2,1)S(1)} %fusion.9.refs_3_), custom_call_target="tpu_custom_call" | custom-call | flops 1459617792 | bytes 9502720 | tf_op jit(solution)/shard_map/pallas_call | solution.py:79
  162.2 6.2 %collective-permute-done.15 = bf16[128,3712]{1,0:T(8,128)(2,1)S(1)} collective-permute-done((bf16[128,3712]{1,0:T(8,128)(2,1)S(1)}, bf16[128,3712]{1,0:T(8,128)(2,1)S(1)}, u32[]{:S(2)}, u32[]{:S(2)}) %collective-permute-start.15) | collective-permute-done | bytes 950304 | tf_op jit(solution)/shard_map/ppermute | solution.py:26
  170.0 1.4 pad_maximum_fusion
  171.5 3.9 %all-to-all-start.1 = ((bf16[4,64,3712]{2,1,0:T(8,128)(2,1)}), bf16[4,64,3712]{2,1,0:T(8,128)(2,1)S(1)}, u32[]{:S(2)}, u32[]{:S(2)}) async-start(bf16[4,64,3712]{2,1,0:T(8,128)(2,1)} %bitcast.26), calls=%async_computation.1 | async-start | bytes 3801088 | tf_op jit(solution)/shard_map/all_to_all | solution.py:36
  175.3 14.3 %all-to-all-done.1 = bf16[4,64,3712]{2,1,0:T(8,128)(2,1)S(1)} async-done(((bf16[4,64,3712]{2,1,0:T(8,128)(2,1)}), bf16[4,64,3712]{2,1,0:T(8,128)(2,1)S(1)}, u32[]{:S(2)}, u32[]{:S(2)}) %all-to-all-start.1) | async-done | bytes 1900576 | tf_op jit(solution)/shard_map/all_to_all | solution.py:36
  189.9 1.7 reshape.29
  191.9 23.0 %all_to_all.29 = bf16[16,64,226]{2,1,0:T(8,128)(2,1)S(1)} all-to-all(bf16[16,64,226]{2,1,0:T(8,128)(2,1)S(1)} %bitcast.29), channel_id=1, replica_groups=mesh['y'=4,'h'=2,'x'=4,'l'=8,'c'=2] {'h','l'}, dimensions={0} | all-to-all | bytes 925696 | tf_op jit(solution)/shard_map/all_to_all | solution.py:243
  215.0 15.3 %collective-permute-start.17 = (bf16[32,226]{1,0:T(8,128)(2,1)S(1)}, bf16[32,226]{1,0:T(8,128)(2,1)S(1)}, u32[]{:S(2)}, u32[]{:S(2)}) collective-permute-start(bf16[32,226]{1,0:T(8,128)(2,1)S(1)} %get-tuple-element.70), channel_id=1, source_target_pairs={{0,1},{1,0},{2,3},{3,2},{4,5},{5,4},{6,7},{7,6},{8,9},{9,8},{10,11... | collective-permute-start | bytes 43400 | tf_op jit(solution)/shard_map/ppermute | solution.py:30
  (76 shorter events, 9.6 us)
Async XLA Ops:
  6.5 137.9 %all-gather.4.cloned.1.call-start = ((), (), s32[]{:S(2)}) async-start(), calls=%async_computation.3 | async-start | bytes 3244032 | tf_op jit(solution)/shard_map/all_gather | solution.py:207
  9.9 19.6 %collective-permute-start = (bf16[32,256]{1,0:T(8,128)(2,1)S(1)}, bf16[32,256]{1,0:T(8,128)(2,1)S(1)}, u32[]{:S(2)}, u32[]{:S(2)}) collective-permute-start(bf16[32,256]{1,0:T(8,128)(2,1)S(1)} %get-tuple-element.72), channel_id=1, source_target_pairs={{0,1},{1,0},{2,3},{3,2},{4,5},{5,4},{6,7},{7,6},{8,9},{9,8},{10,11... | collective-permute-start | bytes 49160 | tf_op jit(solution)/shard_map/ppermute | solution.py:30
  19.5 36.7 %collective-permute-start.1 = (bf16[384,128]{1,0:T(8,128)(2,1)S(1)}, bf16[384,128]{1,0:T(8,128)(2,1)S(1)}, u32[]{:S(2)}, u32[]{:S(2)}) collective-permute-start(bf16[384,128]{1,0:T(8,128)(2,1)S(1)} %bitcast.35), channel_id=1, source_target_pairs={{0,0},{1,64},{64,1},{65,65},{2,2},{3,66},{66,3},{67,67},{4,4},{5,6... | collective-permute-start | bytes 294920 | tf_op jit(solution)/shard_map/ppermute | solution.py:42
  56.2 0.6 copy-start.20
  56.8 13.9 %copy-start.13 = (bf16[1,128,3616]{1,2,0:T(8,128)(2,1)S(1)}, bf16[1,128,3616]{1,2,0:T(8,128)(2,1)}, u32[]{:S(2)}) copy-start(bf16[1,128,3616]{1,2,0:T(8,128)(2,1)} %param.14) | copy-start | bytes 2777092
  56.8 18.6 %all-to-all-start = ((bf16[4,64,3712]{2,1,0:T(8,128)(2,1)}), bf16[4,64,3712]{2,1,0:T(8,128)(2,1)S(1)}, u32[]{:S(2)}, u32[]{:S(2)}) async-start(bf16[4,64,3712]{2,1,0:T(8,128)(2,1)} %bitcast.8), calls=%async_computation | async-start | bytes 3801088 | tf_op jit(solution)/shard_map/all_to_all | solution.py:36
  61.1 12.0 %collective-permute-start.2 = (bf16[3616,128]{1,0:T(8,128)(2,1)}, bf16[3616,128]{1,0:T(8,128)(2,1)S(1)}, u32[]{:S(2)}, u32[]{:S(2)}) collective-permute-start(bf16[3616,128]{1,0:T(8,128)(2,1)} %bitcast.33), channel_id=1, source_target_pairs={{0,1},{1,0},{2,3},{3,2},{4,5},{5,4},{6,7},{7,6},{8,9},{9,8},{10,11... | collective-permute-start | bytes 2777096 | tf_op jit(solution)/shard_map/ppermute | solution.py:30
  68.8 4.6 %collective-permute-start.3 = (bf16[3616,128]{1,0:T(8,128)(2,1)}, bf16[3616,128]{1,0:T(8,128)(2,1)S(1)}, u32[]{:S(2)}, u32[]{:S(2)}) collective-permute-start(bf16[3616,128]{1,0:T(8,128)(2,1)} %bitcast.31), channel_id=1, source_target_pairs={{0,1},{1,0},{2,3},{3,2},{4,5},{5,4},{6,7},{7,6},{8,9},{9,8},{10,11... | collective-permute-start | bytes 2777096 | tf_op jit(solution)/shard_map/ppermute | solution.py:30
  70.8 4.6 %collective-permute-start.4 = (bf16[128,3616]{0,1:T(8,128)(2,1)S(1)}, bf16[128,3616]{0,1:T(8,128)(2,1)}, u32[]{:S(2)}, u32[]{:S(2)}) collective-permute-start(bf16[128,3616]{0,1:T(8,128)(2,1)S(1)} %bitcast.30), channel_id=1, source_target_pairs={{0,1},{1,0},{2,3},{3,2},{4,5},{5,4},{6,7},{7,6},{8,9},{9,8},{10,11... | collective-permute-start | bytes 2777096 | tf_op jit(solution)/shard_map/ppermute | solution.py:30
  73.2 0.9 copy-start.16
  74.1 0.9 copy-start.18
  76.5 36.6 %copy-start.2 = (bf16[128,3712]{1,0:T(8,128)(2,1)}, bf16[128,3712]{1,0:T(8,128)(2,1)S(1)}, u32[]{:S(2)}) copy-start(bf16[128,3712]{1,0:T(8,128)(2,1)S(1)} %get-tuple-element.58.refs_1_) | copy-start | bytes 2850820
  76.5 16.1 %collective-permute-start.6 = (bf16[128,3712]{1,0:T(8,128)(2,1)S(1)}, bf16[128,3712]{1,0:T(8,128)(2,1)}, u32[]{:S(2)}, u32[]{:S(2)}) collective-permute-start(bf16[128,3712]{1,0:T(8,128)(2,1)S(1)} %get-tuple-element.58.refs_1_), channel_id=1, source_target_pairs={{0,48},{1,385},{16,0},{17,401},{32,16},{33,417},{48,32},{49,433},{... | collective-permute-start | bytes 2850824 | tf_op jit(solution)/shard_map/ppermute | solution.py:26
  81.4 16.3 %collective-permute-start.5 = (bf16[128,3712]{1,0:T(8,128)(2,1)}, bf16[128,3712]{1,0:T(8,128)(2,1)}, u32[]{:S(2)}, u32[]{:S(2)}) collective-permute-start(bf16[128,3712]{1,0:T(8,128)(2,1)} %get-tuple-element.57.refs_0_), channel_id=1, source_target_pairs={{0,16},{1,129},{16,32},{17,145},{32,48},{33,161},{48,0},{49,177},{... | collective-permute-start | bytes 2850824 | tf_op jit(solution)/shard_map/ppermute | solution.py:26
  87.9 11.8 %copy-start.14 = (bf16[1,3616,128]{2,1,0:T(8,128)(2,1)S(1)}, bf16[1,3616,128]{2,1,0:T(8,128)(2,1)}, u32[]{:S(2)}) copy-start(bf16[1,3616,128]{2,1,0:T(8,128)(2,1)} %param.13) | copy-start | bytes 2777092
  87.9 11.8 %copy-start.15 = (bf16[1,3616,128]{2,1,0:T(8,128)(2,1)S(1)}, bf16[1,3616,128]{2,1,0:T(8,128)(2,1)}, u32[]{:S(2)}) copy-start(bf16[1,3616,128]{2,1,0:T(8,128)(2,1)} %param.12) | copy-start | bytes 2777092
  87.9 11.8 %copy-start.17 = (bf16[3616,128]{1,0:T(8,128)(2,1)S(1)}, bf16[3616,128]{1,0:T(8,128)(2,1)}, u32[]{:S(2)}) copy-start(bf16[3616,128]{1,0:T(8,128)(2,1)} %copy-done.16) | copy-start | bytes 2777092
  87.9 11.8 %copy-start.19 = (bf16[3616,128]{1,0:T(8,128)(2,1)S(1)}, bf16[3616,128]{1,0:T(8,128)(2,1)}, u32[]{:S(2)}) copy-start(bf16[3616,128]{1,0:T(8,128)(2,1)} %copy-done.18) | copy-start | bytes 2777092
  92.6 22.4 %collective-permute-start.12 = (bf16[128,3712]{1,0:T(8,128)(2,1)}, bf16[128,3712]{1,0:T(8,128)(2,1)S(1)}, u32[]{:S(2)}, u32[]{:S(2)}) collective-permute-start(bf16[128,3712]{1,0:T(8,128)(2,1)} %collective-permute-done.6.refs_1_), channel_id=1, source_target_pairs={{0,48},{1,385},{16,0},{17,401},{32,16},{33,417},{48,32},{49,433},{... | collective-permute-start | bytes 2850824 | tf_op jit(solution)/shard_map/ppermute | solution.py:26
  97.8 22.5 %collective-permute-start.11 = (bf16[128,3712]{1,0:T(8,128)(2,1)}, bf16[128,3712]{1,0:T(8,128)(2,1)S(1)}, u32[]{:S(2)}, u32[]{:S(2)}) collective-permute-start(bf16[128,3712]{1,0:T(8,128)(2,1)} %collective-permute-done.5.refs_0_), channel_id=1, source_target_pairs={{0,16},{1,129},{16,32},{17,145},{32,48},{33,161},{48,0},{49,177},{... | collective-permute-start | bytes 2850824 | tf_op jit(solution)/shard_map/ppermute | solution.py:26
  101.9 38.8 %copy-start = (bf16[3712,512]{1,0:T(8,128)(2,1)}, bf16[3712,512]{1,0:T(8,128)(2,1)S(1)}, u32[]{:S(2)}) copy-start(bf16[3712,512]{1,0:T(8,128)(2,1)S(1)} %fusion.6.refs_2_) | copy-start | bytes 11403268
  106.6 20.6 %collective-permute-start.9 = (bf16[128,3712]{1,0:T(8,128)(2,1)S(1)}, bf16[128,3712]{1,0:T(8,128)(2,1)S(1)}, u32[]{:S(2)}, u32[]{:S(2)}) collective-permute-start(bf16[128,3712]{1,0:T(8,128)(2,1)S(1)} %get-tuple-element.44), channel_id=1, source_target_pairs={{0,48},{1,385},{16,0},{17,401},{32,16},{33,417},{48,32},{49,433},{... | collective-permute-start | bytes 2850824 | tf_op jit(solution)/shard_map/ppermute | solution.py:26
  111.2 19.3 %collective-permute-start.10 = (bf16[128,3712]{1,0:T(8,128)(2,1)S(1)}, bf16[128,3712]{1,0:T(8,128)(2,1)S(1)}, u32[]{:S(2)}, u32[]{:S(2)}) collective-permute-start(bf16[128,3712]{1,0:T(8,128)(2,1)S(1)} %get-tuple-element.45), channel_id=1, source_target_pairs={{0,16},{1,129},{16,32},{17,145},{32,48},{33,161},{48,0},{49,177},{... | collective-permute-start | bytes 2850824 | tf_op jit(solution)/shard_map/ppermute | solution.py:26
  113.1 27.5 %collective-permute-start.7 = (bf16[128,3712]{1,0:T(8,128)(2,1)S(1)}, bf16[128,3712]{1,0:T(8,128)(2,1)S(1)}, u32[]{:S(2)}, u32[]{:S(2)}) collective-permute-start(bf16[128,3712]{1,0:T(8,128)(2,1)S(1)} %get-tuple-element.58.refs_1_), channel_id=1, source_target_pairs={{0,16},{1,129},{16,32},{17,145},{32,48},{33,161},{48,0},{49,177},{... | collective-permute-start | bytes 2850824 | tf_op jit(solution)/shard_map/ppermute | solution.py:26
  115.1 25.6 %collective-permute-start.8 = (bf16[128,3712]{1,0:T(8,128)(2,1)}, bf16[128,3712]{1,0:T(8,128)(2,1)S(1)}, u32[]{:S(2)}, u32[]{:S(2)}) collective-permute-start(bf16[128,3712]{1,0:T(8,128)(2,1)} %get-tuple-element.57.refs_0_), channel_id=1, source_target_pairs={{0,48},{1,385},{16,0},{17,401},{32,16},{33,417},{48,32},{49,433},{... | collective-permute-start | bytes 2850824 | tf_op jit(solution)/shard_map/ppermute | solution.py:26
  123.4 24.5 %collective-permute-start.13 = (bf16[128,3712]{1,0:T(8,128)(2,1)}, bf16[128,3712]{1,0:T(8,128)(2,1)}, u32[]{:S(2)}, u32[]{:S(2)}) collective-permute-start(bf16[128,3712]{1,0:T(8,128)(2,1)} %get-tuple-element.53), channel_id=1, source_target_pairs={{0,48},{1,385},{16,0},{17,401},{32,16},{33,417},{48,32},{49,433},{... | collective-permute-start | bytes 2850824 | tf_op jit(solution)/shard_map/ppermute | solution.py:26
  127.2 13.4 %copy-start.11 = (bf16[128,3712]{1,0:T(8,128)(2,1)}, bf16[128,3712]{1,0:T(8,128)(2,1)S(1)}, u32[]{:S(2)}) copy-start(bf16[128,3712]{1,0:T(8,128)(2,1)S(1)} %collective-permute-done.9) | copy-start | bytes 2850820
  127.3 23.7 %collective-permute-start.14 = (bf16[128,3712]{1,0:T(8,128)(2,1)}, bf16[128,3712]{1,0:T(8,128)(2,1)}, u32[]{:S(2)}, u32[]{:S(2)}) collective-permute-start(bf16[128,3712]{1,0:T(8,128)(2,1)} %get-tuple-element.46), channel_id=1, source_target_pairs={{0,16},{1,129},{16,32},{17,145},{32,48},{33,161},{48,0},{49,177},{... | collective-permute-start | bytes 2850824 | tf_op jit(solution)/shard_map/ppermute | solution.py:26
  130.5 10.2 %copy-start.9 = (bf16[128,3712]{1,0:T(8,128)(2,1)}, bf16[128,3712]{1,0:T(8,128)(2,1)S(1)}, u32[]{:S(2)}) copy-start(bf16[128,3712]{1,0:T(8,128)(2,1)S(1)} %collective-permute-done.10) | copy-start | bytes 2850820
  142.5 1.0 copy-start.5
  143.5 0.9 copy-start.7
  144.4 1.9 copy-start.4
  146.3 1.6 copy-start.8
  147.9 3.0 %copy-start.6 = (bf16[128,3712]{1,0:T(8,128)(2,1)S(1)}, bf16[128,3712]{1,0:T(8,128)(2,1)}, u32[]{:S(2)}) copy-start(bf16[128,3712]{1,0:T(8,128)(2,1)} %copy-done.5) | copy-start | bytes 2850820
  148.0 11.2 %copy-start.1 = (bf16[3712,512]{1,0:T(8,128)(2,1)S(1)}, bf16[3712,512]{1,0:T(8,128)(2,1)}, u32[]{:S(2)}) copy-start(bf16[3712,512]{1,0:T(8,128)(2,1)} %copy-done) | copy-start | bytes 11403268
  149.5 9.7 %copy-start.3 = (bf16[128,3712]{1,0:T(8,128)(2,1)S(1)}, bf16[128,3712]{1,0:T(8,128)(2,1)}, u32[]{:S(2)}) copy-start(bf16[128,3712]{1,0:T(8,128)(2,1)} %copy-done.2) | copy-start | bytes 2850820
  152.4 16.1 %copy-start.12 = (bf16[128,3712]{1,0:T(8,128)(2,1)S(1)}, bf16[128,3712]{1,0:T(8,128)(2,1)}, u32[]{:S(2)}) copy-start(bf16[128,3712]{1,0:T(8,128)(2,1)} %copy-done.11) | copy-start | bytes 2850820
  152.4 16.1 %collective-permute-start.15 = (bf16[128,3712]{1,0:T(8,128)(2,1)S(1)}, bf16[128,3712]{1,0:T(8,128)(2,1)S(1)}, u32[]{:S(2)}, u32[]{:S(2)}) collective-permute-start(bf16[128,3712]{1,0:T(8,128)(2,1)S(1)} %add_convert_fusion.2), channel_id=1, source_target_pairs={{0,16},{1,129},{16,32},{17,145},{32,48},{33,161},{48,0},{49,177},{... | collective-permute-start | bytes 2850824 | tf_op jit(solution)/shard_map/ppermute | solution.py:26
  154.4 15.2 %collective-permute-start.16 = (bf16[128,3712]{1,0:T(8,128)(2,1)S(1)}, bf16[128,3712]{1,0:T(8,128)(2,1)S(1)}, u32[]{:S(2)}, u32[]{:S(2)}) collective-permute-start(bf16[128,3712]{1,0:T(8,128)(2,1)S(1)} %add_convert_fusion.3), channel_id=1, source_target_pairs={{0,48},{1,385},{16,0},{17,401},{32,16},{33,417},{48,32},{49,433},{... | collective-permute-start | bytes 2850824 | tf_op jit(solution)/shard_map/ppermute | solution.py:26
  168.5 1.2 copy-start.10
  171.5 18.2 %all-to-all-start.1 = ((bf16[4,64,3712]{2,1,0:T(8,128)(2,1)}), bf16[4,64,3712]{2,1,0:T(8,128)(2,1)S(1)}, u32[]{:S(2)}, u32[]{:S(2)}) async-start(bf16[4,64,3712]{2,1,0:T(8,128)(2,1)} %bitcast.26), calls=%async_computation.1 | async-start | bytes 3801088 | tf_op jit(solution)/shard_map/all_to_all | solution.py:36
  215.0 16.1 %collective-permute-start.17 = (bf16[32,226]{1,0:T(8,128)(2,1)S(1)}, bf16[32,226]{1,0:T(8,128)(2,1)S(1)}, u32[]{:S(2)}, u32[]{:S(2)}) collective-permute-start(bf16[32,226]{1,0:T(8,128)(2,1)S(1)} %get-tuple-element.70), channel_id=1, source_target_pairs={{0,1},{1,0},{2,3},{3,2},{4,5},{5,4},{6,7},{7,6},{8,9},{9,8},{10,11... | collective-permute-start | bytes 43400 | tf_op jit(solution)/shard_map/ppermute | solution.py:30
Sparse Core Ops, SparseCore 0:
  56.9 60.9 all-gather.3
